TPU v7x, 32 devices: a whole 2x2x4 slice. The times are simulated.
32 devices in a mesh: dp: 16 (over z, y, x), tensor: 2 (over core).
Axes of the slice: x: 2, y: 2, z: 4, core: 2. Of those that a mesh axis runs over, the one named last changes fastest.
Arguments:
- inputs: bfloat16 [2048, 4096], P(('dp', 'tensor')), may hold values from -6 to 6
- out_grad: bfloat16 [2048, 14336], P('dp', 'tensor'), may hold values from -6 to 6
- weight: bfloat16 [4096, 14336], P('dp', 'tensor'), may hold values from -0.09375 to 0.09375
- proj_basis: float32 [4096, 64], replicated, may hold values from -0.09375 to 0.09375
- momentum: float32 [4096, 14336], P('dp', 'tensor'), may hold values from -4 to 4
Outputs:
- input_grad: bfloat16 [2048, 4096], P(('dp', 'tensor'))
- new_momentum: float32 [4096, 14336], P('dp', 'tensor')
All inputs are finite; a program needn't handle non-finite values.
Results may differ from a plain program's by a relative error of at most 0.017.
Values may be sent and summed in bfloat16 or wider, within the bound.
No kernel may reach another device: no remote copies, remote signals or barrier semaphores. Data moves between devices by JAX's collectives and lax.ppermute only.
A program may use at most 128 MiB of HBM per device.

v0:
```python
import math

import jax
import jax.numpy as jnp
from jax import lax
from jax.sharding import PartitionSpec as P

D = 4096
RANK = 64


momentum_decay = 0.9


def local(inputs, out_grad, weight, proj_basis, momentum):
    local_proj = jnp.dot(inputs.astype(jnp.float32), proj_basis, precision=lax.Precision.HIGHEST)
    projected = lax.all_gather(local_proj, "tensor", axis=0, tiled=True).astype(jnp.bfloat16)
    local_panel = lax.dot_general(
        projected, out_grad, (((0,), (0,)), ((), ())), preferred_element_type=jnp.float32
    )
    grad_panel = lax.psum(local_panel, "dp")
    tokens_all = out_grad.shape[0] * lax.axis_size("dp")
    grad_panel = grad_panel / math.sqrt(tokens_all)
    row_count = momentum.shape[0]
    basis_rows = lax.dynamic_slice_in_dim(
        proj_basis, lax.axis_index("dp") * row_count, row_count, 0
    )
    update = jnp.dot(basis_rows, grad_panel, precision=lax.Precision.HIGHEST) * math.sqrt(D / RANK)
    new_momentum = momentum_decay * momentum + update
    partial_value = lax.dot_general(
        out_grad,
        lax.all_gather(weight, "dp", axis=0, tiled=True),
        (((1,), (1,)), ((), ())),
        preferred_element_type=jnp.float32,
    )
    input_grad = lax.psum_scatter(
        partial_value.astype(jnp.bfloat16), "tensor", scatter_dimension=0, tiled=True
    )
    return (input_grad, new_momentum)


def solution(mesh):
    placed = (
        P(("dp", "tensor"), None),
        P("dp", "tensor"),
        P("dp", "tensor"),
        P(),
        P("dp", "tensor"),
    )
    return jax.shard_map(
        local,
        mesh=mesh,
        in_specs=placed,
        out_specs=(P(("dp", "tensor"), None), P("dp", "tensor")),
        check_vma=False,
    )
```

profile of v0, /device:TPU:0, one launch (start us, length us, event | category | flops | bytes accessed | tf_op | source)
XLA Modules:
  0.0 745.9 jit_solution(11059568686879658784)
XLA Ops:
  7.2 0.0 copy-start
  7.2 0.0 copy-start.3
  7.2 0.0 copy-start.2
  7.2 0.0 all-gather.2.cloned.1.call-start
  7.2 0.7 all-gather.2.cloned.1.call-update
  7.9 0.0 all-reduce.2.cloned.1.call-start
  8.0 0.4 copy-done.3
  8.4 0.3 copy-done.2
  8.7 0.6 fusion.8
  9.3 1.9 all_gather.7
  11.3 0.0 copy-done
  11.3 1.7 fusion.9
  13.0 0.0 all-reduce.2.cloned.1.call-update
  13.0 0.0 reduce-scatter.2.cloned.1.call-start
  13.0 589.1 %all-gather.2.cloned.1.call-done = bf16[4096,7168]{1,0:T(8,128)(2,1)} async-done(((bf16[256,7168]{1,0:T(8,128)(2,1)}), bf16[4096,7168]{1,0:T(8,128)(2,1)}) %all-gather.2.cloned.1.call-update) | async-done | bytes 58720272 | tf_op jit(solution)/shard_map/all_gather | solution.py:32
  602.2 26.1 %convolution_convert_fusion = bf16[128,4096]{1,0:T(8,128)(2,1)} fusion(bf16[128,7168]{1,0:T(8,128)(2,1)S(1)} %copy-done, bf16[4096,7168]{1,0:T(8,128)(2,1)} %all-gather.2.cloned.1.call-done), kind=kOutput, calls=%fused_computation.2 | convolution fusion | flops 7516717056 | bytes 61603840 | tf_op jit(solution)/shard_map/dot_general | solution.py:30
  628.3 0.0 reduce-scatter.2.cloned.1.call-update
  628.3 99.6 %all-reduce.2.cloned.1.call-done = f32[64,7168]{1,0:T(8,128)} async-done(((f32[64,7168]{1,0:T(8,128)}), f32[64,7168]{1,0:T(8,128)}) %all-reduce.2.cloned.1.call-update) | async-done | bytes 1835024 | tf_op jit(solution)/shard_map/psum | solution.py:21
  727.9 0.0 copy-start.1
  727.9 11.5 %fusion = f32[256,7168]{1,0:T(8,128)} fusion(f32[256,7168]{1,0:T(8,128)} %param.9, f32[64,7168]{1,0:T(8,128)} %all-reduce.2.cloned.1.call-done, f32[4096,64]{0,1:T(8,128)S(1)} %copy-done.2, s32[]{:T(128)S(6)} %select_n.3), kind=kOutput, calls=%fused_computation.1 | convolution fusion | flops 1415249920 | bytes 16580612 | tf_op jit(solution)/shard_map/dot_general | solution.py:28
  739.4 0.0 reduce-scatter.2.cloned.1.call-done
  739.4 0.0 copy-done.1
Async XLA Ops:
  7.2 4.1 copy-start
  7.2 1.2 copy-start.3
  7.2 1.5 copy-start.2
  7.2 595.0 %all-gather.2.cloned.1.call-start = ((), (), s32[]{:S(2)}) async-start(), calls=%async_computation.1 | async-start | bytes 62390272 | tf_op jit(solution)/shard_map/all_gather | solution.py:32
  7.9 720.0 %all-reduce.2.cloned.1.call-start = ((), (), s32[]{:S(2)}) async-start(), calls=%async_computation.3 | async-start | bytes 3670016 | tf_op jit(solution)/shard_map/psum | solution.py:21
  13.0 726.4 %reduce-scatter.2.cloned.1.call-start = ((), (), s32[]{:S(2)}) async-start(), calls=%async_computation.2 | async-start | bytes 1572864 | tf_op jit(solution)/shard_map/reduce_scatter | solution.py:36
  727.9 11.5 %copy-start.1 = (bf16[128,7168]{1,0:T(8,128)(2,1)S(1)}, bf16[128,7168]{1,0:T(8,128)(2,1)}, u32[]{:S(2)}) copy-start(bf16[128,7168]{1,0:T(8,128)(2,1)} %param.6) | copy-start | bytes 5505028
Sparse Core Ops, SparseCore 0:
  10.8 591.3 all-gather.1
  608.2 119.6 all-reduce.1
  730.8 7.7 reduce-scatter.1
where the time goes:
time: 746 us
  waiting for transfers between devices  689 us (92%)
  matrix products  39.9 us (5%)
  between operations  13.8 us (2%)
    all_gather x1, waiting for transfers between devices, local(): lax.all_gather(weight, 'dp', axis=0, tiled=True)  589 us
    psum x1, waiting for transfers between devices, local(): grad_panel = lax.psum(local_panel, 'dp')  99.6 us
    dot_general x1, matrix products, local(): lax.dot_general(out_grad, lax.all_gather(weight, 'dp', axis=0, tiled=True...  26.1 us
  transfers between devices with their start and end apart: 3, of which 2 were waited for; matrix products, arithmetic and copies ran while one was open for 5% of the time, Pallas kernels for 0%

commit v1 on v0

v1 whole, which is shorter than its diff:
```python
import math

import jax
import jax.numpy as jnp
from jax import lax
from jax.sharding import PartitionSpec as P

momentum_decay = 0.9
PLANE = 4
f32, bf16 = jnp.float32, jnp.bfloat16


def after(x, *first):
    return lax.optimization_barrier((x, first))[0]


def nt(a, b):
    return lax.dot_general(a, b, (((1,), (1,)), ((), ())), preferred_element_type=f32)


def tn(a, b):
    return lax.dot_general(a, b, (((0,), (0,)), ((), ())), preferred_element_type=f32)


class Layout:
    def __init__(self):
        self.replicas, self.cores = lax.axis_size("dp"), lax.axis_size("tensor")
        self.line = self.replicas // PLANE
        self.me, self.core = lax.axis_index("dp"), lax.axis_index("tensor")
        self.place, self.level = self.me % PLANE, self.me // PLANE

    def across(self, x, r):
        return lax.ppermute(x, "dp", [(d, d ^ r) for d in range(self.replicas)])

    def levels(self, x, s, only=None):
        pairs = [
            (d, d ^ (s * PLANE)) for d in range(self.replicas) if only is None or d // PLANE in only
        ]
        return lax.ppermute(x, "dp", pairs)

    def cut(self, x, r):
        quarter = x.shape[1] // PLANE
        return lax.dynamic_slice_in_dim(x, (self.place ^ r) * quarter, quarter, 1)

    def in_order(self, parts, axis):
        size = parts[0].shape[axis]
        shape = list(parts[0].shape)
        shape[axis] *= PLANE
        whole = jnp.zeros(shape, parts[0].dtype)
        for r, part in enumerate(parts):
            whole = lax.dynamic_update_slice_in_dim(whole, part, (self.place ^ r) * size, axis)
        return whole

    def core_sum(self, part, lines):
        width = part.shape[1]
        if self.cores == 2:
            part = part.reshape(lines, 2, -1, width)
            keep = lax.dynamic_index_in_dim(part, self.core, 1, False)
            give = lax.dynamic_index_in_dim(part, 1 - self.core, 1, False)
            got = lax.ppermute(give, "tensor", [(0, 1), (1, 0)])
            return (keep.astype(f32) + got.astype(f32)).astype(bf16)
        return lax.psum_scatter(
            part.reshape(lines, -1, width), "tensor", scatter_dimension=1, tiled=True
        )


def projected(lay, inputs, proj_basis):
    proj = jnp.dot(inputs.astype(f32), proj_basis, precision=lax.Precision.HIGHEST).astype(bf16)
    proj = lax.all_gather(proj, "tensor", axis=0, tiled=True)
    return [proj] + [lay.across(proj, r) for r in range(1, PLANE)]


def panel_shares(lay, plane_proj, pieces):
    panel = sum(tn(q, a) for q, a in zip(plane_proj, pieces))
    share = panel.shape[0] // lay.line
    share_of = lambda x, s: lax.dynamic_slice_in_dim(x, (lay.level ^ s) * share, share, 0)
    half = panel.astype(bf16)
    return [share_of(panel, 0)] + [lay.levels(share_of(half, s), s) for s in range(1, lay.line)]


def panel_quarter(lay, shares):
    summed = sum(x.astype(f32) for x in shares).astype(bf16)
    share, quarter = summed.shape
    panel_q = jnp.zeros((share * lay.line, quarter), bf16)
    for s in range(lay.line):
        got = lay.levels(summed, s) if s else summed
        panel_q = lax.dynamic_update_slice_in_dim(panel_q, got, (lay.level ^ s) * share, 0)
    return panel_q


def panel_whole(lay, panel_q):
    return lay.in_order([panel_q] + [lay.across(panel_q, r) for r in range(1, PLANE)], 1)


def updated(lay, proj_basis, panel, momentum, tokens):
    rows, rank = momentum.shape[0], proj_basis.shape[1]
    basis_rows = lax.dynamic_slice_in_dim(proj_basis, lay.me * rows, rows, 0)
    scale = math.sqrt(proj_basis.shape[0] / rank) / math.sqrt(tokens)
    update = jnp.dot(basis_rows.astype(bf16), panel, preferred_element_type=f32)
    return momentum_decay * momentum + update * scale


def long_line(inputs, out_grad, weight, proj_basis, momentum):
    lay = Layout()
    line, level, cores = lay.line, lay.level, lay.cores
    tokens = out_grad.shape[0]
    pieces = [lay.cut(out_grad, 0)] + [lay.across(lay.cut(out_grad, r), r) for r in range(1, PLANE)]
    weights = [lay.cut(weight, 0)] + [lay.across(lay.cut(weight, r), r) for r in range(1, PLANE)]
    groups = [[p + PLANE * z for z in range(line)] for p in range(PLANE)]
    shares = panel_shares(lay, projected(lay, inputs, proj_basis), pieces)
    panel = panel_whole(lay, panel_quarter(lay, shares))
    new_momentum = updated(lay, proj_basis, panel, momentum, tokens * lay.replicas)
    held = lay.in_order(weights, 0)
    width = held.shape[0]
    total = 0.0
    for r, piece in enumerate(pieces):
        block = lax.all_gather(piece, "dp", axis_index_groups=groups, axis=0, tiled=True)
        part = lay.core_sum(nt(block, held).astype(bf16), line)
        total = total + (lay.across(part, r) if r else part).astype(f32)
    total = total.astype(bf16)
    input_grad = jnp.zeros((tokens // cores, line * width), bf16)
    for s in range(line):
        got = lax.dynamic_index_in_dim(total, level ^ s, 0, False)
        got = lay.levels(got, s) if s else got
        input_grad = lax.dynamic_update_slice_in_dim(input_grad, got, (level ^ s) * width, 1)
    return input_grad, new_momentum


def line_of_four(inputs, out_grad, weight, proj_basis, momentum):
    lay = Layout()
    level, across = lay.level, lay.across
    inner = (level == 1) | (level == 2)
    tokens, hidden = out_grad.shape
    half = hidden // PLANE // 2
    end_swap = lambda x: lay.levels(x, 1)
    mid_swap = lambda x: lay.levels(x, 3, (1, 2))

    a0 = lay.cut(out_grad, 0)
    e0, m0 = end_swap(a0), mid_swap(a0)
    ax, ay = across(lay.cut(out_grad, 1), 1), across(lay.cut(out_grad, 2), 2)
    ad = across(after(lay.cut(out_grad, 3), ax, ay, e0, m0), 3)
    axy = jnp.concatenate([ax, ay], 0)
    axy = after(axy, e0, m0)
    e1, m1 = end_swap(axy), mid_swap(axy)
    plane_proj = projected(lay, after(inputs, a0), proj_basis)
    weight = after(weight, ax, ay)
    w1 = [lay.cut(weight, r)[:, half:] for r in range(PLANE)]
    w0 = [lay.cut(weight, r)[:, :half] for r in range(PLANE)]
    w1 = w1[:1] + [across(after(w1[r], ad), r) for r in range(1, PLANE)]
    shares = panel_shares(lay, plane_proj, [a0, ax, ay, ad])
    e2, m2 = end_swap(ad), mid_swap(ad)
    w0 = w0[:1] + [across(after(w0[r], *w1[1:]), r) for r in range(1, PLANE)]

    near_e, near_m = jnp.concatenate([e0, e1, e2], 0), jnp.concatenate([m0, m1, m2], 0)
    held1 = lay.in_order(w1, 0)
    cut_rows = held1.shape[0] // 2
    send = lambda a, w: jnp.where(inner, a, w)
    far0 = mid_swap(near_e[:, :half])
    got_a = end_swap(send(near_m[:, :half], held1[:cut_rows]))
    panel_q = panel_quarter(lay, shares)
    far1 = mid_swap(after(near_e[:, half:], far0))
    got_b = end_swap(send(far0, after(held1[cut_rows:], got_a)))
    panel = panel_whole(lay, after(panel_q, *w0[1:]))
    held0 = lay.in_order(w0, 0)
    held = jnp.concatenate([held0, held1], 1)
    width = held.shape[0]

    def plane_sum(part):
        part = lay.core_sum(part, PLANE)
        total = part[0].astype(f32)
        for r in range(1, PLANE):
            total = total + across(part[r], r).astype(f32)
        return total.astype(bf16)

    own = jnp.concatenate([a0, axy, ad], 0)
    y0, y1 = nt(own, held).astype(bf16), nt(near_e, held).astype(bf16)
    early = (nt(send(near_m[:, :half], got_a), held0) + nt(near_m[:, half:], held1)).astype(bf16)
    first = plane_sum(jnp.concatenate([y0, y1, early], 1))
    new_momentum = updated(lay, proj_basis, panel, momentum, tokens * lay.replicas)

    far1 = after(far1, new_momentum)
    late = (nt(send(far0, got_b), held0) + nt(far1, held1)).astype(bf16)
    other = jnp.concatenate([got_a, got_b], 0)
    early_other = nt(near_m[:, half:], other).astype(bf16)
    late_other = nt(far1, other).astype(bf16)
    second = plane_sum(after(jnp.concatenate([late, early_other, late_other], 1), first))
    y0, y1, early = [first[:, i * width:(i + 1) * width] for i in range(3)]
    late, early_other, late_other = [second[:, i * width:(i + 1) * width] for i in range(3)]

    z1 = end_swap(y1)
    z3 = mid_swap(early)
    z2 = lay.levels(early, 2, (0, 3))
    z2b = mid_swap(early_other)
    z_late = lay.levels(jnp.concatenate([late, late_other], 1), 2, (1, 2))
    z3b = lay.levels(late, 3, (0, 3))
    add = lambda *xs: sum(x.astype(f32) for x in xs).astype(bf16)
    z2 = add(z2, z2b, z_late[:, :width])
    z3 = add(z3, z3b, z_late[:, width:])
    by_distance = [y0, z1, z2, z3]
    input_grad = jnp.concatenate(
        [
            jnp.where(
                level == b,
                y0,
                jnp.where(level == b ^ 1, z1, jnp.where(level == b ^ 2, z2, z3)),
            )
            for b in range(len(by_distance))
        ],
        1,
    )
    return input_grad, new_momentum


def solution(mesh):
    placed = (
        P(("dp", "tensor"), None),
        P("dp", "tensor"),
        P("dp", "tensor"),
        P(),
        P("dp", "tensor"),
    )
    four = mesh.shape["dp"] == 4 * PLANE
    return jax.shard_map(
        line_of_four if four else long_line,
        mesh=mesh,
        in_specs=placed,
        out_specs=(P(("dp", "tensor"), None), P("dp", "tensor")),
        check_vma=False,
    )
```

time: 746 us -> 201 us (0.27)
  waiting for transfers between devices: 689 us -> 97.9 us
  starting transfers between devices: 0.12 us -> 70.7 us
  matrix products: 39.9 us -> 18 us
  between operations: 13.8 us -> 1.38 us
    all_gather x1 -> x0, waiting for transfers between devices: 589 us -> none  [local(): lax.all_gather(weight, 'dp', axis=0, tiled=True)]
    psum x1 -> x0, waiting for transfers between devices: 99.6 us -> none  [local(): grad_panel = lax.psum(local_panel, 'dp')]
    ppermute x0 -> x45, waiting for transfers between devices: none -> 97.9 us  [the longest x21 53.3 us: across(): return lax.ppermute(x, 'dp', [(d, d ^ r) for d in range(self.replicas)])]
    ppermute x0 -> x45, starting transfers between devices: none -> 70.7 us  [the longest x22 45.8 us: levels(): return lax.ppermute(x, 'dp', pairs)]
    dot_general x4 -> x14, matrix products: 39.9 us -> 18 us  [the longest x8 11.9 us: nt(): lax.dot_general(a, b, (((1,), (1,)), ((), ())), preferred_element_type=f32)]
  transfers between devices with their start and end apart: 3 -> 45, of which waited for: 2 -> 23; matrix products, arithmetic and copies ran while one was open for 5% -> 12% of each run, Pallas kernels for 0% -> 0%
where the time goes in v1:
time: 201 us; the launch traced here: 200 us
  waiting for transfers between devices  97.9 us (49%)
  starting transfers between devices  70.7 us (35%)
  matrix products  18 us (9%)
  local copies, waits for them, and re-layouts  6.85 us (3%)
  other arithmetic  3.54 us (2%)
    ppermute x21, waiting for transfers between devices, across(): return lax.ppermute(x, 'dp', [(d, d ^ r) for d in range(self.replicas)])  53.3 us
    ppermute x22, starting transfers between devices, levels(): return lax.ppermute(x, 'dp', pairs)  45.8 us
    ppermute x22, waiting for transfers between devices, levels(): return lax.ppermute(x, 'dp', pairs)  41.2 us
    ppermute x21, starting transfers between devices, across(): return lax.ppermute(x, 'dp', [(d, d ^ r) for d in range(self.replicas)])  24.8 us
    dot_general x8, matrix products, nt(): lax.dot_general(a, b, (((1,), (1,)), ((), ())), preferred_element_type=f32)  11.9 us
    dot_general x1, matrix products, updated(): update = jnp.dot(basis_rows.astype(bf16), panel, preferred_element_type=f32)  4.46 us
  transfers between devices with their start and end apart: 45, of which 23 were waited for; matrix products, arithmetic and copies ran while one was open for 12% of the time, Pallas kernels for 0%

profile of v1, /device:TPU:0, one launch (start us, length us, event | category | flops | bytes accessed | tf_op | source)
XLA Modules:
  0.0 200.2 jit_solution(11688568306172875397)
XLA Ops:
  0.7 2.4 %constant_dynamic-slice_fusion.12 = (bf16[128,1792]{1,0:T(8,128)(2,1)S(1)}, bf16[128,1792]{1,0:T(8,128)(2,1)}, bf16[128,1792]{1,0:T(8,128)(2,1)S(1)}, bf16[128,1792]{1,0:T(8,128)(2,1)S(1)}) fusion(bf16[128,7168]{1,0:T(8,128)(2,1)} %param.6, s32[]{:T(128)S(6)} %select_n.160, s32[]{:T(128)S(6)} %select_n.161, s32[]{:T(128)S(6)} %select_n.163, s32[]{:T(128)S(6)} %select_n.162), kind=kLoop, calls=%fused_computation.102 | loop fusion | bytes 3670032 | tf_op jit(solution)/shard_map/dynamic_slice | solution.py:43
  4.6 5.1 %collective-permute-start.2 = (bf16[128,1792]{1,0:T(8,128)(2,1)S(1)}, bf16[128,1792]{1,0:T(8,128)(2,1)}, u32[]{:S(2)}, u32[]{:S(2)}) collective-permute-start(bf16[128,1792]{1,0:T(8,128)(2,1)S(1)} %get-tuple-element.48), channel_id=1, source_target_pairs={{0,8},{2,10},{4,12},{6,14},{8,0},{10,2},{12,4},{14,6},{16,24},{18,... | collective-permute-start | bytes 1376264 | tf_op jit(solution)/shard_map/ppermute | solution.py:39
  16.0 6.0 %collective-permute-done = bf16[128,1792]{1,0:T(8,128)(2,1)S(1)} collective-permute-done((bf16[128,1792]{1,0:T(8,128)(2,1)}, bf16[128,1792]{1,0:T(8,128)(2,1)S(1)}, u32[]{:S(2)}, u32[]{:S(2)}) %collective-permute-start) | collective-permute-done | bytes 458784 | tf_op jit(solution)/shard_map/ppermute | solution.py:33
  25.8 2.6 %collective-permute-start.11 = (bf16[256,1792]{1,0:T(8,128)(2,1)S(1)}, bf16[256,1792]{1,0:T(8,128)(2,1)S(1)}, u32[]{:S(2)}, u32[]{:S(2)}) collective-permute-start(bf16[256,1792]{1,0:T(8,128)(2,1)S(1)} %pad_maximum_fusion.9), channel_id=1, source_target_pairs={{0,8},{2,10},{4,12},{6,14},{8,0},{10,2},{12,4},{14,6},{16,24},{18,... | collective-permute-start | bytes 2752520 | tf_op jit(solution)/shard_map/ppermute | solution.py:39
  32.4 6.6 %collective-permute-done.4 = bf16[128,1792]{1,0:T(8,128)(2,1)S(1)} collective-permute-done((bf16[128,1792]{1,0:T(8,128)(2,1)S(1)}, bf16[128,1792]{1,0:T(8,128)(2,1)S(1)}, u32[]{:S(2)}, u32[]{:S(2)}) %collective-permute-start.4) | collective-permute-done | bytes 458784 | tf_op jit(solution)/shard_map/ppermute | solution.py:33
  43.7 5.2 %collective-permute-done.28 = bf16[16,1792]{1,0:T(8,128)(2,1)S(1)} collective-permute-done((bf16[16,1792]{1,0:T(8,128)(2,1)S(1)}, bf16[16,1792]{1,0:T(8,128)(2,1)S(1)}, u32[]{:S(2)}, u32[]{:S(2)}) %collective-permute-start.28) | collective-permute-done | bytes 57376 | tf_op jit(solution)/shard_map/ppermute | solution.py:39
  57.5 4.3 %collective-permute-done.32 = bf16[16,1792]{1,0:T(8,128)(2,1)S(1)} collective-permute-done((bf16[16,1792]{1,0:T(8,128)(2,1)S(1)}, bf16[16,1792]{1,0:T(8,128)(2,1)S(1)}, u32[]{:S(2)}, u32[]{:S(2)}) %collective-permute-start.32) | collective-permute-done | bytes 57376 | tf_op jit(solution)/shard_map/ppermute | solution.py:39
  63.7 4.8 %collective-permute-done.33 = bf16[16,1792]{1,0:T(8,128)(2,1)S(1)} collective-permute-done((bf16[16,1792]{1,0:T(8,128)(2,1)S(1)}, bf16[16,1792]{1,0:T(8,128)(2,1)S(1)}, u32[]{:S(2)}, u32[]{:S(2)}) %collective-permute-start.33) | collective-permute-done | bytes 57376 | tf_op jit(solution)/shard_map/ppermute | solution.py:39
  69.1 7.9 %collective-permute-done.12 = bf16[128,1792]{1,0:T(8,128)(2,1)S(1)} collective-permute-done((bf16[128,1792]{1,0:T(8,128)(2,1)S(1)}, bf16[128,1792]{1,0:T(8,128)(2,1)S(1)}, u32[]{:S(2)}, u32[]{:S(2)}) %collective-permute-start.12) | collective-permute-done | bytes 458784 | tf_op jit(solution)/shard_map/ppermute | solution.py:39
  78.5 4.2 %collective-permute-done.7 = bf16[256,896]{1,0:T(8,128)(2,1)S(1)} collective-permute-done((bf16[256,896]{1,0:T(8,128)(2,1)S(1)}, bf16[256,896]{1,0:T(8,128)(2,1)S(1)}, u32[]{:S(2)}, u32[]{:S(2)}) %collective-permute-start.7) | collective-permute-done | bytes 458784 | tf_op jit(solution)/shard_map/ppermute | solution.py:33
  83.4 2.9 %collective-permute-start.10 = (bf16[256,896]{1,0:T(8,128)(2,1)S(1)}, bf16[256,896]{1,0:T(8,128)(2,1)S(1)}, u32[]{:S(2)}, u32[]{:S(2)}) collective-permute-start(bf16[256,896]{1,0:T(8,128)(2,1)S(1)} %get-tuple-element.25), channel_id=1, source_target_pairs={{0,6},{2,4},{4,2},{6,0},{8,14},{10,12},{12,10},{14,8},{16,22},{18,... | collective-permute-start | bytes 1376264 | tf_op jit(solution)/shard_map/ppermute | solution.py:33
  86.8 6.0 %collective-permute-start.15 = (bf16[512,896]{1,0:T(8,128)(2,1)S(1)}, bf16[512,896]{1,0:T(8,128)(2,1)S(1)}, u32[]{:S(2)}, u32[]{:S(2)}) collective-permute-start(bf16[512,896]{1,0:T(8,128)(2,1)S(1)} %get-tuple-element.45), channel_id=1, source_target_pairs={{0,8},{2,10},{4,12},{6,14},{8,0},{10,2},{12,4},{14,6},{16,24},{18,... | collective-permute-start | bytes 2752520 | tf_op jit(solution)/shard_map/ppermute | solution.py:39
  94.0 7.0 %collective-permute-done.9 = bf16[256,896]{1,0:T(8,128)(2,1)S(1)} collective-permute-done((bf16[256,896]{1,0:T(8,128)(2,1)S(1)}, bf16[256,896]{1,0:T(8,128)(2,1)S(1)}, u32[]{:S(2)}, u32[]{:S(2)}) %collective-permute-start.9) | collective-permute-done | bytes 458784 | tf_op jit(solution)/shard_map/ppermute | solution.py:33
  111.5 4.5 %fusion = f32[256,7168]{1,0:T(8,128)} fusion(bf16[64,7168]{1,0:T(8,128)(2,1)S(1)} %constant_dynamic-update-slice_fusion.8, f32[256,7168]{1,0:T(8,128)S(1)} %bitcast.63, f32[4096,64]{0,1:T(8,128)S(1)} %copy-done, s32[]{:T(128)S(6)} %select_n.177), kind=kOutput, calls=%fused_computation.1 | convolution fusion | flops 240386048 | bytes 15630340 | tf_op jit(solution)/shard_map/dot_general | solution.py:99
  117.0 3.1 %collective-permute-start.23 = (bf16[512,896]{1,0:T(8,128)(2,1)S(1)}, bf16[512,896]{1,0:T(8,128)(2,1)S(1)}, u32[]{:S(2)}, u32[]{:S(2)}) collective-permute-start(bf16[512,896]{1,0:T(8,128)(2,1)S(1)} %broadcast_select_fusion), channel_id=1, source_target_pairs={{0,8},{2,10},{4,12},{6,14},{8,0},{10,2},{12,4},{14,6},{16,24},{18,... | collective-permute-start | bytes 2752520 | tf_op jit(solution)/shard_map/ppermute | solution.py:39
  122.0 10.9 %collective-permute-done.23 = bf16[512,896]{1,0:T(8,128)(2,1)S(1)} collective-permute-done((bf16[512,896]{1,0:T(8,128)(2,1)S(1)}, bf16[512,896]{1,0:T(8,128)(2,1)S(1)}, u32[]{:S(2)}, u32[]{:S(2)}) %collective-permute-start.23) | collective-permute-done | bytes 917536 | tf_op jit(solution)/shard_map/ppermute | solution.py:39
  142.8 4.0 %collective-permute-done.17 = bf16[64,3072]{1,0:T(8,128)(2,1)S(1)} collective-permute-done((bf16[64,3072]{1,0:T(8,128)(2,1)S(1)}, bf16[64,3072]{1,0:T(8,128)(2,1)S(1)}, u32[]{:S(2)}, u32[]{:S(2)}) %collective-permute-start.17) | collective-permute-done | bytes 393248 | tf_op jit(solution)/shard_map/ppermute | solution.py:33
  146.8 4.1 %collective-permute-done.19 = bf16[64,3072]{1,0:T(8,128)(2,1)S(1)} collective-permute-done((bf16[64,3072]{1,0:T(8,128)(2,1)S(1)}, bf16[64,3072]{1,0:T(8,128)(2,1)S(1)}, u32[]{:S(2)}, u32[]{:S(2)}) %collective-permute-start.19) | collective-permute-done | bytes 393248 | tf_op jit(solution)/shard_map/ppermute | solution.py:33
  153.3 3.4 %collective-permute-done.37 = bf16[4,64,3072]{2,1,0:T(8,128)(2,1)S(1)} collective-permute-done((bf16[4,64,3072]{2,1,0:T(8,128)(2,1)S(1)}, bf16[4,64,3072]{2,1,0:T(8,128)(2,1)S(1)}, u32[]{:S(2)}, u32[]{:S(2)}) %collective-permute-start.37) | collective-permute-done | bytes 1572896 | tf_op jit(solution)/shard_map/ppermute | solution.py:60
  162.7 6.6 %collective-permute-done.38 = bf16[64,3072]{1,0:T(8,128)(2,1)S(1)} collective-permute-done((bf16[64,3072]{1,0:T(8,128)(2,1)S(1)}, bf16[64,3072]{1,0:T(8,128)(2,1)S(1)}, u32[]{:S(2)}, u32[]{:S(2)}) %collective-permute-start.38) | collective-permute-done | bytes 393248 | tf_op jit(solution)/shard_map/ppermute | solution.py:33
  169.4 8.8 %collective-permute-done.40 = bf16[64,3072]{1,0:T(8,128)(2,1)S(1)} collective-permute-done((bf16[64,3072]{1,0:T(8,128)(2,1)S(1)}, bf16[64,3072]{1,0:T(8,128)(2,1)S(1)}, u32[]{:S(2)}, u32[]{:S(2)}) %collective-permute-start.40) | collective-permute-done | bytes 393248 | tf_op jit(solution)/shard_map/ppermute | solution.py:33
  181.9 7.8 %collective-permute-start.21 = (bf16[64,1024]{1,0:T(8,128)(2,1)S(1)}, bf16[64,1024]{1,0:T(8,128)(2,1)S(1)}, u32[]{:S(2)}, u32[]{:S(2)}) collective-permute-start(bf16[64,1024]{1,0:T(8,128)(2,1)S(1)} %get-tuple-element.64), channel_id=1, source_target_pairs={{0,16},{2,18},{4,20},{6,22},{24,8},{26,10},{28,12},{30,14},{1,17},... | collective-permute-start | bytes 393224 | tf_op jit(solution)/shard_map/ppermute | solution.py:39
  190.4 3.8 %collective-permute-start.44 = (bf16[64,1024]{1,0:T(8,128)(2,1)S(1)}, bf16[64,1024]{1,0:T(8,128)(2,1)S(1)}, u32[]{:S(2)}, u32[]{:S(2)}) collective-permute-start(bf16[64,1024]{1,0:T(8,128)(2,1)S(1)} %get-tuple-element.63), channel_id=1, source_target_pairs={{0,24},{2,26},{4,28},{6,30},{24,0},{26,2},{28,4},{30,6},{1,25},{3,... | collective-permute-start | bytes 393224 | tf_op jit(solution)/shard_map/ppermute | solution.py:39
  194.2 4.9 %collective-permute-done.44 = bf16[64,1024]{1,0:T(8,128)(2,1)S(1)} collective-permute-done((bf16[64,1024]{1,0:T(8,128)(2,1)S(1)}, bf16[64,1024]{1,0:T(8,128)(2,1)S(1)}, u32[]{:S(2)}, u32[]{:S(2)}) %collective-permute-start.44) | collective-permute-done | bytes 131104 | tf_op jit(solution)/shard_map/ppermute | solution.py:39
  (144 shorter events, 71.8 us)
Async XLA Ops:
  3.1 21.9 %collective-permute-start.3 = (bf16[128,1792]{1,0:T(8,128)(2,1)S(1)}, bf16[128,1792]{1,0:T(8,128)(2,1)}, u32[]{:S(2)}, u32[]{:S(2)}) collective-permute-start(bf16[128,1792]{1,0:T(8,128)(2,1)S(1)} %get-tuple-element.48), channel_id=1, source_target_pairs={{8,16},{10,18},{12,20},{14,22},{16,8},{18,10},{20,12},{22,14},{9,1... | collective-permute-start | bytes 1376264 | tf_op jit(solution)/shard_map/ppermute | solution.py:39
  4.6 20.5 %collective-permute-start.2 = (bf16[128,1792]{1,0:T(8,128)(2,1)S(1)}, bf16[128,1792]{1,0:T(8,128)(2,1)}, u32[]{:S(2)}, u32[]{:S(2)}) collective-permute-start(bf16[128,1792]{1,0:T(8,128)(2,1)S(1)} %get-tuple-element.48), channel_id=1, source_target_pairs={{0,8},{2,10},{4,12},{6,14},{8,0},{10,2},{12,4},{14,6},{16,24},{18,... | collective-permute-start | bytes 1376264 | tf_op jit(solution)/shard_map/ppermute | solution.py:39
  9.7 12.3 %collective-permute-start = (bf16[128,1792]{1,0:T(8,128)(2,1)}, bf16[128,1792]{1,0:T(8,128)(2,1)S(1)}, u32[]{:S(2)}, u32[]{:S(2)}) collective-permute-start(bf16[128,1792]{1,0:T(8,128)(2,1)} %get-tuple-element.49), channel_id=1, source_target_pairs={{0,2},{2,0},{4,6},{6,4},{8,10},{10,8},{12,14},{14,12},{16,18},{18,... | collective-permute-start | bytes 1376264 | tf_op jit(solution)/shard_map/ppermute | solution.py:33
  11.2 12.4 %collective-permute-start.1 = (bf16[128,1792]{1,0:T(8,128)(2,1)S(1)}, bf16[128,1792]{1,0:T(8,128)(2,1)S(1)}, u32[]{:S(2)}, u32[]{:S(2)}) collective-permute-start(bf16[128,1792]{1,0:T(8,128)(2,1)S(1)} %get-tuple-element.51), channel_id=1, source_target_pairs={{0,4},{2,6},{4,0},{6,2},{8,12},{10,14},{12,8},{14,10},{16,20},{18,... | collective-permute-start | bytes 1376264 | tf_op jit(solution)/shard_map/ppermute | solution.py:33
  15.2 17.1 %collective-permute-start.27 = (bf16[128,64]{1,0:T(8,128)(2,1)S(1)}, bf16[128,64]{1,0:T(8,128)(2,1)S(1)}, u32[]{:S(2)}, u32[]{:S(2)}) collective-permute-start(bf16[128,64]{1,0:T(8,128)(2,1)S(1)} %all_gather.3), channel_id=1, source_target_pairs={{0,6},{2,4},{4,2},{6,0},{8,14},{10,12},{12,10},{14,8},{16,22},{18,... | collective-permute-start | bytes 49160 | tf_op jit(solution)/shard_map/ppermute | solution.py:33
  22.0 17.3 %collective-permute-start.26 = (bf16[128,64]{1,0:T(8,128)(2,1)S(1)}, bf16[128,64]{1,0:T(8,128)(2,1)S(1)}, u32[]{:S(2)}, u32[]{:S(2)}) collective-permute-start(bf16[128,64]{1,0:T(8,128)(2,1)S(1)} %all_gather.3), channel_id=1, source_target_pairs={{0,4},{2,6},{4,0},{6,2},{8,12},{10,14},{12,8},{14,10},{16,20},{18,... | collective-permute-start | bytes 49160 | tf_op jit(solution)/shard_map/ppermute | solution.py:33
  25.1 58.3 %collective-permute-start.13 = (bf16[256,1792]{1,0:T(8,128)(2,1)S(1)}, bf16[256,1792]{1,0:T(8,128)(2,1)S(1)}, u32[]{:S(2)}, u32[]{:S(2)}) collective-permute-start(bf16[256,1792]{1,0:T(8,128)(2,1)S(1)} %pad_maximum_fusion.9), channel_id=1, source_target_pairs={{8,16},{10,18},{12,20},{14,22},{16,8},{18,10},{20,12},{22,14},{9,1... | collective-permute-start | bytes 2752520 | tf_op jit(solution)/shard_map/ppermute | solution.py:39
  25.8 42.6 %collective-permute-start.11 = (bf16[256,1792]{1,0:T(8,128)(2,1)S(1)}, bf16[256,1792]{1,0:T(8,128)(2,1)S(1)}, u32[]{:S(2)}, u32[]{:S(2)}) collective-permute-start(bf16[256,1792]{1,0:T(8,128)(2,1)S(1)} %pad_maximum_fusion.9), channel_id=1, source_target_pairs={{0,8},{2,10},{4,12},{6,14},{8,0},{10,2},{12,4},{14,6},{16,24},{18,... | collective-permute-start | bytes 2752520 | tf_op jit(solution)/shard_map/ppermute | solution.py:39
  53.2 24.6 %collective-permute-start.5 = (bf16[256,896]{1,0:T(8,128)(2,1)S(1)}, bf16[256,896]{1,0:T(8,128)(2,1)S(1)}, u32[]{:S(2)}, u32[]{:S(2)}) collective-permute-start(bf16[256,896]{1,0:T(8,128)(2,1)S(1)} %get-tuple-element.20), channel_id=1, source_target_pairs={{0,2},{2,0},{4,6},{6,4},{8,10},{10,8},{12,14},{14,12},{16,18},{18,... | collective-permute-start | bytes 1376264 | tf_op jit(solution)/shard_map/ppermute | solution.py:33
  53.8 24.8 %collective-permute-start.6 = (bf16[256,896]{1,0:T(8,128)(2,1)S(1)}, bf16[256,896]{1,0:T(8,128)(2,1)S(1)}, u32[]{:S(2)}, u32[]{:S(2)}) collective-permute-start(bf16[256,896]{1,0:T(8,128)(2,1)S(1)} %get-tuple-element.21), channel_id=1, source_target_pairs={{0,4},{2,6},{4,0},{6,2},{8,12},{10,14},{12,8},{14,10},{16,20},{18,... | collective-permute-start | bytes 1376264 | tf_op jit(solution)/shard_map/ppermute | solution.py:33
  68.5 14.3 %collective-permute-start.7 = (bf16[256,896]{1,0:T(8,128)(2,1)S(1)}, bf16[256,896]{1,0:T(8,128)(2,1)S(1)}, u32[]{:S(2)}, u32[]{:S(2)}) collective-permute-start(bf16[256,896]{1,0:T(8,128)(2,1)S(1)} %get-tuple-element.22), channel_id=1, source_target_pairs={{0,6},{2,4},{4,2},{6,0},{8,14},{10,12},{12,10},{14,8},{16,22},{18,... | collective-permute-start | bytes 1376264 | tf_op jit(solution)/shard_map/ppermute | solution.py:33
  77.8 38.2 %collective-permute-start.22 = (bf16[512,896]{1,0:T(8,128)(2,1)S(1)}, bf16[512,896]{1,0:T(8,128)(2,1)S(1)}, u32[]{:S(2)}, u32[]{:S(2)}) collective-permute-start(bf16[512,896]{1,0:T(8,128)(2,1)S(1)} %get-tuple-element.46), channel_id=1, source_target_pairs={{8,16},{10,18},{12,20},{14,22},{16,8},{18,10},{20,12},{22,14},{9,1... | collective-permute-start | bytes 2752520 | tf_op jit(solution)/shard_map/ppermute | solution.py:39
  83.4 17.6 %collective-permute-start.9 = (bf16[256,896]{1,0:T(8,128)(2,1)S(1)}, bf16[256,896]{1,0:T(8,128)(2,1)S(1)}, u32[]{:S(2)}, u32[]{:S(2)}) collective-permute-start(bf16[256,896]{1,0:T(8,128)(2,1)S(1)} %get-tuple-element.24), channel_id=1, source_target_pairs={{0,4},{2,6},{4,0},{6,2},{8,12},{10,14},{12,8},{14,10},{16,20},{18,... | collective-permute-start | bytes 1376264 | tf_op jit(solution)/shard_map/ppermute | solution.py:33
  83.4 18.7 %collective-permute-start.10 = (bf16[256,896]{1,0:T(8,128)(2,1)S(1)}, bf16[256,896]{1,0:T(8,128)(2,1)S(1)}, u32[]{:S(2)}, u32[]{:S(2)}) collective-permute-start(bf16[256,896]{1,0:T(8,128)(2,1)S(1)} %get-tuple-element.25), channel_id=1, source_target_pairs={{0,6},{2,4},{4,2},{6,0},{8,14},{10,12},{12,10},{14,8},{16,22},{18,... | collective-permute-start | bytes 1376264 | tf_op jit(solution)/shard_map/ppermute | solution.py:33
  86.8 30.1 %collective-permute-start.15 = (bf16[512,896]{1,0:T(8,128)(2,1)S(1)}, bf16[512,896]{1,0:T(8,128)(2,1)S(1)}, u32[]{:S(2)}, u32[]{:S(2)}) collective-permute-start(bf16[512,896]{1,0:T(8,128)(2,1)S(1)} %get-tuple-element.45), channel_id=1, source_target_pairs={{0,8},{2,10},{4,12},{6,14},{8,0},{10,2},{12,4},{14,6},{16,24},{18,... | collective-permute-start | bytes 2752520 | tf_op jit(solution)/shard_map/ppermute | solution.py:39
  117.0 15.9 %collective-permute-start.23 = (bf16[512,896]{1,0:T(8,128)(2,1)S(1)}, bf16[512,896]{1,0:T(8,128)(2,1)S(1)}, u32[]{:S(2)}, u32[]{:S(2)}) collective-permute-start(bf16[512,896]{1,0:T(8,128)(2,1)S(1)} %broadcast_select_fusion), channel_id=1, source_target_pairs={{0,8},{2,10},{4,12},{6,14},{8,0},{10,2},{12,4},{14,6},{16,24},{18,... | collective-permute-start | bytes 2752520 | tf_op jit(solution)/shard_map/ppermute | solution.py:39
  121.8 16.4 %collective-permute-start.16 = (bf16[4,64,3072]{2,1,0:T(8,128)(2,1)S(1)}, bf16[4,64,3072]{2,1,0:T(8,128)(2,1)S(1)}, u32[]{:S(2)}, u32[]{:S(2)}) collective-permute-start(bf16[4,64,3072]{2,1,0:T(8,128)(2,1)S(1)} %dynamic-slice_bitcast_fusion.1), channel_id=1, source_target_pairs={{0,1},{1,0},{2,3},{3,2},{4,5},{5,4},{6,7},{7,6},{8,9},{9,8},{10,11... | collective-permute-start | bytes 4718600 | tf_op jit(solution)/shard_map/ppermute | solution.py:60
  157.3 12.0 %collective-permute-start.38 = (bf16[64,3072]{1,0:T(8,128)(2,1)S(1)}, bf16[64,3072]{1,0:T(8,128)(2,1)S(1)}, u32[]{:S(2)}, u32[]{:S(2)}) collective-permute-start(bf16[64,3072]{1,0:T(8,128)(2,1)S(1)} %get-tuple-element.52), channel_id=1, source_target_pairs={{0,2},{2,0},{4,6},{6,4},{8,10},{10,8},{12,14},{14,12},{16,18},{18,... | collective-permute-start | bytes 1179656 | tf_op jit(solution)/shard_map/ppermute | solution.py:33
  158.4 19.8 %collective-permute-start.40 = (bf16[64,3072]{1,0:T(8,128)(2,1)S(1)}, bf16[64,3072]{1,0:T(8,128)(2,1)S(1)}, u32[]{:S(2)}, u32[]{:S(2)}) collective-permute-start(bf16[64,3072]{1,0:T(8,128)(2,1)S(1)} %get-tuple-element.53), channel_id=1, source_target_pairs={{0,6},{2,4},{4,2},{6,0},{8,14},{10,12},{12,10},{14,8},{16,22},{18,... | collective-permute-start | bytes 1179656 | tf_op jit(solution)/shard_map/ppermute | solution.py:33
  160.5 19.0 %collective-permute-start.39 = (bf16[64,3072]{1,0:T(8,128)(2,1)S(1)}, bf16[64,3072]{1,0:T(8,128)(2,1)S(1)}, u32[]{:S(2)}, u32[]{:S(2)}) collective-permute-start(bf16[64,3072]{1,0:T(8,128)(2,1)S(1)} %get-tuple-element.54), channel_id=1, source_target_pairs={{0,4},{2,6},{4,0},{6,2},{8,12},{10,14},{12,8},{14,10},{16,20},{18,... | collective-permute-start | bytes 1179656 | tf_op jit(solution)/shard_map/ppermute | solution.py:33
  160.9 29.4 %collective-permute-start.20 = (bf16[64,1024]{1,0:T(8,128)(2,1)S(1)}, bf16[64,1024]{1,0:T(8,128)(2,1)S(1)}, u32[]{:S(2)}, u32[]{:S(2)}) collective-permute-start(bf16[64,1024]{1,0:T(8,128)(2,1)S(1)} %get-tuple-element.65), channel_id=1, source_target_pairs={{0,8},{2,10},{4,12},{6,14},{8,0},{10,2},{12,4},{14,6},{16,24},{18,... | collective-permute-start | bytes 393224 | tf_op jit(solution)/shard_map/ppermute | solution.py:39
  179.8 19.3 %collective-permute-start.42 = (bf16[64,2048]{1,0:T(8,128)(2,1)S(1)}, bf16[64,2048]{1,0:T(8,128)(2,1)S(1)}, u32[]{:S(2)}, u32[]{:S(2)}) collective-permute-start(bf16[64,2048]{1,0:T(8,128)(2,1)S(1)} %pad_maximum_fusion.11), channel_id=1, source_target_pairs={{8,24},{10,26},{12,28},{14,30},{16,0},{18,2},{20,4},{22,6},{9,25},... | collective-permute-start | bytes 786440 | tf_op jit(solution)/shard_map/ppermute | solution.py:39
  181.2 12.9 %collective-permute-start.43 = (bf16[64,1024]{1,0:T(8,128)(2,1)S(1)}, bf16[64,1024]{1,0:T(8,128)(2,1)S(1)}, u32[]{:S(2)}, u32[]{:S(2)}) collective-permute-start(bf16[64,1024]{1,0:T(8,128)(2,1)S(1)} %get-tuple-element.64), channel_id=1, source_target_pairs={{8,16},{10,18},{12,20},{14,22},{16,8},{18,10},{20,12},{22,14},{9,1... | collective-permute-start | bytes 393224 | tf_op jit(solution)/shard_map/ppermute | solution.py:39
  181.9 12.3 %collective-permute-start.21 = (bf16[64,1024]{1,0:T(8,128)(2,1)S(1)}, bf16[64,1024]{1,0:T(8,128)(2,1)S(1)}, u32[]{:S(2)}, u32[]{:S(2)}) collective-permute-start(bf16[64,1024]{1,0:T(8,128)(2,1)S(1)} %get-tuple-element.64), channel_id=1, source_target_pairs={{0,16},{2,18},{4,20},{6,22},{24,8},{26,10},{28,12},{30,14},{1,17},... | collective-permute-start | bytes 393224 | tf_op jit(solution)/shard_map/ppermute | solution.py:39
  (27 other events, 227.5 us)

commit v2 on v1

--- a/solution.py
+++ b/solution.py
@@ -3,6 +3,8 @@
 import jax
 import jax.numpy as jnp
 from jax import lax
+from jax.experimental import pallas as pl
+from jax.experimental.pallas import tpu as pltpu
 from jax.sharding import PartitionSpec as P
 
 momentum_decay = 0.9
@@ -126,64 +128,172 @@
     return input_grad, new_momentum
 
 
+def products(lay, sources, buffers, fills, jobs, width):
+    scalars = jnp.stack([lay.place, lay.core]).astype(jnp.int32)
+    rows = buffers[jobs[0][0]][0]
+    half = rows // PLANE // 2
+    piece = width // PLANE
+
+    def kernel(scalar_ref, *refs):
+        ins, refs = refs[: len(sources)], refs[len(sources):]
+        keep_ref, give_ref, *scratch = refs
+        buffer_refs, sems = scratch[:-1], scratch[-1]
+        place, core = scalar_ref[0], scalar_ref[1]
+        copies = []
+        for i, (s, c0, b, r0, c1, cols) in enumerate(fills):
+            n = sources[s].shape[0]
+            copies.append(
+                pltpu.make_async_copy(
+                    ins[s].at[:, pl.ds(c0, cols)],
+                    buffer_refs[b].at[pl.ds(r0, n), pl.ds(c1, cols)],
+                    sems.at[i],
+                )
+            )
+        for copy in copies:
+            copy.start()
+        waited = set()
+
+        def need(ids):
+            for i in ids:
+                if i not in waited:
+                    copies[i].wait()
+                    waited.add(i)
+
+        for at, (a, b, a0, b0, cols, a_ids, b_ids) in enumerate(jobs):
+            need(a_ids)
+            for r in range(PLANE):
+                need(b_ids(r))
+                x = nt(
+                    buffer_refs[a][:, a0:a0 + cols],
+                    buffer_refs[b][r * piece:(r + 1) * piece, b0:b0 + cols],
+                ).astype(bf16)
+                column = at * width + pl.multiple_of((place ^ r) * piece, piece)
+                for p in range(PLANE):
+                    low = x[2 * p * half:(2 * p + 1) * half]
+                    high = x[(2 * p + 1) * half:(2 * p + 2) * half]
+                    keep_ref[p, :, pl.ds(column, piece)] = jnp.where(core == 0, low, high)
+                    give_ref[p, :, pl.ds(column, piece)] = jnp.where(core == 0, high, low)
+        need(range(len(copies)))
+
+    out = jax.ShapeDtypeStruct((PLANE, half, len(jobs) * width), bf16)
+    return pl.pallas_call(
+        kernel,
+        out_shape=(out, out),
+        in_specs=[pl.BlockSpec(memory_space=pltpu.SMEM)]
+        + [pl.BlockSpec(memory_space=pl.ANY)] * len(sources),
+        out_specs=[pl.BlockSpec(memory_space=pltpu.VMEM)] * 2,
+        scratch_shapes=[pltpu.VMEM(shape, bf16) for shape in buffers]
+        + [pltpu.SemaphoreType.DMA((len(fills),))],
+        compiler_params=pltpu.CompilerParams(vmem_limit_bytes=36 * 2**20),
+        cost_estimate=pl.CostEstimate(flops=10**6, bytes_accessed=10**5, transcendentals=0),
+    )(scalars, *sources)
+
+
 def line_of_four(inputs, out_grad, weight, proj_basis, momentum):
     lay = Layout()
     level, across = lay.level, lay.across
     inner = (level == 1) | (level == 2)
     tokens, hidden = out_grad.shape
+    rows = weight.shape[0]
+    width = rows * PLANE
     half = hidden // PLANE // 2
     end_swap = lambda x: lay.levels(x, 1)
     mid_swap = lambda x: lay.levels(x, 3, (1, 2))
+    outward = lambda x: lay.levels(x, 1, (1, 2))
+    inward = lambda x: lay.levels(x, 1, (0, 3))
+    send = lambda a, w: jnp.where(inner, a, w)
+    end_sent, mid_sent = [], []
+
+    def queued(move, sent, x, *first):
+        got = move(after(x, *sent[-2:-1], *first))
+        sent.append(got)
+        return got
 
     a0 = lay.cut(out_grad, 0)
-    e0, m0 = end_swap(a0), mid_swap(a0)
-    ax, ay = across(lay.cut(out_grad, 1), 1), across(lay.cut(out_grad, 2), 2)
-    ad = across(after(lay.cut(out_grad, 3), ax, ay, e0, m0), 3)
-    axy = jnp.concatenate([ax, ay], 0)
-    axy = after(axy, e0, m0)
-    e1, m1 = end_swap(axy), mid_swap(axy)
-    plane_proj = projected(lay, after(inputs, a0), proj_basis)
+    e0, m0 = queued(end_swap, end_sent, a0), queued(mid_swap, mid_sent, a0)
+    cuts = [lay.cut(after(out_grad, a0), r) for r in range(1, PLANE)]
+    ax, ay = across(cuts[0], 1), across(cuts[1], 2)
+    ad = across(after(cuts[2], ax, ay, e0, m0), 3)
+    axy = after(jnp.concatenate([ax, ay], 0), e0, m0)
+    e1, m1 = queued(end_swap, end_sent, axy), queued(mid_swap, mid_sent, axy)
+    proj = projected(lay, after(inputs, *cuts), proj_basis)
     weight = after(weight, ax, ay)
-    w1 = [lay.cut(weight, r)[:, half:] for r in range(PLANE)]
-    w0 = [lay.cut(weight, r)[:, :half] for r in range(PLANE)]
-    w1 = w1[:1] + [across(after(w1[r], ad), r) for r in range(1, PLANE)]
-    shares = panel_shares(lay, plane_proj, [a0, ax, ay, ad])
-    e2, m2 = end_swap(ad), mid_swap(ad)
-    w0 = w0[:1] + [across(after(w0[r], *w1[1:]), r) for r in range(1, PLANE)]
+    parts = [lay.cut(weight, r) for r in range(PLANE)]
+    parts[1:3] = [across(after(parts[r], ad), r) for r in (1, 2)]
+    parts[3] = across(after(parts[3], parts[1], parts[2]), 3)
+    e2, m2 = queued(end_swap, end_sent, ad), queued(mid_swap, mid_sent, ad)
+
+    panel = sum(tn(q, a) for q, a in zip(proj, [a0, ax, ay, ad]))
+    panel = panel + inward(after(panel.astype(bf16), e1, m1)).astype(f32)
 
     near_e, near_m = jnp.concatenate([e0, e1, e2], 0), jnp.concatenate([m0, m1, m2], 0)
-    held1 = lay.in_order(w1, 0)
-    cut_rows = held1.shape[0] // 2
-    send = lambda a, w: jnp.where(inner, a, w)
-    far0 = mid_swap(near_e[:, :half])
-    got_a = end_swap(send(near_m[:, :half], held1[:cut_rows]))
-    panel_q = panel_quarter(lay, shares)
-    far1 = mid_swap(after(near_e[:, half:], far0))
-    got_b = end_swap(send(far0, after(held1[cut_rows:], got_a)))
-    panel = panel_whole(lay, after(panel_q, *w0[1:]))
-    held0 = lay.in_order(w0, 0)
-    held = jnp.concatenate([held0, held1], 1)
-    width = held.shape[0]
+    pair = 2 * tokens
+    far0, far1, got = [], [], []
+    for i in range(2):
+        far0.append(queued(mid_swap, mid_sent, near_e[i * pair:(i + 1) * pair, :half]))
+        got.append(queued(end_swap, end_sent, send(near_m[i * pair:(i + 1) * pair, :half], parts[i][:, half:])))
+    pair_panel = panel
+    other_pair = mid_swap(after(panel.astype(bf16), far0[0], got[0]))
+    for i in range(2):
+        far1.append(queued(mid_swap, mid_sent, near_e[i * pair:(i + 1) * pair, half:]))
+        got.append(queued(end_swap, end_sent, send(far0[i], parts[2 + i][:, half:]), parts[3]))
+    def weight_fills(first, buffer):
+        return [(first + r, 0, buffer, r * rows, 0, 2 * half) for r in range(PLANE)]
+
+    def block_fills(first, buffer, sizes, column, cols):
+        out, row = [], 0
+        for i, n in enumerate(sizes):
+            out.append((first + i, column, buffer, row, column, cols))
+            row += n
+        return out
+
+    both = 2 * half
+    early0 = send(near_m[:, :half], jnp.concatenate(got[:2], 0))
+    sources = [after(a0, *far0, pair_panel), ax, ay, ad, *parts, near_e, early0, near_m]
+    fills = block_fills(0, 0, [tokens] * PLANE, 0, both) + weight_fills(4, 3)
+    fills += [(8, 0, 1, 0, 0, both), (9, 0, 2, 0, 0, half), (10, half, 2, 0, half, half)]
+    wide, tall = (PLANE * tokens, both), (width, both)
+    of_weight = lambda r: (4 + r,)
+    none = lambda r: ()
+    jobs = [
+        (0, 3, 0, 0, both, range(4), of_weight),
+        (1, 3, 0, 0, both, (8,), none),
+        (2, 3, 0, 0, both, (9, 10), none),
+    ]
+    keep, give = products(lay, sources, [wide, wide, wide, tall], fills, jobs, width)
+    swap = lambda x: lax.ppermute(x, "tensor", [(0, 1), (1, 0)])
+    give = after(give, far1[0], got[2])
+    panel = (panel + after(other_pair, keep).astype(f32)).astype(bf16)
+    panel = send(panel, outward(after(panel, far1[0], got[2])))
+    first = (keep.astype(f32) + swap(give).astype(f32)).astype(bf16)
+
+    late0 = [send(far0[i], got[2 + i]) for i in range(2)]
+    late0[0] = after(late0[0], first)
+    sources = [*late0, *far1, near_m, *parts, *got]
+    fills = [(i, 0, 0, i * pair, 0, half) for i in range(2)]
+    fills += [(2 + i, 0, 0, i * pair, half, half) for i in range(2)]
+    fills += weight_fills(5, 2) + [(4, half, 1, 0, 0, half)]
+    fills += [(9 + r, 0, 3, r * rows, 0, half) for r in range(PLANE)]
+    jobs = [
+        (0, 2, 0, 0, both, range(4), of_weight),
+        (1, 3, 0, 0, half, (8,), lambda r: (9 + r,)),
+        (0, 3, half, 0, half, (), none),
+    ]
+    buffers = [wide, (PLANE * tokens, half), tall, (width, half)]
+    keep, give = products(lay, sources, buffers, fills, jobs, width)
 
     def plane_sum(part):
-        part = lay.core_sum(part, PLANE)
         total = part[0].astype(f32)
         for r in range(1, PLANE):
             total = total + across(part[r], r).astype(f32)
         return total.astype(bf16)
 
-    own = jnp.concatenate([a0, axy, ad], 0)
-    y0, y1 = nt(own, held).astype(bf16), nt(near_e, held).astype(bf16)
-    early = (nt(send(near_m[:, :half], got_a), held0) + nt(near_m[:, half:], held1)).astype(bf16)
-    first = plane_sum(jnp.concatenate([y0, y1, early], 1))
+    first = plane_sum(first)
+    second = (keep.astype(f32) + swap(after(give, first, panel)).astype(f32)).astype(bf16)
+    panel = after(panel, second)
+    panel = lay.in_order([panel] + [across(panel, r) for r in range(1, PLANE)], 1)
     new_momentum = updated(lay, proj_basis, panel, momentum, tokens * lay.replicas)
-
-    far1 = after(far1, new_momentum)
-    late = (nt(send(far0, got_b), held0) + nt(far1, held1)).astype(bf16)
-    other = jnp.concatenate([got_a, got_b], 0)
-    early_other = nt(near_m[:, half:], other).astype(bf16)
-    late_other = nt(far1, other).astype(bf16)
-    second = plane_sum(after(jnp.concatenate([late, early_other, late_other], 1), first))
+    second = plane_sum(second)
     y0, y1, early = [first[:, i * width:(i + 1) * width] for i in range(3)]
     late, early_other, late_other = [second[:, i * width:(i + 1) * width] for i in range(3)]
 
@@ -196,7 +306,6 @@
     add = lambda *xs: sum(x.astype(f32) for x in xs).astype(bf16)
     z2 = add(z2, z2b, z_late[:, :width])
     z3 = add(z3, z3b, z_late[:, width:])
-    by_distance = [y0, z1, z2, z3]
     input_grad = jnp.concatenate(
         [
             jnp.where(
@@ -204,7 +313,7 @@
                 y0,
                 jnp.where(level == b ^ 1, z1, jnp.where(level == b ^ 2, z2, z3)),
             )
-            for b in range(len(by_distance))
+            for b in range(lay.line)
         ],
         1,
     )
@@ -219,7 +328,7 @@
         P(),
         P("dp", "tensor"),
     )
-    four = mesh.shape["dp"] == 4 * PLANE
+    four = mesh.shape["dp"] == 4 * PLANE and mesh.shape["tensor"] == 2
     return jax.shard_map(
         line_of_four if four else long_line,
         mesh=mesh,

time: 201 us -> 201 us (level)
  Pallas kernels: 0 us -> 24.3 us
  waiting for transfers between devices: 97.9 us -> 75.1 us
  matrix products: 18 us -> 10.2 us
  starting transfers between devices: 70.7 us -> 74.6 us
  other arithmetic: 3.54 us -> 6.12 us
    pallas_call x0 -> x2, Pallas kernels: none -> 24.3 us  [products(): pl.pallas_call(kernel, out_shape=(out, out), in_specs=[pl.BlockSpec(memor...]
    ppermute x22 -> x23, waiting for transfers between devices: 41.2 us -> 22.6 us  [levels(): return lax.ppermute(x, 'dp', pairs)]
    dot_general x8 -> x0, matrix products: 11.9 us -> none  [nt(): lax.dot_general(a, b, (((1,), (1,)), ((), ())), preferred_element_type=f32)]
    ppermute x22 -> x23, starting transfers between devices: 45.8 us -> 51.3 us  [levels(): return lax.ppermute(x, 'dp', pairs)]
    ppermute x2, waiting for transfers between devices: 3.4 us -> 0.01 us  [line_of_four(): swap = lambda x: lax.ppermute(x, 'tensor', [(0, 1), (1, 0)])]
    dynamic_slice x1 -> x3, local copies, waits for them, and re-layouts: 2.44 us -> 5.8 us  [cut(): return lax.dynamic_slice_in_dim(x, (self.place ^ r) * quarter, quarter, 1)]
    dot_general x1, matrix products: 4.46 us -> 7.57 us  [updated(): update = jnp.dot(basis_rows.astype(bf16), panel, preferred_element_type=f32)]
    unnamed x17 -> x8, local copies, waits for them, and re-layouts: 2.34 us -> 0.26 us
  transfers between devices with their start and end apart: 45 -> 43, of which waited for: 23 -> 16; matrix products, arithmetic and copies ran while one was open for 12% -> 10% of each run, Pallas kernels for 0% -> 12%
where the time goes in v2:
time: 201 us; the launch traced here: 200 us
  waiting for transfers between devices  75.1 us (37%)
  starting transfers between devices  74.6 us (37%)
  Pallas kernels  24.3 us (12%)
  matrix products  10.2 us (5%)
  local copies, waits for them, and re-layouts  6.63 us (3%)
  other arithmetic  6.12 us (3%)
    ppermute x18, waiting for transfers between devices, across(): return lax.ppermute(x, 'dp', [(d, d ^ r) for d in range(self.replicas)])  52.5 us
    ppermute x23, starting transfers between devices, levels(): return lax.ppermute(x, 'dp', pairs)  51.3 us
    pallas_call x2, Pallas kernels, products(): pl.pallas_call(kernel, out_shape=(out, out), in_specs=[pl.BlockSpec(memor...  24.3 us
    ppermute x18, starting transfers between devices, across(): return lax.ppermute(x, 'dp', [(d, d ^ r) for d in range(self.replicas)])  23.1 us
    ppermute x23, waiting for transfers between devices, levels(): return lax.ppermute(x, 'dp', pairs)  22.6 us
    dot_general x1, matrix products, updated(): update = jnp.dot(basis_rows.astype(bf16), panel, preferred_element_type=f32)  7.57 us
    dynamic_slice x3, local copies, waits for them, and re-layouts, cut(): return lax.dynamic_slice_in_dim(x, (self.place ^ r) * quarter, quarter, 1)  5.8 us
  transfers between devices with their start and end apart: 43, of which 16 were waited for; matrix products, arithmetic and copies ran while one was open for 10% of the time, Pallas kernels for 12%

profile of v2, /device:TPU:0, one launch (start us, length us, event | category | flops | bytes accessed | tf_op | source)
XLA Modules:
  0.0 200.0 jit_solution(3621797959100532160)
XLA Ops:
  1.8 3.1 %collective-permute-start = (bf16[128,1792]{1,0:T(8,128)(2,1)S(1)}, bf16[128,1792]{1,0:T(8,128)(2,1)S(1)}, u32[]{:S(2)}, u32[]{:S(2)}) collective-permute-start(bf16[128,1792]{1,0:T(8,128)(2,1)S(1)} %constant_dynamic-slice_fusion.7.refs_0_), channel_id=1, source_target_pairs={{0,8},{2,10},{4,12},{6,14},{8,0},{10,2},{12,4},{14,6},{16,24},{18,... | collective-permute-start | bytes 1376264 | tf_op jit(solution)/shard_map/ppermute | solution.py:41
  15.4 5.1 %collective-permute-done.1.refs_1_ = bf16[128,1792]{1,0:T(8,128)(2,1)S(1)} collective-permute-done((bf16[128,1792]{1,0:T(8,128)(2,1)}, bf16[128,1792]{1,0:T(8,128)(2,1)S(1)}, u32[]{:S(2)}, u32[]{:S(2)}) %collective-permute-start.1) | collective-permute-done | bytes 458784 | tf_op jit(solution)/shard_map/ppermute | solution.py:35
  20.6 2.4 %collective-permute-start.13 = (bf16[128,64]{1,0:T(8,128)(2,1)S(1)}, bf16[128,64]{1,0:T(8,128)(2,1)S(1)}, u32[]{:S(2)}, u32[]{:S(2)}) collective-permute-start(bf16[128,64]{1,0:T(8,128)(2,1)S(1)} %all_gather.3), channel_id=1, source_target_pairs={{0,6},{2,4},{4,2},{6,0},{8,14},{10,12},{12,10},{14,8},{16,22},{18,... | collective-permute-start | bytes 49160 | tf_op jit(solution)/shard_map/ppermute | solution.py:35
  24.5 5.6 %collective-permute-start.4 = (bf16[256,1792]{1,0:T(8,128)(2,1)S(1)}, bf16[256,1792]{1,0:T(8,128)(2,1)S(1)}, u32[]{:S(2)}, u32[]{:S(2)}) collective-permute-start(bf16[256,1792]{1,0:T(8,128)(2,1)S(1)} %pad_maximum_fusion.1), channel_id=1, source_target_pairs={{0,8},{2,10},{4,12},{6,14},{8,0},{10,2},{12,4},{14,6},{16,24},{18,... | collective-permute-start | bytes 2752520 | tf_op jit(solution)/shard_map/ppermute | solution.py:41
  34.3 8.8 %collective-permute-done.7.refs_3_ = bf16[128,1792]{1,0:T(8,128)(2,1)S(1)} collective-permute-done((bf16[128,1792]{1,0:T(8,128)(2,1)S(1)}, bf16[128,1792]{1,0:T(8,128)(2,1)S(1)}, u32[]{:S(2)}, u32[]{:S(2)}) %collective-permute-start.7) | collective-permute-done | bytes 458784 | tf_op jit(solution)/shard_map/ppermute | solution.py:35
  44.6 3.0 %collective-permute-start.8 = (bf16[128,1792]{1,0:T(8,128)(2,1)S(1)}, bf16[128,1792]{1,0:T(8,128)(2,1)S(1)}, u32[]{:S(2)}, u32[]{:S(2)}) collective-permute-start(bf16[128,1792]{1,0:T(8,128)(2,1)S(1)} %collective-permute-done.7.refs_3_), channel_id=1, source_target_pairs={{0,8},{2,10},{4,12},{6,14},{8,0},{10,2},{12,4},{14,6},{16,24},{18,... | collective-permute-start | bytes 1376264 | tf_op jit(solution)/shard_map/ppermute | solution.py:41
  47.9 2.5 %collective-permute-start.16 = (bf16[256,1792]{1,0:T(8,128)(2,1)S(1)}, bf16[256,1792]{1,0:T(8,128)(2,1)S(1)}, u32[]{:S(2)}, u32[]{:S(2)}) collective-permute-start(bf16[256,1792]{1,0:T(8,128)(2,1)S(1)} %get-tuple-element.45), channel_id=1, source_target_pairs={{0,4},{2,6},{4,0},{6,2},{8,12},{10,14},{12,8},{14,10},{16,20},{18,... | collective-permute-start | bytes 2752520 | tf_op jit(solution)/shard_map/ppermute | solution.py:35
  51.4 5.1 %collective-permute-start.14 = (bf16[64,1792]{1,0:T(8,128)(2,1)S(1)}, bf16[64,1792]{1,0:T(8,128)(2,1)S(1)}, u32[]{:S(2)}, u32[]{:S(2)}) collective-permute-start(bf16[64,1792]{1,0:T(8,128)(2,1)S(1)} %get-tuple-element.41), channel_id=1, source_target_pairs={{0,8},{2,10},{4,12},{6,14},{24,16},{26,18},{28,20},{30,22},{1,9},{... | collective-permute-start | bytes 688136 | tf_op jit(solution)/shard_map/ppermute | solution.py:41
  56.7 3.0 %collective-permute-done.8 = bf16[128,1792]{1,0:T(8,128)(2,1)S(1)} collective-permute-done((bf16[128,1792]{1,0:T(8,128)(2,1)S(1)}, bf16[128,1792]{1,0:T(8,128)(2,1)S(1)}, u32[]{:S(2)}, u32[]{:S(2)}) %collective-permute-start.8) | collective-permute-done | bytes 458784 | tf_op jit(solution)/shard_map/ppermute | solution.py:41
  63.0 12.3 %collective-permute-done.16.refs_6_.refs_7_ = bf16[256,1792]{1,0:T(8,128)(2,1)S(1)} collective-permute-done((bf16[256,1792]{1,0:T(8,128)(2,1)S(1)}, bf16[256,1792]{1,0:T(8,128)(2,1)S(1)}, u32[]{:S(2)}, u32[]{:S(2)}) %collective-permute-start.16) | collective-permute-done | bytes 917536 | tf_op jit(solution)/shard_map/ppermute | solution.py:35
  75.3 2.4 %collective-permute-start.17 = (bf16[256,1792]{1,0:T(8,128)(2,1)S(1)}, bf16[256,1792]{1,0:T(8,128)(2,1)S(1)}, u32[]{:S(2)}, u32[]{:S(2)}) collective-permute-start(bf16[256,1792]{1,0:T(8,128)(2,1)S(1)} %get-tuple-element.46), channel_id=1, source_target_pairs={{0,6},{2,4},{4,2},{6,0},{8,14},{10,12},{12,10},{14,8},{16,22},{18,... | collective-permute-start | bytes 2752520 | tf_op jit(solution)/shard_map/ppermute | solution.py:35
  81.3 6.3 %collective-permute-done.18.refs_9_ = bf16[256,896]{1,0:T(8,128)(2,1)S(1)} collective-permute-done((bf16[256,896]{1,0:T(8,128)(2,1)S(1)}, bf16[256,896]{1,0:T(8,128)(2,1)S(1)}, u32[]{:S(2)}, u32[]{:S(2)}) %collective-permute-start.18) | collective-permute-done | bytes 458784 | tf_op jit(solution)/shard_map/ppermute | solution.py:41
  89.6 2.8 %collective-permute-start.21 = (bf16[256,896]{1,0:T(8,128)(2,1)S(1)}, bf16[256,896]{1,0:T(8,128)(2,1)S(1)}, u32[]{:S(2)}, u32[]{:S(2)}) collective-permute-start(bf16[256,896]{1,0:T(8,128)(2,1)S(1)} %slice_select_fusion.2), channel_id=1, source_target_pairs={{0,8},{2,10},{4,12},{6,14},{8,0},{10,2},{12,4},{14,6},{16,24},{18,... | collective-permute-start | bytes 1376264 | tf_op jit(solution)/shard_map/ppermute | solution.py:41
  92.7 11.7 %shard_map.68 = (bf16[4,64,3072]{2,1,0:T(8,128)(2,1)S(1)}, bf16[4,64,3072]{2,1,0:T(8,128)(2,1)S(1)}) custom-call(s32[2]{0:T(128)S(1)} %pad_add_fusion.scalar_ref, bf16[128,1792]{1,0:T(8,128)(2,1)S(1)} %constant_dynamic-slice_fusion.7.refs_0_, bf16[128,1792]{1,0:T(8,128)(2,1)S(1)} %collective-permute-done.1.refs_1_, ...), custom_call_target="tpu_custom_call" | custom-call | flops 1000000 | bytes 100000 | tf_op jit(solution)/shard_map/pallas_call | solution.py:179
  106.0 10.8 %collective-permute-start.28 = (bf16[256,896]{1,0:T(8,128)(2,1)S(1)}, bf16[256,896]{1,0:T(8,128)(2,1)S(1)}, u32[]{:S(2)}, u32[]{:S(2)}) collective-permute-start(bf16[256,896]{1,0:T(8,128)(2,1)S(1)} %slice_select_fusion.1), channel_id=1, source_target_pairs={{0,8},{2,10},{4,12},{6,14},{8,0},{10,2},{12,4},{14,6},{16,24},{18,... | collective-permute-start | bytes 1376264 | tf_op jit(solution)/shard_map/ppermute | solution.py:41
  118.4 9.8 %collective-permute-done.28.refs_12_ = bf16[256,896]{1,0:T(8,128)(2,1)S(1)} collective-permute-done((bf16[256,896]{1,0:T(8,128)(2,1)S(1)}, bf16[256,896]{1,0:T(8,128)(2,1)S(1)}, u32[]{:S(2)}, u32[]{:S(2)}) %collective-permute-start.28) | collective-permute-done | bytes 458784 | tf_op jit(solution)/shard_map/ppermute | solution.py:41
  132.5 12.6 %shard_map.69 = (bf16[4,64,3072]{2,1,0:T(8,128)(2,1)S(1)}, bf16[4,64,3072]{2,1,0:T(8,128)(2,1)}) custom-call(s32[2]{0:T(128)S(1)} %pad_add_fusion.scalar_ref, bf16[256,896]{1,0:T(8,128)(2,1)S(1)} %broadcast_select_fusion.1.refs_0_, bf16[256,896]{1,0:T(8,128)(2,1)S(1)} %broadcast_select_fusion.refs_1_, bf16[256,896]{1,0:T(8,128)(2,1)S(1)} %collective-permute-done.20.refs_2_, ...), custom_call_target="tpu_custom_call" | custom-call | flops 1000000 | bytes 100000 | tf_op jit(solution)/shard_map/pallas_call | solution.py:179
  147.2 3.7 %collective-permute-start.27 = (bf16[64,1024]{1,0:T(8,128)(2,1)S(1)}, bf16[64,1024]{1,0:T(8,128)(2,1)S(1)}, u32[]{:S(2)}, u32[]{:S(2)}) collective-permute-start(bf16[64,1024]{1,0:T(8,128)(2,1)S(1)} %get-tuple-element.96), channel_id=1, source_target_pairs={{0,16},{2,18},{4,20},{6,22},{24,8},{26,10},{28,12},{30,14},{1,17},... | collective-permute-start | bytes 393224 | tf_op jit(solution)/shard_map/ppermute | solution.py:41
  157.2 4.2 %collective-permute-done.40 = bf16[64,1792]{1,0:T(8,128)(2,1)S(1)} collective-permute-done((bf16[64,1792]{1,0:T(8,128)(2,1)S(1)}, bf16[64,1792]{1,0:T(8,128)(2,1)S(1)}, u32[]{:S(2)}, u32[]{:S(2)}) %collective-permute-start.40) | collective-permute-done | bytes 229408 | tf_op jit(solution)/shard_map/ppermute | solution.py:35
  161.9 3.8 %collective-permute-done.41 = bf16[64,1792]{1,0:T(8,128)(2,1)S(1)} collective-permute-done((bf16[64,1792]{1,0:T(8,128)(2,1)S(1)}, bf16[64,1792]{1,0:T(8,128)(2,1)S(1)}, u32[]{:S(2)}, u32[]{:S(2)}) %collective-permute-start.41) | collective-permute-done | bytes 229408 | tf_op jit(solution)/shard_map/ppermute | solution.py:35
  167.6 7.2 %collective-permute-done.33 = bf16[64,3072]{1,0:T(8,128)(2,1)S(1)} collective-permute-done((bf16[64,3072]{1,0:T(8,128)(2,1)S(1)}, bf16[64,3072]{1,0:T(8,128)(2,1)S(1)}, u32[]{:S(2)}, u32[]{:S(2)}) %collective-permute-start.33) | collective-permute-done | bytes 393248 | tf_op jit(solution)/shard_map/ppermute | solution.py:35
  176.2 6.5 %collective-permute-done.34 = bf16[64,3072]{1,0:T(8,128)(2,1)S(1)} collective-permute-done((bf16[64,3072]{1,0:T(8,128)(2,1)S(1)}, bf16[64,3072]{1,0:T(8,128)(2,1)S(1)}, u32[]{:S(2)}, u32[]{:S(2)}) %collective-permute-start.34) | collective-permute-done | bytes 393248 | tf_op jit(solution)/shard_map/ppermute | solution.py:35
  182.9 4.0 %collective-permute-start.39 = (bf16[64,1024]{1,0:T(8,128)(2,1)S(1)}, bf16[64,1024]{1,0:T(8,128)(2,1)S(1)}, u32[]{:S(2)}, u32[]{:S(2)}) collective-permute-start(bf16[64,1024]{1,0:T(8,128)(2,1)S(1)} %get-tuple-element.95), channel_id=1, source_target_pairs={{0,24},{2,26},{4,28},{6,30},{24,0},{26,2},{28,4},{30,6},{1,25},{3,... | collective-permute-start | bytes 393224 | tf_op jit(solution)/shard_map/ppermute | solution.py:41
  188.9 7.6 %fusion = f32[256,7168]{1,0:T(8,128)} fusion(bf16[64,7168]{1,0:T(8,128)(2,1)S(1)} %constant_dynamic-update-slice_fusion.7, f32[256,7168]{1,0:T(8,128)} %param.9, f32[4096,64]{0,1:T(8,128)S(1)} %copy-done, s32[]{:T(128)S(6)} %select_n.169), kind=kOutput, calls=%fused_computation.1 | convolution fusion | flops 240386048 | bytes 15630340 | tf_op jit(solution)/shard_map/dot_general | solution.py:101
  (115 shorter events, 54.6 us)
Async XLA Ops:
  1.8 21.8 %collective-permute-start = (bf16[128,1792]{1,0:T(8,128)(2,1)S(1)}, bf16[128,1792]{1,0:T(8,128)(2,1)S(1)}, u32[]{:S(2)}, u32[]{:S(2)}) collective-permute-start(bf16[128,1792]{1,0:T(8,128)(2,1)S(1)} %constant_dynamic-slice_fusion.7.refs_0_), channel_id=1, source_target_pairs={{0,8},{2,10},{4,12},{6,14},{8,0},{10,2},{12,4},{14,6},{16,24},{18,... | collective-permute-start | bytes 1376264 | tf_op jit(solution)/shard_map/ppermute | solution.py:41
  4.9 18.7 %collective-permute-start.3 = (bf16[128,1792]{1,0:T(8,128)(2,1)S(1)}, bf16[128,1792]{1,0:T(8,128)(2,1)S(1)}, u32[]{:S(2)}, u32[]{:S(2)}) collective-permute-start(bf16[128,1792]{1,0:T(8,128)(2,1)S(1)} %constant_dynamic-slice_fusion.7.refs_0_), channel_id=1, source_target_pairs={{8,16},{10,18},{12,20},{14,22},{16,8},{18,10},{20,12},{22,14},{9,1... | collective-permute-start | bytes 1376264 | tf_op jit(solution)/shard_map/ppermute | solution.py:41
  14.6 17.8 %collective-permute-start.11 = (bf16[128,64]{1,0:T(8,128)(2,1)S(1)}, bf16[128,64]{1,0:T(8,128)(2,1)S(1)}, u32[]{:S(2)}, u32[]{:S(2)}) collective-permute-start(bf16[128,64]{1,0:T(8,128)(2,1)S(1)} %all_gather.3), channel_id=1, source_target_pairs={{0,2},{2,0},{4,6},{6,4},{8,10},{10,8},{12,14},{14,12},{16,18},{18,... | collective-permute-start | bytes 49160 | tf_op jit(solution)/shard_map/ppermute | solution.py:35
  20.6 23.1 %collective-permute-start.13 = (bf16[128,64]{1,0:T(8,128)(2,1)S(1)}, bf16[128,64]{1,0:T(8,128)(2,1)S(1)}, u32[]{:S(2)}, u32[]{:S(2)}) collective-permute-start(bf16[128,64]{1,0:T(8,128)(2,1)S(1)} %all_gather.3), channel_id=1, source_target_pairs={{0,6},{2,4},{4,2},{6,0},{8,14},{10,12},{12,10},{14,8},{16,22},{18,... | collective-permute-start | bytes 49160 | tf_op jit(solution)/shard_map/ppermute | solution.py:35
  23.0 21.6 %collective-permute-start.12 = (bf16[128,64]{1,0:T(8,128)(2,1)S(1)}, bf16[128,64]{1,0:T(8,128)(2,1)S(1)}, u32[]{:S(2)}, u32[]{:S(2)}) collective-permute-start(bf16[128,64]{1,0:T(8,128)(2,1)S(1)} %all_gather.3), channel_id=1, source_target_pairs={{0,4},{2,6},{4,0},{6,2},{8,12},{10,14},{12,8},{14,10},{16,20},{18,... | collective-permute-start | bytes 49160 | tf_op jit(solution)/shard_map/ppermute | solution.py:35
  23.6 24.3 %collective-permute-start.5 = (bf16[256,1792]{1,0:T(8,128)(2,1)S(1)}, bf16[256,1792]{1,0:T(8,128)(2,1)S(1)}, u32[]{:S(2)}, u32[]{:S(2)}) collective-permute-start(bf16[256,1792]{1,0:T(8,128)(2,1)S(1)} %pad_maximum_fusion.1), channel_id=1, source_target_pairs={{8,16},{10,18},{12,20},{14,22},{16,8},{18,10},{20,12},{22,14},{9,1... | collective-permute-start | bytes 2752520 | tf_op jit(solution)/shard_map/ppermute | solution.py:41
  24.5 26.9 %collective-permute-start.4 = (bf16[256,1792]{1,0:T(8,128)(2,1)S(1)}, bf16[256,1792]{1,0:T(8,128)(2,1)S(1)}, u32[]{:S(2)}, u32[]{:S(2)}) collective-permute-start(bf16[256,1792]{1,0:T(8,128)(2,1)S(1)} %pad_maximum_fusion.1), channel_id=1, source_target_pairs={{0,8},{2,10},{4,12},{6,14},{8,0},{10,2},{12,4},{14,6},{16,24},{18,... | collective-permute-start | bytes 2752520 | tf_op jit(solution)/shard_map/ppermute | solution.py:41
  43.1 19.9 %collective-permute-start.15 = (bf16[256,1792]{1,0:T(8,128)(2,1)S(1)}, bf16[256,1792]{1,0:T(8,128)(2,1)S(1)}, u32[]{:S(2)}, u32[]{:S(2)}) collective-permute-start(bf16[256,1792]{1,0:T(8,128)(2,1)S(1)} %get-tuple-element.44), channel_id=1, source_target_pairs={{0,2},{2,0},{4,6},{6,4},{8,10},{10,8},{12,14},{14,12},{16,18},{18,... | collective-permute-start | bytes 2752520 | tf_op jit(solution)/shard_map/ppermute | solution.py:35
  43.7 16.7 %collective-permute-start.9 = (bf16[128,1792]{1,0:T(8,128)(2,1)S(1)}, bf16[128,1792]{1,0:T(8,128)(2,1)S(1)}, u32[]{:S(2)}, u32[]{:S(2)}) collective-permute-start(bf16[128,1792]{1,0:T(8,128)(2,1)S(1)} %collective-permute-done.7.refs_3_), channel_id=1, source_target_pairs={{8,16},{10,18},{12,20},{14,22},{16,8},{18,10},{20,12},{22,14},{9,1... | collective-permute-start | bytes 1376264 | tf_op jit(solution)/shard_map/ppermute | solution.py:41
  47.9 27.3 %collective-permute-start.16 = (bf16[256,1792]{1,0:T(8,128)(2,1)S(1)}, bf16[256,1792]{1,0:T(8,128)(2,1)S(1)}, u32[]{:S(2)}, u32[]{:S(2)}) collective-permute-start(bf16[256,1792]{1,0:T(8,128)(2,1)S(1)} %get-tuple-element.45), channel_id=1, source_target_pairs={{0,4},{2,6},{4,0},{6,2},{8,12},{10,14},{12,8},{14,10},{16,20},{18,... | collective-permute-start | bytes 2752520 | tf_op jit(solution)/shard_map/ppermute | solution.py:35
  51.4 40.9 %collective-permute-start.14 = (bf16[64,1792]{1,0:T(8,128)(2,1)S(1)}, bf16[64,1792]{1,0:T(8,128)(2,1)S(1)}, u32[]{:S(2)}, u32[]{:S(2)}) collective-permute-start(bf16[64,1792]{1,0:T(8,128)(2,1)S(1)} %get-tuple-element.41), channel_id=1, source_target_pairs={{0,8},{2,10},{4,12},{6,14},{24,16},{26,18},{28,20},{30,22},{1,9},{... | collective-permute-start | bytes 688136 | tf_op jit(solution)/shard_map/ppermute | solution.py:41
  59.6 21.3 %collective-permute-start.6 = (bf16[256,896]{1,0:T(8,128)(2,1)S(1)}, bf16[256,896]{1,0:T(8,128)(2,1)S(1)}, u32[]{:S(2)}, u32[]{:S(2)}) collective-permute-start(bf16[256,896]{1,0:T(8,128)(2,1)S(1)} %get-tuple-element.35), channel_id=1, source_target_pairs={{8,16},{10,18},{12,20},{14,22},{16,8},{18,10},{20,12},{22,14},{9,1... | collective-permute-start | bytes 1376264 | tf_op jit(solution)/shard_map/ppermute | solution.py:41
  60.5 31.9 %collective-permute-start.10 = (bf16[256,896]{1,0:T(8,128)(2,1)S(1)}, bf16[256,896]{1,0:T(8,128)(2,1)S(1)}, u32[]{:S(2)}, u32[]{:S(2)}) collective-permute-start(bf16[256,896]{1,0:T(8,128)(2,1)S(1)} %get-tuple-element.39), channel_id=1, source_target_pairs={{8,16},{10,18},{12,20},{14,22},{16,8},{18,10},{20,12},{22,14},{9,1... | collective-permute-start | bytes 1376264 | tf_op jit(solution)/shard_map/ppermute | solution.py:41
  87.6 16.9 %collective-permute-start.20 = (bf16[256,896]{1,0:T(8,128)(2,1)S(1)}, bf16[256,896]{1,0:T(8,128)(2,1)S(1)}, u32[]{:S(2)}, u32[]{:S(2)}) collective-permute-start(bf16[256,896]{1,0:T(8,128)(2,1)S(1)} %get-tuple-element.51), channel_id=1, source_target_pairs={{8,16},{10,18},{12,20},{14,22},{16,8},{18,10},{20,12},{22,14},{9,1... | collective-permute-start | bytes 1376264 | tf_op jit(solution)/shard_map/ppermute | solution.py:41
  104.5 23.8 %collective-permute-start.22 = (bf16[4,64,3072]{2,1,0:T(8,128)(2,1)S(1)}, bf16[4,64,3072]{2,1,0:T(8,128)(2,1)S(1)}, u32[]{:S(2)}, u32[]{:S(2)}) collective-permute-start(bf16[4,64,3072]{2,1,0:T(8,128)(2,1)S(1)} %get-tuple-element.53), channel_id=1, source_target_pairs={{0,1},{1,0},{2,3},{3,2},{4,5},{5,4},{6,7},{7,6},{8,9},{9,8},{10,11... | collective-permute-start | bytes 4718600 | tf_op jit(solution)/shard_map/ppermute | solution.py:264
  105.2 27.3 %collective-permute-start.29 = (bf16[256,896]{1,0:T(8,128)(2,1)S(1)}, bf16[256,896]{1,0:T(8,128)(2,1)S(1)}, u32[]{:S(2)}, u32[]{:S(2)}) collective-permute-start(bf16[256,896]{1,0:T(8,128)(2,1)S(1)} %get-tuple-element.56), channel_id=1, source_target_pairs={{8,16},{10,18},{12,20},{14,22},{16,8},{18,10},{20,12},{22,14},{9,1... | collective-permute-start | bytes 1376264 | tf_op jit(solution)/shard_map/ppermute | solution.py:41
  106.0 22.2 %collective-permute-start.28 = (bf16[256,896]{1,0:T(8,128)(2,1)S(1)}, bf16[256,896]{1,0:T(8,128)(2,1)S(1)}, u32[]{:S(2)}, u32[]{:S(2)}) collective-permute-start(bf16[256,896]{1,0:T(8,128)(2,1)S(1)} %slice_select_fusion.1), channel_id=1, source_target_pairs={{0,8},{2,10},{4,12},{6,14},{8,0},{10,2},{12,4},{14,6},{16,24},{18,... | collective-permute-start | bytes 1376264 | tf_op jit(solution)/shard_map/ppermute | solution.py:41
  128.9 16.2 %collective-permute-start.23 = (bf16[64,3072]{1,0:T(8,128)(2,1)S(1)}, bf16[64,3072]{1,0:T(8,128)(2,1)S(1)}, u32[]{:S(2)}, u32[]{:S(2)}) collective-permute-start(bf16[64,3072]{1,0:T(8,128)(2,1)S(1)} %get-tuple-element.79), channel_id=1, source_target_pairs={{0,2},{2,0},{4,6},{6,4},{8,10},{10,8},{12,14},{14,12},{16,18},{18,... | collective-permute-start | bytes 1179656 | tf_op jit(solution)/shard_map/ppermute | solution.py:35
  130.5 16.4 %collective-permute-start.24 = (bf16[64,3072]{1,0:T(8,128)(2,1)S(1)}, bf16[64,3072]{1,0:T(8,128)(2,1)S(1)}, u32[]{:S(2)}, u32[]{:S(2)}) collective-permute-start(bf16[64,3072]{1,0:T(8,128)(2,1)S(1)} %get-tuple-element.81), channel_id=1, source_target_pairs={{0,4},{2,6},{4,0},{6,2},{8,12},{10,14},{12,8},{14,10},{16,20},{18,... | collective-permute-start | bytes 1179656 | tf_op jit(solution)/shard_map/ppermute | solution.py:35
  147.2 49.3 %collective-permute-start.27 = (bf16[64,1024]{1,0:T(8,128)(2,1)S(1)}, bf16[64,1024]{1,0:T(8,128)(2,1)S(1)}, u32[]{:S(2)}, u32[]{:S(2)}) collective-permute-start(bf16[64,1024]{1,0:T(8,128)(2,1)S(1)} %get-tuple-element.96), channel_id=1, source_target_pairs={{0,16},{2,18},{4,20},{6,22},{24,8},{26,10},{28,12},{30,14},{1,17},... | collective-permute-start | bytes 393224 | tf_op jit(solution)/shard_map/ppermute | solution.py:41
  156.5 18.3 %collective-permute-start.33 = (bf16[64,3072]{1,0:T(8,128)(2,1)S(1)}, bf16[64,3072]{1,0:T(8,128)(2,1)S(1)}, u32[]{:S(2)}, u32[]{:S(2)}) collective-permute-start(bf16[64,3072]{1,0:T(8,128)(2,1)S(1)} %get-tuple-element.76), channel_id=1, source_target_pairs={{0,2},{2,0},{4,6},{6,4},{8,10},{10,8},{12,14},{14,12},{16,18},{18,... | collective-permute-start | bytes 1179656 | tf_op jit(solution)/shard_map/ppermute | solution.py:35
  161.4 21.3 %collective-permute-start.34 = (bf16[64,3072]{1,0:T(8,128)(2,1)S(1)}, bf16[64,3072]{1,0:T(8,128)(2,1)S(1)}, u32[]{:S(2)}, u32[]{:S(2)}) collective-permute-start(bf16[64,3072]{1,0:T(8,128)(2,1)S(1)} %get-tuple-element.78), channel_id=1, source_target_pairs={{0,4},{2,6},{4,0},{6,2},{8,12},{10,14},{12,8},{14,10},{16,20},{18,... | collective-permute-start | bytes 1179656 | tf_op jit(solution)/shard_map/ppermute | solution.py:35
  165.7 17.0 %collective-permute-start.35 = (bf16[64,3072]{1,0:T(8,128)(2,1)S(1)}, bf16[64,3072]{1,0:T(8,128)(2,1)S(1)}, u32[]{:S(2)}, u32[]{:S(2)}) collective-permute-start(bf16[64,3072]{1,0:T(8,128)(2,1)S(1)} %get-tuple-element.77), channel_id=1, source_target_pairs={{0,6},{2,4},{4,2},{6,0},{8,14},{10,12},{12,10},{14,8},{16,22},{18,... | collective-permute-start | bytes 1179656 | tf_op jit(solution)/shard_map/ppermute | solution.py:35
  166.9 29.6 %collective-permute-start.38 = (bf16[64,1024]{1,0:T(8,128)(2,1)S(1)}, bf16[64,1024]{1,0:T(8,128)(2,1)S(1)}, u32[]{:S(2)}, u32[]{:S(2)}) collective-permute-start(bf16[64,1024]{1,0:T(8,128)(2,1)S(1)} %get-tuple-element.96), channel_id=1, source_target_pairs={{8,16},{10,18},{12,20},{14,22},{16,8},{18,10},{20,12},{22,14},{9,1... | collective-permute-start | bytes 393224 | tf_op jit(solution)/shard_map/ppermute | solution.py:41
  (21 other events, 237.2 us)

commit v3 on v2

--- a/solution.py
+++ b/solution.py
@@ -128,11 +128,11 @@
     return input_grad, new_momentum
 
 
-def products(lay, sources, buffers, fills, jobs, width):
+def products(lay, sources, buffers, fills, jobs, width, blocks):
     scalars = jnp.stack([lay.place, lay.core]).astype(jnp.int32)
-    rows = buffers[jobs[0][0]][0]
-    half = rows // PLANE // 2
     piece = width // PLANE
+    block = sum(job[2] for job in jobs) // blocks
+    half = block // PLANE // 2
 
     def kernel(scalar_ref, *refs):
         ins, refs = refs[: len(sources)], refs[len(sources):]
@@ -159,23 +159,24 @@
                     copies[i].wait()
                     waited.add(i)
 
-        for at, (a, b, a0, b0, cols, a_ids, b_ids) in enumerate(jobs):
+        for a, row, count, a0, b, b0, cols, a_ids, b_ids, first in jobs:
             need(a_ids)
             for r in range(PLANE):
                 need(b_ids(r))
                 x = nt(
-                    buffer_refs[a][:, a0:a0 + cols],
+                    buffer_refs[a][row:row + count, a0:a0 + cols],
                     buffer_refs[b][r * piece:(r + 1) * piece, b0:b0 + cols],
                 ).astype(bf16)
-                column = at * width + pl.multiple_of((place ^ r) * piece, piece)
-                for p in range(PLANE):
-                    low = x[2 * p * half:(2 * p + 1) * half]
-                    high = x[(2 * p + 1) * half:(2 * p + 2) * half]
-                    keep_ref[p, :, pl.ds(column, piece)] = jnp.where(core == 0, low, high)
-                    give_ref[p, :, pl.ds(column, piece)] = jnp.where(core == 0, high, low)
+                for at in range(count // block):
+                    column = (first + at) * width + pl.multiple_of((place ^ r) * piece, piece)
+                    for p in range(PLANE):
+                        low = x[at * block + 2 * p * half:][:half]
+                        high = x[at * block + (2 * p + 1) * half:][:half]
+                        keep_ref[p, :, pl.ds(column, piece)] = jnp.where(core == 0, low, high)
+                        give_ref[p, :, pl.ds(column, piece)] = jnp.where(core == 0, high, low)
         need(range(len(copies)))
 
-    out = jax.ShapeDtypeStruct((PLANE, half, len(jobs) * width), bf16)
+    out = jax.ShapeDtypeStruct((PLANE, half, blocks * width), bf16)
     return pl.pallas_call(
         kernel,
         out_shape=(out, out),
@@ -209,78 +210,82 @@
         sent.append(got)
         return got
 
-    a0 = lay.cut(out_grad, 0)
-    e0, m0 = queued(end_swap, end_sent, a0), queued(mid_swap, mid_sent, a0)
-    cuts = [lay.cut(after(out_grad, a0), r) for r in range(1, PLANE)]
-    ax, ay = across(cuts[0], 1), across(cuts[1], 2)
-    ad = across(after(cuts[2], ax, ay, e0, m0), 3)
-    axy = after(jnp.concatenate([ax, ay], 0), e0, m0)
-    e1, m1 = queued(end_swap, end_sent, axy), queued(mid_swap, mid_sent, axy)
+    cuts = [lay.cut(out_grad, r) for r in range(PLANE)]
+    ax, ay = across(cuts[1], 1), across(cuts[2], 2)
+    e0, m0 = queued(end_swap, end_sent, cuts[0]), queued(mid_swap, mid_sent, cuts[0])
     proj = projected(lay, after(inputs, *cuts), proj_basis)
-    weight = after(weight, ax, ay)
+    weight = after(weight, proj[0])
     parts = [lay.cut(weight, r) for r in range(PLANE)]
-    parts[1:3] = [across(after(parts[r], ad), r) for r in (1, 2)]
-    parts[3] = across(after(parts[3], parts[1], parts[2]), 3)
-    e2, m2 = queued(end_swap, end_sent, ad), queued(mid_swap, mid_sent, ad)
-
-    panel = sum(tn(q, a) for q, a in zip(proj, [a0, ax, ay, ad]))
+    ad = across(after(cuts[3], proj[0], ax, ay), 3)
+    e1, m1 = queued(end_swap, end_sent, ax), queued(mid_swap, mid_sent, ax)
+    parts[1:3] = [across(after(parts[r], ax, ay), r) for r in (1, 2)]
+    ayd = jnp.concatenate([ay, ad], 0)
+    e2, m2 = queued(end_swap, end_sent, ayd), queued(mid_swap, mid_sent, ayd)
+    parts[3] = across(after(parts[3], ad, parts[1]), 3)
+    own, near_e, near_m = [cuts[0], ax, ayd], [e0, e1, e2], [m0, m1, m2]
+    halves = lambda x, c: [jnp.concatenate([x[0][:, c], x[1][:, c]], 0), x[2][:, c]]
+    low, high = slice(0, half), slice(half, 2 * half)
+
+    panel = sum(tn(q, a) for q, a in zip(proj, [cuts[0], ax, ay, ad]))
     panel = panel + inward(after(panel.astype(bf16), e1, m1)).astype(f32)
 
-    near_e, near_m = jnp.concatenate([e0, e1, e2], 0), jnp.concatenate([m0, m1, m2], 0)
-    pair = 2 * tokens
     far0, far1, got = [], [], []
-    for i in range(2):
-        far0.append(queued(mid_swap, mid_sent, near_e[i * pair:(i + 1) * pair, :half]))
-        got.append(queued(end_swap, end_sent, send(near_m[i * pair:(i + 1) * pair, :half], parts[i][:, half:])))
-    pair_panel = panel
-    other_pair = mid_swap(after(panel.astype(bf16), far0[0], got[0]))
-    for i in range(2):
-        far1.append(queued(mid_swap, mid_sent, near_e[i * pair:(i + 1) * pair, half:]))
-        got.append(queued(end_swap, end_sent, send(far0[i], parts[2 + i][:, half:]), parts[3]))
+    for x, m, w in zip(halves(near_e, low), halves(near_m, low), parts):
+        far0.append(queued(mid_swap, mid_sent, x))
+        got.append(queued(end_swap, end_sent, send(m, w[:, high])))
+    other_pair = mid_swap(after(panel.astype(bf16), far0[0]))
+    for x, f, w in zip(halves(near_e, high), far0, parts[2:]):
+        far1.append(queued(mid_swap, mid_sent, x))
+        got.append(queued(end_swap, end_sent, send(f, w[:, high]), parts[3]))
+
     def weight_fills(first, buffer):
         return [(first + r, 0, buffer, r * rows, 0, 2 * half) for r in range(PLANE)]
 
-    def block_fills(first, buffer, sizes, column, cols):
-        out, row = [], 0
+    def block_fills(first, buffer, sizes, column, row, cols):
+        out = []
         for i, n in enumerate(sizes):
             out.append((first + i, column, buffer, row, column, cols))
             row += n
         return out
 
     both = 2 * half
-    early0 = send(near_m[:, :half], jnp.concatenate(got[:2], 0))
-    sources = [after(a0, *far0, pair_panel), ax, ay, ad, *parts, near_e, early0, near_m]
-    fills = block_fills(0, 0, [tokens] * PLANE, 0, both) + weight_fills(4, 3)
-    fills += [(8, 0, 1, 0, 0, both), (9, 0, 2, 0, 0, half), (10, half, 2, 0, half, half)]
-    wide, tall = (PLANE * tokens, both), (width, both)
-    of_weight = lambda r: (4 + r,)
+    sizes = [tokens, tokens, 2 * tokens]
+    block = PLANE * tokens
+    early0 = jnp.concatenate([send(m, g) for m, g in zip(halves(near_m, low), got)], 0)
+    sources = [*own, *near_e, *near_m, early0, *parts]
+    sources[0] = after(sources[0], *far0, panel)
+    fills = block_fills(0, 0, sizes, 0, 0, both)
+    fills += weight_fills(10, 1)
+    fills += block_fills(3, 0, sizes, 0, block, both) + [(9, 0, 0, 2 * block, 0, half)]
+    fills += block_fills(6, 0, sizes, half, 2 * block, half)
+    of_weight = lambda r: (3 + r,)
     none = lambda r: ()
-    jobs = [
-        (0, 3, 0, 0, both, range(4), of_weight),
-        (1, 3, 0, 0, both, (8,), none),
-        (2, 3, 0, 0, both, (9, 10), none),
-    ]
-    keep, give = products(lay, sources, [wide, wide, wide, tall], fills, jobs, width)
+    jobs = [(0, 0, 3 * block, 0, 1, 0, both, (*range(3), *range(7, 14)), of_weight, 0)]
+    buffers = [(3 * block, both), (width, both)]
+    keep, give = products(lay, sources, buffers, fills, jobs, width, 3)
     swap = lambda x: lax.ppermute(x, "tensor", [(0, 1), (1, 0)])
     give = after(give, far1[0], got[2])
-    panel = (panel + after(other_pair, keep).astype(f32)).astype(bf16)
+    first = (keep.astype(f32) + swap(give).astype(f32)).astype(bf16)
+    panel = (panel + after(other_pair, first).astype(f32)).astype(bf16)
     panel = send(panel, outward(after(panel, far1[0], got[2])))
-    first = (keep.astype(f32) + swap(give).astype(f32)).astype(bf16)
 
     late0 = [send(far0[i], got[2 + i]) for i in range(2)]
-    late0[0] = after(late0[0], first)
-    sources = [*late0, *far1, near_m, *parts, *got]
+    sources = [*late0, *far1, *near_m, *parts, *got]
+    sources[0] = after(sources[0], first)
+    pair = 2 * tokens
     fills = [(i, 0, 0, i * pair, 0, half) for i in range(2)]
     fills += [(2 + i, 0, 0, i * pair, half, half) for i in range(2)]
-    fills += weight_fills(5, 2) + [(4, half, 1, 0, 0, half)]
-    fills += [(9 + r, 0, 3, r * rows, 0, half) for r in range(PLANE)]
+    fills += weight_fills(7, 2)
+    fills += [(s, c, b, r0, 0, n) for s, c, b, r0, _, n in block_fills(4, 1, sizes, half, 0, half)]
+    fills += [(2 + i, 0, 1, block + i * pair, 0, half) for i in range(2)]
+    fills += [(11 + r, 0, 3, r * rows, 0, half) for r in range(PLANE)]
+    of_weight = lambda r: (4 + r,)
     jobs = [
-        (0, 2, 0, 0, both, range(4), of_weight),
-        (1, 3, 0, 0, half, (8,), lambda r: (9 + r,)),
-        (0, 3, half, 0, half, (), none),
+        (0, 0, block, 0, 2, 0, both, range(4), of_weight, 0),
+        (1, 0, 2 * block, 0, 3, 0, half, range(8, 13), lambda r: (13 + r,), 1),
     ]
-    buffers = [wide, (PLANE * tokens, half), tall, (width, half)]
-    keep, give = products(lay, sources, buffers, fills, jobs, width)
+    buffers = [(block, both), (2 * block, half), (width, both), (width, half)]
+    keep, give = products(lay, sources, buffers, fills, jobs, width, 3)
 
     def plane_sum(part):
         total = part[0].astype(f32)
@@ -290,10 +295,10 @@
 
     first = plane_sum(first)
     second = (keep.astype(f32) + swap(after(give, first, panel)).astype(f32)).astype(bf16)
+    second = plane_sum(second)
     panel = after(panel, second)
     panel = lay.in_order([panel] + [across(panel, r) for r in range(1, PLANE)], 1)
     new_momentum = updated(lay, proj_basis, panel, momentum, tokens * lay.replicas)
-    second = plane_sum(second)
     y0, y1, early = [first[:, i * width:(i + 1) * width] for i in range(3)]
     late, early_other, late_other = [second[:, i * width:(i + 1) * width] for i in range(3)]
 

time: 201 us -> 211 us (1.050); the launches traced: 200 us -> 208 us
  Pallas kernels: 24.3 us -> 28.2 us
  waiting for transfers between devices: 75.1 us -> 78.4 us
    pallas_call x2, Pallas kernels: 24.3 us -> 28.2 us  [products(): pl.pallas_call(kernel, out_shape=(out, out), in_specs=[pl.BlockSpec(memor...]
    ppermute x2, waiting for transfers between devices: 0.01 us -> 3.4 us  [line_of_four(): swap = lambda x: lax.ppermute(x, 'tensor', [(0, 1), (1, 0)])]
    dot_general x4, matrix products: 0.96 us -> 3.93 us  [tn(): lax.dot_general(a, b, (((0,), (0,)), ((), ())), preferred_element_type=f32)]
    ppermute x18, waiting for transfers between devices: 52.5 us -> 50.4 us  [across(): return lax.ppermute(x, 'dp', [(d, d ^ r) for d in range(self.replicas)])]
    dynamic_slice x3 -> x2, local copies, waits for them, and re-layouts: 5.8 us -> 4.33 us  [cut(): return lax.dynamic_slice_in_dim(x, (self.place ^ r) * quarter, quarter, 1)]
  transfers between devices with their start and end apart: 43 -> 43, of which waited for: 16 -> 15; matrix products, arithmetic and copies ran while one was open for 10% -> 9% of each run, Pallas kernels for 12% -> 14%
where the time goes in v3:
time: 211 us; the launch traced here: 208 us
  waiting for transfers between devices  78.4 us (37%)
  starting transfers between devices  73 us (35%)
  Pallas kernels  28.2 us (13%)
  matrix products  12.2 us (6%)
  local copies, waits for them, and re-layouts  6.94 us (3%)
  other arithmetic  5.86 us (3%)
    ppermute x18, waiting for transfers between devices, across(): return lax.ppermute(x, 'dp', [(d, d ^ r) for d in range(self.replicas)])  50.4 us
    ppermute x23, starting transfers between devices, levels(): return lax.ppermute(x, 'dp', pairs)  50 us
    pallas_call x2, Pallas kernels, products(): pl.pallas_call(kernel, out_shape=(out, out), in_specs=[pl.BlockSpec(memor...  28.2 us
    ppermute x23, waiting for transfers between devices, levels(): return lax.ppermute(x, 'dp', pairs)  24.6 us
    ppermute x18, starting transfers between devices, across(): return lax.ppermute(x, 'dp', [(d, d ^ r) for d in range(self.replicas)])  22.8 us
    dot_general x1, matrix products, updated(): update = jnp.dot(basis_rows.astype(bf16), panel, preferred_element_type=f32)  7.58 us
    dynamic_slice x2, local copies, waits for them, and re-layouts, cut(): return lax.dynamic_slice_in_dim(x, (self.place ^ r) * quarter, quarter, 1)  4.33 us
  transfers between devices with their start and end apart: 43, of which 15 were waited for; matrix products, arithmetic and copies ran while one was open for 9% of the time, Pallas kernels for 14%

profile of v3, /device:TPU:0, one launch (start us, length us, event | category | flops | bytes accessed | tf_op | source)
XLA Modules:
  0.0 207.6 jit_solution(4827690461835070735)
XLA Ops:
  0.7 2.7 %constant_dynamic-slice_fusion.4 = (bf16[128,1792]{1,0:T(8,128)(2,1)}, bf16[128,1792]{1,0:T(8,128)(2,1)}, bf16[128,1792]{1,0:T(8,128)(2,1)S(1)}, bf16[128,1792]{1,0:T(8,128)(2,1)}) fusion(bf16[128,7168]{1,0:T(8,128)(2,1)} %param.6, s32[]{:T(128)S(6)} %select_n.142, s32[]{:T(128)S(6)} %select_n.140, s32[]{:T(128)S(6)} %select_n.139, s32[]{:T(128)S(6)} %select_n.141), kind=kLoop, calls=%fused_computation.59 | loop fusion | bytes 3670032 | tf_op jit(solution)/shard_map/dynamic_slice | solution.py:45
  3.4 3.0 %collective-permute-start = (bf16[128,1792]{1,0:T(8,128)(2,1)S(1)}, bf16[128,1792]{1,0:T(8,128)(2,1)S(1)}, u32[]{:S(2)}, u32[]{:S(2)}) collective-permute-start(bf16[128,1792]{1,0:T(8,128)(2,1)S(1)} %get-tuple-element.38.refs_0_), channel_id=1, source_target_pairs={{0,8},{2,10},{4,12},{6,14},{8,0},{10,2},{12,4},{14,6},{16,24},{18,... | collective-permute-start | bytes 1376264 | tf_op jit(solution)/shard_map/ppermute | solution.py:41
  16.0 3.8 %collective-permute-done.1.refs_1_ = bf16[128,1792]{1,0:T(8,128)(2,1)} collective-permute-done((bf16[128,1792]{1,0:T(8,128)(2,1)}, bf16[128,1792]{1,0:T(8,128)(2,1)}, u32[]{:S(2)}, u32[]{:S(2)}) %collective-permute-start.1) | collective-permute-done | bytes 458784 | tf_op jit(solution)/shard_map/ppermute | solution.py:35
  19.8 2.4 %collective-permute-start.13 = (bf16[128,64]{1,0:T(8,128)(2,1)S(1)}, bf16[128,64]{1,0:T(8,128)(2,1)S(1)}, u32[]{:S(2)}, u32[]{:S(2)}) collective-permute-start(bf16[128,64]{1,0:T(8,128)(2,1)S(1)} %all_gather.3), channel_id=1, source_target_pairs={{0,6},{2,4},{4,2},{6,0},{8,14},{10,12},{12,10},{14,8},{16,22},{18,... | collective-permute-start | bytes 49160 | tf_op jit(solution)/shard_map/ppermute | solution.py:35
  22.8 4.1 %collective-permute-start.2 = (bf16[128,1792]{1,0:T(8,128)(2,1)}, bf16[128,1792]{1,0:T(8,128)(2,1)S(1)}, u32[]{:S(2)}, u32[]{:S(2)}) collective-permute-start(bf16[128,1792]{1,0:T(8,128)(2,1)} %collective-permute-done.1.refs_1_), channel_id=1, source_target_pairs={{0,8},{2,10},{4,12},{6,14},{8,0},{10,2},{12,4},{14,6},{16,24},{18,... | collective-permute-start | bytes 1376264 | tf_op jit(solution)/shard_map/ppermute | solution.py:41
  33.3 9.7 %collective-permute-done.6 = bf16[128,1792]{1,0:T(8,128)(2,1)S(1)} collective-permute-done((bf16[128,1792]{1,0:T(8,128)(2,1)}, bf16[128,1792]{1,0:T(8,128)(2,1)S(1)}, u32[]{:S(2)}, u32[]{:S(2)}) %collective-permute-start.6) | collective-permute-done | bytes 458784 | tf_op jit(solution)/shard_map/ppermute | solution.py:35
  46.8 5.4 %collective-permute-start.14 = (bf16[64,1792]{1,0:T(8,128)(2,1)S(1)}, bf16[64,1792]{1,0:T(8,128)(2,1)S(1)}, u32[]{:S(2)}, u32[]{:S(2)}) collective-permute-start(bf16[64,1792]{1,0:T(8,128)(2,1)S(1)} %get-tuple-element.37), channel_id=1, source_target_pairs={{0,8},{2,10},{4,12},{6,14},{24,16},{26,18},{28,20},{30,22},{1,9},{... | collective-permute-start | bytes 688136 | tf_op jit(solution)/shard_map/ppermute | solution.py:41
  53.6 5.5 %collective-permute-done.16.refs_11_.refs_8_ = bf16[256,1792]{1,0:T(8,128)(2,1)S(1)} collective-permute-done((bf16[256,1792]{1,0:T(8,128)(2,1)S(1)}, bf16[256,1792]{1,0:T(8,128)(2,1)S(1)}, u32[]{:S(2)}, u32[]{:S(2)}) %collective-permute-start.16) | collective-permute-done | bytes 917536 | tf_op jit(solution)/shard_map/ppermute | solution.py:35
  63.1 10.8 %collective-permute-start.15 = (bf16[256,896]{1,0:T(8,128)(2,1)S(1)}, bf16[256,896]{1,0:T(8,128)(2,1)S(1)}, u32[]{:S(2)}, u32[]{:S(2)}) collective-permute-start(bf16[256,896]{1,0:T(8,128)(2,1)S(1)} %dynamic-slice_select_fusion), channel_id=1, source_target_pairs={{0,8},{2,10},{4,12},{6,14},{8,0},{10,2},{12,4},{14,6},{16,24},{18,... | collective-permute-start | bytes 1376264 | tf_op jit(solution)/shard_map/ppermute | solution.py:41
  75.6 4.1 %collective-permute-done.18.refs_12_.refs_9_ = bf16[256,1792]{1,0:T(8,128)(2,1)S(1)} collective-permute-done((bf16[256,1792]{1,0:T(8,128)(2,1)S(1)}, bf16[256,1792]{1,0:T(8,128)(2,1)S(1)}, u32[]{:S(2)}, u32[]{:S(2)}) %collective-permute-start.18) | collective-permute-done | bytes 917536 | tf_op jit(solution)/shard_map/ppermute | solution.py:35
  80.2 4.6 %collective-permute-done.15.refs_11_ = bf16[256,896]{1,0:T(8,128)(2,1)S(1)} collective-permute-done((bf16[256,896]{1,0:T(8,128)(2,1)S(1)}, bf16[256,896]{1,0:T(8,128)(2,1)S(1)}, u32[]{:S(2)}, u32[]{:S(2)}) %collective-permute-start.15) | collective-permute-done | bytes 458784 | tf_op jit(solution)/shard_map/ppermute | solution.py:41
  86.7 7.9 %collective-permute-done.17.refs_12_ = bf16[256,896]{1,0:T(8,128)(2,1)S(1)} collective-permute-done((bf16[256,896]{1,0:T(8,128)(2,1)S(1)}, bf16[256,896]{1,0:T(8,128)(2,1)S(1)}, u32[]{:S(2)}, u32[]{:S(2)}) %collective-permute-start.17) | collective-permute-done | bytes 458784 | tf_op jit(solution)/shard_map/ppermute | solution.py:41
  94.8 15.2 %shard_map.68 = (bf16[4,64,3072]{2,1,0:T(8,128)(2,1)S(1)}, bf16[4,64,3072]{2,1,0:T(8,128)(2,1)S(1)}) custom-call(s32[2]{0:T(128)S(1)} %pad_add_fusion.scalar_ref, bf16[128,1792]{1,0:T(8,128)(2,1)S(1)} %get-tuple-element.38.refs_0_, bf16[128,1792]{1,0:T(8,128)(2,1)} %collective-permute-done.1.refs_1_, ...), custom_call_target="tpu_custom_call" | custom-call | flops 1000000 | bytes 100000 | tf_op jit(solution)/shard_map/pallas_call | solution.py:180
  113.4 9.7 %collective-permute-done.28.refs_14_ = bf16[256,896]{1,0:T(8,128)(2,1)S(1)} collective-permute-done((bf16[256,896]{1,0:T(8,128)(2,1)S(1)}, bf16[256,896]{1,0:T(8,128)(2,1)S(1)}, u32[]{:S(2)}, u32[]{:S(2)}) %collective-permute-start.28) | collective-permute-done | bytes 458784 | tf_op jit(solution)/shard_map/ppermute | solution.py:41
  129.1 13.0 %shard_map.69 = (bf16[4,64,3072]{2,1,0:T(8,128)(2,1)S(1)}, bf16[4,64,3072]{2,1,0:T(8,128)(2,1)S(1)}) custom-call(s32[2]{0:T(128)S(1)} %pad_add_fusion.scalar_ref, bf16[256,896]{1,0:T(8,128)(2,1)S(1)} %broadcast_select_fusion.1.refs_0_, bf16[256,896]{1,0:T(8,128)(2,1)S(1)} %broadcast_select_fusion.refs_1_, ...), custom_call_target="tpu_custom_call" | custom-call | flops 1000000 | bytes 100000 | tf_op jit(solution)/shard_map/pallas_call | solution.py:180
  142.2 3.2 %collective-permute-done.24 = bf16[64,3072]{1,0:T(8,128)(2,1)S(1)} collective-permute-done((bf16[64,3072]{1,0:T(8,128)(2,1)S(1)}, bf16[64,3072]{1,0:T(8,128)(2,1)S(1)}, u32[]{:S(2)}, u32[]{:S(2)}) %collective-permute-start.24) | collective-permute-done | bytes 393248 | tf_op jit(solution)/shard_map/ppermute | solution.py:35
  145.6 3.4 %collective-permute-done.32 = bf16[4,64,3072]{2,1,0:T(8,128)(2,1)S(1)} collective-permute-done((bf16[4,64,3072]{2,1,0:T(8,128)(2,1)S(1)}, bf16[4,64,3072]{2,1,0:T(8,128)(2,1)S(1)}, u32[]{:S(2)}, u32[]{:S(2)}) %collective-permute-start.32) | collective-permute-done | bytes 1572896 | tf_op jit(solution)/shard_map/ppermute | solution.py:266
  154.8 7.0 %collective-permute-start.27 = (bf16[64,1024]{1,0:T(8,128)(2,1)S(1)}, bf16[64,1024]{1,0:T(8,128)(2,1)S(1)}, u32[]{:S(2)}, u32[]{:S(2)}) collective-permute-start(bf16[64,1024]{1,0:T(8,128)(2,1)S(1)} %get-tuple-element.91), channel_id=1, source_target_pairs={{0,16},{2,18},{4,20},{6,22},{24,8},{26,10},{28,12},{30,14},{1,17},... | collective-permute-start | bytes 393224 | tf_op jit(solution)/shard_map/ppermute | solution.py:41
  166.2 5.2 %collective-permute-done.34 = bf16[64,3072]{1,0:T(8,128)(2,1)} collective-permute-done((bf16[64,3072]{1,0:T(8,128)(2,1)}, bf16[64,3072]{1,0:T(8,128)(2,1)}, u32[]{:S(2)}, u32[]{:S(2)}) %collective-permute-start.34) | collective-permute-done | bytes 393248 | tf_op jit(solution)/shard_map/ppermute | solution.py:35
  172.9 3.4 %collective-permute-start.39 = (bf16[64,1024]{1,0:T(8,128)(2,1)S(1)}, bf16[64,1024]{1,0:T(8,128)(2,1)S(1)}, u32[]{:S(2)}, u32[]{:S(2)}) collective-permute-start(bf16[64,1024]{1,0:T(8,128)(2,1)S(1)} %get-tuple-element.90), channel_id=1, source_target_pairs={{0,24},{2,26},{4,28},{6,30},{24,0},{26,2},{28,4},{30,6},{1,25},{3,... | collective-permute-start | bytes 393224 | tf_op jit(solution)/shard_map/ppermute | solution.py:41
  177.6 6.0 %collective-permute-done.40 = bf16[64,1792]{1,0:T(8,128)(2,1)S(1)} collective-permute-done((bf16[64,1792]{1,0:T(8,128)(2,1)S(1)}, bf16[64,1792]{1,0:T(8,128)(2,1)S(1)}, u32[]{:S(2)}, u32[]{:S(2)}) %collective-permute-start.40) | collective-permute-done | bytes 229408 | tf_op jit(solution)/shard_map/ppermute | solution.py:35
  184.9 5.1 %collective-permute-done.41 = bf16[64,1792]{1,0:T(8,128)(2,1)S(1)} collective-permute-done((bf16[64,1792]{1,0:T(8,128)(2,1)S(1)}, bf16[64,1792]{1,0:T(8,128)(2,1)S(1)}, u32[]{:S(2)}, u32[]{:S(2)}) %collective-permute-start.41) | collective-permute-done | bytes 229408 | tf_op jit(solution)/shard_map/ppermute | solution.py:35
  191.2 5.7 %collective-permute-done.42 = bf16[64,1792]{1,0:T(8,128)(2,1)S(1)} collective-permute-done((bf16[64,1792]{1,0:T(8,128)(2,1)S(1)}, bf16[64,1792]{1,0:T(8,128)(2,1)S(1)}, u32[]{:S(2)}, u32[]{:S(2)}) %collective-permute-start.42) | collective-permute-done | bytes 229408 | tf_op jit(solution)/shard_map/ppermute | solution.py:35
  198.9 7.6 %fusion = f32[256,7168]{1,0:T(8,128)} fusion(bf16[64,7168]{1,0:T(8,128)(2,1)S(1)} %constant_dynamic-update-slice_fusion.2, f32[256,7168]{1,0:T(8,128)} %param.9, f32[4096,64]{0,1:T(8,128)S(1)} %copy-done, s32[]{:T(128)S(6)} %select_n.169), kind=kOutput, calls=%fused_computation.1 | convolution fusion | flops 240386048 | bytes 15630340 | tf_op jit(solution)/shard_map/dot_general | solution.py:101
  (124 shorter events, 57.7 us)
Async XLA Ops:
  3.4 24.9 %collective-permute-start = (bf16[128,1792]{1,0:T(8,128)(2,1)S(1)}, bf16[128,1792]{1,0:T(8,128)(2,1)S(1)}, u32[]{:S(2)}, u32[]{:S(2)}) collective-permute-start(bf16[128,1792]{1,0:T(8,128)(2,1)S(1)} %get-tuple-element.38.refs_0_), channel_id=1, source_target_pairs={{0,8},{2,10},{4,12},{6,14},{8,0},{10,2},{12,4},{14,6},{16,24},{18,... | collective-permute-start | bytes 1376264 | tf_op jit(solution)/shard_map/ppermute | solution.py:41
  6.4 24.5 %collective-permute-start.8 = (bf16[128,1792]{1,0:T(8,128)(2,1)S(1)}, bf16[128,1792]{1,0:T(8,128)(2,1)S(1)}, u32[]{:S(2)}, u32[]{:S(2)}) collective-permute-start(bf16[128,1792]{1,0:T(8,128)(2,1)S(1)} %get-tuple-element.38.refs_0_), channel_id=1, source_target_pairs={{8,16},{10,18},{12,20},{14,22},{16,8},{18,10},{20,12},{22,14},{9,1... | collective-permute-start | bytes 1376264 | tf_op jit(solution)/shard_map/ppermute | solution.py:41
  22.3 22.5 %collective-permute-start.12 = (bf16[128,64]{1,0:T(8,128)(2,1)S(1)}, bf16[128,64]{1,0:T(8,128)(2,1)S(1)}, u32[]{:S(2)}, u32[]{:S(2)}) collective-permute-start(bf16[128,64]{1,0:T(8,128)(2,1)S(1)} %all_gather.3), channel_id=1, source_target_pairs={{0,4},{2,6},{4,0},{6,2},{8,12},{10,14},{12,8},{14,10},{16,20},{18,... | collective-permute-start | bytes 49160 | tf_op jit(solution)/shard_map/ppermute | solution.py:35
  22.8 23.3 %collective-permute-start.2 = (bf16[128,1792]{1,0:T(8,128)(2,1)}, bf16[128,1792]{1,0:T(8,128)(2,1)S(1)}, u32[]{:S(2)}, u32[]{:S(2)}) collective-permute-start(bf16[128,1792]{1,0:T(8,128)(2,1)} %collective-permute-done.1.refs_1_), channel_id=1, source_target_pairs={{0,8},{2,10},{4,12},{6,14},{8,0},{10,2},{12,4},{14,6},{16,24},{18,... | collective-permute-start | bytes 1376264 | tf_op jit(solution)/shard_map/ppermute | solution.py:41
  31.0 15.9 %collective-permute-start.3 = (bf16[128,1792]{1,0:T(8,128)(2,1)}, bf16[128,1792]{1,0:T(8,128)(2,1)S(1)}, u32[]{:S(2)}, u32[]{:S(2)}) collective-permute-start(bf16[128,1792]{1,0:T(8,128)(2,1)} %collective-permute-done.1.refs_1_), channel_id=1, source_target_pairs={{8,16},{10,18},{12,20},{14,22},{16,8},{18,10},{20,12},{22,14},{9,1... | collective-permute-start | bytes 1376264 | tf_op jit(solution)/shard_map/ppermute | solution.py:41
  31.7 27.5 %collective-permute-start.16 = (bf16[256,1792]{1,0:T(8,128)(2,1)S(1)}, bf16[256,1792]{1,0:T(8,128)(2,1)S(1)}, u32[]{:S(2)}, u32[]{:S(2)}) collective-permute-start(bf16[256,1792]{1,0:T(8,128)(2,1)S(1)} %copy-done.4), channel_id=1, source_target_pairs={{0,2},{2,0},{4,6},{6,4},{8,10},{10,8},{12,14},{14,12},{16,18},{18,... | collective-permute-start | bytes 2752520 | tf_op jit(solution)/shard_map/ppermute | solution.py:35
  42.9 36.8 %collective-permute-start.18 = (bf16[256,1792]{1,0:T(8,128)(2,1)S(1)}, bf16[256,1792]{1,0:T(8,128)(2,1)S(1)}, u32[]{:S(2)}, u32[]{:S(2)}) collective-permute-start(bf16[256,1792]{1,0:T(8,128)(2,1)S(1)} %copy-done.3), channel_id=1, source_target_pairs={{0,4},{2,6},{4,0},{6,2},{8,12},{10,14},{12,8},{14,10},{16,20},{18,... | collective-permute-start | bytes 2752520 | tf_op jit(solution)/shard_map/ppermute | solution.py:35
  44.7 29.2 %collective-permute-start.7 = (bf16[256,1792]{1,0:T(8,128)(2,1)S(1)}, bf16[256,1792]{1,0:T(8,128)(2,1)S(1)}, u32[]{:S(2)}, u32[]{:S(2)}) collective-permute-start(bf16[256,1792]{1,0:T(8,128)(2,1)S(1)} %constant_dynamic-update-slice_fusion.refs_2_), channel_id=1, source_target_pairs={{0,8},{2,10},{4,12},{6,14},{8,0},{10,2},{12,4},{14,6},{16,24},{18,... | collective-permute-start | bytes 2752520 | tf_op jit(solution)/shard_map/ppermute | solution.py:41
  46.1 28.6 %collective-permute-start.9 = (bf16[256,1792]{1,0:T(8,128)(2,1)S(1)}, bf16[256,1792]{1,0:T(8,128)(2,1)S(1)}, u32[]{:S(2)}, u32[]{:S(2)}) collective-permute-start(bf16[256,1792]{1,0:T(8,128)(2,1)S(1)} %constant_dynamic-update-slice_fusion.refs_2_), channel_id=1, source_target_pairs={{8,16},{10,18},{12,20},{14,22},{16,8},{18,10},{20,12},{22,14},{9,1... | collective-permute-start | bytes 2752520 | tf_op jit(solution)/shard_map/ppermute | solution.py:41
  62.2 22.7 %collective-permute-start.19 = (bf16[256,1792]{1,0:T(8,128)(2,1)S(1)}, bf16[256,1792]{1,0:T(8,128)(2,1)S(1)}, u32[]{:S(2)}, u32[]{:S(2)}) collective-permute-start(bf16[256,1792]{1,0:T(8,128)(2,1)S(1)} %copy-done.2), channel_id=1, source_target_pairs={{0,6},{2,4},{4,2},{6,0},{8,14},{10,12},{12,10},{14,8},{16,22},{18,... | collective-permute-start | bytes 2752520 | tf_op jit(solution)/shard_map/ppermute | solution.py:35
  63.1 21.7 %collective-permute-start.15 = (bf16[256,896]{1,0:T(8,128)(2,1)S(1)}, bf16[256,896]{1,0:T(8,128)(2,1)S(1)}, u32[]{:S(2)}, u32[]{:S(2)}) collective-permute-start(bf16[256,896]{1,0:T(8,128)(2,1)S(1)} %dynamic-slice_select_fusion), channel_id=1, source_target_pairs={{0,8},{2,10},{4,12},{6,14},{8,0},{10,2},{12,4},{14,6},{16,24},{18,... | collective-permute-start | bytes 1376264 | tf_op jit(solution)/shard_map/ppermute | solution.py:41
  73.9 36.1 %collective-permute-start.20 = (bf16[256,896]{1,0:T(8,128)(2,1)S(1)}, bf16[256,896]{1,0:T(8,128)(2,1)S(1)}, u32[]{:S(2)}, u32[]{:S(2)}) collective-permute-start(bf16[256,896]{1,0:T(8,128)(2,1)S(1)} %pad_maximum_fusion.4), channel_id=1, source_target_pairs={{8,16},{10,18},{12,20},{14,22},{16,8},{18,10},{20,12},{22,14},{9,1... | collective-permute-start | bytes 1376264 | tf_op jit(solution)/shard_map/ppermute | solution.py:41
  84.8 25.2 %collective-permute-start.21 = (bf16[256,896]{1,0:T(8,128)(2,1)S(1)}, bf16[256,896]{1,0:T(8,128)(2,1)S(1)}, u32[]{:S(2)}, u32[]{:S(2)}) collective-permute-start(bf16[256,896]{1,0:T(8,128)(2,1)S(1)} %slice_select_fusion.1), channel_id=1, source_target_pairs={{0,8},{2,10},{4,12},{6,14},{8,0},{10,2},{12,4},{14,6},{16,24},{18,... | collective-permute-start | bytes 1376264 | tf_op jit(solution)/shard_map/ppermute | solution.py:41
  112.7 16.4 %collective-permute-start.29 = (bf16[256,896]{1,0:T(8,128)(2,1)S(1)}, bf16[256,896]{1,0:T(8,128)(2,1)S(1)}, u32[]{:S(2)}, u32[]{:S(2)}) collective-permute-start(bf16[256,896]{1,0:T(8,128)(2,1)S(1)} %get-tuple-element.52), channel_id=1, source_target_pairs={{8,16},{10,18},{12,20},{14,22},{16,8},{18,10},{20,12},{22,14},{9,1... | collective-permute-start | bytes 1376264 | tf_op jit(solution)/shard_map/ppermute | solution.py:41
  123.9 18.2 %collective-permute-start.31 = (bf16[64,1792]{1,0:T(8,128)(2,1)S(1)}, bf16[64,1792]{1,0:T(8,128)(2,1)S(1)}, u32[]{:S(2)}, u32[]{:S(2)}) collective-permute-start(bf16[64,1792]{1,0:T(8,128)(2,1)S(1)} %add_convert_fusion.2), channel_id=1, source_target_pairs={{8,0},{10,2},{12,4},{14,6},{16,24},{18,26},{20,28},{22,30},{9,1},{... | collective-permute-start | bytes 688136 | tf_op jit(solution)/shard_map/ppermute | solution.py:41
  125.5 16.7 %collective-permute-start.25 = (bf16[64,3072]{1,0:T(8,128)(2,1)S(1)}, bf16[64,3072]{1,0:T(8,128)(2,1)S(1)}, u32[]{:S(2)}, u32[]{:S(2)}) collective-permute-start(bf16[64,3072]{1,0:T(8,128)(2,1)S(1)} %get-tuple-element.77), channel_id=1, source_target_pairs={{0,6},{2,4},{4,2},{6,0},{8,14},{10,12},{12,10},{14,8},{16,22},{18,... | collective-permute-start | bytes 1179656 | tf_op jit(solution)/shard_map/ppermute | solution.py:35
  126.4 18.9 %collective-permute-start.24 = (bf16[64,3072]{1,0:T(8,128)(2,1)S(1)}, bf16[64,3072]{1,0:T(8,128)(2,1)S(1)}, u32[]{:S(2)}, u32[]{:S(2)}) collective-permute-start(bf16[64,3072]{1,0:T(8,128)(2,1)S(1)} %get-tuple-element.78), channel_id=1, source_target_pairs={{0,4},{2,6},{4,0},{6,2},{8,12},{10,14},{12,8},{14,10},{16,20},{18,... | collective-permute-start | bytes 1179656 | tf_op jit(solution)/shard_map/ppermute | solution.py:35
  127.9 17.5 %collective-permute-start.23 = (bf16[64,3072]{1,0:T(8,128)(2,1)S(1)}, bf16[64,3072]{1,0:T(8,128)(2,1)S(1)}, u32[]{:S(2)}, u32[]{:S(2)}) collective-permute-start(bf16[64,3072]{1,0:T(8,128)(2,1)S(1)} %get-tuple-element.76), channel_id=1, source_target_pairs={{0,2},{2,0},{4,6},{6,4},{8,10},{10,8},{12,14},{14,12},{16,18},{18,... | collective-permute-start | bytes 1179656 | tf_op jit(solution)/shard_map/ppermute | solution.py:35
  151.9 19.6 %collective-permute-start.34 = (bf16[64,3072]{1,0:T(8,128)(2,1)}, bf16[64,3072]{1,0:T(8,128)(2,1)}, u32[]{:S(2)}, u32[]{:S(2)}) collective-permute-start(bf16[64,3072]{1,0:T(8,128)(2,1)} %get-tuple-element.75), channel_id=1, source_target_pairs={{0,4},{2,6},{4,0},{6,2},{8,12},{10,14},{12,8},{14,10},{16,20},{18,... | collective-permute-start | bytes 1179656 | tf_op jit(solution)/shard_map/ppermute | solution.py:35
  153.3 18.2 %collective-permute-start.33 = (bf16[64,3072]{1,0:T(8,128)(2,1)}, bf16[64,3072]{1,0:T(8,128)(2,1)}, u32[]{:S(2)}, u32[]{:S(2)}) collective-permute-start(bf16[64,3072]{1,0:T(8,128)(2,1)} %get-tuple-element.73), channel_id=1, source_target_pairs={{0,2},{2,0},{4,6},{6,4},{8,10},{10,8},{12,14},{14,12},{16,18},{18,... | collective-permute-start | bytes 1179656 | tf_op jit(solution)/shard_map/ppermute | solution.py:35
  154.1 52.4 %collective-permute-start.38 = (bf16[64,1024]{1,0:T(8,128)(2,1)S(1)}, bf16[64,1024]{1,0:T(8,128)(2,1)S(1)}, u32[]{:S(2)}, u32[]{:S(2)}) collective-permute-start(bf16[64,1024]{1,0:T(8,128)(2,1)S(1)} %get-tuple-element.91), channel_id=1, source_target_pairs={{8,16},{10,18},{12,20},{14,22},{16,8},{18,10},{20,12},{22,14},{9,1... | collective-permute-start | bytes 393224 | tf_op jit(solution)/shard_map/ppermute | solution.py:41
  154.8 51.7 %collective-permute-start.27 = (bf16[64,1024]{1,0:T(8,128)(2,1)S(1)}, bf16[64,1024]{1,0:T(8,128)(2,1)S(1)}, u32[]{:S(2)}, u32[]{:S(2)}) collective-permute-start(bf16[64,1024]{1,0:T(8,128)(2,1)S(1)} %get-tuple-element.91), channel_id=1, source_target_pairs={{0,16},{2,18},{4,20},{6,22},{24,8},{26,10},{28,12},{30,14},{1,17},... | collective-permute-start | bytes 393224 | tf_op jit(solution)/shard_map/ppermute | solution.py:41
  163.9 34.4 %collective-permute-start.26 = (bf16[64,1024]{1,0:T(8,128)(2,1)S(1)}, bf16[64,1024]{1,0:T(8,128)(2,1)S(1)}, u32[]{:S(2)}, u32[]{:S(2)}) collective-permute-start(bf16[64,1024]{1,0:T(8,128)(2,1)S(1)} %get-tuple-element.92), channel_id=1, source_target_pairs={{0,8},{2,10},{4,12},{6,14},{8,0},{10,2},{12,4},{14,6},{16,24},{18,... | collective-permute-start | bytes 393224 | tf_op jit(solution)/shard_map/ppermute | solution.py:41
  172.9 33.6 %collective-permute-start.39 = (bf16[64,1024]{1,0:T(8,128)(2,1)S(1)}, bf16[64,1024]{1,0:T(8,128)(2,1)S(1)}, u32[]{:S(2)}, u32[]{:S(2)}) collective-permute-start(bf16[64,1024]{1,0:T(8,128)(2,1)S(1)} %get-tuple-element.90), channel_id=1, source_target_pairs={{0,24},{2,26},{4,28},{6,30},{24,0},{26,2},{28,4},{30,6},{1,25},{3,... | collective-permute-start | bytes 393224 | tf_op jit(solution)/shard_map/ppermute | solution.py:41
  (25 other events, 286.6 us)

commit v4 on v2

--- a/solution.py
+++ b/solution.py
@@ -130,8 +130,8 @@
 
 def products(lay, sources, buffers, fills, jobs, width):
     scalars = jnp.stack([lay.place, lay.core]).astype(jnp.int32)
-    rows = buffers[jobs[0][0]][0]
-    half = rows // PLANE // 2
+    block = buffers[jobs[0][0]][0]
+    half = block // PLANE // 2
     piece = width // PLANE
 
     def kernel(scalar_ref, *refs):
@@ -163,16 +163,16 @@
             need(a_ids)
             for r in range(PLANE):
                 need(b_ids(r))
-                x = nt(
-                    buffer_refs[a][:, a0:a0 + cols],
-                    buffer_refs[b][r * piece:(r + 1) * piece, b0:b0 + cols],
-                ).astype(bf16)
                 column = at * width + pl.multiple_of((place ^ r) * piece, piece)
-                for p in range(PLANE):
-                    low = x[2 * p * half:(2 * p + 1) * half]
-                    high = x[(2 * p + 1) * half:(2 * p + 2) * half]
-                    keep_ref[p, :, pl.ds(column, piece)] = jnp.where(core == 0, low, high)
-                    give_ref[p, :, pl.ds(column, piece)] = jnp.where(core == 0, high, low)
+                for p in range(0, PLANE, 2):
+                    x = nt(
+                        buffer_refs[a][2 * p * half:(2 * p + 4) * half, a0:a0 + cols],
+                        buffer_refs[b][r * piece:(r + 1) * piece, b0:b0 + cols],
+                    ).astype(bf16)
+                    for i in range(2):
+                        low, high = x[2 * i * half:][:half], x[(2 * i + 1) * half:][:half]
+                        keep_ref[p + i, :, pl.ds(column, piece)] = jnp.where(core == 0, low, high)
+                        give_ref[p + i, :, pl.ds(column, piece)] = jnp.where(core == 0, high, low)
         need(range(len(copies)))
 
     out = jax.ShapeDtypeStruct((PLANE, half, len(jobs) * width), bf16)
@@ -195,111 +195,92 @@
     inner = (level == 1) | (level == 2)
     tokens, hidden = out_grad.shape
     rows = weight.shape[0]
-    width = rows * PLANE
-    half = hidden // PLANE // 2
+    width, block, pair = rows * PLANE, tokens * PLANE, tokens * 2
+    both = hidden // PLANE
+    half = both // 2
+    low, high = slice(0, half), slice(half, both)
     end_swap = lambda x: lay.levels(x, 1)
     mid_swap = lambda x: lay.levels(x, 3, (1, 2))
-    outward = lambda x: lay.levels(x, 1, (1, 2))
-    inward = lambda x: lay.levels(x, 1, (0, 3))
+    swap = lambda x: lax.ppermute(x, "tensor", [(0, 1), (1, 0)])
     send = lambda a, w: jnp.where(inner, a, w)
-    end_sent, mid_sent = [], []
-
-    def queued(move, sent, x, *first):
-        got = move(after(x, *sent[-2:-1], *first))
-        sent.append(got)
-        return got
-
-    a0 = lay.cut(out_grad, 0)
-    e0, m0 = queued(end_swap, end_sent, a0), queued(mid_swap, mid_sent, a0)
-    cuts = [lay.cut(after(out_grad, a0), r) for r in range(1, PLANE)]
-    ax, ay = across(cuts[0], 1), across(cuts[1], 2)
-    ad = across(after(cuts[2], ax, ay, e0, m0), 3)
-    axy = after(jnp.concatenate([ax, ay], 0), e0, m0)
-    e1, m1 = queued(end_swap, end_sent, axy), queued(mid_swap, mid_sent, axy)
-    proj = projected(lay, after(inputs, *cuts), proj_basis)
-    weight = after(weight, ax, ay)
+
+    cuts = [lay.cut(out_grad, r) for r in range(PLANE)]
+    plane = [across(cuts[r], r) for r in range(1, PLANE)]
+    e0, m0 = end_swap(cuts[0]), mid_swap(cuts[0])
+    proj = projected(lay, after(inputs, plane[0]), proj_basis)
+    weight = after(weight, plane[0])
     parts = [lay.cut(weight, r) for r in range(PLANE)]
-    parts[1:3] = [across(after(parts[r], ad), r) for r in (1, 2)]
-    parts[3] = across(after(parts[3], parts[1], parts[2]), 3)
-    e2, m2 = queued(end_swap, end_sent, ad), queued(mid_swap, mid_sent, ad)
-
-    panel = sum(tn(q, a) for q, a in zip(proj, [a0, ax, ay, ad]))
-    panel = panel + inward(after(panel.astype(bf16), e1, m1)).astype(f32)
-
-    near_e, near_m = jnp.concatenate([e0, e1, e2], 0), jnp.concatenate([m0, m1, m2], 0)
-    pair = 2 * tokens
-    far0, far1, got = [], [], []
-    for i in range(2):
-        far0.append(queued(mid_swap, mid_sent, near_e[i * pair:(i + 1) * pair, :half]))
-        got.append(queued(end_swap, end_sent, send(near_m[i * pair:(i + 1) * pair, :half], parts[i][:, half:])))
-    pair_panel = panel
-    other_pair = mid_swap(after(panel.astype(bf16), far0[0], got[0]))
-    for i in range(2):
-        far1.append(queued(mid_swap, mid_sent, near_e[i * pair:(i + 1) * pair, half:]))
-        got.append(queued(end_swap, end_sent, send(far0[i], parts[2 + i][:, half:]), parts[3]))
-    def weight_fills(first, buffer):
-        return [(first + r, 0, buffer, r * rows, 0, 2 * half) for r in range(PLANE)]
-
-    def block_fills(first, buffer, sizes, column, cols):
-        out, row = [], 0
-        for i, n in enumerate(sizes):
-            out.append((first + i, column, buffer, row, column, cols))
-            row += n
-        return out
-
-    both = 2 * half
-    early0 = send(near_m[:, :half], jnp.concatenate(got[:2], 0))
-    sources = [after(a0, *far0, pair_panel), ax, ay, ad, *parts, near_e, early0, near_m]
-    fills = block_fills(0, 0, [tokens] * PLANE, 0, both) + weight_fills(4, 3)
-    fills += [(8, 0, 1, 0, 0, both), (9, 0, 2, 0, 0, half), (10, half, 2, 0, half, half)]
-    wide, tall = (PLANE * tokens, both), (width, both)
-    of_weight = lambda r: (4 + r,)
+    panel = sum(tn(q, a) for q, a in zip(proj, [cuts[0], *plane]))
+    panel = panel + end_swap(panel.astype(bf16)).astype(f32)
+    rest = after(jnp.concatenate(plane, 0), e0, m0)
+    e1, m1 = end_swap(rest), mid_swap(rest)
+    parts[1:3] = [across(after(parts[r], *plane), r) for r in (1, 2)]
+    parts[3] = across(after(parts[3], *parts[1:3]), 3)
+    panel = (panel + lay.levels(panel.astype(bf16), 2).astype(f32)).astype(bf16)
+
+    joined = lambda x, c: jnp.concatenate([x[0][:, c], x[1][:, c]], 0)
+    near_e, near_m = [e0, e1], [m0, m1]
+    e_high = joined(near_e, high)
+    m_low = joined(near_m, low)
+    far0 = mid_swap(joined(near_e, low))
+    got_a = send(m_low, jnp.concatenate([w[:, high] for w in parts[:2]], 0))
+    got_a = end_swap(got_a)
+    far1, got = [], []
+    for i, w in enumerate(parts[2:]):
+        rows_i = slice(i * pair, (i + 1) * pair)
+        far1.append(mid_swap(after(e_high[rows_i], far0, got_a)))
+        got.append(end_swap(after(send(far0[rows_i], w[:, high]), got_a, parts[3], panel)))
+    weight_fills = lambda first, b: [(first + r, 0, b, r * rows, 0, both) for r in range(PLANE)]
     none = lambda r: ()
+    early0 = send(m_low, got_a)
+    sources = [after(cuts[0], far0), rest, *near_e, early0, *near_m, *parts]
+    fills = [(0, 0, 0, 0, 0, both), (1, 0, 0, tokens, 0, both)] + weight_fills(7, 3)
+    fills += [(2, 0, 1, 0, 0, both), (3, 0, 1, tokens, 0, both)]
+    fills += [(4, 0, 2, 0, 0, half), (5, half, 2, 0, half, half), (6, half, 2, tokens, half, half)]
     jobs = [
-        (0, 3, 0, 0, both, range(4), of_weight),
-        (1, 3, 0, 0, both, (8,), none),
-        (2, 3, 0, 0, both, (9, 10), none),
+        (0, 3, 0, 0, both, (0, 1), lambda r: (2 + r,)),
+        (1, 3, 0, 0, both, (6, 7), none),
+        (2, 3, 0, 0, both, (8, 9, 10), none),
     ]
-    keep, give = products(lay, sources, [wide, wide, wide, tall], fills, jobs, width)
-    swap = lambda x: lax.ppermute(x, "tensor", [(0, 1), (1, 0)])
-    give = after(give, far1[0], got[2])
-    panel = (panel + after(other_pair, keep).astype(f32)).astype(bf16)
-    panel = send(panel, outward(after(panel, far1[0], got[2])))
+    keep, give = products(lay, sources, [(block, both)] * 3 + [(width, both)], fills, jobs, width)
+    give = after(give, far1[0], got[0])
     first = (keep.astype(f32) + swap(give).astype(f32)).astype(bf16)
-
-    late0 = [send(far0[i], got[2 + i]) for i in range(2)]
-    late0[0] = after(late0[0], first)
-    sources = [*late0, *far1, near_m, *parts, *got]
-    fills = [(i, 0, 0, i * pair, 0, half) for i in range(2)]
-    fills += [(2 + i, 0, 0, i * pair, half, half) for i in range(2)]
-    fills += weight_fills(5, 2) + [(4, half, 1, 0, 0, half)]
-    fills += [(9 + r, 0, 3, r * rows, 0, half) for r in range(PLANE)]
+    first_x, first_y = across(first[1], 1), across(first[2], 2)
+
+    late0 = send(far0, jnp.concatenate(got, 0))
+    sources = [after(late0, first_x, first_y), *far1, *near_m, *parts, got_a, *got]
+    fills = [(0, 0, 0, 0, 0, half)]
+    fills += [(1 + i, 0, 0, i * pair, half, half) for i in range(2)]
+    fills += weight_fills(5, 2)
+    fills += [(3, half, 1, 0, 0, half), (4, half, 1, tokens, 0, half)]
+    fills += [(9, 0, 3, 0, 0, half), (10, 0, 3, 2 * rows, 0, half), (11, 0, 3, 3 * rows, 0, half)]
     jobs = [
-        (0, 2, 0, 0, both, range(4), of_weight),
-        (1, 3, 0, 0, half, (8,), lambda r: (9 + r,)),
+        (0, 2, 0, 0, both, (0, 1, 2), lambda r: (3 + r,)),
+        (1, 3, 0, 0, half, (7, 8), lambda r: ((9,), (), (10,), (11,))[r]),
         (0, 3, half, 0, half, (), none),
     ]
-    buffers = [wide, (PLANE * tokens, half), tall, (width, half)]
+    buffers = [(block, both), (block, half), (width, both), (width, half)]
     keep, give = products(lay, sources, buffers, fills, jobs, width)
 
-    def plane_sum(part):
-        total = part[0].astype(f32)
-        for r in range(1, PLANE):
-            total = total + across(part[r], r).astype(f32)
-        return total.astype(bf16)
-
-    first = plane_sum(first)
-    second = (keep.astype(f32) + swap(after(give, first, panel)).astype(f32)).astype(bf16)
+    def plane_sum(own, *others):
+        return sum(x.astype(f32) for x in (own, *others)).astype(bf16)
+
+    first = plane_sum(first[0], first_x, first_y, after(across(first[3], 3), keep))
+    second = (keep.astype(f32) + swap(give).astype(f32)).astype(bf16)
+    second = plane_sum(second[0], *[across(second[r], r) for r in range(1, PLANE)])
     panel = after(panel, second)
-    panel = lay.in_order([panel] + [across(panel, r) for r in range(1, PLANE)], 1)
+    panel = jnp.stack([panel] + [across(panel, r) for r in range(1, PLANE)])
+    panel = jnp.concatenate(
+        [lax.dynamic_index_in_dim(panel, lay.place ^ p, 0, False) for p in range(PLANE)], 1
+    )
     new_momentum = updated(lay, proj_basis, panel, momentum, tokens * lay.replicas)
-    second = plane_sum(second)
     y0, y1, early = [first[:, i * width:(i + 1) * width] for i in range(3)]
     late, early_other, late_other = [second[:, i * width:(i + 1) * width] for i in range(3)]
 
     z1 = end_swap(y1)
     z3 = mid_swap(early)
     z2 = lay.levels(early, 2, (0, 3))
+    late, early_other = after((late, early_other), z1, z2, z3)
     z2b = mid_swap(early_other)
     z_late = lay.levels(jnp.concatenate([late, late_other], 1), 2, (1, 2))
     z3b = lay.levels(late, 3, (0, 3))

time: 201 us -> 210 us (1.045)
  waiting for transfers between devices: 75.1 us -> 93.3 us
  starting transfers between devices: 74.6 us -> 60.3 us
  local copies, waits for them, and re-layouts: 6.63 us -> 15.9 us
  Pallas kernels: 24.3 us -> 18.2 us
  other arithmetic: 6.12 us -> 11.6 us
  matrix products: 10.2 us -> 7 us
    ppermute x23 -> x18, waiting for transfers between devices: 22.6 us -> 37.2 us  [levels(): return lax.ppermute(x, 'dp', pairs)]
    ppermute x23 -> x18, starting transfers between devices: 51.3 us -> 37 us  [levels(): return lax.ppermute(x, 'dp', pairs)]
    unnamed x8 -> x84, local copies, waits for them, and re-layouts: 0.26 us -> 10.3 us
    pallas_call x2, Pallas kernels: 24.3 us -> 18.2 us  [products(): pl.pallas_call(kernel, out_shape=(out, out), in_specs=[pl.BlockSpec(memor...]
    ppermute x18, waiting for transfers between devices: 52.5 us -> 56.1 us  [across(): return lax.ppermute(x, 'dp', [(d, d ^ r) for d in range(self.replicas)])]
    dot_general x1, matrix products: 7.57 us -> 4.35 us  [updated(): update = jnp.dot(basis_rows.astype(bf16), panel, preferred_element_type=f32)]
    select_n x7 -> x4, other arithmetic: 1.71 us -> 4.39 us  [line_of_four(): send = lambda a, w: jnp.where(inner, a, w)]
    dynamic_slice x3 -> x2, local copies, waits for them, and re-layouts: 5.8 us -> 3.13 us  [cut(): return lax.dynamic_slice_in_dim(x, (self.place ^ r) * quarter, quarter, 1)]
  transfers between devices with their start and end apart: 43 -> 38, of which waited for: 16 -> 15; matrix products, arithmetic and copies ran while one was open for 10% -> 9% of each run, Pallas kernels for 12% -> 4%
where the time goes in v4:
time: 210 us
  waiting for transfers between devices  93.3 us (44%)
  starting transfers between devices  60.3 us (29%)
  Pallas kernels  18.2 us (9%)
  local copies, waits for them, and re-layouts  15.9 us (8%)
  other arithmetic  11.6 us (6%)
  matrix products  7 us (3%)
    ppermute x18, waiting for transfers between devices, across(): return lax.ppermute(x, 'dp', [(d, d ^ r) for d in range(self.replicas)])  56.1 us
    ppermute x18, waiting for transfers between devices, levels(): return lax.ppermute(x, 'dp', pairs)  37.2 us
    ppermute x18, starting transfers between devices, levels(): return lax.ppermute(x, 'dp', pairs)  37 us
    ppermute x18, starting transfers between devices, across(): return lax.ppermute(x, 'dp', [(d, d ^ r) for d in range(self.replicas)])  23.3 us
    pallas_call x2, Pallas kernels, products(): pl.pallas_call(kernel, out_shape=(out, out), in_specs=[pl.BlockSpec(memor...  18.2 us
    unnamed x84, local copies, waits for them, and re-layouts  10.3 us
    select_n x4, other arithmetic, line_of_four(): send = lambda a, w: jnp.where(inner, a, w)  4.39 us
    dot_general x1, matrix products, updated(): update = jnp.dot(basis_rows.astype(bf16), panel, preferred_element_type=f32)  4.35 us
  transfers between devices with their start and end apart: 38, of which 15 were waited for; matrix products, arithmetic and copies ran while one was open for 9% of the time, Pallas kernels for 4%

profile of v4, /device:TPU:0, one launch (start us, length us, event | category | flops | bytes accessed | tf_op | source)
XLA Modules:
  0.0 209.5 jit_solution(15474722427491991050)
XLA Ops:
  0.7 2.7 %constant_dynamic-slice_fusion.7 = (bf16[128,1792]{1,0:T(8,128)(2,1)}, bf16[128,1792]{1,0:T(8,128)(2,1)S(1)}, bf16[128,1792]{1,0:T(8,128)(2,1)}, bf16[128,1792]{1,0:T(8,128)(2,1)}) fusion(bf16[128,7168]{1,0:T(8,128)(2,1)} %param.6, s32[]{:T(128)S(6)} %select_n.133, s32[]{:T(128)S(6)} %select_n.132, s32[]{:T(128)S(6)} %select_n.135, s32[]{:T(128)S(6)} %select_n.134), kind=kLoop, calls=%fused_computation.65 | loop fusion | bytes 3670032 | tf_op jit(solution)/shard_map/dynamic_slice | solution.py:45
  3.3 2.9 %collective-permute-start.1 = (bf16[128,1792]{1,0:T(8,128)(2,1)}, bf16[128,1792]{1,0:T(8,128)(2,1)S(1)}, u32[]{:S(2)}, u32[]{:S(2)}) collective-permute-start(bf16[128,1792]{1,0:T(8,128)(2,1)} %get-tuple-element.51), channel_id=1, source_target_pairs={{0,2},{2,0},{4,6},{6,4},{8,10},{10,8},{12,14},{14,12},{16,18},{18,... | collective-permute-start | bytes 1376264 | tf_op jit(solution)/shard_map/ppermute | solution.py:35
  8.5 4.9 %collective-permute-start = (bf16[128,1792]{1,0:T(8,128)(2,1)S(1)}, bf16[128,1792]{1,0:T(8,128)(2,1)}, u32[]{:S(2)}, u32[]{:S(2)}) collective-permute-start(bf16[128,1792]{1,0:T(8,128)(2,1)S(1)} %get-tuple-element.24.refs_0_), channel_id=1, source_target_pairs={{0,8},{2,10},{4,12},{6,14},{8,0},{10,2},{12,4},{14,6},{16,24},{18,... | collective-permute-start | bytes 1376264 | tf_op jit(solution)/shard_map/ppermute | solution.py:41
  13.4 4.4 %collective-permute-done.1 = bf16[128,1792]{1,0:T(8,128)(2,1)S(1)} collective-permute-done((bf16[128,1792]{1,0:T(8,128)(2,1)}, bf16[128,1792]{1,0:T(8,128)(2,1)S(1)}, u32[]{:S(2)}, u32[]{:S(2)}) %collective-permute-start.1) | collective-permute-done | bytes 458784 | tf_op jit(solution)/shard_map/ppermute | solution.py:35
  17.8 10.3 %collective-permute-done.3 = bf16[128,1792]{1,0:T(8,128)(2,1)S(1)} collective-permute-done((bf16[128,1792]{1,0:T(8,128)(2,1)}, bf16[128,1792]{1,0:T(8,128)(2,1)S(1)}, u32[]{:S(2)}, u32[]{:S(2)}) %collective-permute-start.3) | collective-permute-done | bytes 458784 | tf_op jit(solution)/shard_map/ppermute | solution.py:35
  31.3 4.4 %collective-permute-start.5 = (bf16[384,1792]{1,0:T(8,128)(2,1)S(1)}, bf16[384,1792]{1,0:T(8,128)(2,1)S(1)}, u32[]{:S(2)}, u32[]{:S(2)}) collective-permute-start(bf16[384,1792]{1,0:T(8,128)(2,1)S(1)} %pad_maximum_fusion.refs_1_), channel_id=1, source_target_pairs={{0,8},{2,10},{4,12},{6,14},{8,0},{10,2},{12,4},{14,6},{16,24},{18,... | collective-permute-start | bytes 4128776 | tf_op jit(solution)/shard_map/ppermute | solution.py:41
  37.4 1.8 all_gather.3
  43.7 2.7 %collective-permute-start.15 = (bf16[128,64]{1,0:T(8,128)(2,1)S(1)}, bf16[128,64]{1,0:T(8,128)(2,1)S(1)}, u32[]{:S(2)}, u32[]{:S(2)}) collective-permute-start(bf16[128,64]{1,0:T(8,128)(2,1)S(1)} %all_gather.3), channel_id=1, source_target_pairs={{0,6},{2,4},{4,2},{6,0},{8,14},{10,12},{12,10},{14,8},{16,22},{18,... | collective-permute-start | bytes 49160 | tf_op jit(solution)/shard_map/ppermute | solution.py:35
  46.7 17.5 %collective-permute-done.15 = bf16[128,64]{1,0:T(8,128)(2,1)S(1)} collective-permute-done((bf16[128,64]{1,0:T(8,128)(2,1)S(1)}, bf16[128,64]{1,0:T(8,128)(2,1)S(1)}, u32[]{:S(2)}, u32[]{:S(2)}) %collective-permute-start.15) | collective-permute-done | bytes 16416 | tf_op jit(solution)/shard_map/ppermute | solution.py:35
  65.9 2.3 %collective-permute-done.14 = bf16[128,64]{1,0:T(8,128)(2,1)S(1)} collective-permute-done((bf16[128,64]{1,0:T(8,128)(2,1)S(1)}, bf16[128,64]{1,0:T(8,128)(2,1)S(1)}, u32[]{:S(2)}, u32[]{:S(2)}) %collective-permute-start.14) | collective-permute-done | bytes 16416 | tf_op jit(solution)/shard_map/ppermute | solution.py:35
  72.3 3.7 %collective-permute-start.9 = (bf16[512,896]{1,0:T(8,128)(2,1)S(1)}, bf16[512,896]{1,0:T(8,128)(2,1)S(1)}, u32[]{:S(2)}, u32[]{:S(2)}) collective-permute-start(bf16[512,896]{1,0:T(8,128)(2,1)S(1)} %maximum_select_fusion), channel_id=1, source_target_pairs={{0,8},{2,10},{4,12},{6,14},{8,0},{10,2},{12,4},{14,6},{16,24},{18,... | collective-permute-start | bytes 2752520 | tf_op jit(solution)/shard_map/ppermute | solution.py:41
  77.6 26.6 %collective-permute-done.17 = bf16[64,1792]{1,0:T(8,128)(2,1)S(1)} collective-permute-done((bf16[64,1792]{1,0:T(8,128)(2,1)S(1)}, bf16[64,1792]{1,0:T(8,128)(2,1)S(1)}, u32[]{:S(2)}, u32[]{:S(2)}) %collective-permute-start.17) | collective-permute-done | bytes 229408 | tf_op jit(solution)/shard_map/ppermute | solution.py:41
  110.1 1.8 broadcast_select_fusion.refs_4_
  117.0 9.3 %shard_map.68 = (bf16[4,64,3072]{2,1,0:T(8,128)(2,1)S(1)}, bf16[4,64,3072]{2,1,0:T(8,128)(2,1)S(1)}) custom-call(s32[2]{0:T(128)S(1)} %pad_add_fusion.scalar_ref, bf16[128,1792]{1,0:T(8,128)(2,1)S(1)} %copy-done.15, bf16[384,1792]{1,0:T(8,128)(2,1)S(1)} %copy-done.12, bf16[128,1792]{1,0:T(8,128)(2,1)} %collective-permute-done.refs_2_, ...), custom_call_target="tpu_custom_call" | custom-call | flops 1000000 | bytes 100000 | tf_op jit(solution)/shard_map/pallas_call | solution.py:179
  127.3 2.6 %collective-permute-start.23 = (bf16[256,896]{1,0:T(8,128)(2,1)S(1)}, bf16[256,896]{1,0:T(8,128)(2,1)S(1)}, u32[]{:S(2)}, u32[]{:S(2)}) collective-permute-start(bf16[256,896]{1,0:T(8,128)(2,1)S(1)} %copy-done.35), channel_id=1, source_target_pairs={{0,8},{2,10},{4,12},{6,14},{8,0},{10,2},{12,4},{14,6},{16,24},{18,... | collective-permute-start | bytes 1376264 | tf_op jit(solution)/shard_map/ppermute | solution.py:41
  133.1 7.9 %collective-permute-done.23.refs_11_ = bf16[256,896]{1,0:T(8,128)(2,1)S(1)} collective-permute-done((bf16[256,896]{1,0:T(8,128)(2,1)S(1)}, bf16[256,896]{1,0:T(8,128)(2,1)S(1)}, u32[]{:S(2)}, u32[]{:S(2)}) %collective-permute-start.23) | collective-permute-done | bytes 458784 | tf_op jit(solution)/shard_map/ppermute | solution.py:41
  144.0 8.9 %shard_map.69 = (bf16[4,64,3072]{2,1,0:T(8,128)(2,1)S(1)}, bf16[4,64,3072]{2,1,0:T(8,128)(2,1)}) custom-call(s32[2]{0:T(128)S(1)} %pad_add_fusion.scalar_ref, bf16[512,896]{1,0:T(8,128)(2,1)S(1)} %maximum_select_fusion.1.refs_0_, bf16[256,896]{1,0:T(8,128)(2,1)} %collective-permute-done.12.refs_1_, bf16[256,896]{1,0:T(8,128)(2,1)S(1)} %collective-permute-done.24.refs_2_, ...), custom_call_target="tpu_custom_call" | custom-call | flops 1000000 | bytes 100000 | tf_op jit(solution)/shard_map/pallas_call | solution.py:179
  155.8 11.0 %collective-permute-done.22 = bf16[64,3072]{1,0:T(8,128)(2,1)S(1)} collective-permute-done((bf16[64,3072]{1,0:T(8,128)(2,1)}, bf16[64,3072]{1,0:T(8,128)(2,1)S(1)}, u32[]{:S(2)}, u32[]{:S(2)}) %collective-permute-start.22) | collective-permute-done | bytes 393248 | tf_op jit(solution)/shard_map/ppermute | solution.py:35
  166.7 2.1 %add_convert_fusion = bf16[4,64,3072]{2,1,0:T(8,128)(2,1)S(1)} fusion(bf16[4,64,3072]{2,1,0:T(8,128)(2,1)S(1)} %collective-permute-done.27, bf16[4,64,3072]{2,1,0:T(8,128)(2,1)} %copy-done.21), kind=kLoop, calls=%fused_computation.2 | loop fusion | flops 3145728 | bytes 4718592 | tf_op jit(solution)/shard_map/convert_element_type | solution.py:269
  174.5 6.1 %collective-permute-start.26 = (bf16[64,1024]{1,0:T(8,128)(2,1)S(1)}, bf16[64,1024]{1,0:T(8,128)(2,1)S(1)}, u32[]{:S(2)}, u32[]{:S(2)}) collective-permute-start(bf16[64,1024]{1,0:T(8,128)(2,1)S(1)} %get-tuple-element.74), channel_id=1, source_target_pairs={{0,16},{2,18},{4,20},{6,22},{24,8},{26,10},{28,12},{30,14},{1,17},... | collective-permute-start | bytes 393224 | tf_op jit(solution)/shard_map/ppermute | solution.py:41
  182.6 6.2 %collective-permute-done.30 = bf16[64,3072]{1,0:T(8,128)(2,1)S(1)} collective-permute-done((bf16[64,3072]{1,0:T(8,128)(2,1)S(1)}, bf16[64,3072]{1,0:T(8,128)(2,1)S(1)}, u32[]{:S(2)}, u32[]{:S(2)}) %collective-permute-start.30) | collective-permute-done | bytes 393248 | tf_op jit(solution)/shard_map/ppermute | solution.py:35
  194.7 4.5 %collective-permute-start.34 = (bf16[64,1024]{1,0:T(8,128)(2,1)S(1)}, bf16[64,1024]{1,0:T(8,128)(2,1)S(1)}, u32[]{:S(2)}, u32[]{:S(2)}) collective-permute-start(bf16[64,1024]{1,0:T(8,128)(2,1)S(1)} %get-tuple-element.42), channel_id=1, source_target_pairs={{0,24},{2,26},{4,28},{6,30},{24,0},{26,2},{28,4},{30,6},{1,25},{3,... | collective-permute-start | bytes 393224 | tf_op jit(solution)/shard_map/ppermute | solution.py:41
  201.4 4.4 %fusion = f32[256,7168]{1,0:T(8,128)} fusion(f32[256,7168]{1,0:T(8,128)S(1)} %bitcast.47, bf16[64,1792]{1,0:T(8,128)(2,1)S(1)} %get-tuple-element.64, bf16[64,1792]{1,0:T(8,128)(2,1)S(1)} %get-tuple-element.65, bf16[64,1792]{1,0:T(8,128)(2,1)S(1)} %get-tuple-element.66, bf16[64,1792]{1,0:T(8,128)(2,1)S(1)} %get-tuple-element.63, f32[4096,64]{0,1:T(8,128)S(1)} %copy-done, ...), kind=kOutput, calls=%fused_computation.1 | convolution fusion | flops 244056064 | bytes 15630340 | tf_op jit(solution)/shard_map/dot_general | solution.py:101
  205.7 2.7 %collective-permute-done.33 = bf16[64,2048]{1,0:T(8,128)(2,1)S(1)} collective-permute-done((bf16[64,2048]{1,0:T(8,128)(2,1)S(1)}, bf16[64,2048]{1,0:T(8,128)(2,1)S(1)}, u32[]{:S(2)}, u32[]{:S(2)}) %collective-permute-start.33) | collective-permute-done | bytes 262176 | tf_op jit(solution)/shard_map/ppermute | solution.py:41
  (180 shorter events, 56.5 us)
Async XLA Ops:
  3.3 14.5 %collective-permute-start.1 = (bf16[128,1792]{1,0:T(8,128)(2,1)}, bf16[128,1792]{1,0:T(8,128)(2,1)S(1)}, u32[]{:S(2)}, u32[]{:S(2)}) collective-permute-start(bf16[128,1792]{1,0:T(8,128)(2,1)} %get-tuple-element.51), channel_id=1, source_target_pairs={{0,2},{2,0},{4,6},{6,4},{8,10},{10,8},{12,14},{14,12},{16,18},{18,... | collective-permute-start | bytes 1376264 | tf_op jit(solution)/shard_map/ppermute | solution.py:35
  6.3 21.9 %collective-permute-start.3 = (bf16[128,1792]{1,0:T(8,128)(2,1)}, bf16[128,1792]{1,0:T(8,128)(2,1)S(1)}, u32[]{:S(2)}, u32[]{:S(2)}) collective-permute-start(bf16[128,1792]{1,0:T(8,128)(2,1)} %get-tuple-element.53), channel_id=1, source_target_pairs={{0,6},{2,4},{4,2},{6,0},{8,14},{10,12},{12,10},{14,8},{16,22},{18,... | collective-permute-start | bytes 1376264 | tf_op jit(solution)/shard_map/ppermute | solution.py:35
  7.8 21.7 %collective-permute-start.2 = (bf16[128,1792]{1,0:T(8,128)(2,1)}, bf16[128,1792]{1,0:T(8,128)(2,1)S(1)}, u32[]{:S(2)}, u32[]{:S(2)}) collective-permute-start(bf16[128,1792]{1,0:T(8,128)(2,1)} %get-tuple-element.54), channel_id=1, source_target_pairs={{0,4},{2,6},{4,0},{6,2},{8,12},{10,14},{12,8},{14,10},{16,20},{18,... | collective-permute-start | bytes 1376264 | tf_op jit(solution)/shard_map/ppermute | solution.py:35
  7.8 21.8 %collective-permute-start.4 = (bf16[128,1792]{1,0:T(8,128)(2,1)S(1)}, bf16[128,1792]{1,0:T(8,128)(2,1)S(1)}, u32[]{:S(2)}, u32[]{:S(2)}) collective-permute-start(bf16[128,1792]{1,0:T(8,128)(2,1)S(1)} %get-tuple-element.24.refs_0_), channel_id=1, source_target_pairs={{8,16},{10,18},{12,20},{14,22},{16,8},{18,10},{20,12},{22,14},{9,1... | collective-permute-start | bytes 1376264 | tf_op jit(solution)/shard_map/ppermute | solution.py:41
  8.5 22.1 %collective-permute-start = (bf16[128,1792]{1,0:T(8,128)(2,1)S(1)}, bf16[128,1792]{1,0:T(8,128)(2,1)}, u32[]{:S(2)}, u32[]{:S(2)}) collective-permute-start(bf16[128,1792]{1,0:T(8,128)(2,1)S(1)} %get-tuple-element.24.refs_0_), channel_id=1, source_target_pairs={{0,8},{2,10},{4,12},{6,14},{8,0},{10,2},{12,4},{14,6},{16,24},{18,... | collective-permute-start | bytes 1376264 | tf_op jit(solution)/shard_map/ppermute | solution.py:41
  30.6 41.4 %collective-permute-start.7 = (bf16[384,1792]{1,0:T(8,128)(2,1)S(1)}, bf16[384,1792]{1,0:T(8,128)(2,1)S(1)}, u32[]{:S(2)}, u32[]{:S(2)}) collective-permute-start(bf16[384,1792]{1,0:T(8,128)(2,1)S(1)} %pad_maximum_fusion.refs_1_), channel_id=1, source_target_pairs={{8,16},{10,18},{12,20},{14,22},{16,8},{18,10},{20,12},{22,14},{9,1... | collective-permute-start | bytes 4128776 | tf_op jit(solution)/shard_map/ppermute | solution.py:41
  31.3 38.9 %collective-permute-start.5 = (bf16[384,1792]{1,0:T(8,128)(2,1)S(1)}, bf16[384,1792]{1,0:T(8,128)(2,1)S(1)}, u32[]{:S(2)}, u32[]{:S(2)}) collective-permute-start(bf16[384,1792]{1,0:T(8,128)(2,1)S(1)} %pad_maximum_fusion.refs_1_), channel_id=1, source_target_pairs={{0,8},{2,10},{4,12},{6,14},{8,0},{10,2},{12,4},{14,6},{16,24},{18,... | collective-permute-start | bytes 4128776 | tf_op jit(solution)/shard_map/ppermute | solution.py:41
  41.3 27.2 %collective-permute-start.8 = (bf16[256,1792]{1,0:T(8,128)(2,1)S(1)}, bf16[256,1792]{1,0:T(8,128)(2,1)S(1)}, u32[]{:S(2)}, u32[]{:S(2)}) collective-permute-start(bf16[256,1792]{1,0:T(8,128)(2,1)S(1)} %get-tuple-element.26), channel_id=1, source_target_pairs={{0,2},{2,0},{4,6},{6,4},{8,10},{10,8},{12,14},{14,12},{16,18},{18,... | collective-permute-start | bytes 2752520 | tf_op jit(solution)/shard_map/ppermute | solution.py:35
  41.7 26.8 %collective-permute-start.10 = (bf16[256,1792]{1,0:T(8,128)(2,1)S(1)}, bf16[256,1792]{1,0:T(8,128)(2,1)S(1)}, u32[]{:S(2)}, u32[]{:S(2)}) collective-permute-start(bf16[256,1792]{1,0:T(8,128)(2,1)S(1)} %get-tuple-element.27), channel_id=1, source_target_pairs={{0,4},{2,6},{4,0},{6,2},{8,12},{10,14},{12,8},{14,10},{16,20},{18,... | collective-permute-start | bytes 2752520 | tf_op jit(solution)/shard_map/ppermute | solution.py:35
  43.7 20.5 %collective-permute-start.15 = (bf16[128,64]{1,0:T(8,128)(2,1)S(1)}, bf16[128,64]{1,0:T(8,128)(2,1)S(1)}, u32[]{:S(2)}, u32[]{:S(2)}) collective-permute-start(bf16[128,64]{1,0:T(8,128)(2,1)S(1)} %all_gather.3), channel_id=1, source_target_pairs={{0,6},{2,4},{4,2},{6,0},{8,14},{10,12},{12,10},{14,8},{16,22},{18,... | collective-permute-start | bytes 49160 | tf_op jit(solution)/shard_map/ppermute | solution.py:35
  68.5 39.7 %collective-permute-start.11 = (bf16[256,1792]{1,0:T(8,128)(2,1)S(1)}, bf16[256,1792]{1,0:T(8,128)(2,1)S(1)}, u32[]{:S(2)}, u32[]{:S(2)}) collective-permute-start(bf16[256,1792]{1,0:T(8,128)(2,1)S(1)} %get-tuple-element.28), channel_id=1, source_target_pairs={{0,6},{2,4},{4,2},{6,0},{8,14},{10,12},{12,10},{14,8},{16,22},{18,... | collective-permute-start | bytes 2752520 | tf_op jit(solution)/shard_map/ppermute | solution.py:35
  71.3 34.5 %collective-permute-start.6 = (bf16[512,896]{1,0:T(8,128)(2,1)S(1)}, bf16[512,896]{1,0:T(8,128)(2,1)S(1)}, u32[]{:S(2)}, u32[]{:S(2)}) collective-permute-start(bf16[512,896]{1,0:T(8,128)(2,1)S(1)} %pad_maximum_fusion.1), channel_id=1, source_target_pairs={{8,16},{10,18},{12,20},{14,22},{16,8},{18,10},{20,12},{22,14},{9,1... | collective-permute-start | bytes 2752520 | tf_op jit(solution)/shard_map/ppermute | solution.py:41
  72.3 33.5 %collective-permute-start.9 = (bf16[512,896]{1,0:T(8,128)(2,1)S(1)}, bf16[512,896]{1,0:T(8,128)(2,1)S(1)}, u32[]{:S(2)}, u32[]{:S(2)}) collective-permute-start(bf16[512,896]{1,0:T(8,128)(2,1)S(1)} %maximum_select_fusion), channel_id=1, source_target_pairs={{0,8},{2,10},{4,12},{6,14},{8,0},{10,2},{12,4},{14,6},{16,24},{18,... | collective-permute-start | bytes 2752520 | tf_op jit(solution)/shard_map/ppermute | solution.py:41
  76.1 28.1 %collective-permute-start.17 = (bf16[64,1792]{1,0:T(8,128)(2,1)S(1)}, bf16[64,1792]{1,0:T(8,128)(2,1)S(1)}, u32[]{:S(2)}, u32[]{:S(2)}) collective-permute-start(bf16[64,1792]{1,0:T(8,128)(2,1)S(1)} %fusion.15), channel_id=1, source_target_pairs={{0,16},{2,18},{4,20},{6,22},{8,24},{10,26},{12,28},{14,30},{16,0},... | collective-permute-start | bytes 688136 | tf_op jit(solution)/shard_map/ppermute | solution.py:41
  106.7 19.6 %collective-permute-start.12 = (bf16[256,896]{1,0:T(8,128)(2,1)}, bf16[256,896]{1,0:T(8,128)(2,1)}, u32[]{:S(2)}, u32[]{:S(2)}) collective-permute-start(bf16[256,896]{1,0:T(8,128)(2,1)} %pad_maximum_fusion.5), channel_id=1, source_target_pairs={{8,16},{10,18},{12,20},{14,22},{16,8},{18,10},{20,12},{22,14},{9,1... | collective-permute-start | bytes 1376264 | tf_op jit(solution)/shard_map/ppermute | solution.py:41
  109.5 16.9 %collective-permute-start.18 = (bf16[256,896]{1,0:T(8,128)(2,1)}, bf16[256,896]{1,0:T(8,128)(2,1)}, u32[]{:S(2)}, u32[]{:S(2)}) collective-permute-start(bf16[256,896]{1,0:T(8,128)(2,1)} %get-tuple-element.33), channel_id=1, source_target_pairs={{0,8},{2,10},{4,12},{6,14},{8,0},{10,2},{12,4},{14,6},{16,24},{18,... | collective-permute-start | bytes 1376264 | tf_op jit(solution)/shard_map/ppermute | solution.py:41
  126.4 17.6 %collective-permute-start.24 = (bf16[256,896]{1,0:T(8,128)(2,1)S(1)}, bf16[256,896]{1,0:T(8,128)(2,1)S(1)}, u32[]{:S(2)}, u32[]{:S(2)}) collective-permute-start(bf16[256,896]{1,0:T(8,128)(2,1)S(1)} %slice.136), channel_id=1, source_target_pairs={{8,16},{10,18},{12,20},{14,22},{16,8},{18,10},{20,12},{22,14},{9,1... | collective-permute-start | bytes 1376264 | tf_op jit(solution)/shard_map/ppermute | solution.py:41
  127.3 13.7 %collective-permute-start.23 = (bf16[256,896]{1,0:T(8,128)(2,1)S(1)}, bf16[256,896]{1,0:T(8,128)(2,1)S(1)}, u32[]{:S(2)}, u32[]{:S(2)}) collective-permute-start(bf16[256,896]{1,0:T(8,128)(2,1)S(1)} %copy-done.35), channel_id=1, source_target_pairs={{0,8},{2,10},{4,12},{6,14},{8,0},{10,2},{12,4},{14,6},{16,24},{18,... | collective-permute-start | bytes 1376264 | tf_op jit(solution)/shard_map/ppermute | solution.py:41
  154.1 12.6 %collective-permute-start.27 = (bf16[4,64,3072]{2,1,0:T(8,128)(2,1)}, bf16[4,64,3072]{2,1,0:T(8,128)(2,1)S(1)}, u32[]{:S(2)}, u32[]{:S(2)}) collective-permute-start(bf16[4,64,3072]{2,1,0:T(8,128)(2,1)} %get-tuple-element.40), channel_id=1, source_target_pairs={{0,1},{1,0},{2,3},{3,2},{4,5},{5,4},{6,7},{7,6},{8,9},{9,8},{10,11... | collective-permute-start | bytes 4718600 | tf_op jit(solution)/shard_map/ppermute | solution.py:204
  154.1 12.6 %collective-permute-start.22 = (bf16[64,3072]{1,0:T(8,128)(2,1)}, bf16[64,3072]{1,0:T(8,128)(2,1)S(1)}, u32[]{:S(2)}, u32[]{:S(2)}) collective-permute-start(bf16[64,3072]{1,0:T(8,128)(2,1)} %get-tuple-element.59), channel_id=1, source_target_pairs={{0,6},{2,4},{4,2},{6,0},{8,14},{10,12},{12,10},{14,8},{16,22},{18,... | collective-permute-start | bytes 1179656 | tf_op jit(solution)/shard_map/ppermute | solution.py:35
  170.3 18.5 %collective-permute-start.30 = (bf16[64,3072]{1,0:T(8,128)(2,1)S(1)}, bf16[64,3072]{1,0:T(8,128)(2,1)S(1)}, u32[]{:S(2)}, u32[]{:S(2)}) collective-permute-start(bf16[64,3072]{1,0:T(8,128)(2,1)S(1)} %get-tuple-element.56), channel_id=1, source_target_pairs={{0,6},{2,4},{4,2},{6,0},{8,14},{10,12},{12,10},{14,8},{16,22},{18,... | collective-permute-start | bytes 1179656 | tf_op jit(solution)/shard_map/ppermute | solution.py:35
  171.5 18.6 %collective-permute-start.29 = (bf16[64,3072]{1,0:T(8,128)(2,1)S(1)}, bf16[64,3072]{1,0:T(8,128)(2,1)S(1)}, u32[]{:S(2)}, u32[]{:S(2)}) collective-permute-start(bf16[64,3072]{1,0:T(8,128)(2,1)S(1)} %get-tuple-element.57), channel_id=1, source_target_pairs={{0,4},{2,6},{4,0},{6,2},{8,12},{10,14},{12,8},{14,10},{16,20},{18,... | collective-permute-start | bytes 1179656 | tf_op jit(solution)/shard_map/ppermute | solution.py:35
  173.8 20.2 %collective-permute-start.31 = (bf16[64,1024]{1,0:T(8,128)(2,1)S(1)}, bf16[64,1024]{1,0:T(8,128)(2,1)S(1)}, u32[]{:S(2)}, u32[]{:S(2)}) collective-permute-start(bf16[64,1024]{1,0:T(8,128)(2,1)S(1)} %get-tuple-element.74), channel_id=1, source_target_pairs={{8,16},{10,18},{12,20},{14,22},{16,8},{18,10},{20,12},{22,14},{9,1... | collective-permute-start | bytes 393224 | tf_op jit(solution)/shard_map/ppermute | solution.py:41
  174.5 19.5 %collective-permute-start.26 = (bf16[64,1024]{1,0:T(8,128)(2,1)S(1)}, bf16[64,1024]{1,0:T(8,128)(2,1)S(1)}, u32[]{:S(2)}, u32[]{:S(2)}) collective-permute-start(bf16[64,1024]{1,0:T(8,128)(2,1)S(1)} %get-tuple-element.74), channel_id=1, source_target_pairs={{0,16},{2,18},{4,20},{6,22},{24,8},{26,10},{28,12},{30,14},{1,17},... | collective-permute-start | bytes 393224 | tf_op jit(solution)/shard_map/ppermute | solution.py:41
  (57 other events, 569.4 us)

commit v5 on v4

--- a/solution.py
+++ b/solution.py
@@ -195,7 +195,7 @@
     inner = (level == 1) | (level == 2)
     tokens, hidden = out_grad.shape
     rows = weight.shape[0]
-    width, block, pair = rows * PLANE, tokens * PLANE, tokens * 2
+    width, block = rows * PLANE, tokens * PLANE
     both = hidden // PLANE
     half = both // 2
     low, high = slice(0, half), slice(half, both)
@@ -205,58 +205,62 @@
     send = lambda a, w: jnp.where(inner, a, w)
 
     cuts = [lay.cut(out_grad, r) for r in range(PLANE)]
-    plane = [across(cuts[r], r) for r in range(1, PLANE)]
+    plane = [across(cuts[r], r) for r in (1, 2)]
     e0, m0 = end_swap(cuts[0]), mid_swap(cuts[0])
-    proj = projected(lay, after(inputs, plane[0]), proj_basis)
-    weight = after(weight, plane[0])
+    plane.append(across(after(cuts[3], *plane), 3))
+    weight = after(weight, e0, m0)
     parts = [lay.cut(weight, r) for r in range(PLANE)]
-    panel = sum(tn(q, a) for q, a in zip(proj, [cuts[0], *plane]))
-    panel = panel + end_swap(panel.astype(bf16)).astype(f32)
-    rest = after(jnp.concatenate(plane, 0), e0, m0)
-    e1, m1 = end_swap(rest), mid_swap(rest)
+    sides = after(jnp.concatenate(plane[:2], 0), e0, m0)
+    e1, m1 = end_swap(sides), mid_swap(sides)
+    e2, m2 = end_swap(plane[2]), mid_swap(plane[2])
     parts[1:3] = [across(after(parts[r], *plane), r) for r in (1, 2)]
     parts[3] = across(after(parts[3], *parts[1:3]), 3)
-    panel = (panel + lay.levels(panel.astype(bf16), 2).astype(f32)).astype(bf16)
-
-    joined = lambda x, c: jnp.concatenate([x[0][:, c], x[1][:, c]], 0)
-    near_e, near_m = [e0, e1], [m0, m1]
+    joined = lambda x, c: jnp.concatenate([y[:, c] for y in x], 0)
+    near_e, near_m = [e0, e1, e2], [m0, m1, m2]
     e_high = joined(near_e, high)
     m_low = joined(near_m, low)
     far0 = mid_swap(joined(near_e, low))
     got_a = send(m_low, jnp.concatenate([w[:, high] for w in parts[:2]], 0))
     got_a = end_swap(got_a)
+    proj = projected(lay, after(inputs, e1, m1), proj_basis)
     far1, got = [], []
     for i, w in enumerate(parts[2:]):
-        rows_i = slice(i * pair, (i + 1) * pair)
+        rows_i = slice(i * 2 * tokens, (i + 1) * 2 * tokens)
         far1.append(mid_swap(after(e_high[rows_i], far0, got_a)))
-        got.append(end_swap(after(send(far0[rows_i], w[:, high]), got_a, parts[3], panel)))
+        got.append(end_swap(after(send(far0[rows_i], w[:, high]), got_a, parts[3], *proj)))
+
     weight_fills = lambda first, b: [(first + r, 0, b, r * rows, 0, both) for r in range(PLANE)]
     none = lambda r: ()
     early0 = send(m_low, got_a)
-    sources = [after(cuts[0], far0), rest, *near_e, early0, *near_m, *parts]
-    fills = [(0, 0, 0, 0, 0, both), (1, 0, 0, tokens, 0, both)] + weight_fills(7, 3)
-    fills += [(2, 0, 1, 0, 0, both), (3, 0, 1, tokens, 0, both)]
-    fills += [(4, 0, 2, 0, 0, half), (5, half, 2, 0, half, half), (6, half, 2, tokens, half, half)]
+    own = [after(cuts[0], far0), sides, plane[2]]
+    sources = [*own, *near_e, early0, *near_m, *parts]
+    starts = (0, tokens, 3 * tokens)
+    fills = [(i, 0, 0, row, 0, both) for i, row in enumerate(starts)] + weight_fills(10, 3)
+    fills += [(3 + i, 0, 1, row, 0, both) for i, row in enumerate(starts)]
+    fills += [(6, 0, 2, 0, 0, half)]
+    fills += [(7 + i, half, 2, row, half, half) for i, row in enumerate(starts)]
     jobs = [
-        (0, 3, 0, 0, both, (0, 1), lambda r: (2 + r,)),
-        (1, 3, 0, 0, both, (6, 7), none),
-        (2, 3, 0, 0, both, (8, 9, 10), none),
+        (0, 3, 0, 0, both, (0, 1, 2), lambda r: (3 + r,)),
+        (1, 3, 0, 0, both, (7, 8, 9), none),
+        (2, 3, 0, 0, both, (10, 11, 12, 13), none),
     ]
     keep, give = products(lay, sources, [(block, both)] * 3 + [(width, both)], fills, jobs, width)
     give = after(give, far1[0], got[0])
     first = (keep.astype(f32) + swap(give).astype(f32)).astype(bf16)
     first_x, first_y = across(first[1], 1), across(first[2], 2)
 
+    panel = sum(tn(q, a) for q, a in zip(proj, [after(cuts[0], give), *plane]))
+    panel = panel + end_swap(after(panel.astype(bf16), first)).astype(f32)
+
     late0 = send(far0, jnp.concatenate(got, 0))
-    sources = [after(late0, first_x, first_y), *far1, *near_m, *parts, got_a, *got]
+    sources = [after(late0, first), *far1, *near_m, *parts, got_a, *got]
     fills = [(0, 0, 0, 0, 0, half)]
-    fills += [(1 + i, 0, 0, i * pair, half, half) for i in range(2)]
-    fills += weight_fills(5, 2)
-    fills += [(3, half, 1, 0, 0, half), (4, half, 1, tokens, 0, half)]
-    fills += [(9, 0, 3, 0, 0, half), (10, 0, 3, 2 * rows, 0, half), (11, 0, 3, 3 * rows, 0, half)]
+    fills += [(1 + i, 0, 0, 2 * i * tokens, half, half) for i in range(2)] + weight_fills(6, 2)
+    fills += [(3 + i, half, 1, row, 0, half) for i, row in enumerate(starts)]
+    fills += [(10, 0, 3, 0, 0, half), (11, 0, 3, 2 * rows, 0, half), (12, 0, 3, 3 * rows, 0, half)]
     jobs = [
         (0, 2, 0, 0, both, (0, 1, 2), lambda r: (3 + r,)),
-        (1, 3, 0, 0, half, (7, 8), lambda r: ((9,), (), (10,), (11,))[r]),
+        (1, 3, 0, 0, half, (7, 8, 9), lambda r: ((10,), (), (11,), (12,))[r]),
         (0, 3, half, 0, half, (), none),
     ]
     buffers = [(block, both), (block, half), (width, both), (width, half)]
@@ -265,10 +269,12 @@
     def plane_sum(own, *others):
         return sum(x.astype(f32) for x in (own, *others)).astype(bf16)
 
-    first = plane_sum(first[0], first_x, first_y, after(across(first[3], 3), keep))
+    first = plane_sum(first[0], first_x, first_y, across(first[3], 3))
+    give = after(give, first)
     second = (keep.astype(f32) + swap(give).astype(f32)).astype(bf16)
     second = plane_sum(second[0], *[across(second[r], r) for r in range(1, PLANE)])
-    panel = after(panel, second)
+    panel = (panel + lay.levels(after(panel.astype(bf16), second), 2).astype(f32)).astype(bf16)
+    summed_panel = panel
     panel = jnp.stack([panel] + [across(panel, r) for r in range(1, PLANE)])
     panel = jnp.concatenate(
         [lax.dynamic_index_in_dim(panel, lay.place ^ p, 0, False) for p in range(PLANE)], 1
@@ -280,7 +286,7 @@
     z1 = end_swap(y1)
     z3 = mid_swap(early)
     z2 = lay.levels(early, 2, (0, 3))
-    late, early_other = after((late, early_other), z1, z2, z3)
+    late, early_other = after((late, early_other), z1, z2, z3, summed_panel)
     z2b = mid_swap(early_other)
     z_late = lay.levels(jnp.concatenate([late, late_other], 1), 2, (1, 2))
     z3b = lay.levels(late, 3, (0, 3))

time: 210 us -> 197 us (0.938)
  waiting for transfers between devices: 93.3 us -> 63 us
  starting transfers between devices: 60.3 us -> 76.3 us
    ppermute x18, waiting for transfers between devices: 56.1 us -> 20 us  [across(): return lax.ppermute(x, 'dp', [(d, d ^ r) for d in range(self.replicas)])]
    ppermute x18 -> x20, starting transfers between devices: 37 us -> 53.3 us  [levels(): return lax.ppermute(x, 'dp', pairs)]
    ppermute x18 -> x20, waiting for transfers between devices: 37.2 us -> 43 us  [levels(): return lax.ppermute(x, 'dp', pairs)]
    unnamed x84 -> x76, local copies, waits for them, and re-layouts: 10.3 us -> 11.2 us
  transfers between devices with their start and end apart: 38 -> 40, of which waited for: 15 -> 16; matrix products, arithmetic and copies ran while one was open for 9% -> 11% of each run, Pallas kernels for 4% -> 9%
where the time goes in v5:
time: 197 us; the launch traced here: 196 us
  starting transfers between devices  76.3 us (39%)
  waiting for transfers between devices  63 us (32%)
  Pallas kernels  18.6 us (9%)
  local copies, waits for them, and re-layouts  17.9 us (9%)
  other arithmetic  10.1 us (5%)
  matrix products  7.02 us (4%)
    ppermute x20, starting transfers between devices, levels(): return lax.ppermute(x, 'dp', pairs)  53.3 us
    ppermute x20, waiting for transfers between devices, levels(): return lax.ppermute(x, 'dp', pairs)  43 us
    ppermute x18, starting transfers between devices, across(): return lax.ppermute(x, 'dp', [(d, d ^ r) for d in range(self.replicas)])  22.8 us
    ppermute x18, waiting for transfers between devices, across(): return lax.ppermute(x, 'dp', [(d, d ^ r) for d in range(self.replicas)])  20 us
    pallas_call x2, Pallas kernels, products(): pl.pallas_call(kernel, out_shape=(out, out), in_specs=[pl.BlockSpec(memor...  18.6 us
    unnamed x76, local copies, waits for them, and re-layouts  11.2 us
    select_n x4, other arithmetic, line_of_four(): send = lambda a, w: jnp.where(inner, a, w)  4.45 us
    dot_general x1, matrix products, updated(): update = jnp.dot(basis_rows.astype(bf16), panel, preferred_element_type=f32)  4.35 us
  transfers between devices with their start and end apart: 40, of which 16 were waited for; matrix products, arithmetic and copies ran while one was open for 11% of the time, Pallas kernels for 9%

profile of v5, /device:TPU:0, one launch (start us, length us, event | category | flops | bytes accessed | tf_op | source)
XLA Modules:
  0.0 196.2 jit_solution(12166935938461870689)
XLA Ops:
  2.3 3.0 %collective-permute-start.2 = (bf16[128,1792]{1,0:T(8,128)(2,1)S(1)}, bf16[128,1792]{1,0:T(8,128)(2,1)S(1)}, u32[]{:S(2)}, u32[]{:S(2)}) collective-permute-start(bf16[128,1792]{1,0:T(8,128)(2,1)S(1)} %get-tuple-element.57), channel_id=1, source_target_pairs={{0,4},{2,6},{4,0},{6,2},{8,12},{10,14},{12,8},{14,10},{16,20},{18,... | collective-permute-start | bytes 1376264 | tf_op jit(solution)/shard_map/ppermute | solution.py:35
  7.5 4.4 %collective-permute-start = (bf16[128,1792]{1,0:T(8,128)(2,1)S(1)}, bf16[128,1792]{1,0:T(8,128)(2,1)}, u32[]{:S(2)}, u32[]{:S(2)}) collective-permute-start(bf16[128,1792]{1,0:T(8,128)(2,1)S(1)} %get-tuple-element.45.refs_0_), channel_id=1, source_target_pairs={{0,8},{2,10},{4,12},{6,14},{8,0},{10,2},{12,4},{14,6},{16,24},{18,... | collective-permute-start | bytes 1376264 | tf_op jit(solution)/shard_map/ppermute | solution.py:41
  12.0 3.9 %collective-permute-done.2 = bf16[128,1792]{1,0:T(8,128)(2,1)S(1)} collective-permute-done((bf16[128,1792]{1,0:T(8,128)(2,1)S(1)}, bf16[128,1792]{1,0:T(8,128)(2,1)S(1)}, u32[]{:S(2)}, u32[]{:S(2)}) %collective-permute-start.2) | collective-permute-done | bytes 458784 | tf_op jit(solution)/shard_map/ppermute | solution.py:35
  19.7 2.0 %collective-permute-done.refs_3_ = bf16[128,1792]{1,0:T(8,128)(2,1)} collective-permute-done((bf16[128,1792]{1,0:T(8,128)(2,1)S(1)}, bf16[128,1792]{1,0:T(8,128)(2,1)}, u32[]{:S(2)}, u32[]{:S(2)}) %collective-permute-start) | collective-permute-done | bytes 458784 | tf_op jit(solution)/shard_map/ppermute | solution.py:41
  22.6 3.9 %collective-permute-start.4 = (bf16[256,1792]{1,0:T(8,128)(2,1)S(1)}, bf16[256,1792]{1,0:T(8,128)(2,1)S(1)}, u32[]{:S(2)}, u32[]{:S(2)}) collective-permute-start(bf16[256,1792]{1,0:T(8,128)(2,1)S(1)} %pad_maximum_fusion.refs_1_), channel_id=1, source_target_pairs={{0,8},{2,10},{4,12},{6,14},{8,0},{10,2},{12,4},{14,6},{16,24},{18,... | collective-permute-start | bytes 2752520 | tf_op jit(solution)/shard_map/ppermute | solution.py:41
  26.5 3.0 %collective-permute-done.5.refs_2_ = bf16[128,1792]{1,0:T(8,128)(2,1)} collective-permute-done((bf16[128,1792]{1,0:T(8,128)(2,1)S(1)}, bf16[128,1792]{1,0:T(8,128)(2,1)}, u32[]{:S(2)}, u32[]{:S(2)}) %collective-permute-start.5) | collective-permute-done | bytes 458784 | tf_op jit(solution)/shard_map/ppermute | solution.py:35
  31.1 2.3 %constant_dynamic-slice_fusion.1 = (bf16[256,1792]{1,0:T(8,128)(2,1)S(1)}, bf16[256,1792]{1,0:T(8,128)(2,1)S(1)}, bf16[256,1792]{1,0:T(8,128)(2,1)S(1)}, bf16[256,1792]{1,0:T(8,128)(2,1)S(1)}) fusion(bf16[256,7168]{1,0:T(8,128)(2,1)} %param.7, s32[]{:T(128)S(6)} %select_n.135, s32[]{:T(128)S(6)} %select_n.134, s32[]{:T(128)S(6)} %select_n.133, s32[]{:T(128)S(6)} %select_n.132), kind=kLoop, calls=%fused_computation.60 | loop fusion | bytes 7340048 | tf_op jit(solution)/shard_map/dynamic_slice | solution.py:45
  37.9 17.2 %collective-permute-done.6.refs_5_ = bf16[128,1792]{1,0:T(8,128)(2,1)S(1)} collective-permute-done((bf16[128,1792]{1,0:T(8,128)(2,1)}, bf16[128,1792]{1,0:T(8,128)(2,1)S(1)}, u32[]{:S(2)}, u32[]{:S(2)}) %collective-permute-start.6) | collective-permute-done | bytes 458784 | tf_op jit(solution)/shard_map/ppermute | solution.py:41
  59.5 15.0 %collective-permute-start.11 = (bf16[512,896]{1,0:T(8,128)(2,1)S(1)}, bf16[512,896]{1,0:T(8,128)(2,1)S(1)}, u32[]{:S(2)}, u32[]{:S(2)}) collective-permute-start(bf16[512,896]{1,0:T(8,128)(2,1)S(1)} %maximum_select_fusion), channel_id=1, source_target_pairs={{0,8},{2,10},{4,12},{6,14},{8,0},{10,2},{12,4},{14,6},{16,24},{18,... | collective-permute-start | bytes 2752520 | tf_op jit(solution)/shard_map/ppermute | solution.py:41
  75.6 1.8 all_gather.3
  77.4 2.5 %collective-permute-start.17 = (bf16[128,64]{1,0:T(8,128)(2,1)S(1)}, bf16[128,64]{1,0:T(8,128)(2,1)S(1)}, u32[]{:S(2)}, u32[]{:S(2)}) collective-permute-start(bf16[128,64]{1,0:T(8,128)(2,1)S(1)} %all_gather.3), channel_id=1, source_target_pairs={{0,6},{2,4},{4,2},{6,0},{8,14},{10,12},{12,10},{14,8},{16,22},{18,... | collective-permute-start | bytes 49160 | tf_op jit(solution)/shard_map/ppermute | solution.py:35
  82.0 5.5 %collective-permute-done.11.refs_10_ = bf16[512,896]{1,0:T(8,128)(2,1)S(1)} collective-permute-done((bf16[512,896]{1,0:T(8,128)(2,1)S(1)}, bf16[512,896]{1,0:T(8,128)(2,1)S(1)}, u32[]{:S(2)}, u32[]{:S(2)}) %collective-permute-start.11) | collective-permute-done | bytes 917536 | tf_op jit(solution)/shard_map/ppermute | solution.py:41
  101.1 9.7 %shard_map.68 = (bf16[4,64,3072]{2,1,0:T(8,128)(2,1)S(1)}, bf16[4,64,3072]{2,1,0:T(8,128)(2,1)S(1)}) custom-call(s32[2]{0:T(128)S(1)} %pad_add_fusion.scalar_ref, bf16[128,1792]{1,0:T(8,128)(2,1)S(1)} %get-tuple-element.45.refs_0_, bf16[256,1792]{1,0:T(8,128)(2,1)S(1)} %copy-done.8, bf16[128,1792]{1,0:T(8,128)(2,1)} %collective-permute-done.5.refs_2_, ...), custom_call_target="tpu_custom_call" | custom-call | flops 1000000 | bytes 100000 | tf_op jit(solution)/shard_map/pallas_call | solution.py:179
  111.8 3.1 %collective-permute-start.25 = (bf16[256,896]{1,0:T(8,128)(2,1)S(1)}, bf16[256,896]{1,0:T(8,128)(2,1)S(1)}, u32[]{:S(2)}, u32[]{:S(2)}) collective-permute-start(bf16[256,896]{1,0:T(8,128)(2,1)S(1)} %copy-done.35), channel_id=1, source_target_pairs={{0,8},{2,10},{4,12},{6,14},{8,0},{10,2},{12,4},{14,6},{16,24},{18,... | collective-permute-start | bytes 1376264 | tf_op jit(solution)/shard_map/ppermute | solution.py:41
  119.2 6.6 %collective-permute-done.25.refs_12_ = bf16[256,896]{1,0:T(8,128)(2,1)S(1)} collective-permute-done((bf16[256,896]{1,0:T(8,128)(2,1)S(1)}, bf16[256,896]{1,0:T(8,128)(2,1)S(1)}, u32[]{:S(2)}, u32[]{:S(2)}) %collective-permute-start.25) | collective-permute-done | bytes 458784 | tf_op jit(solution)/shard_map/ppermute | solution.py:41
  127.1 8.9 %shard_map.69 = (bf16[4,64,3072]{2,1,0:T(8,128)(2,1)S(1)}, bf16[4,64,3072]{2,1,0:T(8,128)(2,1)}) custom-call(s32[2]{0:T(128)S(1)} %pad_add_fusion.scalar_ref, bf16[512,896]{1,0:T(8,128)(2,1)S(1)} %maximum_select_fusion.1.refs_0_, bf16[256,896]{1,0:T(8,128)(2,1)} %collective-permute-done.14.refs_1_, bf16[256,896]{1,0:T(8,128)(2,1)S(1)} %collective-permute-done.26.refs_2_, ...), custom_call_target="tpu_custom_call" | custom-call | flops 1000000 | bytes 100000 | tf_op jit(solution)/shard_map/pallas_call | solution.py:179
  139.6 1.8 collective-permute-start.32
  141.4 2.1 %add_convert_fusion = bf16[4,64,3072]{2,1,0:T(8,128)(2,1)S(1)} fusion(bf16[4,64,3072]{2,1,0:T(8,128)(2,1)} %collective-permute-done.27, bf16[4,64,3072]{2,1,0:T(8,128)(2,1)S(1)} %copy-done.23), kind=kLoop, calls=%fused_computation.2 | loop fusion | flops 3145728 | bytes 4718592 | tf_op jit(solution)/shard_map/convert_element_type | solution.py:274
  148.5 6.5 %collective-permute-start.24 = (bf16[64,1024]{1,0:T(8,128)(2,1)S(1)}, bf16[64,1024]{1,0:T(8,128)(2,1)S(1)}, u32[]{:S(2)}, u32[]{:S(2)}) collective-permute-start(bf16[64,1024]{1,0:T(8,128)(2,1)S(1)} %get-tuple-element.84), channel_id=1, source_target_pairs={{0,16},{2,18},{4,20},{6,22},{24,8},{26,10},{28,12},{30,14},{1,17},... | collective-permute-start | bytes 393224 | tf_op jit(solution)/shard_map/ppermute | solution.py:41
  157.2 6.3 %collective-permute-done.30 = bf16[64,3072]{1,0:T(8,128)(2,1)S(1)} collective-permute-done((bf16[64,3072]{1,0:T(8,128)(2,1)S(1)}, bf16[64,3072]{1,0:T(8,128)(2,1)S(1)}, u32[]{:S(2)}, u32[]{:S(2)}) %collective-permute-start.30) | collective-permute-done | bytes 393248 | tf_op jit(solution)/shard_map/ppermute | solution.py:35
  166.7 9.6 %collective-permute-done.33 = bf16[64,1792]{1,0:T(8,128)(2,1)S(1)} collective-permute-done((bf16[64,1792]{1,0:T(8,128)(2,1)S(1)}, bf16[64,1792]{1,0:T(8,128)(2,1)S(1)}, u32[]{:S(2)}, u32[]{:S(2)}) %collective-permute-start.33) | collective-permute-done | bytes 229408 | tf_op jit(solution)/shard_map/ppermute | solution.py:41
  176.4 2.0 %collective-permute-start.39 = (bf16[64,1792]{1,0:T(8,128)(2,1)S(1)}, bf16[64,1792]{1,0:T(8,128)(2,1)S(1)}, u32[]{:S(2)}, u32[]{:S(2)}) collective-permute-start(bf16[64,1792]{1,0:T(8,128)(2,1)S(1)} %add_convert_fusion.2), channel_id=1, source_target_pairs={{0,6},{2,4},{4,2},{6,0},{8,14},{10,12},{12,10},{14,8},{16,22},{18,... | collective-permute-start | bytes 688136 | tf_op jit(solution)/shard_map/ppermute | solution.py:35
  180.6 4.4 %collective-permute-start.36 = (bf16[64,1024]{1,0:T(8,128)(2,1)S(1)}, bf16[64,1024]{1,0:T(8,128)(2,1)S(1)}, u32[]{:S(2)}, u32[]{:S(2)}) collective-permute-start(bf16[64,1024]{1,0:T(8,128)(2,1)S(1)} %get-tuple-element.49), channel_id=1, source_target_pairs={{0,24},{2,26},{4,28},{6,30},{24,0},{26,2},{28,4},{30,6},{1,25},{3,... | collective-permute-start | bytes 393224 | tf_op jit(solution)/shard_map/ppermute | solution.py:41
  189.1 4.4 %fusion = f32[256,7168]{1,0:T(8,128)} fusion(f32[256,7168]{1,0:T(8,128)S(1)} %bitcast.47, bf16[64,1792]{1,0:T(8,128)(2,1)S(1)} %get-tuple-element.68, bf16[64,1792]{1,0:T(8,128)(2,1)S(1)} %get-tuple-element.69, bf16[64,1792]{1,0:T(8,128)(2,1)S(1)} %get-tuple-element.70, bf16[64,1792]{1,0:T(8,128)(2,1)S(1)} %get-tuple-element.67, f32[4096,64]{0,1:T(8,128)S(1)} %copy-done, ...), kind=kOutput, calls=%fused_computation.1 | convolution fusion | flops 244056064 | bytes 15630340 | tf_op jit(solution)/shard_map/dot_general | solution.py:101
  (176 shorter events, 64.8 us)
Async XLA Ops:
  2.3 13.6 %collective-permute-start.2 = (bf16[128,1792]{1,0:T(8,128)(2,1)S(1)}, bf16[128,1792]{1,0:T(8,128)(2,1)S(1)}, u32[]{:S(2)}, u32[]{:S(2)}) collective-permute-start(bf16[128,1792]{1,0:T(8,128)(2,1)S(1)} %get-tuple-element.57), channel_id=1, source_target_pairs={{0,4},{2,6},{4,0},{6,2},{8,12},{10,14},{12,8},{14,10},{16,20},{18,... | collective-permute-start | bytes 1376264 | tf_op jit(solution)/shard_map/ppermute | solution.py:35
  7.5 14.2 %collective-permute-start = (bf16[128,1792]{1,0:T(8,128)(2,1)S(1)}, bf16[128,1792]{1,0:T(8,128)(2,1)}, u32[]{:S(2)}, u32[]{:S(2)}) collective-permute-start(bf16[128,1792]{1,0:T(8,128)(2,1)S(1)} %get-tuple-element.45.refs_0_), channel_id=1, source_target_pairs={{0,8},{2,10},{4,12},{6,14},{8,0},{10,2},{12,4},{14,6},{16,24},{18,... | collective-permute-start | bytes 1376264 | tf_op jit(solution)/shard_map/ppermute | solution.py:41
  21.8 35.7 %collective-permute-start.8 = (bf16[256,1792]{1,0:T(8,128)(2,1)S(1)}, bf16[256,1792]{1,0:T(8,128)(2,1)S(1)}, u32[]{:S(2)}, u32[]{:S(2)}) collective-permute-start(bf16[256,1792]{1,0:T(8,128)(2,1)S(1)} %pad_maximum_fusion.refs_1_), channel_id=1, source_target_pairs={{8,16},{10,18},{12,20},{14,22},{16,8},{18,10},{20,12},{22,14},{9,1... | collective-permute-start | bytes 2752520 | tf_op jit(solution)/shard_map/ppermute | solution.py:41
  22.6 33.2 %collective-permute-start.4 = (bf16[256,1792]{1,0:T(8,128)(2,1)S(1)}, bf16[256,1792]{1,0:T(8,128)(2,1)S(1)}, u32[]{:S(2)}, u32[]{:S(2)}) collective-permute-start(bf16[256,1792]{1,0:T(8,128)(2,1)S(1)} %pad_maximum_fusion.refs_1_), channel_id=1, source_target_pairs={{0,8},{2,10},{4,12},{6,14},{8,0},{10,2},{12,4},{14,6},{16,24},{18,... | collective-permute-start | bytes 2752520 | tf_op jit(solution)/shard_map/ppermute | solution.py:41
  29.5 25.5 %collective-permute-start.6 = (bf16[128,1792]{1,0:T(8,128)(2,1)}, bf16[128,1792]{1,0:T(8,128)(2,1)S(1)}, u32[]{:S(2)}, u32[]{:S(2)}) collective-permute-start(bf16[128,1792]{1,0:T(8,128)(2,1)} %collective-permute-done.5.refs_2_), channel_id=1, source_target_pairs={{0,8},{2,10},{4,12},{6,14},{8,0},{10,2},{12,4},{14,6},{16,24},{18,... | collective-permute-start | bytes 1376264 | tf_op jit(solution)/shard_map/ppermute | solution.py:41
  33.4 24.2 %collective-permute-start.10 = (bf16[256,1792]{1,0:T(8,128)(2,1)S(1)}, bf16[256,1792]{1,0:T(8,128)(2,1)S(1)}, u32[]{:S(2)}, u32[]{:S(2)}) collective-permute-start(bf16[256,1792]{1,0:T(8,128)(2,1)S(1)} %get-tuple-element.30), channel_id=1, source_target_pairs={{0,2},{2,0},{4,6},{6,4},{8,10},{10,8},{12,14},{14,12},{16,18},{18,... | collective-permute-start | bytes 2752520 | tf_op jit(solution)/shard_map/ppermute | solution.py:35
  34.9 39.5 %collective-permute-start.12 = (bf16[256,1792]{1,0:T(8,128)(2,1)S(1)}, bf16[256,1792]{1,0:T(8,128)(2,1)S(1)}, u32[]{:S(2)}, u32[]{:S(2)}) collective-permute-start(bf16[256,1792]{1,0:T(8,128)(2,1)S(1)} %get-tuple-element.31), channel_id=1, source_target_pairs={{0,4},{2,6},{4,0},{6,2},{8,12},{10,14},{12,8},{14,10},{16,20},{18,... | collective-permute-start | bytes 2752520 | tf_op jit(solution)/shard_map/ppermute | solution.py:35
  56.7 24.7 %collective-permute-start.7 = (bf16[512,896]{1,0:T(8,128)(2,1)S(1)}, bf16[512,896]{1,0:T(8,128)(2,1)S(1)}, u32[]{:S(2)}, u32[]{:S(2)}) collective-permute-start(bf16[512,896]{1,0:T(8,128)(2,1)S(1)} %pad_maximum_fusion.1), channel_id=1, source_target_pairs={{8,16},{10,18},{12,20},{14,22},{16,8},{18,10},{20,12},{22,14},{9,1... | collective-permute-start | bytes 2752520 | tf_op jit(solution)/shard_map/ppermute | solution.py:41
  59.5 28.0 %collective-permute-start.11 = (bf16[512,896]{1,0:T(8,128)(2,1)S(1)}, bf16[512,896]{1,0:T(8,128)(2,1)S(1)}, u32[]{:S(2)}, u32[]{:S(2)}) collective-permute-start(bf16[512,896]{1,0:T(8,128)(2,1)S(1)} %maximum_select_fusion), channel_id=1, source_target_pairs={{0,8},{2,10},{4,12},{6,14},{8,0},{10,2},{12,4},{14,6},{16,24},{18,... | collective-permute-start | bytes 2752520 | tf_op jit(solution)/shard_map/ppermute | solution.py:41
  74.5 16.2 %collective-permute-start.13 = (bf16[256,1792]{1,0:T(8,128)(2,1)S(1)}, bf16[256,1792]{1,0:T(8,128)(2,1)S(1)}, u32[]{:S(2)}, u32[]{:S(2)}) collective-permute-start(bf16[256,1792]{1,0:T(8,128)(2,1)S(1)} %get-tuple-element.32), channel_id=1, source_target_pairs={{0,6},{2,4},{4,2},{6,0},{8,14},{10,12},{12,10},{14,8},{16,22},{18,... | collective-permute-start | bytes 2752520 | tf_op jit(solution)/shard_map/ppermute | solution.py:35
  77.4 14.5 %collective-permute-start.17 = (bf16[128,64]{1,0:T(8,128)(2,1)S(1)}, bf16[128,64]{1,0:T(8,128)(2,1)S(1)}, u32[]{:S(2)}, u32[]{:S(2)}) collective-permute-start(bf16[128,64]{1,0:T(8,128)(2,1)S(1)} %all_gather.3), channel_id=1, source_target_pairs={{0,6},{2,4},{4,2},{6,0},{8,14},{10,12},{12,10},{14,8},{16,22},{18,... | collective-permute-start | bytes 49160 | tf_op jit(solution)/shard_map/ppermute | solution.py:35
  88.4 22.4 %collective-permute-start.14 = (bf16[256,896]{1,0:T(8,128)(2,1)}, bf16[256,896]{1,0:T(8,128)(2,1)}, u32[]{:S(2)}, u32[]{:S(2)}) collective-permute-start(bf16[256,896]{1,0:T(8,128)(2,1)} %get-tuple-element.35), channel_id=1, source_target_pairs={{8,16},{10,18},{12,20},{14,22},{16,8},{18,10},{20,12},{22,14},{9,1... | collective-permute-start | bytes 1376264 | tf_op jit(solution)/shard_map/ppermute | solution.py:41
  91.9 18.9 %collective-permute-start.18 = (bf16[256,896]{1,0:T(8,128)(2,1)}, bf16[256,896]{1,0:T(8,128)(2,1)}, u32[]{:S(2)}, u32[]{:S(2)}) collective-permute-start(bf16[256,896]{1,0:T(8,128)(2,1)} %get-tuple-element.37), channel_id=1, source_target_pairs={{0,8},{2,10},{4,12},{6,14},{8,0},{10,2},{12,4},{14,6},{16,24},{18,... | collective-permute-start | bytes 1376264 | tf_op jit(solution)/shard_map/ppermute | solution.py:41
  110.9 16.1 %collective-permute-start.26 = (bf16[256,896]{1,0:T(8,128)(2,1)S(1)}, bf16[256,896]{1,0:T(8,128)(2,1)S(1)}, u32[]{:S(2)}, u32[]{:S(2)}) collective-permute-start(bf16[256,896]{1,0:T(8,128)(2,1)S(1)} %copy-done.34), channel_id=1, source_target_pairs={{8,16},{10,18},{12,20},{14,22},{16,8},{18,10},{20,12},{22,14},{9,1... | collective-permute-start | bytes 1376264 | tf_op jit(solution)/shard_map/ppermute | solution.py:41
  111.8 14.0 %collective-permute-start.25 = (bf16[256,896]{1,0:T(8,128)(2,1)S(1)}, bf16[256,896]{1,0:T(8,128)(2,1)S(1)}, u32[]{:S(2)}, u32[]{:S(2)}) collective-permute-start(bf16[256,896]{1,0:T(8,128)(2,1)S(1)} %copy-done.35), channel_id=1, source_target_pairs={{0,8},{2,10},{4,12},{6,14},{8,0},{10,2},{12,4},{14,6},{16,24},{18,... | collective-permute-start | bytes 1376264 | tf_op jit(solution)/shard_map/ppermute | solution.py:41
  115.6 21.5 %collective-permute-start.20 = (bf16[64,3072]{1,0:T(8,128)(2,1)S(1)}, bf16[64,3072]{1,0:T(8,128)(2,1)S(1)}, u32[]{:S(2)}, u32[]{:S(2)}) collective-permute-start(bf16[64,3072]{1,0:T(8,128)(2,1)S(1)} %get-tuple-element.64), channel_id=1, source_target_pairs={{0,2},{2,0},{4,6},{6,4},{8,10},{10,8},{12,14},{14,12},{16,18},{18,... | collective-permute-start | bytes 1179656 | tf_op jit(solution)/shard_map/ppermute | solution.py:35
  116.8 20.3 %collective-permute-start.22 = (bf16[64,3072]{1,0:T(8,128)(2,1)S(1)}, bf16[64,3072]{1,0:T(8,128)(2,1)S(1)}, u32[]{:S(2)}, u32[]{:S(2)}) collective-permute-start(bf16[64,3072]{1,0:T(8,128)(2,1)S(1)} %get-tuple-element.65), channel_id=1, source_target_pairs={{0,6},{2,4},{4,2},{6,0},{8,14},{10,12},{12,10},{14,8},{16,22},{18,... | collective-permute-start | bytes 1179656 | tf_op jit(solution)/shard_map/ppermute | solution.py:35
  117.7 19.5 %collective-permute-start.21 = (bf16[64,3072]{1,0:T(8,128)(2,1)S(1)}, bf16[64,3072]{1,0:T(8,128)(2,1)S(1)}, u32[]{:S(2)}, u32[]{:S(2)}) collective-permute-start(bf16[64,3072]{1,0:T(8,128)(2,1)S(1)} %get-tuple-element.66), channel_id=1, source_target_pairs={{0,4},{2,6},{4,0},{6,2},{8,12},{10,14},{12,8},{14,10},{16,20},{18,... | collective-permute-start | bytes 1179656 | tf_op jit(solution)/shard_map/ppermute | solution.py:35
  144.8 18.7 %collective-permute-start.30 = (bf16[64,3072]{1,0:T(8,128)(2,1)S(1)}, bf16[64,3072]{1,0:T(8,128)(2,1)S(1)}, u32[]{:S(2)}, u32[]{:S(2)}) collective-permute-start(bf16[64,3072]{1,0:T(8,128)(2,1)S(1)} %get-tuple-element.62), channel_id=1, source_target_pairs={{0,6},{2,4},{4,2},{6,0},{8,14},{10,12},{12,10},{14,8},{16,22},{18,... | collective-permute-start | bytes 1179656 | tf_op jit(solution)/shard_map/ppermute | solution.py:35
  145.8 19.0 %collective-permute-start.29 = (bf16[64,3072]{1,0:T(8,128)(2,1)S(1)}, bf16[64,3072]{1,0:T(8,128)(2,1)S(1)}, u32[]{:S(2)}, u32[]{:S(2)}) collective-permute-start(bf16[64,3072]{1,0:T(8,128)(2,1)S(1)} %get-tuple-element.63), channel_id=1, source_target_pairs={{0,4},{2,6},{4,0},{6,2},{8,12},{10,14},{12,8},{14,10},{16,20},{18,... | collective-permute-start | bytes 1179656 | tf_op jit(solution)/shard_map/ppermute | solution.py:35
  147.7 32.3 %collective-permute-start.31 = (bf16[64,1024]{1,0:T(8,128)(2,1)S(1)}, bf16[64,1024]{1,0:T(8,128)(2,1)S(1)}, u32[]{:S(2)}, u32[]{:S(2)}) collective-permute-start(bf16[64,1024]{1,0:T(8,128)(2,1)S(1)} %get-tuple-element.84), channel_id=1, source_target_pairs={{8,16},{10,18},{12,20},{14,22},{16,8},{18,10},{20,12},{22,14},{9,1... | collective-permute-start | bytes 393224 | tf_op jit(solution)/shard_map/ppermute | solution.py:41
  148.5 31.5 %collective-permute-start.24 = (bf16[64,1024]{1,0:T(8,128)(2,1)S(1)}, bf16[64,1024]{1,0:T(8,128)(2,1)S(1)}, u32[]{:S(2)}, u32[]{:S(2)}) collective-permute-start(bf16[64,1024]{1,0:T(8,128)(2,1)S(1)} %get-tuple-element.84), channel_id=1, source_target_pairs={{0,16},{2,18},{4,20},{6,22},{24,8},{26,10},{28,12},{30,14},{1,17},... | collective-permute-start | bytes 393224 | tf_op jit(solution)/shard_map/ppermute | solution.py:41
  155.6 23.4 %collective-permute-start.23 = (bf16[64,1024]{1,0:T(8,128)(2,1)S(1)}, bf16[64,1024]{1,0:T(8,128)(2,1)S(1)}, u32[]{:S(2)}, u32[]{:S(2)}) collective-permute-start(bf16[64,1024]{1,0:T(8,128)(2,1)S(1)} %get-tuple-element.85), channel_id=1, source_target_pairs={{0,8},{2,10},{4,12},{6,14},{8,0},{10,2},{12,4},{14,6},{16,24},{18,... | collective-permute-start | bytes 393224 | tf_op jit(solution)/shard_map/ppermute | solution.py:41
  179.9 13.5 %collective-permute-start.34 = (bf16[64,1024]{1,0:T(8,128)(2,1)S(1)}, bf16[64,1024]{1,0:T(8,128)(2,1)S(1)}, u32[]{:S(2)}, u32[]{:S(2)}) collective-permute-start(bf16[64,1024]{1,0:T(8,128)(2,1)S(1)} %get-tuple-element.48), channel_id=1, source_target_pairs={{8,16},{10,18},{12,20},{14,22},{16,8},{18,10},{20,12},{22,14},{9,1... | collective-permute-start | bytes 393224 | tf_op jit(solution)/shard_map/ppermute | solution.py:41
  (54 other events, 521.9 us)

commit v6 on v5

--- a/solution.py
+++ b/solution.py
@@ -164,15 +164,14 @@
             for r in range(PLANE):
                 need(b_ids(r))
                 column = at * width + pl.multiple_of((place ^ r) * piece, piece)
-                for p in range(0, PLANE, 2):
+                for p in range(PLANE):
                     x = nt(
-                        buffer_refs[a][2 * p * half:(2 * p + 4) * half, a0:a0 + cols],
+                        buffer_refs[a][2 * p * half:(2 * p + 2) * half, a0:a0 + cols],
                         buffer_refs[b][r * piece:(r + 1) * piece, b0:b0 + cols],
                     ).astype(bf16)
-                    for i in range(2):
-                        low, high = x[2 * i * half:][:half], x[(2 * i + 1) * half:][:half]
-                        keep_ref[p + i, :, pl.ds(column, piece)] = jnp.where(core == 0, low, high)
-                        give_ref[p + i, :, pl.ds(column, piece)] = jnp.where(core == 0, high, low)
+                    low, high = x[:half], x[half:]
+                    keep_ref[p, :, pl.ds(column, piece)] = jnp.where(core == 0, low, high)
+                    give_ref[p, :, pl.ds(column, piece)] = jnp.where(core == 0, high, low)
         need(range(len(copies)))
 
     out = jax.ShapeDtypeStruct((PLANE, half, len(jobs) * width), bf16)
@@ -211,12 +210,12 @@
     weight = after(weight, e0, m0)
     parts = [lay.cut(weight, r) for r in range(PLANE)]
     sides = after(jnp.concatenate(plane[:2], 0), e0, m0)
-    e1, m1 = end_swap(sides), mid_swap(sides)
-    e2, m2 = end_swap(plane[2]), mid_swap(plane[2])
+    e1, e2 = end_swap(sides), end_swap(plane[2])
+    m1 = mid_swap(jnp.concatenate([sides, plane[2]], 0))
     parts[1:3] = [across(after(parts[r], *plane), r) for r in (1, 2)]
     parts[3] = across(after(parts[3], *parts[1:3]), 3)
     joined = lambda x, c: jnp.concatenate([y[:, c] for y in x], 0)
-    near_e, near_m = [e0, e1, e2], [m0, m1, m2]
+    near_e, near_m = [e0, e1, e2], [m0, m1]
     e_high = joined(near_e, high)
     m_low = joined(near_m, low)
     far0 = mid_swap(joined(near_e, low))
@@ -235,14 +234,14 @@
     own = [after(cuts[0], far0), sides, plane[2]]
     sources = [*own, *near_e, early0, *near_m, *parts]
     starts = (0, tokens, 3 * tokens)
-    fills = [(i, 0, 0, row, 0, both) for i, row in enumerate(starts)] + weight_fills(10, 3)
+    fills = [(i, 0, 0, row, 0, both) for i, row in enumerate(starts)] + weight_fills(9, 3)
     fills += [(3 + i, 0, 1, row, 0, both) for i, row in enumerate(starts)]
     fills += [(6, 0, 2, 0, 0, half)]
-    fills += [(7 + i, half, 2, row, half, half) for i, row in enumerate(starts)]
+    fills += [(7, half, 2, 0, half, half), (8, half, 2, tokens, half, half)]
     jobs = [
         (0, 3, 0, 0, both, (0, 1, 2), lambda r: (3 + r,)),
         (1, 3, 0, 0, both, (7, 8, 9), none),
-        (2, 3, 0, 0, both, (10, 11, 12, 13), none),
+        (2, 3, 0, 0, both, (10, 11, 12), none),
     ]
     keep, give = products(lay, sources, [(block, both)] * 3 + [(width, both)], fills, jobs, width)
     give = after(give, far1[0], got[0])
@@ -253,14 +252,14 @@
     panel = panel + end_swap(after(panel.astype(bf16), first)).astype(f32)
 
     late0 = send(far0, jnp.concatenate(got, 0))
-    sources = [after(late0, first), *far1, *near_m, *parts, got_a, *got]
+    sources = [late0, *far1, after(m0, first, panel), m1, *parts, got_a, *got]
     fills = [(0, 0, 0, 0, 0, half)]
-    fills += [(1 + i, 0, 0, 2 * i * tokens, half, half) for i in range(2)] + weight_fills(6, 2)
-    fills += [(3 + i, half, 1, row, 0, half) for i, row in enumerate(starts)]
-    fills += [(10, 0, 3, 0, 0, half), (11, 0, 3, 2 * rows, 0, half), (12, 0, 3, 3 * rows, 0, half)]
+    fills += [(1 + i, 0, 0, 2 * i * tokens, half, half) for i in range(2)] + weight_fills(5, 2)
+    fills += [(3, half, 1, 0, 0, half), (4, half, 1, tokens, 0, half)]
+    fills += [(9, 0, 3, 0, 0, half), (10, 0, 3, 2 * rows, 0, half), (11, 0, 3, 3 * rows, 0, half)]
     jobs = [
         (0, 2, 0, 0, both, (0, 1, 2), lambda r: (3 + r,)),
-        (1, 3, 0, 0, half, (7, 8, 9), lambda r: ((10,), (), (11,), (12,))[r]),
+        (1, 3, 0, 0, half, (7, 8), lambda r: ((9,), (), (10,), (11,))[r]),
         (0, 3, half, 0, half, (), none),
     ]
     buffers = [(block, both), (block, half), (width, both), (width, half)]
@@ -270,11 +269,11 @@
         return sum(x.astype(f32) for x in (own, *others)).astype(bf16)
 
     first = plane_sum(first[0], first_x, first_y, across(first[3], 3))
-    give = after(give, first)
+    panel = (panel + lay.levels(panel.astype(bf16), 2).astype(f32)).astype(bf16)
+    give = after(give, first, panel)
     second = (keep.astype(f32) + swap(give).astype(f32)).astype(bf16)
     second = plane_sum(second[0], *[across(second[r], r) for r in range(1, PLANE)])
-    panel = (panel + lay.levels(after(panel.astype(bf16), second), 2).astype(f32)).astype(bf16)
-    summed_panel = panel
+    panel = after(panel, second)
     panel = jnp.stack([panel] + [across(panel, r) for r in range(1, PLANE)])
     panel = jnp.concatenate(
         [lax.dynamic_index_in_dim(panel, lay.place ^ p, 0, False) for p in range(PLANE)], 1
@@ -286,7 +285,7 @@
     z1 = end_swap(y1)
     z3 = mid_swap(early)
     z2 = lay.levels(early, 2, (0, 3))
-    late, early_other = after((late, early_other), z1, z2, z3, summed_panel)
+    late, early_other = after((late, early_other), z1, z2, z3)
     z2b = mid_swap(early_other)
     z_late = lay.levels(jnp.concatenate([late, late_other], 1), 2, (1, 2))
     z3b = lay.levels(late, 3, (0, 3))

time: 197 us -> 201 us (1.020)
  Pallas kernels: 18.6 us -> 29.2 us
  starting transfers between devices: 76.3 us -> 65.7 us
  other arithmetic: 10.1 us -> 13.4 us
  local copies, waits for them, and re-layouts: 17.9 us -> 15.3 us
  matrix products: 7.02 us -> 9.05 us
    ppermute x20 -> x19, waiting for transfers between devices: 43 us -> 26.9 us  [levels(): return lax.ppermute(x, 'dp', pairs)]
    ppermute x18, waiting for transfers between devices: 20 us -> 34.5 us  [across(): return lax.ppermute(x, 'dp', [(d, d ^ r) for d in range(self.replicas)])]
    ppermute x20 -> x19, starting transfers between devices: 53.3 us -> 41.1 us  [levels(): return lax.ppermute(x, 'dp', pairs)]
    pallas_call x2, Pallas kernels: 18.6 us -> 29.2 us  [products(): pl.pallas_call(kernel, out_shape=(out, out), in_specs=[pl.BlockSpec(memor...]
    unnamed x76 -> x56, local copies, waits for them, and re-layouts: 11.2 us -> 5.15 us
    ppermute x2, waiting for transfers between devices: 0.01 us -> 3.4 us  [line_of_four(): swap = lambda x: lax.ppermute(x, 'tensor', [(0, 1), (1, 0)])]
    dot_general x1, matrix products: 4.35 us -> 7.43 us  [updated(): update = jnp.dot(basis_rows.astype(bf16), panel, preferred_element_type=f32)]
    slice x6 -> x5, local copies, waits for them, and re-layouts: 1.28 us -> 3.54 us  [line_of_four(): joined = lambda x, c: jnp.concatenate([y[:, c] for y in x], 0)]
  transfers between devices with their start and end apart: 40 -> 39, of which waited for: 16 -> 14; matrix products, arithmetic and copies ran while one was open for 11% -> 14% of each run, Pallas kernels for 9% -> 15%
where the time goes in v6:
time: 201 us; the launch traced here: 200 us
  starting transfers between devices  65.7 us (33%)
  waiting for transfers between devices  64.8 us (32%)
  Pallas kernels  29.2 us (15%)
  local copies, waits for them, and re-layouts  15.3 us (8%)
  other arithmetic  13.4 us (7%)
  matrix products  9.05 us (5%)
    ppermute x19, starting transfers between devices, levels(): return lax.ppermute(x, 'dp', pairs)  41.1 us
    ppermute x18, waiting for transfers between devices, across(): return lax.ppermute(x, 'dp', [(d, d ^ r) for d in range(self.replicas)])  34.5 us
    pallas_call x2, Pallas kernels, products(): pl.pallas_call(kernel, out_shape=(out, out), in_specs=[pl.BlockSpec(memor...  29.2 us
    ppermute x19, waiting for transfers between devices, levels(): return lax.ppermute(x, 'dp', pairs)  26.9 us
    ppermute x18, starting transfers between devices, across(): return lax.ppermute(x, 'dp', [(d, d ^ r) for d in range(self.replicas)])  24.4 us
    dot_general x1, matrix products, updated(): update = jnp.dot(basis_rows.astype(bf16), panel, preferred_element_type=f32)  7.43 us
    select_n x4, other arithmetic, line_of_four(): send = lambda a, w: jnp.where(inner, a, w)  5.82 us
    unnamed x56, local copies, waits for them, and re-layouts  5.15 us
  transfers between devices with their start and end apart: 39, of which 14 were waited for; matrix products, arithmetic and copies ran while one was open for 14% of the time, Pallas kernels for 15%

profile of v6, /device:TPU:0, one launch (start us, length us, event | category | flops | bytes accessed | tf_op | source)
XLA Modules:
  0.0 200.4 jit_solution(16181192254239150236)
XLA Ops:
  2.3 3.0 %collective-permute-start.1 = (bf16[128,1792]{1,0:T(8,128)(2,1)S(1)}, bf16[128,1792]{1,0:T(8,128)(2,1)S(1)}, u32[]{:S(2)}, u32[]{:S(2)}) collective-permute-start(bf16[128,1792]{1,0:T(8,128)(2,1)S(1)} %get-tuple-element.60), channel_id=1, source_target_pairs={{0,2},{2,0},{4,6},{6,4},{8,10},{10,8},{12,14},{14,12},{16,18},{18,... | collective-permute-start | bytes 1376264 | tf_op jit(solution)/shard_map/ppermute | solution.py:35
  9.1 6.7 %collective-permute-done.1 = bf16[128,1792]{1,0:T(8,128)(2,1)S(1)} collective-permute-done((bf16[128,1792]{1,0:T(8,128)(2,1)S(1)}, bf16[128,1792]{1,0:T(8,128)(2,1)S(1)}, u32[]{:S(2)}, u32[]{:S(2)}) %collective-permute-start.1) | collective-permute-done | bytes 458784 | tf_op jit(solution)/shard_map/ppermute | solution.py:35
  19.8 4.2 %collective-permute-start.4 = (bf16[256,1792]{1,0:T(8,128)(2,1)S(1)}, bf16[256,1792]{1,0:T(8,128)(2,1)S(1)}, u32[]{:S(2)}, u32[]{:S(2)}) collective-permute-start(bf16[256,1792]{1,0:T(8,128)(2,1)S(1)} %pad_maximum_fusion.1.refs_1_), channel_id=1, source_target_pairs={{0,8},{2,10},{4,12},{6,14},{8,0},{10,2},{12,4},{14,6},{16,24},{18,... | collective-permute-start | bytes 2752520 | tf_op jit(solution)/shard_map/ppermute | solution.py:41
  24.0 5.3 %collective-permute-done.5.refs_2_ = bf16[128,1792]{1,0:T(8,128)(2,1)S(1)} collective-permute-done((bf16[128,1792]{1,0:T(8,128)(2,1)S(1)}, bf16[128,1792]{1,0:T(8,128)(2,1)S(1)}, u32[]{:S(2)}, u32[]{:S(2)}) %collective-permute-start.5) | collective-permute-done | bytes 458784 | tf_op jit(solution)/shard_map/ppermute | solution.py:35
  31.3 4.4 %collective-permute-start.6 = (bf16[128,1792]{1,0:T(8,128)(2,1)S(1)}, bf16[128,1792]{1,0:T(8,128)(2,1)S(1)}, u32[]{:S(2)}, u32[]{:S(2)}) collective-permute-start(bf16[128,1792]{1,0:T(8,128)(2,1)S(1)} %collective-permute-done.5.refs_2_), channel_id=1, source_target_pairs={{0,8},{2,10},{4,12},{6,14},{8,0},{10,2},{12,4},{14,6},{16,24},{18,... | collective-permute-start | bytes 1376264 | tf_op jit(solution)/shard_map/ppermute | solution.py:41
  40.6 12.0 %collective-permute-done.6.refs_5_ = bf16[128,1792]{1,0:T(8,128)(2,1)S(1)} collective-permute-done((bf16[128,1792]{1,0:T(8,128)(2,1)S(1)}, bf16[128,1792]{1,0:T(8,128)(2,1)S(1)}, u32[]{:S(2)}, u32[]{:S(2)}) %collective-permute-start.6) | collective-permute-done | bytes 458784 | tf_op jit(solution)/shard_map/ppermute | solution.py:41
  57.2 2.2 %collective-permute-start.12 = (bf16[256,1792]{1,0:T(8,128)(2,1)}, bf16[256,1792]{1,0:T(8,128)(2,1)}, u32[]{:S(2)}, u32[]{:S(2)}) collective-permute-start(bf16[256,1792]{1,0:T(8,128)(2,1)} %get-tuple-element.32), channel_id=1, source_target_pairs={{0,6},{2,4},{4,2},{6,0},{8,14},{10,12},{12,10},{14,8},{16,22},{18,... | collective-permute-start | bytes 2752520 | tf_op jit(solution)/shard_map/ppermute | solution.py:35
  62.9 4.8 %collective-permute-start.10 = (bf16[512,896]{1,0:T(8,128)(2,1)S(1)}, bf16[512,896]{1,0:T(8,128)(2,1)}, u32[]{:S(2)}, u32[]{:S(2)}) collective-permute-start(bf16[512,896]{1,0:T(8,128)(2,1)S(1)} %maximum_select_fusion), channel_id=1, source_target_pairs={{0,8},{2,10},{4,12},{6,14},{8,0},{10,2},{12,4},{14,6},{16,24},{18,... | collective-permute-start | bytes 2752520 | tf_op jit(solution)/shard_map/ppermute | solution.py:41
  69.4 1.8 all_gather.3
  74.8 4.5 %collective-permute-done.12.refs_12_.refs_8_ = bf16[256,1792]{1,0:T(8,128)(2,1)} collective-permute-done((bf16[256,1792]{1,0:T(8,128)(2,1)}, bf16[256,1792]{1,0:T(8,128)(2,1)}, u32[]{:S(2)}, u32[]{:S(2)}) %collective-permute-start.12) | collective-permute-done | bytes 917536 | tf_op jit(solution)/shard_map/ppermute | solution.py:35
  79.2 2.6 %slice_select_fusion = (bf16[256,896]{1,0:T(8,128)(2,1)}, bf16[256,896]{1,0:T(8,128)(2,1)}) fusion(bf16[256,1792]{1,0:T(8,128)(2,1)} %collective-permute-done.12.refs_12_.refs_8_, bf16[512,896]{1,0:T(8,128)(2,1)} %collective-permute-done.7, pred[]{:T(512)S(6)} %or.3, bf16[256,1792]{1,0:T(8,128)(2,1)} %collective-permute-done.11.refs_11_.refs_7_), kind=kLoop, calls=%fused_computation.33 | loop fusion | flops 458752 | bytes 2752513 | tf_op jit(solution)/shard_map/jit(_where)/select_n | solution.py:204
  83.6 8.2 %collective-permute-start.17 = (bf16[256,896]{1,0:T(8,128)(2,1)}, bf16[256,896]{1,0:T(8,128)(2,1)}, u32[]{:S(2)}, u32[]{:S(2)}) collective-permute-start(bf16[256,896]{1,0:T(8,128)(2,1)} %get-tuple-element.37), channel_id=1, source_target_pairs={{0,8},{2,10},{4,12},{6,14},{8,0},{10,2},{12,4},{14,6},{16,24},{18,... | collective-permute-start | bytes 1376264 | tf_op jit(solution)/shard_map/ppermute | solution.py:41
  92.0 1.8 broadcast_select_fusion.refs_6_
  97.2 17.2 %shard_map.68 = (bf16[4,64,3072]{2,1,0:T(8,128)(2,1)S(1)}, bf16[4,64,3072]{2,1,0:T(8,128)(2,1)S(1)}) custom-call(s32[2]{0:T(128)S(1)} %pad_add_fusion.scalar_ref, bf16[128,1792]{1,0:T(8,128)(2,1)S(1)} %copy-done.4, bf16[256,1792]{1,0:T(8,128)(2,1)S(1)} %copy-done.2, bf16[128,1792]{1,0:T(8,128)(2,1)S(1)} %copy-done.6, bf16[128,1792]{1,0:T(8,128)(2,1)S(1)} %copy-done.12, ...), custom_call_target="tpu_custom_call" | custom-call | flops 1000000 | bytes 100000 | tf_op jit(solution)/shard_map/pallas_call | solution.py:178
  116.3 11.5 %collective-permute-done.24.refs_11_ = bf16[256,896]{1,0:T(8,128)(2,1)S(1)} collective-permute-done((bf16[256,896]{1,0:T(8,128)(2,1)S(1)}, bf16[256,896]{1,0:T(8,128)(2,1)S(1)}, u32[]{:S(2)}, u32[]{:S(2)}) %collective-permute-start.24) | collective-permute-done | bytes 458784 | tf_op jit(solution)/shard_map/ppermute | solution.py:41
  134.2 3.0 %collective-permute-done.26 = bf16[64,1792]{1,0:T(8,128)(2,1)S(1)} collective-permute-done((bf16[64,1792]{1,0:T(8,128)(2,1)S(1)}, bf16[64,1792]{1,0:T(8,128)(2,1)S(1)}, u32[]{:S(2)}, u32[]{:S(2)}) %collective-permute-start.26) | collective-permute-done | bytes 229408 | tf_op jit(solution)/shard_map/ppermute | solution.py:41
  138.0 12.0 %shard_map.69 = (bf16[4,64,3072]{2,1,0:T(8,128)(2,1)S(1)}, bf16[4,64,3072]{2,1,0:T(8,128)(2,1)S(1)}) custom-call(s32[2]{0:T(128)S(1)} %pad_add_fusion.scalar_ref, bf16[512,896]{1,0:T(8,128)(2,1)S(1)} %maximum_select_fusion.1.refs_0_, bf16[256,896]{1,0:T(8,128)(2,1)} %collective-permute-done.13.refs_1_, bf16[256,896]{1,0:T(8,128)(2,1)S(1)} %collective-permute-done.25.refs_2_, ...), custom_call_target="tpu_custom_call" | custom-call | flops 1000000 | bytes 100000 | tf_op jit(solution)/shard_map/pallas_call | solution.py:178
  151.0 3.4 %collective-permute-done.28 = bf16[4,64,3072]{2,1,0:T(8,128)(2,1)S(1)} collective-permute-done((bf16[4,64,3072]{2,1,0:T(8,128)(2,1)S(1)}, bf16[4,64,3072]{2,1,0:T(8,128)(2,1)S(1)}, u32[]{:S(2)}, u32[]{:S(2)}) %collective-permute-start.28) | collective-permute-done | bytes 1572896 | tf_op jit(solution)/shard_map/ppermute | solution.py:203
  159.6 3.5 %collective-permute-start.23 = (bf16[64,1024]{1,0:T(8,128)(2,1)S(1)}, bf16[64,1024]{1,0:T(8,128)(2,1)S(1)}, u32[]{:S(2)}, u32[]{:S(2)}) collective-permute-start(bf16[64,1024]{1,0:T(8,128)(2,1)S(1)} %get-tuple-element.86), channel_id=1, source_target_pairs={{0,16},{2,18},{4,20},{6,22},{24,8},{26,10},{28,12},{30,14},{1,17},... | collective-permute-start | bytes 393224 | tf_op jit(solution)/shard_map/ppermute | solution.py:41
  163.8 5.5 %collective-permute-done.31 = bf16[64,3072]{1,0:T(8,128)(2,1)} collective-permute-done((bf16[64,3072]{1,0:T(8,128)(2,1)}, bf16[64,3072]{1,0:T(8,128)(2,1)}, u32[]{:S(2)}, u32[]{:S(2)}) %collective-permute-start.31) | collective-permute-done | bytes 393248 | tf_op jit(solution)/shard_map/ppermute | solution.py:35
  170.6 6.3 %collective-permute-done.30 = bf16[64,3072]{1,0:T(8,128)(2,1)} collective-permute-done((bf16[64,3072]{1,0:T(8,128)(2,1)}, bf16[64,3072]{1,0:T(8,128)(2,1)}, u32[]{:S(2)}, u32[]{:S(2)}) %collective-permute-start.30) | collective-permute-done | bytes 393248 | tf_op jit(solution)/shard_map/ppermute | solution.py:35
  182.0 3.7 %collective-permute-start.35 = (bf16[64,1024]{1,0:T(8,128)(2,1)S(1)}, bf16[64,1024]{1,0:T(8,128)(2,1)S(1)}, u32[]{:S(2)}, u32[]{:S(2)}) collective-permute-start(bf16[64,1024]{1,0:T(8,128)(2,1)S(1)} %get-tuple-element.48), channel_id=1, source_target_pairs={{0,24},{2,26},{4,28},{6,30},{24,0},{26,2},{28,4},{30,6},{1,25},{3,... | collective-permute-start | bytes 393224 | tf_op jit(solution)/shard_map/ppermute | solution.py:41
  188.4 3.3 %collective-permute-done.37 = bf16[64,1792]{1,0:T(8,128)(2,1)S(1)} collective-permute-done((bf16[64,1792]{1,0:T(8,128)(2,1)S(1)}, bf16[64,1792]{1,0:T(8,128)(2,1)S(1)}, u32[]{:S(2)}, u32[]{:S(2)}) %collective-permute-start.37) | collective-permute-done | bytes 229408 | tf_op jit(solution)/shard_map/ppermute | solution.py:35
  191.9 7.4 %fusion = f32[256,7168]{1,0:T(8,128)} fusion(f32[256,7168]{1,0:T(8,128)} %param.9, bf16[64,1792]{1,0:T(8,128)(2,1)S(1)} %get-tuple-element.70, bf16[64,1792]{1,0:T(8,128)(2,1)S(1)} %get-tuple-element.71, bf16[64,1792]{1,0:T(8,128)(2,1)S(1)} %get-tuple-element.72, bf16[64,1792]{1,0:T(8,128)(2,1)S(1)} %get-tuple-element.69, f32[4096,64]{0,1:T(8,128)S(1)} %copy-done, ...), kind=kOutput, calls=%fused_computation.1 | convolution fusion | flops 244056064 | bytes 15630340 | tf_op jit(solution)/shard_map/dot_general | solution.py:101
  (153 shorter events, 60.9 us)
Async XLA Ops:
  2.3 13.5 %collective-permute-start.1 = (bf16[128,1792]{1,0:T(8,128)(2,1)S(1)}, bf16[128,1792]{1,0:T(8,128)(2,1)S(1)}, u32[]{:S(2)}, u32[]{:S(2)}) collective-permute-start(bf16[128,1792]{1,0:T(8,128)(2,1)S(1)} %get-tuple-element.60), channel_id=1, source_target_pairs={{0,2},{2,0},{4,6},{6,4},{8,10},{10,8},{12,14},{14,12},{16,18},{18,... | collective-permute-start | bytes 1376264 | tf_op jit(solution)/shard_map/ppermute | solution.py:35
  19.8 33.7 %collective-permute-start.4 = (bf16[256,1792]{1,0:T(8,128)(2,1)S(1)}, bf16[256,1792]{1,0:T(8,128)(2,1)S(1)}, u32[]{:S(2)}, u32[]{:S(2)}) collective-permute-start(bf16[256,1792]{1,0:T(8,128)(2,1)S(1)} %pad_maximum_fusion.1.refs_1_), channel_id=1, source_target_pairs={{0,8},{2,10},{4,12},{6,14},{8,0},{10,2},{12,4},{14,6},{16,24},{18,... | collective-permute-start | bytes 2752520 | tf_op jit(solution)/shard_map/ppermute | solution.py:41
  30.5 32.1 %collective-permute-start.8 = (bf16[384,1792]{1,0:T(8,128)(2,1)}, bf16[384,1792]{1,0:T(8,128)(2,1)S(1)}, u32[]{:S(2)}, u32[]{:S(2)}) collective-permute-start(bf16[384,1792]{1,0:T(8,128)(2,1)} %pad_maximum_fusion), channel_id=1, source_target_pairs={{8,16},{10,18},{12,20},{14,22},{16,8},{18,10},{20,12},{22,14},{9,1... | collective-permute-start | bytes 4128776 | tf_op jit(solution)/shard_map/ppermute | solution.py:41
  31.3 21.4 %collective-permute-start.6 = (bf16[128,1792]{1,0:T(8,128)(2,1)S(1)}, bf16[128,1792]{1,0:T(8,128)(2,1)S(1)}, u32[]{:S(2)}, u32[]{:S(2)}) collective-permute-start(bf16[128,1792]{1,0:T(8,128)(2,1)S(1)} %collective-permute-done.5.refs_2_), channel_id=1, source_target_pairs={{0,8},{2,10},{4,12},{6,14},{8,0},{10,2},{12,4},{14,6},{16,24},{18,... | collective-permute-start | bytes 1376264 | tf_op jit(solution)/shard_map/ppermute | solution.py:41
  37.1 20.0 %collective-permute-start.9 = (bf16[256,1792]{1,0:T(8,128)(2,1)S(1)}, bf16[256,1792]{1,0:T(8,128)(2,1)}, u32[]{:S(2)}, u32[]{:S(2)}) collective-permute-start(bf16[256,1792]{1,0:T(8,128)(2,1)S(1)} %get-tuple-element.30), channel_id=1, source_target_pairs={{0,2},{2,0},{4,6},{6,4},{8,10},{10,8},{12,14},{14,12},{16,18},{18,... | collective-permute-start | bytes 2752520 | tf_op jit(solution)/shard_map/ppermute | solution.py:35
  37.6 19.6 %collective-permute-start.11 = (bf16[256,1792]{1,0:T(8,128)(2,1)S(1)}, bf16[256,1792]{1,0:T(8,128)(2,1)}, u32[]{:S(2)}, u32[]{:S(2)}) collective-permute-start(bf16[256,1792]{1,0:T(8,128)(2,1)S(1)} %get-tuple-element.31), channel_id=1, source_target_pairs={{0,4},{2,6},{4,0},{6,2},{8,12},{10,14},{12,8},{14,10},{16,20},{18,... | collective-permute-start | bytes 2752520 | tf_op jit(solution)/shard_map/ppermute | solution.py:35
  55.6 17.9 %collective-permute-start.7 = (bf16[512,896]{1,0:T(8,128)(2,1)}, bf16[512,896]{1,0:T(8,128)(2,1)}, u32[]{:S(2)}, u32[]{:S(2)}) collective-permute-start(bf16[512,896]{1,0:T(8,128)(2,1)} %pad_maximum_fusion.2), channel_id=1, source_target_pairs={{8,16},{10,18},{12,20},{14,22},{16,8},{18,10},{20,12},{22,14},{9,1... | collective-permute-start | bytes 2752520 | tf_op jit(solution)/shard_map/ppermute | solution.py:41
  57.2 22.0 %collective-permute-start.12 = (bf16[256,1792]{1,0:T(8,128)(2,1)}, bf16[256,1792]{1,0:T(8,128)(2,1)}, u32[]{:S(2)}, u32[]{:S(2)}) collective-permute-start(bf16[256,1792]{1,0:T(8,128)(2,1)} %get-tuple-element.32), channel_id=1, source_target_pairs={{0,6},{2,4},{4,2},{6,0},{8,14},{10,12},{12,10},{14,8},{16,22},{18,... | collective-permute-start | bytes 2752520 | tf_op jit(solution)/shard_map/ppermute | solution.py:35
  62.9 19.2 %collective-permute-start.10 = (bf16[512,896]{1,0:T(8,128)(2,1)S(1)}, bf16[512,896]{1,0:T(8,128)(2,1)}, u32[]{:S(2)}, u32[]{:S(2)}) collective-permute-start(bf16[512,896]{1,0:T(8,128)(2,1)S(1)} %maximum_select_fusion), channel_id=1, source_target_pairs={{0,8},{2,10},{4,12},{6,14},{8,0},{10,2},{12,4},{14,6},{16,24},{18,... | collective-permute-start | bytes 2752520 | tf_op jit(solution)/shard_map/ppermute | solution.py:41
  82.2 32.3 %collective-permute-start.13 = (bf16[256,896]{1,0:T(8,128)(2,1)}, bf16[256,896]{1,0:T(8,128)(2,1)}, u32[]{:S(2)}, u32[]{:S(2)}) collective-permute-start(bf16[256,896]{1,0:T(8,128)(2,1)} %get-tuple-element.35), channel_id=1, source_target_pairs={{8,16},{10,18},{12,20},{14,22},{16,8},{18,10},{20,12},{22,14},{9,1... | collective-permute-start | bytes 1376264 | tf_op jit(solution)/shard_map/ppermute | solution.py:41
  83.6 30.8 %collective-permute-start.17 = (bf16[256,896]{1,0:T(8,128)(2,1)}, bf16[256,896]{1,0:T(8,128)(2,1)}, u32[]{:S(2)}, u32[]{:S(2)}) collective-permute-start(bf16[256,896]{1,0:T(8,128)(2,1)} %get-tuple-element.37), channel_id=1, source_target_pairs={{0,8},{2,10},{4,12},{6,14},{8,0},{10,2},{12,4},{14,6},{16,24},{18,... | collective-permute-start | bytes 1376264 | tf_op jit(solution)/shard_map/ppermute | solution.py:41
  114.5 14.8 %collective-permute-start.18 = (bf16[4,64,3072]{2,1,0:T(8,128)(2,1)S(1)}, bf16[4,64,3072]{2,1,0:T(8,128)(2,1)S(1)}, u32[]{:S(2)}, u32[]{:S(2)}) collective-permute-start(bf16[4,64,3072]{2,1,0:T(8,128)(2,1)S(1)} %get-tuple-element.38), channel_id=1, source_target_pairs={{0,1},{1,0},{2,3},{3,2},{4,5},{5,4},{6,7},{7,6},{8,9},{9,8},{10,11... | collective-permute-start | bytes 4718600 | tf_op jit(solution)/shard_map/ppermute | solution.py:203
  114.9 23.1 %collective-permute-start.25 = (bf16[256,896]{1,0:T(8,128)(2,1)S(1)}, bf16[256,896]{1,0:T(8,128)(2,1)S(1)}, u32[]{:S(2)}, u32[]{:S(2)}) collective-permute-start(bf16[256,896]{1,0:T(8,128)(2,1)S(1)} %copy-done.26), channel_id=1, source_target_pairs={{8,16},{10,18},{12,20},{14,22},{16,8},{18,10},{20,12},{22,14},{9,1... | collective-permute-start | bytes 1376264 | tf_op jit(solution)/shard_map/ppermute | solution.py:41
  130.6 19.4 %collective-permute-start.21 = (bf16[64,3072]{1,0:T(8,128)(2,1)S(1)}, bf16[64,3072]{1,0:T(8,128)(2,1)S(1)}, u32[]{:S(2)}, u32[]{:S(2)}) collective-permute-start(bf16[64,3072]{1,0:T(8,128)(2,1)S(1)} %get-tuple-element.67), channel_id=1, source_target_pairs={{0,6},{2,4},{4,2},{6,0},{8,14},{10,12},{12,10},{14,8},{16,22},{18,... | collective-permute-start | bytes 1179656 | tf_op jit(solution)/shard_map/ppermute | solution.py:35
  131.9 18.8 %collective-permute-start.20 = (bf16[64,3072]{1,0:T(8,128)(2,1)S(1)}, bf16[64,3072]{1,0:T(8,128)(2,1)S(1)}, u32[]{:S(2)}, u32[]{:S(2)}) collective-permute-start(bf16[64,3072]{1,0:T(8,128)(2,1)S(1)} %get-tuple-element.68), channel_id=1, source_target_pairs={{0,4},{2,6},{4,0},{6,2},{8,12},{10,14},{12,8},{14,10},{16,20},{18,... | collective-permute-start | bytes 1179656 | tf_op jit(solution)/shard_map/ppermute | solution.py:35
  133.4 17.3 %collective-permute-start.19 = (bf16[64,3072]{1,0:T(8,128)(2,1)S(1)}, bf16[64,3072]{1,0:T(8,128)(2,1)S(1)}, u32[]{:S(2)}, u32[]{:S(2)}) collective-permute-start(bf16[64,3072]{1,0:T(8,128)(2,1)S(1)} %get-tuple-element.66), channel_id=1, source_target_pairs={{0,2},{2,0},{4,6},{6,4},{8,10},{10,8},{12,14},{14,12},{16,18},{18,... | collective-permute-start | bytes 1179656 | tf_op jit(solution)/shard_map/ppermute | solution.py:35
  137.3 13.6 %collective-permute-start.27 = (bf16[64,1792]{1,0:T(8,128)(2,1)S(1)}, bf16[64,1792]{1,0:T(8,128)(2,1)S(1)}, u32[]{:S(2)}, u32[]{:S(2)}) collective-permute-start(bf16[64,1792]{1,0:T(8,128)(2,1)S(1)} %get-tuple-element.53), channel_id=1, source_target_pairs={{0,16},{2,18},{4,20},{6,22},{8,24},{10,26},{12,28},{14,30},{16,0},... | collective-permute-start | bytes 688136 | tf_op jit(solution)/shard_map/ppermute | solution.py:41
  156.1 13.2 %collective-permute-start.31 = (bf16[64,3072]{1,0:T(8,128)(2,1)}, bf16[64,3072]{1,0:T(8,128)(2,1)}, u32[]{:S(2)}, u32[]{:S(2)}) collective-permute-start(bf16[64,3072]{1,0:T(8,128)(2,1)} %get-tuple-element.64), channel_id=1, source_target_pairs={{0,6},{2,4},{4,2},{6,0},{8,14},{10,12},{12,10},{14,8},{16,22},{18,... | collective-permute-start | bytes 1179656 | tf_op jit(solution)/shard_map/ppermute | solution.py:35
  157.4 19.5 %collective-permute-start.30 = (bf16[64,3072]{1,0:T(8,128)(2,1)}, bf16[64,3072]{1,0:T(8,128)(2,1)}, u32[]{:S(2)}, u32[]{:S(2)}) collective-permute-start(bf16[64,3072]{1,0:T(8,128)(2,1)} %get-tuple-element.65), channel_id=1, source_target_pairs={{0,4},{2,6},{4,0},{6,2},{8,12},{10,14},{12,8},{14,10},{16,20},{18,... | collective-permute-start | bytes 1179656 | tf_op jit(solution)/shard_map/ppermute | solution.py:35
  158.4 18.5 %collective-permute-start.29 = (bf16[64,3072]{1,0:T(8,128)(2,1)}, bf16[64,3072]{1,0:T(8,128)(2,1)}, u32[]{:S(2)}, u32[]{:S(2)}) collective-permute-start(bf16[64,3072]{1,0:T(8,128)(2,1)} %get-tuple-element.63), channel_id=1, source_target_pairs={{0,2},{2,0},{4,6},{6,4},{8,10},{10,8},{12,14},{14,12},{16,18},{18,... | collective-permute-start | bytes 1179656 | tf_op jit(solution)/shard_map/ppermute | solution.py:35
  159.6 22.4 %collective-permute-start.23 = (bf16[64,1024]{1,0:T(8,128)(2,1)S(1)}, bf16[64,1024]{1,0:T(8,128)(2,1)S(1)}, u32[]{:S(2)}, u32[]{:S(2)}) collective-permute-start(bf16[64,1024]{1,0:T(8,128)(2,1)S(1)} %get-tuple-element.86), channel_id=1, source_target_pairs={{0,16},{2,18},{4,20},{6,22},{24,8},{26,10},{28,12},{30,14},{1,17},... | collective-permute-start | bytes 393224 | tf_op jit(solution)/shard_map/ppermute | solution.py:41
  163.1 18.9 %collective-permute-start.32 = (bf16[64,1024]{1,0:T(8,128)(2,1)S(1)}, bf16[64,1024]{1,0:T(8,128)(2,1)S(1)}, u32[]{:S(2)}, u32[]{:S(2)}) collective-permute-start(bf16[64,1024]{1,0:T(8,128)(2,1)S(1)} %get-tuple-element.86), channel_id=1, source_target_pairs={{8,16},{10,18},{12,20},{14,22},{16,8},{18,10},{20,12},{22,14},{9,1... | collective-permute-start | bytes 393224 | tf_op jit(solution)/shard_map/ppermute | solution.py:41
  182.0 17.4 %collective-permute-start.35 = (bf16[64,1024]{1,0:T(8,128)(2,1)S(1)}, bf16[64,1024]{1,0:T(8,128)(2,1)S(1)}, u32[]{:S(2)}, u32[]{:S(2)}) collective-permute-start(bf16[64,1024]{1,0:T(8,128)(2,1)S(1)} %get-tuple-element.48), channel_id=1, source_target_pairs={{0,24},{2,26},{4,28},{6,30},{24,0},{26,2},{28,4},{30,6},{1,25},{3,... | collective-permute-start | bytes 393224 | tf_op jit(solution)/shard_map/ppermute | solution.py:41
  185.7 13.6 %collective-permute-start.34 = (bf16[64,2048]{1,0:T(8,128)(2,1)S(1)}, bf16[64,2048]{1,0:T(8,128)(2,1)S(1)}, u32[]{:S(2)}, u32[]{:S(2)}) collective-permute-start(bf16[64,2048]{1,0:T(8,128)(2,1)S(1)} %pad_maximum_fusion.8), channel_id=1, source_target_pairs={{8,24},{10,26},{12,28},{14,30},{16,0},{18,2},{20,4},{22,6},{9,25},... | collective-permute-start | bytes 786440 | tf_op jit(solution)/shard_map/ppermute | solution.py:41
  (43 other events, 408.0 us)

commit v7 on v5

--- a/solution.py
+++ b/solution.py
@@ -212,7 +212,8 @@
     parts = [lay.cut(weight, r) for r in range(PLANE)]
     sides = after(jnp.concatenate(plane[:2], 0), e0, m0)
     e1, m1 = end_swap(sides), mid_swap(sides)
-    e2, m2 = end_swap(plane[2]), mid_swap(plane[2])
+    m2 = mid_swap(plane[2])
+    e2 = after(end_swap(plane[2]), m2)
     parts[1:3] = [across(after(parts[r], *plane), r) for r in (1, 2)]
     parts[3] = across(after(parts[3], *parts[1:3]), 3)
     joined = lambda x, c: jnp.concatenate([y[:, c] for y in x], 0)
@@ -274,7 +275,6 @@
     second = (keep.astype(f32) + swap(give).astype(f32)).astype(bf16)
     second = plane_sum(second[0], *[across(second[r], r) for r in range(1, PLANE)])
     panel = (panel + lay.levels(after(panel.astype(bf16), second), 2).astype(f32)).astype(bf16)
-    summed_panel = panel
     panel = jnp.stack([panel] + [across(panel, r) for r in range(1, PLANE)])
     panel = jnp.concatenate(
         [lax.dynamic_index_in_dim(panel, lay.place ^ p, 0, False) for p in range(PLANE)], 1
@@ -286,7 +286,7 @@
     z1 = end_swap(y1)
     z3 = mid_swap(early)
     z2 = lay.levels(early, 2, (0, 3))
-    late, early_other = after((late, early_other), z1, z2, z3, summed_panel)
+    late, early_other = after((late, early_other), z1, z2, z3)
     z2b = mid_swap(early_other)
     z_late = lay.levels(jnp.concatenate([late, late_other], 1), 2, (1, 2))
     z3b = lay.levels(late, 3, (0, 3))

time: 197 us -> 199 us (1.010)
  waiting for transfers between devices: 63 us -> 76.6 us
  starting transfers between devices: 76.3 us -> 65.7 us
    ppermute x20, starting transfers between devices: 53.3 us -> 41.5 us  [levels(): return lax.ppermute(x, 'dp', pairs)]
    ppermute x18, waiting for transfers between devices: 20 us -> 28.5 us  [across(): return lax.ppermute(x, 'dp', [(d, d ^ r) for d in range(self.replicas)])]
    ppermute x20, waiting for transfers between devices: 43 us -> 48 us  [levels(): return lax.ppermute(x, 'dp', pairs)]
  transfers between devices with their start and end apart: 40 -> 40, of which waited for: 16 -> 16; matrix products, arithmetic and copies ran while one was open for 11% -> 9% of each run, Pallas kernels for 9% -> 9%
where the time goes in v7:
time: 199 us
  waiting for transfers between devices  76.6 us (38%)
  starting transfers between devices  65.7 us (33%)
  Pallas kernels  18.7 us (9%)
  local copies, waits for them, and re-layouts  17.3 us (9%)
  other arithmetic  9.98 us (5%)
  matrix products  7.01 us (4%)
    ppermute x20, waiting for transfers between devices, levels(): return lax.ppermute(x, 'dp', pairs)  48 us
    ppermute x20, starting transfers between devices, levels(): return lax.ppermute(x, 'dp', pairs)  41.5 us
    ppermute x18, waiting for transfers between devices, across(): return lax.ppermute(x, 'dp', [(d, d ^ r) for d in range(self.replicas)])  28.5 us
    ppermute x18, starting transfers between devices, across(): return lax.ppermute(x, 'dp', [(d, d ^ r) for d in range(self.replicas)])  24.1 us
    pallas_call x2, Pallas kernels, products(): pl.pallas_call(kernel, out_shape=(out, out), in_specs=[pl.BlockSpec(memor...  18.7 us
    unnamed x76, local copies, waits for them, and re-layouts  10.6 us
    select_n x4, other arithmetic, line_of_four(): send = lambda a, w: jnp.where(inner, a, w)  4.45 us
    dot_general x1, matrix products, updated(): update = jnp.dot(basis_rows.astype(bf16), panel, preferred_element_type=f32)  4.34 us
  transfers between devices with their start and end apart: 40, of which 16 were waited for; matrix products, arithmetic and copies ran while one was open for 9% of the time, Pallas kernels for 9%

profile of v7, /device:TPU:0, one launch (start us, length us, event | category | flops | bytes accessed | tf_op | source)
XLA Modules:
  0.0 198.6 jit_solution(6246432080127976663)
XLA Ops:
  2.3 3.0 %collective-permute-start.2 = (bf16[128,1792]{1,0:T(8,128)(2,1)S(1)}, bf16[128,1792]{1,0:T(8,128)(2,1)S(1)}, u32[]{:S(2)}, u32[]{:S(2)}) collective-permute-start(bf16[128,1792]{1,0:T(8,128)(2,1)S(1)} %get-tuple-element.59), channel_id=1, source_target_pairs={{0,4},{2,6},{4,0},{6,2},{8,12},{10,14},{12,8},{14,10},{16,20},{18,... | collective-permute-start | bytes 1376264 | tf_op jit(solution)/shard_map/ppermute | solution.py:35
  6.9 9.0 %collective-permute-done.2 = bf16[128,1792]{1,0:T(8,128)(2,1)S(1)} collective-permute-done((bf16[128,1792]{1,0:T(8,128)(2,1)S(1)}, bf16[128,1792]{1,0:T(8,128)(2,1)S(1)}, u32[]{:S(2)}, u32[]{:S(2)}) %collective-permute-start.2) | collective-permute-done | bytes 458784 | tf_op jit(solution)/shard_map/ppermute | solution.py:35
  19.5 4.4 %collective-permute-start = (bf16[128,1792]{1,0:T(8,128)(2,1)S(1)}, bf16[128,1792]{1,0:T(8,128)(2,1)}, u32[]{:S(2)}, u32[]{:S(2)}) collective-permute-start(bf16[128,1792]{1,0:T(8,128)(2,1)S(1)} %get-tuple-element.49.refs_0_), channel_id=1, source_target_pairs={{0,8},{2,10},{4,12},{6,14},{8,0},{10,2},{12,4},{14,6},{16,24},{18,... | collective-permute-start | bytes 1376264 | tf_op jit(solution)/shard_map/ppermute | solution.py:41
  23.9 5.5 %collective-permute-done.5.refs_2_ = bf16[128,1792]{1,0:T(8,128)(2,1)} collective-permute-done((bf16[128,1792]{1,0:T(8,128)(2,1)S(1)}, bf16[128,1792]{1,0:T(8,128)(2,1)}, u32[]{:S(2)}, u32[]{:S(2)}) %collective-permute-start.5) | collective-permute-done | bytes 458784 | tf_op jit(solution)/shard_map/ppermute | solution.py:35
  31.1 1.9 collective-permute-done.refs_3_
  33.8 4.2 %collective-permute-start.4 = (bf16[256,1792]{1,0:T(8,128)(2,1)S(1)}, bf16[256,1792]{1,0:T(8,128)(2,1)S(1)}, u32[]{:S(2)}, u32[]{:S(2)}) collective-permute-start(bf16[256,1792]{1,0:T(8,128)(2,1)S(1)} %pad_maximum_fusion.refs_1_), channel_id=1, source_target_pairs={{0,8},{2,10},{4,12},{6,14},{8,0},{10,2},{12,4},{14,6},{16,24},{18,... | collective-permute-start | bytes 2752520 | tf_op jit(solution)/shard_map/ppermute | solution.py:41
  38.1 2.3 %constant_dynamic-slice_fusion.1 = (bf16[256,1792]{1,0:T(8,128)(2,1)S(1)}, bf16[256,1792]{1,0:T(8,128)(2,1)S(1)}, bf16[256,1792]{1,0:T(8,128)(2,1)S(1)}, bf16[256,1792]{1,0:T(8,128)(2,1)S(1)}) fusion(bf16[256,7168]{1,0:T(8,128)(2,1)} %param.7, s32[]{:T(128)S(6)} %select_n.135, s32[]{:T(128)S(6)} %select_n.134, s32[]{:T(128)S(6)} %select_n.133, s32[]{:T(128)S(6)} %select_n.132), kind=kLoop, calls=%fused_computation.60 | loop fusion | bytes 7340048 | tf_op jit(solution)/shard_map/dynamic_slice | solution.py:45
  44.9 20.6 %collective-permute-done.6.refs_5_ = bf16[128,1792]{1,0:T(8,128)(2,1)S(1)} collective-permute-done((bf16[128,1792]{1,0:T(8,128)(2,1)}, bf16[128,1792]{1,0:T(8,128)(2,1)S(1)}, u32[]{:S(2)}, u32[]{:S(2)}) %collective-permute-start.6) | collective-permute-done | bytes 458784 | tf_op jit(solution)/shard_map/ppermute | solution.py:41
  68.7 4.6 %collective-permute-start.11 = (bf16[512,896]{1,0:T(8,128)(2,1)S(1)}, bf16[512,896]{1,0:T(8,128)(2,1)S(1)}, u32[]{:S(2)}, u32[]{:S(2)}) collective-permute-start(bf16[512,896]{1,0:T(8,128)(2,1)S(1)} %maximum_select_fusion), channel_id=1, source_target_pairs={{0,8},{2,10},{4,12},{6,14},{8,0},{10,2},{12,4},{14,6},{16,24},{18,... | collective-permute-start | bytes 2752520 | tf_op jit(solution)/shard_map/ppermute | solution.py:41
  82.0 7.7 %collective-permute-done.11.refs_10_ = bf16[512,896]{1,0:T(8,128)(2,1)S(1)} collective-permute-done((bf16[512,896]{1,0:T(8,128)(2,1)S(1)}, bf16[512,896]{1,0:T(8,128)(2,1)S(1)}, u32[]{:S(2)}, u32[]{:S(2)}) %collective-permute-start.11) | collective-permute-done | bytes 917536 | tf_op jit(solution)/shard_map/ppermute | solution.py:41
  94.1 1.9 collective-permute-start.18
  103.8 9.8 %shard_map.68 = (bf16[4,64,3072]{2,1,0:T(8,128)(2,1)S(1)}, bf16[4,64,3072]{2,1,0:T(8,128)(2,1)S(1)}) custom-call(s32[2]{0:T(128)S(1)} %pad_add_fusion.scalar_ref, bf16[128,1792]{1,0:T(8,128)(2,1)S(1)} %get-tuple-element.49.refs_0_, bf16[256,1792]{1,0:T(8,128)(2,1)S(1)} %copy-done.8, bf16[128,1792]{1,0:T(8,128)(2,1)} %collective-permute-done.5.refs_2_, ...), custom_call_target="tpu_custom_call" | custom-call | flops 1000000 | bytes 100000 | tf_op jit(solution)/shard_map/pallas_call | solution.py:179
  114.6 2.5 %collective-permute-start.25 = (bf16[256,896]{1,0:T(8,128)(2,1)S(1)}, bf16[256,896]{1,0:T(8,128)(2,1)S(1)}, u32[]{:S(2)}, u32[]{:S(2)}) collective-permute-start(bf16[256,896]{1,0:T(8,128)(2,1)S(1)} %copy-done.35), channel_id=1, source_target_pairs={{0,8},{2,10},{4,12},{6,14},{8,0},{10,2},{12,4},{14,6},{16,24},{18,... | collective-permute-start | bytes 1376264 | tf_op jit(solution)/shard_map/ppermute | solution.py:41
  121.4 6.6 %collective-permute-done.25.refs_12_ = bf16[256,896]{1,0:T(8,128)(2,1)S(1)} collective-permute-done((bf16[256,896]{1,0:T(8,128)(2,1)S(1)}, bf16[256,896]{1,0:T(8,128)(2,1)S(1)}, u32[]{:S(2)}, u32[]{:S(2)}) %collective-permute-start.25) | collective-permute-done | bytes 458784 | tf_op jit(solution)/shard_map/ppermute | solution.py:41
  129.3 8.9 %shard_map.69 = (bf16[4,64,3072]{2,1,0:T(8,128)(2,1)S(1)}, bf16[4,64,3072]{2,1,0:T(8,128)(2,1)}) custom-call(s32[2]{0:T(128)S(1)} %pad_add_fusion.scalar_ref, bf16[512,896]{1,0:T(8,128)(2,1)S(1)} %maximum_select_fusion.1.refs_0_, bf16[256,896]{1,0:T(8,128)(2,1)} %collective-permute-done.14.refs_1_, bf16[256,896]{1,0:T(8,128)(2,1)S(1)} %collective-permute-done.26.refs_2_, ...), custom_call_target="tpu_custom_call" | custom-call | flops 1000000 | bytes 100000 | tf_op jit(solution)/shard_map/pallas_call | solution.py:179
  143.6 2.0 %add_convert_fusion = bf16[4,64,3072]{2,1,0:T(8,128)(2,1)S(1)} fusion(bf16[4,64,3072]{2,1,0:T(8,128)(2,1)} %collective-permute-done.27, bf16[4,64,3072]{2,1,0:T(8,128)(2,1)S(1)} %copy-done.23), kind=kLoop, calls=%fused_computation.2 | loop fusion | flops 3145728 | bytes 4718592 | tf_op jit(solution)/shard_map/convert_element_type | solution.py:275
  150.5 6.4 %collective-permute-start.24 = (bf16[64,1024]{1,0:T(8,128)(2,1)S(1)}, bf16[64,1024]{1,0:T(8,128)(2,1)S(1)}, u32[]{:S(2)}, u32[]{:S(2)}) collective-permute-start(bf16[64,1024]{1,0:T(8,128)(2,1)S(1)} %get-tuple-element.86), channel_id=1, source_target_pairs={{0,16},{2,18},{4,20},{6,22},{24,8},{26,10},{28,12},{30,14},{1,17},... | collective-permute-start | bytes 393224 | tf_op jit(solution)/shard_map/ppermute | solution.py:41
  159.3 6.6 %collective-permute-done.30 = bf16[64,3072]{1,0:T(8,128)(2,1)S(1)} collective-permute-done((bf16[64,3072]{1,0:T(8,128)(2,1)S(1)}, bf16[64,3072]{1,0:T(8,128)(2,1)S(1)}, u32[]{:S(2)}, u32[]{:S(2)}) %collective-permute-start.30) | collective-permute-done | bytes 393248 | tf_op jit(solution)/shard_map/ppermute | solution.py:35
  169.8 4.3 %collective-permute-start.34 = (bf16[64,1024]{1,0:T(8,128)(2,1)S(1)}, bf16[64,1024]{1,0:T(8,128)(2,1)S(1)}, u32[]{:S(2)}, u32[]{:S(2)}) collective-permute-start(bf16[64,1024]{1,0:T(8,128)(2,1)S(1)} %get-tuple-element.48), channel_id=1, source_target_pairs={{0,24},{2,26},{4,28},{6,30},{24,0},{26,2},{28,4},{30,6},{1,25},{3,... | collective-permute-start | bytes 393224 | tf_op jit(solution)/shard_map/ppermute | solution.py:41
  175.6 7.0 %collective-permute-done.36 = bf16[64,1792]{1,0:T(8,128)(2,1)S(1)} collective-permute-done((bf16[64,1792]{1,0:T(8,128)(2,1)S(1)}, bf16[64,1792]{1,0:T(8,128)(2,1)S(1)}, u32[]{:S(2)}, u32[]{:S(2)}) %collective-permute-start.36) | collective-permute-done | bytes 229408 | tf_op jit(solution)/shard_map/ppermute | solution.py:41
  182.7 2.2 %collective-permute-start.39 = (bf16[64,1792]{1,0:T(8,128)(2,1)S(1)}, bf16[64,1792]{1,0:T(8,128)(2,1)S(1)}, u32[]{:S(2)}, u32[]{:S(2)}) collective-permute-start(bf16[64,1792]{1,0:T(8,128)(2,1)S(1)} %add_convert_fusion.2), channel_id=1, source_target_pairs={{0,6},{2,4},{4,2},{6,0},{8,14},{10,12},{12,10},{14,8},{16,22},{18,... | collective-permute-start | bytes 688136 | tf_op jit(solution)/shard_map/ppermute | solution.py:35
  186.3 3.7 %collective-permute-done.33 = bf16[64,2048]{1,0:T(8,128)(2,1)S(1)} collective-permute-done((bf16[64,2048]{1,0:T(8,128)(2,1)S(1)}, bf16[64,2048]{1,0:T(8,128)(2,1)S(1)}, u32[]{:S(2)}, u32[]{:S(2)}) %collective-permute-start.33) | collective-permute-done | bytes 262176 | tf_op jit(solution)/shard_map/ppermute | solution.py:41
  191.7 2.3 %collective-permute-done.38 = bf16[64,1792]{1,0:T(8,128)(2,1)S(1)} collective-permute-done((bf16[64,1792]{1,0:T(8,128)(2,1)S(1)}, bf16[64,1792]{1,0:T(8,128)(2,1)S(1)}, u32[]{:S(2)}, u32[]{:S(2)}) %collective-permute-start.38) | collective-permute-done | bytes 229408 | tf_op jit(solution)/shard_map/ppermute | solution.py:35
  194.2 4.3 %fusion = f32[256,7168]{1,0:T(8,128)} fusion(f32[256,7168]{1,0:T(8,128)S(1)} %bitcast.47, bf16[64,1792]{1,0:T(8,128)(2,1)S(1)} %get-tuple-element.70, bf16[64,1792]{1,0:T(8,128)(2,1)S(1)} %get-tuple-element.71, bf16[64,1792]{1,0:T(8,128)(2,1)S(1)} %get-tuple-element.72, bf16[64,1792]{1,0:T(8,128)(2,1)S(1)} %get-tuple-element.69, f32[4096,64]{0,1:T(8,128)S(1)} %copy-done, ...), kind=kOutput, calls=%fused_computation.1 | convolution fusion | flops 244056064 | bytes 15630340 | tf_op jit(solution)/shard_map/dot_general | solution.py:101
  (176 shorter events, 65.4 us)
Async XLA Ops:
  32.9 34.4 %collective-permute-start.9 = (bf16[256,1792]{1,0:T(8,128)(2,1)S(1)}, bf16[256,1792]{1,0:T(8,128)(2,1)S(1)}, u32[]{:S(2)}, u32[]{:S(2)}) collective-permute-start(bf16[256,1792]{1,0:T(8,128)(2,1)S(1)} %pad_maximum_fusion.refs_1_), channel_id=1, source_target_pairs={{8,16},{10,18},{12,20},{14,22},{16,8},{18,10},{20,12},{22,14},{9,1... | collective-permute-start | bytes 2752520 | tf_op jit(solution)/shard_map/ppermute | solution.py:41
  33.8 31.8 %collective-permute-start.4 = (bf16[256,1792]{1,0:T(8,128)(2,1)S(1)}, bf16[256,1792]{1,0:T(8,128)(2,1)S(1)}, u32[]{:S(2)}, u32[]{:S(2)}) collective-permute-start(bf16[256,1792]{1,0:T(8,128)(2,1)S(1)} %pad_maximum_fusion.refs_1_), channel_id=1, source_target_pairs={{0,8},{2,10},{4,12},{6,14},{8,0},{10,2},{12,4},{14,6},{16,24},{18,... | collective-permute-start | bytes 2752520 | tf_op jit(solution)/shard_map/ppermute | solution.py:41
  38.0 27.5 %collective-permute-start.6 = (bf16[128,1792]{1,0:T(8,128)(2,1)}, bf16[128,1792]{1,0:T(8,128)(2,1)S(1)}, u32[]{:S(2)}, u32[]{:S(2)}) collective-permute-start(bf16[128,1792]{1,0:T(8,128)(2,1)} %collective-permute-done.5.refs_2_), channel_id=1, source_target_pairs={{0,8},{2,10},{4,12},{6,14},{8,0},{10,2},{12,4},{14,6},{16,24},{18,... | collective-permute-start | bytes 1376264 | tf_op jit(solution)/shard_map/ppermute | solution.py:41
  40.4 27.1 %collective-permute-start.10 = (bf16[256,1792]{1,0:T(8,128)(2,1)S(1)}, bf16[256,1792]{1,0:T(8,128)(2,1)S(1)}, u32[]{:S(2)}, u32[]{:S(2)}) collective-permute-start(bf16[256,1792]{1,0:T(8,128)(2,1)S(1)} %get-tuple-element.32), channel_id=1, source_target_pairs={{0,2},{2,0},{4,6},{6,4},{8,10},{10,8},{12,14},{14,12},{16,18},{18,... | collective-permute-start | bytes 2752520 | tf_op jit(solution)/shard_map/ppermute | solution.py:35
  41.9 31.3 %collective-permute-start.12 = (bf16[256,1792]{1,0:T(8,128)(2,1)S(1)}, bf16[256,1792]{1,0:T(8,128)(2,1)S(1)}, u32[]{:S(2)}, u32[]{:S(2)}) collective-permute-start(bf16[256,1792]{1,0:T(8,128)(2,1)S(1)} %get-tuple-element.33), channel_id=1, source_target_pairs={{0,4},{2,6},{4,0},{6,2},{8,12},{10,14},{12,8},{14,10},{16,20},{18,... | collective-permute-start | bytes 2752520 | tf_op jit(solution)/shard_map/ppermute | solution.py:35
  66.6 14.0 %collective-permute-start.8 = (bf16[512,896]{1,0:T(8,128)(2,1)S(1)}, bf16[512,896]{1,0:T(8,128)(2,1)S(1)}, u32[]{:S(2)}, u32[]{:S(2)}) collective-permute-start(bf16[512,896]{1,0:T(8,128)(2,1)S(1)} %pad_maximum_fusion.1), channel_id=1, source_target_pairs={{8,16},{10,18},{12,20},{14,22},{16,8},{18,10},{20,12},{22,14},{9,1... | collective-permute-start | bytes 2752520 | tf_op jit(solution)/shard_map/ppermute | solution.py:41
  68.7 21.0 %collective-permute-start.11 = (bf16[512,896]{1,0:T(8,128)(2,1)S(1)}, bf16[512,896]{1,0:T(8,128)(2,1)S(1)}, u32[]{:S(2)}, u32[]{:S(2)}) collective-permute-start(bf16[512,896]{1,0:T(8,128)(2,1)S(1)} %maximum_select_fusion), channel_id=1, source_target_pairs={{0,8},{2,10},{4,12},{6,14},{8,0},{10,2},{12,4},{14,6},{16,24},{18,... | collective-permute-start | bytes 2752520 | tf_op jit(solution)/shard_map/ppermute | solution.py:41
  73.2 19.6 %collective-permute-start.13 = (bf16[256,1792]{1,0:T(8,128)(2,1)S(1)}, bf16[256,1792]{1,0:T(8,128)(2,1)S(1)}, u32[]{:S(2)}, u32[]{:S(2)}) collective-permute-start(bf16[256,1792]{1,0:T(8,128)(2,1)S(1)} %get-tuple-element.34), channel_id=1, source_target_pairs={{0,6},{2,4},{4,2},{6,0},{8,14},{10,12},{12,10},{14,8},{16,22},{18,... | collective-permute-start | bytes 2752520 | tf_op jit(solution)/shard_map/ppermute | solution.py:35
  77.5 16.6 %collective-permute-start.17 = (bf16[128,64]{1,0:T(8,128)(2,1)S(1)}, bf16[128,64]{1,0:T(8,128)(2,1)S(1)}, u32[]{:S(2)}, u32[]{:S(2)}) collective-permute-start(bf16[128,64]{1,0:T(8,128)(2,1)S(1)} %all_gather.3), channel_id=1, source_target_pairs={{0,6},{2,4},{4,2},{6,0},{8,14},{10,12},{12,10},{14,8},{16,22},{18,... | collective-permute-start | bytes 49160 | tf_op jit(solution)/shard_map/ppermute | solution.py:35
  78.7 15.4 %collective-permute-start.16 = (bf16[128,64]{1,0:T(8,128)(2,1)S(1)}, bf16[128,64]{1,0:T(8,128)(2,1)S(1)}, u32[]{:S(2)}, u32[]{:S(2)}) collective-permute-start(bf16[128,64]{1,0:T(8,128)(2,1)S(1)} %all_gather.3), channel_id=1, source_target_pairs={{0,4},{2,6},{4,0},{6,2},{8,12},{10,14},{12,8},{14,10},{16,20},{18,... | collective-permute-start | bytes 49160 | tf_op jit(solution)/shard_map/ppermute | solution.py:35
  90.6 22.9 %collective-permute-start.14 = (bf16[256,896]{1,0:T(8,128)(2,1)}, bf16[256,896]{1,0:T(8,128)(2,1)}, u32[]{:S(2)}, u32[]{:S(2)}) collective-permute-start(bf16[256,896]{1,0:T(8,128)(2,1)} %get-tuple-element.37), channel_id=1, source_target_pairs={{8,16},{10,18},{12,20},{14,22},{16,8},{18,10},{20,12},{22,14},{9,1... | collective-permute-start | bytes 1376264 | tf_op jit(solution)/shard_map/ppermute | solution.py:41
  94.1 19.5 %collective-permute-start.18 = (bf16[256,896]{1,0:T(8,128)(2,1)}, bf16[256,896]{1,0:T(8,128)(2,1)}, u32[]{:S(2)}, u32[]{:S(2)}) collective-permute-start(bf16[256,896]{1,0:T(8,128)(2,1)} %get-tuple-element.39), channel_id=1, source_target_pairs={{0,8},{2,10},{4,12},{6,14},{8,0},{10,2},{12,4},{14,6},{16,24},{18,... | collective-permute-start | bytes 1376264 | tf_op jit(solution)/shard_map/ppermute | solution.py:41
  113.7 15.6 %collective-permute-start.26 = (bf16[256,896]{1,0:T(8,128)(2,1)S(1)}, bf16[256,896]{1,0:T(8,128)(2,1)S(1)}, u32[]{:S(2)}, u32[]{:S(2)}) collective-permute-start(bf16[256,896]{1,0:T(8,128)(2,1)S(1)} %copy-done.34), channel_id=1, source_target_pairs={{8,16},{10,18},{12,20},{14,22},{16,8},{18,10},{20,12},{22,14},{9,1... | collective-permute-start | bytes 1376264 | tf_op jit(solution)/shard_map/ppermute | solution.py:41
  117.8 21.5 %collective-permute-start.20 = (bf16[64,3072]{1,0:T(8,128)(2,1)S(1)}, bf16[64,3072]{1,0:T(8,128)(2,1)S(1)}, u32[]{:S(2)}, u32[]{:S(2)}) collective-permute-start(bf16[64,3072]{1,0:T(8,128)(2,1)S(1)} %get-tuple-element.66), channel_id=1, source_target_pairs={{0,2},{2,0},{4,6},{6,4},{8,10},{10,8},{12,14},{14,12},{16,18},{18,... | collective-permute-start | bytes 1179656 | tf_op jit(solution)/shard_map/ppermute | solution.py:35
  119.5 19.8 %collective-permute-start.22 = (bf16[64,3072]{1,0:T(8,128)(2,1)S(1)}, bf16[64,3072]{1,0:T(8,128)(2,1)S(1)}, u32[]{:S(2)}, u32[]{:S(2)}) collective-permute-start(bf16[64,3072]{1,0:T(8,128)(2,1)S(1)} %get-tuple-element.67), channel_id=1, source_target_pairs={{0,6},{2,4},{4,2},{6,0},{8,14},{10,12},{12,10},{14,8},{16,22},{18,... | collective-permute-start | bytes 1179656 | tf_op jit(solution)/shard_map/ppermute | solution.py:35
  120.3 19.0 %collective-permute-start.21 = (bf16[64,3072]{1,0:T(8,128)(2,1)S(1)}, bf16[64,3072]{1,0:T(8,128)(2,1)S(1)}, u32[]{:S(2)}, u32[]{:S(2)}) collective-permute-start(bf16[64,3072]{1,0:T(8,128)(2,1)S(1)} %get-tuple-element.68), channel_id=1, source_target_pairs={{0,4},{2,6},{4,0},{6,2},{8,12},{10,14},{12,8},{14,10},{16,20},{18,... | collective-permute-start | bytes 1179656 | tf_op jit(solution)/shard_map/ppermute | solution.py:35
  147.3 18.5 %collective-permute-start.30 = (bf16[64,3072]{1,0:T(8,128)(2,1)S(1)}, bf16[64,3072]{1,0:T(8,128)(2,1)S(1)}, u32[]{:S(2)}, u32[]{:S(2)}) collective-permute-start(bf16[64,3072]{1,0:T(8,128)(2,1)S(1)} %get-tuple-element.64), channel_id=1, source_target_pairs={{0,6},{2,4},{4,2},{6,0},{8,14},{10,12},{12,10},{14,8},{16,22},{18,... | collective-permute-start | bytes 1179656 | tf_op jit(solution)/shard_map/ppermute | solution.py:35
  148.2 19.0 %collective-permute-start.29 = (bf16[64,3072]{1,0:T(8,128)(2,1)S(1)}, bf16[64,3072]{1,0:T(8,128)(2,1)S(1)}, u32[]{:S(2)}, u32[]{:S(2)}) collective-permute-start(bf16[64,3072]{1,0:T(8,128)(2,1)S(1)} %get-tuple-element.65), channel_id=1, source_target_pairs={{0,4},{2,6},{4,0},{6,2},{8,12},{10,14},{12,8},{14,10},{16,20},{18,... | collective-permute-start | bytes 1179656 | tf_op jit(solution)/shard_map/ppermute | solution.py:35
  149.9 19.2 %collective-permute-start.31 = (bf16[64,1024]{1,0:T(8,128)(2,1)S(1)}, bf16[64,1024]{1,0:T(8,128)(2,1)S(1)}, u32[]{:S(2)}, u32[]{:S(2)}) collective-permute-start(bf16[64,1024]{1,0:T(8,128)(2,1)S(1)} %get-tuple-element.86), channel_id=1, source_target_pairs={{8,16},{10,18},{12,20},{14,22},{16,8},{18,10},{20,12},{22,14},{9,1... | collective-permute-start | bytes 393224 | tf_op jit(solution)/shard_map/ppermute | solution.py:41
  150.5 18.6 %collective-permute-start.24 = (bf16[64,1024]{1,0:T(8,128)(2,1)S(1)}, bf16[64,1024]{1,0:T(8,128)(2,1)S(1)}, u32[]{:S(2)}, u32[]{:S(2)}) collective-permute-start(bf16[64,1024]{1,0:T(8,128)(2,1)S(1)} %get-tuple-element.86), channel_id=1, source_target_pairs={{0,16},{2,18},{4,20},{6,22},{24,8},{26,10},{28,12},{30,14},{1,17},... | collective-permute-start | bytes 393224 | tf_op jit(solution)/shard_map/ppermute | solution.py:41
  167.4 15.2 %collective-permute-start.36 = (bf16[64,1792]{1,0:T(8,128)(2,1)S(1)}, bf16[64,1792]{1,0:T(8,128)(2,1)S(1)}, u32[]{:S(2)}, u32[]{:S(2)}) collective-permute-start(bf16[64,1792]{1,0:T(8,128)(2,1)S(1)} %fusion.15), channel_id=1, source_target_pairs={{0,16},{2,18},{4,20},{6,22},{8,24},{10,26},{12,28},{14,30},{16,0},... | collective-permute-start | bytes 688136 | tf_op jit(solution)/shard_map/ppermute | solution.py:41
  169.1 16.7 %collective-permute-start.32 = (bf16[64,1024]{1,0:T(8,128)(2,1)S(1)}, bf16[64,1024]{1,0:T(8,128)(2,1)S(1)}, u32[]{:S(2)}, u32[]{:S(2)}) collective-permute-start(bf16[64,1024]{1,0:T(8,128)(2,1)S(1)} %get-tuple-element.47), channel_id=1, source_target_pairs={{8,16},{10,18},{12,20},{14,22},{16,8},{18,10},{20,12},{22,14},{9,1... | collective-permute-start | bytes 393224 | tf_op jit(solution)/shard_map/ppermute | solution.py:41
  169.8 16.5 %collective-permute-start.34 = (bf16[64,1024]{1,0:T(8,128)(2,1)S(1)}, bf16[64,1024]{1,0:T(8,128)(2,1)S(1)}, u32[]{:S(2)}, u32[]{:S(2)}) collective-permute-start(bf16[64,1024]{1,0:T(8,128)(2,1)S(1)} %get-tuple-element.48), channel_id=1, source_target_pairs={{0,24},{2,26},{4,28},{6,30},{24,0},{26,2},{28,4},{30,6},{1,25},{3,... | collective-permute-start | bytes 393224 | tf_op jit(solution)/shard_map/ppermute | solution.py:41
  174.1 15.9 %collective-permute-start.33 = (bf16[64,2048]{1,0:T(8,128)(2,1)S(1)}, bf16[64,2048]{1,0:T(8,128)(2,1)S(1)}, u32[]{:S(2)}, u32[]{:S(2)}) collective-permute-start(bf16[64,2048]{1,0:T(8,128)(2,1)S(1)} %pad_maximum_fusion.7), channel_id=1, source_target_pairs={{8,24},{10,26},{12,28},{14,30},{16,0},{18,2},{20,4},{22,6},{9,25},... | collective-permute-start | bytes 786440 | tf_op jit(solution)/shard_map/ppermute | solution.py:41
  (54 other events, 549.9 us)

commit v8 on v7

--- a/solution.py
+++ b/solution.py
@@ -212,12 +212,11 @@
     parts = [lay.cut(weight, r) for r in range(PLANE)]
     sides = after(jnp.concatenate(plane[:2], 0), e0, m0)
     e1, m1 = end_swap(sides), mid_swap(sides)
-    m2 = mid_swap(plane[2])
-    e2 = after(end_swap(plane[2]), m2)
+    e2, m2 = end_swap(plane[2]), mid_swap(plane[2])
     parts[1:3] = [across(after(parts[r], *plane), r) for r in (1, 2)]
     parts[3] = across(after(parts[3], *parts[1:3]), 3)
     joined = lambda x, c: jnp.concatenate([y[:, c] for y in x], 0)
-    near_e, near_m = [e0, e1, e2], [m0, m1, m2]
+    near_e, near_m = [e0, after(e1, m2), e2], [m0, m1, m2]
     e_high = joined(near_e, high)
     m_low = joined(near_m, low)
     far0 = mid_swap(joined(near_e, low))

time: 199 us -> 191 us (0.960)
  waiting for transfers between devices: 76.6 us -> 66.1 us
  starting transfers between devices: 65.7 us -> 69.8 us
  local copies, waits for them, and re-layouts: 17.3 us -> 14.5 us
    ppermute x20, waiting for transfers between devices: 48 us -> 35.3 us  [levels(): return lax.ppermute(x, 'dp', pairs)]
    ppermute x20, starting transfers between devices: 41.5 us -> 45.7 us  [levels(): return lax.ppermute(x, 'dp', pairs)]
    unnamed x76 -> x68, local copies, waits for them, and re-layouts: 10.6 us -> 6.63 us
  transfers between devices with their start and end apart: 40 -> 40, of which waited for: 16 -> 21; matrix products, arithmetic and copies ran while one was open for 9% -> 10% of each run, Pallas kernels for 9% -> 10%
where the time goes in v8:
time: 191 us; the launch traced here: 190 us
  starting transfers between devices  69.8 us (37%)
  waiting for transfers between devices  66.1 us (35%)
  Pallas kernels  18.5 us (10%)
  local copies, waits for them, and re-layouts  14.5 us (8%)
  other arithmetic  10.9 us (6%)
  matrix products  7.01 us (4%)
    ppermute x20, starting transfers between devices, levels(): return lax.ppermute(x, 'dp', pairs)  45.7 us
    ppermute x20, waiting for transfers between devices, levels(): return lax.ppermute(x, 'dp', pairs)  35.3 us
    ppermute x18, waiting for transfers between devices, across(): return lax.ppermute(x, 'dp', [(d, d ^ r) for d in range(self.replicas)])  29 us
    ppermute x18, starting transfers between devices, across(): return lax.ppermute(x, 'dp', [(d, d ^ r) for d in range(self.replicas)])  24 us
    pallas_call x2, Pallas kernels, products(): pl.pallas_call(kernel, out_shape=(out, out), in_specs=[pl.BlockSpec(memor...  18.5 us
    unnamed x68, local copies, waits for them, and re-layouts  6.63 us
    select_n x4, other arithmetic, line_of_four(): send = lambda a, w: jnp.where(inner, a, w)  4.45 us
    dot_general x1, matrix products, updated(): update = jnp.dot(basis_rows.astype(bf16), panel, preferred_element_type=f32)  4.35 us
  transfers between devices with their start and end apart: 40, of which 21 were waited for; matrix products, arithmetic and copies ran while one was open for 10% of the time, Pallas kernels for 10%

profile of v8, /device:TPU:0, one launch (start us, length us, event | category | flops | bytes accessed | tf_op | source)
XLA Modules:
  0.0 189.9 jit_solution(6949597177898774888)
XLA Ops:
  2.3 3.0 %collective-permute-start.2 = (bf16[128,1792]{1,0:T(8,128)(2,1)S(1)}, bf16[128,1792]{1,0:T(8,128)(2,1)S(1)}, u32[]{:S(2)}, u32[]{:S(2)}) collective-permute-start(bf16[128,1792]{1,0:T(8,128)(2,1)S(1)} %get-tuple-element.59), channel_id=1, source_target_pairs={{0,4},{2,6},{4,0},{6,2},{8,12},{10,14},{12,8},{14,10},{16,20},{18,... | collective-permute-start | bytes 1376264 | tf_op jit(solution)/shard_map/ppermute | solution.py:35
  7.5 4.4 %collective-permute-start = (bf16[128,1792]{1,0:T(8,128)(2,1)S(1)}, bf16[128,1792]{1,0:T(8,128)(2,1)S(1)}, u32[]{:S(2)}, u32[]{:S(2)}) collective-permute-start(bf16[128,1792]{1,0:T(8,128)(2,1)S(1)} %get-tuple-element.49.refs_0_), channel_id=1, source_target_pairs={{0,8},{2,10},{4,12},{6,14},{8,0},{10,2},{12,4},{14,6},{16,24},{18,... | collective-permute-start | bytes 1376264 | tf_op jit(solution)/shard_map/ppermute | solution.py:41
  12.0 3.9 %collective-permute-done.2 = bf16[128,1792]{1,0:T(8,128)(2,1)S(1)} collective-permute-done((bf16[128,1792]{1,0:T(8,128)(2,1)S(1)}, bf16[128,1792]{1,0:T(8,128)(2,1)S(1)}, u32[]{:S(2)}, u32[]{:S(2)}) %collective-permute-start.2) | collective-permute-done | bytes 458784 | tf_op jit(solution)/shard_map/ppermute | solution.py:35
  19.8 1.9 collective-permute-done.refs_3_
  23.4 6.0 %collective-permute-done.5.refs_2_ = bf16[128,1792]{1,0:T(8,128)(2,1)} collective-permute-done((bf16[128,1792]{1,0:T(8,128)(2,1)S(1)}, bf16[128,1792]{1,0:T(8,128)(2,1)}, u32[]{:S(2)}, u32[]{:S(2)}) %collective-permute-start.5) | collective-permute-done | bytes 458784 | tf_op jit(solution)/shard_map/ppermute | solution.py:35
  31.8 5.3 %collective-permute-start.7 = (bf16[128,1792]{1,0:T(8,128)(2,1)}, bf16[128,1792]{1,0:T(8,128)(2,1)S(1)}, u32[]{:S(2)}, u32[]{:S(2)}) collective-permute-start(bf16[128,1792]{1,0:T(8,128)(2,1)} %collective-permute-done.5.refs_2_), channel_id=1, source_target_pairs={{0,8},{2,10},{4,12},{6,14},{8,0},{10,2},{12,4},{14,6},{16,24},{18,... | collective-permute-start | bytes 1376264 | tf_op jit(solution)/shard_map/ppermute | solution.py:41
  37.1 2.3 %constant_dynamic-slice_fusion.1 = (bf16[256,1792]{1,0:T(8,128)(2,1)S(1)}, bf16[256,1792]{1,0:T(8,128)(2,1)S(1)}, bf16[256,1792]{1,0:T(8,128)(2,1)S(1)}, bf16[256,1792]{1,0:T(8,128)(2,1)S(1)}) fusion(bf16[256,7168]{1,0:T(8,128)(2,1)} %param.7, s32[]{:T(128)S(6)} %select_n.135, s32[]{:T(128)S(6)} %select_n.134, s32[]{:T(128)S(6)} %select_n.133, s32[]{:T(128)S(6)} %select_n.132), kind=kLoop, calls=%fused_computation.60 | loop fusion | bytes 7340048 | tf_op jit(solution)/shard_map/dynamic_slice | solution.py:45
  42.8 2.4 %collective-permute-done.4.refs_4_ = bf16[256,1792]{1,0:T(8,128)(2,1)} collective-permute-done((bf16[256,1792]{1,0:T(8,128)(2,1)}, bf16[256,1792]{1,0:T(8,128)(2,1)}, u32[]{:S(2)}, u32[]{:S(2)}) %collective-permute-start.4) | collective-permute-done | bytes 917536 | tf_op jit(solution)/shard_map/ppermute | solution.py:41
  45.3 7.0 %collective-permute-done.7.refs_5_ = bf16[128,1792]{1,0:T(8,128)(2,1)S(1)} collective-permute-done((bf16[128,1792]{1,0:T(8,128)(2,1)}, bf16[128,1792]{1,0:T(8,128)(2,1)S(1)}, u32[]{:S(2)}, u32[]{:S(2)}) %collective-permute-start.7) | collective-permute-done | bytes 458784 | tf_op jit(solution)/shard_map/ppermute | solution.py:41
  55.6 3.0 %collective-permute-done.10.refs_11_.refs_7_ = bf16[256,1792]{1,0:T(8,128)(2,1)S(1)} collective-permute-done((bf16[256,1792]{1,0:T(8,128)(2,1)S(1)}, bf16[256,1792]{1,0:T(8,128)(2,1)S(1)}, u32[]{:S(2)}, u32[]{:S(2)}) %collective-permute-start.10) | collective-permute-done | bytes 917536 | tf_op jit(solution)/shard_map/ppermute | solution.py:35
  59.8 7.8 %collective-permute-start.11 = (bf16[512,896]{1,0:T(8,128)(2,1)S(1)}, bf16[512,896]{1,0:T(8,128)(2,1)S(1)}, u32[]{:S(2)}, u32[]{:S(2)}) collective-permute-start(bf16[512,896]{1,0:T(8,128)(2,1)S(1)} %maximum_select_fusion), channel_id=1, source_target_pairs={{0,8},{2,10},{4,12},{6,14},{8,0},{10,2},{12,4},{14,6},{16,24},{18,... | collective-permute-start | bytes 2752520 | tf_op jit(solution)/shard_map/ppermute | solution.py:41
  76.2 5.4 %collective-permute-done.11.refs_10_ = bf16[512,896]{1,0:T(8,128)(2,1)S(1)} collective-permute-done((bf16[512,896]{1,0:T(8,128)(2,1)S(1)}, bf16[512,896]{1,0:T(8,128)(2,1)S(1)}, u32[]{:S(2)}, u32[]{:S(2)}) %collective-permute-start.11) | collective-permute-done | bytes 917536 | tf_op jit(solution)/shard_map/ppermute | solution.py:41
  86.0 3.8 %collective-permute-start.18 = (bf16[256,896]{1,0:T(8,128)(2,1)}, bf16[256,896]{1,0:T(8,128)(2,1)}, u32[]{:S(2)}, u32[]{:S(2)}) collective-permute-start(bf16[256,896]{1,0:T(8,128)(2,1)} %get-tuple-element.39), channel_id=1, source_target_pairs={{0,8},{2,10},{4,12},{6,14},{8,0},{10,2},{12,4},{14,6},{16,24},{18,... | collective-permute-start | bytes 1376264 | tf_op jit(solution)/shard_map/ppermute | solution.py:41
  95.2 9.6 %shard_map.68 = (bf16[4,64,3072]{2,1,0:T(8,128)(2,1)S(1)}, bf16[4,64,3072]{2,1,0:T(8,128)(2,1)S(1)}) custom-call(s32[2]{0:T(128)S(1)} %pad_add_fusion.scalar_ref, bf16[128,1792]{1,0:T(8,128)(2,1)S(1)} %get-tuple-element.49.refs_0_, bf16[256,1792]{1,0:T(8,128)(2,1)} %pad_maximum_fusion.refs_1_, bf16[128,1792]{1,0:T(8,128)(2,1)} %collective-permute-done.5.refs_2_, ...), custom_call_target="tpu_custom_call" | custom-call | flops 1000000 | bytes 100000 | tf_op jit(solution)/shard_map/pallas_call | solution.py:179
  112.6 6.2 %collective-permute-done.25.refs_12_ = bf16[256,896]{1,0:T(8,128)(2,1)S(1)} collective-permute-done((bf16[256,896]{1,0:T(8,128)(2,1)S(1)}, bf16[256,896]{1,0:T(8,128)(2,1)S(1)}, u32[]{:S(2)}, u32[]{:S(2)}) %collective-permute-start.25) | collective-permute-done | bytes 458784 | tf_op jit(solution)/shard_map/ppermute | solution.py:41
  120.1 8.9 %shard_map.69 = (bf16[4,64,3072]{2,1,0:T(8,128)(2,1)S(1)}, bf16[4,64,3072]{2,1,0:T(8,128)(2,1)}) custom-call(s32[2]{0:T(128)S(1)} %pad_add_fusion.scalar_ref, bf16[512,896]{1,0:T(8,128)(2,1)S(1)} %maximum_select_fusion.1.refs_0_, bf16[256,896]{1,0:T(8,128)(2,1)} %collective-permute-done.14.refs_1_, bf16[256,896]{1,0:T(8,128)(2,1)S(1)} %collective-permute-done.26.refs_2_, ...), custom_call_target="tpu_custom_call" | custom-call | flops 1000000 | bytes 100000 | tf_op jit(solution)/shard_map/pallas_call | solution.py:179
  134.3 2.0 %add_convert_fusion = bf16[4,64,3072]{2,1,0:T(8,128)(2,1)S(1)} fusion(bf16[4,64,3072]{2,1,0:T(8,128)(2,1)} %collective-permute-done.27, bf16[4,64,3072]{2,1,0:T(8,128)(2,1)S(1)} %copy-done.19), kind=kLoop, calls=%fused_computation.2 | loop fusion | flops 3145728 | bytes 4718592 | tf_op jit(solution)/shard_map/convert_element_type | solution.py:274
  141.4 5.5 %collective-permute-start.24 = (bf16[64,1024]{1,0:T(8,128)(2,1)S(1)}, bf16[64,1024]{1,0:T(8,128)(2,1)S(1)}, u32[]{:S(2)}, u32[]{:S(2)}) collective-permute-start(bf16[64,1024]{1,0:T(8,128)(2,1)S(1)} %get-tuple-element.86), channel_id=1, source_target_pairs={{0,16},{2,18},{4,20},{6,22},{24,8},{26,10},{28,12},{30,14},{1,17},... | collective-permute-start | bytes 393224 | tf_op jit(solution)/shard_map/ppermute | solution.py:41
  149.3 7.6 %collective-permute-done.30 = bf16[64,3072]{1,0:T(8,128)(2,1)S(1)} collective-permute-done((bf16[64,3072]{1,0:T(8,128)(2,1)S(1)}, bf16[64,3072]{1,0:T(8,128)(2,1)S(1)}, u32[]{:S(2)}, u32[]{:S(2)}) %collective-permute-start.30) | collective-permute-done | bytes 393248 | tf_op jit(solution)/shard_map/ppermute | solution.py:35
  160.8 3.2 %collective-permute-start.34 = (bf16[64,1024]{1,0:T(8,128)(2,1)S(1)}, bf16[64,1024]{1,0:T(8,128)(2,1)S(1)}, u32[]{:S(2)}, u32[]{:S(2)}) collective-permute-start(bf16[64,1024]{1,0:T(8,128)(2,1)S(1)} %get-tuple-element.48), channel_id=1, source_target_pairs={{0,24},{2,26},{4,28},{6,30},{24,0},{26,2},{28,4},{30,6},{1,25},{3,... | collective-permute-start | bytes 393224 | tf_op jit(solution)/shard_map/ppermute | solution.py:41
  165.6 7.6 %collective-permute-done.36 = bf16[64,1792]{1,0:T(8,128)(2,1)S(1)} collective-permute-done((bf16[64,1792]{1,0:T(8,128)(2,1)S(1)}, bf16[64,1792]{1,0:T(8,128)(2,1)S(1)}, u32[]{:S(2)}, u32[]{:S(2)}) %collective-permute-start.36) | collective-permute-done | bytes 229408 | tf_op jit(solution)/shard_map/ppermute | solution.py:41
  176.9 4.0 %collective-permute-done.33 = bf16[64,2048]{1,0:T(8,128)(2,1)S(1)} collective-permute-done((bf16[64,2048]{1,0:T(8,128)(2,1)S(1)}, bf16[64,2048]{1,0:T(8,128)(2,1)S(1)}, u32[]{:S(2)}, u32[]{:S(2)}) %collective-permute-start.33) | collective-permute-done | bytes 262176 | tf_op jit(solution)/shard_map/ppermute | solution.py:41
  182.8 2.5 %collective-permute-done.38 = bf16[64,1792]{1,0:T(8,128)(2,1)S(1)} collective-permute-done((bf16[64,1792]{1,0:T(8,128)(2,1)S(1)}, bf16[64,1792]{1,0:T(8,128)(2,1)S(1)}, u32[]{:S(2)}, u32[]{:S(2)}) %collective-permute-start.38) | collective-permute-done | bytes 229408 | tf_op jit(solution)/shard_map/ppermute | solution.py:35
  185.6 4.3 %fusion = f32[256,7168]{1,0:T(8,128)} fusion(f32[256,7168]{1,0:T(8,128)S(1)} %bitcast.47, bf16[64,1792]{1,0:T(8,128)(2,1)S(1)} %get-tuple-element.70, bf16[64,1792]{1,0:T(8,128)(2,1)S(1)} %get-tuple-element.71, bf16[64,1792]{1,0:T(8,128)(2,1)S(1)} %get-tuple-element.72, bf16[64,1792]{1,0:T(8,128)(2,1)S(1)} %get-tuple-element.69, f32[4096,64]{0,1:T(8,128)S(1)} %copy-done, ...), kind=kOutput, calls=%fused_computation.1 | convolution fusion | flops 244056064 | bytes 15630340 | tf_op jit(solution)/shard_map/dot_general | solution.py:101
  (168 shorter events, 70.8 us)
Async XLA Ops:
  7.5 14.1 %collective-permute-start = (bf16[128,1792]{1,0:T(8,128)(2,1)S(1)}, bf16[128,1792]{1,0:T(8,128)(2,1)S(1)}, u32[]{:S(2)}, u32[]{:S(2)}) collective-permute-start(bf16[128,1792]{1,0:T(8,128)(2,1)S(1)} %get-tuple-element.49.refs_0_), channel_id=1, source_target_pairs={{0,8},{2,10},{4,12},{6,14},{8,0},{10,2},{12,4},{14,6},{16,24},{18,... | collective-permute-start | bytes 1376264 | tf_op jit(solution)/shard_map/ppermute | solution.py:41
  21.7 23.6 %collective-permute-start.4 = (bf16[256,1792]{1,0:T(8,128)(2,1)}, bf16[256,1792]{1,0:T(8,128)(2,1)}, u32[]{:S(2)}, u32[]{:S(2)}) collective-permute-start(bf16[256,1792]{1,0:T(8,128)(2,1)} %pad_maximum_fusion.refs_1_), channel_id=1, source_target_pairs={{0,8},{2,10},{4,12},{6,14},{8,0},{10,2},{12,4},{14,6},{16,24},{18,... | collective-permute-start | bytes 2752520 | tf_op jit(solution)/shard_map/ppermute | solution.py:41
  30.9 24.6 %collective-permute-start.9 = (bf16[256,1792]{1,0:T(8,128)(2,1)}, bf16[256,1792]{1,0:T(8,128)(2,1)S(1)}, u32[]{:S(2)}, u32[]{:S(2)}) collective-permute-start(bf16[256,1792]{1,0:T(8,128)(2,1)} %pad_maximum_fusion.refs_1_), channel_id=1, source_target_pairs={{8,16},{10,18},{12,20},{14,22},{16,8},{18,10},{20,12},{22,14},{9,1... | collective-permute-start | bytes 2752520 | tf_op jit(solution)/shard_map/ppermute | solution.py:41
  31.8 20.5 %collective-permute-start.7 = (bf16[128,1792]{1,0:T(8,128)(2,1)}, bf16[128,1792]{1,0:T(8,128)(2,1)S(1)}, u32[]{:S(2)}, u32[]{:S(2)}) collective-permute-start(bf16[128,1792]{1,0:T(8,128)(2,1)} %collective-permute-done.5.refs_2_), channel_id=1, source_target_pairs={{0,8},{2,10},{4,12},{6,14},{8,0},{10,2},{12,4},{14,6},{16,24},{18,... | collective-permute-start | bytes 1376264 | tf_op jit(solution)/shard_map/ppermute | solution.py:41
  39.4 19.2 %collective-permute-start.10 = (bf16[256,1792]{1,0:T(8,128)(2,1)S(1)}, bf16[256,1792]{1,0:T(8,128)(2,1)S(1)}, u32[]{:S(2)}, u32[]{:S(2)}) collective-permute-start(bf16[256,1792]{1,0:T(8,128)(2,1)S(1)} %get-tuple-element.32), channel_id=1, source_target_pairs={{0,2},{2,0},{4,6},{6,4},{8,10},{10,8},{12,14},{14,12},{16,18},{18,... | collective-permute-start | bytes 2752520 | tf_op jit(solution)/shard_map/ppermute | solution.py:35
  40.9 26.7 %collective-permute-start.12 = (bf16[256,1792]{1,0:T(8,128)(2,1)S(1)}, bf16[256,1792]{1,0:T(8,128)(2,1)S(1)}, u32[]{:S(2)}, u32[]{:S(2)}) collective-permute-start(bf16[256,1792]{1,0:T(8,128)(2,1)S(1)} %get-tuple-element.33), channel_id=1, source_target_pairs={{0,4},{2,6},{4,0},{6,2},{8,12},{10,14},{12,8},{14,10},{16,20},{18,... | collective-permute-start | bytes 2752520 | tf_op jit(solution)/shard_map/ppermute | solution.py:35
  53.8 20.9 %collective-permute-start.8 = (bf16[512,896]{1,0:T(8,128)(2,1)S(1)}, bf16[512,896]{1,0:T(8,128)(2,1)S(1)}, u32[]{:S(2)}, u32[]{:S(2)}) collective-permute-start(bf16[512,896]{1,0:T(8,128)(2,1)S(1)} %pad_maximum_fusion.1), channel_id=1, source_target_pairs={{8,16},{10,18},{12,20},{14,22},{16,8},{18,10},{20,12},{22,14},{9,1... | collective-permute-start | bytes 2752520 | tf_op jit(solution)/shard_map/ppermute | solution.py:41
  59.8 21.8 %collective-permute-start.11 = (bf16[512,896]{1,0:T(8,128)(2,1)S(1)}, bf16[512,896]{1,0:T(8,128)(2,1)S(1)}, u32[]{:S(2)}, u32[]{:S(2)}) collective-permute-start(bf16[512,896]{1,0:T(8,128)(2,1)S(1)} %maximum_select_fusion), channel_id=1, source_target_pairs={{0,8},{2,10},{4,12},{6,14},{8,0},{10,2},{12,4},{14,6},{16,24},{18,... | collective-permute-start | bytes 2752520 | tf_op jit(solution)/shard_map/ppermute | solution.py:41
  67.6 17.2 %collective-permute-start.13 = (bf16[256,1792]{1,0:T(8,128)(2,1)S(1)}, bf16[256,1792]{1,0:T(8,128)(2,1)S(1)}, u32[]{:S(2)}, u32[]{:S(2)}) collective-permute-start(bf16[256,1792]{1,0:T(8,128)(2,1)S(1)} %get-tuple-element.34), channel_id=1, source_target_pairs={{0,6},{2,4},{4,2},{6,0},{8,14},{10,12},{12,10},{14,8},{16,22},{18,... | collective-permute-start | bytes 2752520 | tf_op jit(solution)/shard_map/ppermute | solution.py:35
  71.7 14.3 %collective-permute-start.17 = (bf16[128,64]{1,0:T(8,128)(2,1)S(1)}, bf16[128,64]{1,0:T(8,128)(2,1)S(1)}, u32[]{:S(2)}, u32[]{:S(2)}) collective-permute-start(bf16[128,64]{1,0:T(8,128)(2,1)S(1)} %all_gather.3), channel_id=1, source_target_pairs={{0,6},{2,4},{4,2},{6,0},{8,14},{10,12},{12,10},{14,8},{16,22},{18,... | collective-permute-start | bytes 49160 | tf_op jit(solution)/shard_map/ppermute | solution.py:35
  82.5 22.3 %collective-permute-start.14 = (bf16[256,896]{1,0:T(8,128)(2,1)}, bf16[256,896]{1,0:T(8,128)(2,1)}, u32[]{:S(2)}, u32[]{:S(2)}) collective-permute-start(bf16[256,896]{1,0:T(8,128)(2,1)} %get-tuple-element.37), channel_id=1, source_target_pairs={{8,16},{10,18},{12,20},{14,22},{16,8},{18,10},{20,12},{22,14},{9,1... | collective-permute-start | bytes 1376264 | tf_op jit(solution)/shard_map/ppermute | solution.py:41
  86.0 18.8 %collective-permute-start.18 = (bf16[256,896]{1,0:T(8,128)(2,1)}, bf16[256,896]{1,0:T(8,128)(2,1)}, u32[]{:S(2)}, u32[]{:S(2)}) collective-permute-start(bf16[256,896]{1,0:T(8,128)(2,1)} %get-tuple-element.39), channel_id=1, source_target_pairs={{0,8},{2,10},{4,12},{6,14},{8,0},{10,2},{12,4},{14,6},{16,24},{18,... | collective-permute-start | bytes 1376264 | tf_op jit(solution)/shard_map/ppermute | solution.py:41
  104.9 15.1 %collective-permute-start.26 = (bf16[256,896]{1,0:T(8,128)(2,1)S(1)}, bf16[256,896]{1,0:T(8,128)(2,1)S(1)}, u32[]{:S(2)}, u32[]{:S(2)}) collective-permute-start(bf16[256,896]{1,0:T(8,128)(2,1)S(1)} %copy-done.30), channel_id=1, source_target_pairs={{8,16},{10,18},{12,20},{14,22},{16,8},{18,10},{20,12},{22,14},{9,1... | collective-permute-start | bytes 1376264 | tf_op jit(solution)/shard_map/ppermute | solution.py:41
  109.0 21.1 %collective-permute-start.20 = (bf16[64,3072]{1,0:T(8,128)(2,1)S(1)}, bf16[64,3072]{1,0:T(8,128)(2,1)S(1)}, u32[]{:S(2)}, u32[]{:S(2)}) collective-permute-start(bf16[64,3072]{1,0:T(8,128)(2,1)S(1)} %get-tuple-element.66), channel_id=1, source_target_pairs={{0,2},{2,0},{4,6},{6,4},{8,10},{10,8},{12,14},{14,12},{16,18},{18,... | collective-permute-start | bytes 1179656 | tf_op jit(solution)/shard_map/ppermute | solution.py:35
  109.8 20.3 %collective-permute-start.22 = (bf16[64,3072]{1,0:T(8,128)(2,1)S(1)}, bf16[64,3072]{1,0:T(8,128)(2,1)S(1)}, u32[]{:S(2)}, u32[]{:S(2)}) collective-permute-start(bf16[64,3072]{1,0:T(8,128)(2,1)S(1)} %get-tuple-element.67), channel_id=1, source_target_pairs={{0,6},{2,4},{4,2},{6,0},{8,14},{10,12},{12,10},{14,8},{16,22},{18,... | collective-permute-start | bytes 1179656 | tf_op jit(solution)/shard_map/ppermute | solution.py:35
  111.2 19.0 %collective-permute-start.21 = (bf16[64,3072]{1,0:T(8,128)(2,1)S(1)}, bf16[64,3072]{1,0:T(8,128)(2,1)S(1)}, u32[]{:S(2)}, u32[]{:S(2)}) collective-permute-start(bf16[64,3072]{1,0:T(8,128)(2,1)S(1)} %get-tuple-element.68), channel_id=1, source_target_pairs={{0,4},{2,6},{4,0},{6,2},{8,12},{10,14},{12,8},{14,10},{16,20},{18,... | collective-permute-start | bytes 1179656 | tf_op jit(solution)/shard_map/ppermute | solution.py:35
  137.5 19.4 %collective-permute-start.30 = (bf16[64,3072]{1,0:T(8,128)(2,1)S(1)}, bf16[64,3072]{1,0:T(8,128)(2,1)S(1)}, u32[]{:S(2)}, u32[]{:S(2)}) collective-permute-start(bf16[64,3072]{1,0:T(8,128)(2,1)S(1)} %get-tuple-element.64), channel_id=1, source_target_pairs={{0,6},{2,4},{4,2},{6,0},{8,14},{10,12},{12,10},{14,8},{16,22},{18,... | collective-permute-start | bytes 1179656 | tf_op jit(solution)/shard_map/ppermute | solution.py:35
  139.2 19.0 %collective-permute-start.29 = (bf16[64,3072]{1,0:T(8,128)(2,1)S(1)}, bf16[64,3072]{1,0:T(8,128)(2,1)S(1)}, u32[]{:S(2)}, u32[]{:S(2)}) collective-permute-start(bf16[64,3072]{1,0:T(8,128)(2,1)S(1)} %get-tuple-element.65), channel_id=1, source_target_pairs={{0,4},{2,6},{4,0},{6,2},{8,12},{10,14},{12,8},{14,10},{16,20},{18,... | collective-permute-start | bytes 1179656 | tf_op jit(solution)/shard_map/ppermute | solution.py:35
  140.7 19.4 %collective-permute-start.31 = (bf16[64,1024]{1,0:T(8,128)(2,1)S(1)}, bf16[64,1024]{1,0:T(8,128)(2,1)S(1)}, u32[]{:S(2)}, u32[]{:S(2)}) collective-permute-start(bf16[64,1024]{1,0:T(8,128)(2,1)S(1)} %get-tuple-element.86), channel_id=1, source_target_pairs={{8,16},{10,18},{12,20},{14,22},{16,8},{18,10},{20,12},{22,14},{9,1... | collective-permute-start | bytes 393224 | tf_op jit(solution)/shard_map/ppermute | solution.py:41
  141.4 18.7 %collective-permute-start.24 = (bf16[64,1024]{1,0:T(8,128)(2,1)S(1)}, bf16[64,1024]{1,0:T(8,128)(2,1)S(1)}, u32[]{:S(2)}, u32[]{:S(2)}) collective-permute-start(bf16[64,1024]{1,0:T(8,128)(2,1)S(1)} %get-tuple-element.86), channel_id=1, source_target_pairs={{0,16},{2,18},{4,20},{6,22},{24,8},{26,10},{28,12},{30,14},{1,17},... | collective-permute-start | bytes 393224 | tf_op jit(solution)/shard_map/ppermute | solution.py:41
  158.5 14.8 %collective-permute-start.36 = (bf16[64,1792]{1,0:T(8,128)(2,1)S(1)}, bf16[64,1792]{1,0:T(8,128)(2,1)S(1)}, u32[]{:S(2)}, u32[]{:S(2)}) collective-permute-start(bf16[64,1792]{1,0:T(8,128)(2,1)S(1)} %fusion.15), channel_id=1, source_target_pairs={{0,16},{2,18},{4,20},{6,22},{8,24},{10,26},{12,28},{14,30},{16,0},... | collective-permute-start | bytes 688136 | tf_op jit(solution)/shard_map/ppermute | solution.py:41
  160.1 15.5 %collective-permute-start.32 = (bf16[64,1024]{1,0:T(8,128)(2,1)S(1)}, bf16[64,1024]{1,0:T(8,128)(2,1)S(1)}, u32[]{:S(2)}, u32[]{:S(2)}) collective-permute-start(bf16[64,1024]{1,0:T(8,128)(2,1)S(1)} %get-tuple-element.47), channel_id=1, source_target_pairs={{8,16},{10,18},{12,20},{14,22},{16,8},{18,10},{20,12},{22,14},{9,1... | collective-permute-start | bytes 393224 | tf_op jit(solution)/shard_map/ppermute | solution.py:41
  160.8 16.1 %collective-permute-start.34 = (bf16[64,1024]{1,0:T(8,128)(2,1)S(1)}, bf16[64,1024]{1,0:T(8,128)(2,1)S(1)}, u32[]{:S(2)}, u32[]{:S(2)}) collective-permute-start(bf16[64,1024]{1,0:T(8,128)(2,1)S(1)} %get-tuple-element.48), channel_id=1, source_target_pairs={{0,24},{2,26},{4,28},{6,30},{24,0},{26,2},{28,4},{30,6},{1,25},{3,... | collective-permute-start | bytes 393224 | tf_op jit(solution)/shard_map/ppermute | solution.py:41
  164.1 16.9 %collective-permute-start.33 = (bf16[64,2048]{1,0:T(8,128)(2,1)S(1)}, bf16[64,2048]{1,0:T(8,128)(2,1)S(1)}, u32[]{:S(2)}, u32[]{:S(2)}) collective-permute-start(bf16[64,2048]{1,0:T(8,128)(2,1)S(1)} %pad_maximum_fusion.7), channel_id=1, source_target_pairs={{8,24},{10,26},{12,28},{14,30},{16,0},{18,2},{20,4},{22,6},{9,25},... | collective-permute-start | bytes 786440 | tf_op jit(solution)/shard_map/ppermute | solution.py:41
  (50 other events, 500.3 us)

commit v9 on v8

--- a/solution.py
+++ b/solution.py
@@ -213,21 +213,24 @@
     sides = after(jnp.concatenate(plane[:2], 0), e0, m0)
     e1, m1 = end_swap(sides), mid_swap(sides)
     e2, m2 = end_swap(plane[2]), mid_swap(plane[2])
-    parts[1:3] = [across(after(parts[r], *plane), r) for r in (1, 2)]
+    proj = projected(lay, after(inputs, plane[0]), proj_basis)
+    parts[1:3] = [across(after(parts[r], *plane, *proj), r) for r in (1, 2)]
     parts[3] = across(after(parts[3], *parts[1:3]), 3)
     joined = lambda x, c: jnp.concatenate([y[:, c] for y in x], 0)
     near_e, near_m = [e0, after(e1, m2), e2], [m0, m1, m2]
     e_high = joined(near_e, high)
     m_low = joined(near_m, low)
-    far0 = mid_swap(joined(near_e, low))
+    panel = sum(tn(q, a) for q, a in zip(proj, [cuts[0], *plane]))
+    far0 = mid_swap(after(joined(near_e, low), panel))
+    panel = panel + end_swap(panel.astype(bf16)).astype(f32)
     got_a = send(m_low, jnp.concatenate([w[:, high] for w in parts[:2]], 0))
-    got_a = end_swap(got_a)
-    proj = projected(lay, after(inputs, e1, m1), proj_basis)
+    got_a = end_swap(after(got_a, panel))
+    panel = (panel + lay.levels(panel.astype(bf16), 2).astype(f32)).astype(bf16)
     far1, got = [], []
     for i, w in enumerate(parts[2:]):
         rows_i = slice(i * 2 * tokens, (i + 1) * 2 * tokens)
         far1.append(mid_swap(after(e_high[rows_i], far0, got_a)))
-        got.append(end_swap(after(send(far0[rows_i], w[:, high]), got_a, parts[3], *proj)))
+        got.append(end_swap(after(send(far0[rows_i], w[:, high]), got_a, parts[3], panel)))
 
     weight_fills = lambda first, b: [(first + r, 0, b, r * rows, 0, both) for r in range(PLANE)]
     none = lambda r: ()
@@ -249,9 +252,6 @@
     first = (keep.astype(f32) + swap(give).astype(f32)).astype(bf16)
     first_x, first_y = across(first[1], 1), across(first[2], 2)
 
-    panel = sum(tn(q, a) for q, a in zip(proj, [after(cuts[0], give), *plane]))
-    panel = panel + end_swap(after(panel.astype(bf16), first)).astype(f32)
-
     late0 = send(far0, jnp.concatenate(got, 0))
     sources = [after(late0, first), *far1, *near_m, *parts, got_a, *got]
     fills = [(0, 0, 0, 0, 0, half)]
@@ -273,7 +273,7 @@
     give = after(give, first)
     second = (keep.astype(f32) + swap(give).astype(f32)).astype(bf16)
     second = plane_sum(second[0], *[across(second[r], r) for r in range(1, PLANE)])
-    panel = (panel + lay.levels(after(panel.astype(bf16), second), 2).astype(f32)).astype(bf16)
+    panel = after(panel, second)
     panel = jnp.stack([panel] + [across(panel, r) for r in range(1, PLANE)])
     panel = jnp.concatenate(
         [lax.dynamic_index_in_dim(panel, lay.place ^ p, 0, False) for p in range(PLANE)], 1

time: 191 us -> 208 us (1.089)
  waiting for transfers between devices: 66.1 us -> 78.5 us
  local copies, waits for them, and re-layouts: 14.5 us -> 18.5 us
  matrix products: 7.01 us -> 10.2 us
    ppermute x20, waiting for transfers between devices: 35.3 us -> 52.9 us  [levels(): return lax.ppermute(x, 'dp', pairs)]
    ppermute x18, waiting for transfers between devices: 29 us -> 22.1 us  [across(): return lax.ppermute(x, 'dp', [(d, d ^ r) for d in range(self.replicas)])]
    unnamed x68 -> x72, local copies, waits for them, and re-layouts: 6.63 us -> 9.83 us
    dot_general x1, matrix products: 4.35 us -> 7.43 us  [updated(): update = jnp.dot(basis_rows.astype(bf16), panel, preferred_element_type=f32)]
  transfers between devices with their start and end apart: 40 -> 40, of which waited for: 21 -> 14; matrix products, arithmetic and copies ran while one was open for 10% -> 12% of each run, Pallas kernels for 10% -> 9%
where the time goes in v9:
time: 208 us; the launch traced here: 207 us
  waiting for transfers between devices  78.5 us (38%)
  starting transfers between devices  68.5 us (33%)
  local copies, waits for them, and re-layouts  18.5 us (9%)
  Pallas kernels  17.8 us (9%)
  other arithmetic  10.4 us (5%)
  matrix products  10.2 us (5%)
    ppermute x20, waiting for transfers between devices, levels(): return lax.ppermute(x, 'dp', pairs)  52.9 us
    ppermute x20, starting transfers between devices, levels(): return lax.ppermute(x, 'dp', pairs)  43.7 us
    ppermute x18, starting transfers between devices, across(): return lax.ppermute(x, 'dp', [(d, d ^ r) for d in range(self.replicas)])  24.7 us
    ppermute x18, waiting for transfers between devices, across(): return lax.ppermute(x, 'dp', [(d, d ^ r) for d in range(self.replicas)])  22.1 us
    pallas_call x2, Pallas kernels, products(): pl.pallas_call(kernel, out_shape=(out, out), in_specs=[pl.BlockSpec(memor...  17.8 us
    unnamed x72, local copies, waits for them, and re-layouts  9.83 us
    dot_general x1, matrix products, updated(): update = jnp.dot(basis_rows.astype(bf16), panel, preferred_element_type=f32)  7.43 us
    dynamic_slice x2, local copies, waits for them, and re-layouts, cut(): return lax.dynamic_slice_in_dim(x, (self.place ^ r) * quarter, quarter, 1)  4.8 us
  transfers between devices with their start and end apart: 40, of which 14 were waited for; matrix products, arithmetic and copies ran while one was open for 12% of the time, Pallas kernels for 9%

profile of v9, /device:TPU:0, one launch (start us, length us, event | category | flops | bytes accessed | tf_op | source)
XLA Modules:
  0.0 207.1 jit_solution(6464722059620711960)
XLA Ops:
  0.7 2.5 %constant_dynamic-slice_fusion.6 = (bf16[128,1792]{1,0:T(8,128)(2,1)S(1)}, bf16[128,1792]{1,0:T(8,128)(2,1)}, bf16[128,1792]{1,0:T(8,128)(2,1)S(1)}, bf16[128,1792]{1,0:T(8,128)(2,1)}) fusion(bf16[128,7168]{1,0:T(8,128)(2,1)} %param.6, s32[]{:T(128)S(6)} %select_n.134, s32[]{:T(128)S(6)} %select_n.133, s32[]{:T(128)S(6)} %select_n.132, s32[]{:T(128)S(6)} %select_n.135), kind=kLoop, calls=%fused_computation.64 | loop fusion | bytes 3670032 | tf_op jit(solution)/shard_map/dynamic_slice | solution.py:45
  3.2 2.9 %collective-permute-start.1 = (bf16[128,1792]{1,0:T(8,128)(2,1)}, bf16[128,1792]{1,0:T(8,128)(2,1)S(1)}, u32[]{:S(2)}, u32[]{:S(2)}) collective-permute-start(bf16[128,1792]{1,0:T(8,128)(2,1)} %get-tuple-element.62), channel_id=1, source_target_pairs={{0,2},{2,0},{4,6},{6,4},{8,10},{10,8},{12,14},{14,12},{16,18},{18,... | collective-permute-start | bytes 1376264 | tf_op jit(solution)/shard_map/ppermute | solution.py:35
  8.4 4.4 %collective-permute-start = (bf16[128,1792]{1,0:T(8,128)(2,1)S(1)}, bf16[128,1792]{1,0:T(8,128)(2,1)}, u32[]{:S(2)}, u32[]{:S(2)}) collective-permute-start(bf16[128,1792]{1,0:T(8,128)(2,1)S(1)} %get-tuple-element.32.refs_0_), channel_id=1, source_target_pairs={{0,8},{2,10},{4,12},{6,14},{8,0},{10,2},{12,4},{14,6},{16,24},{18,... | collective-permute-start | bytes 1376264 | tf_op jit(solution)/shard_map/ppermute | solution.py:41
  12.8 4.1 %collective-permute-done.1 = bf16[128,1792]{1,0:T(8,128)(2,1)S(1)} collective-permute-done((bf16[128,1792]{1,0:T(8,128)(2,1)}, bf16[128,1792]{1,0:T(8,128)(2,1)S(1)}, u32[]{:S(2)}, u32[]{:S(2)}) %collective-permute-start.1) | collective-permute-done | bytes 458784 | tf_op jit(solution)/shard_map/ppermute | solution.py:35
  20.6 2.7 %collective-permute-start.10 = (bf16[128,64]{1,0:T(8,128)(2,1)S(1)}, bf16[128,64]{1,0:T(8,128)(2,1)S(1)}, u32[]{:S(2)}, u32[]{:S(2)}) collective-permute-start(bf16[128,64]{1,0:T(8,128)(2,1)S(1)} %all_gather.3), channel_id=1, source_target_pairs={{0,6},{2,4},{4,2},{6,0},{8,14},{10,12},{12,10},{14,8},{16,22},{18,... | collective-permute-start | bytes 49160 | tf_op jit(solution)/shard_map/ppermute | solution.py:35
  24.1 2.7 %collective-permute-start.5 = (bf16[128,1792]{1,0:T(8,128)(2,1)}, bf16[128,1792]{1,0:T(8,128)(2,1)S(1)}, u32[]{:S(2)}, u32[]{:S(2)}) collective-permute-start(bf16[128,1792]{1,0:T(8,128)(2,1)} %get-tuple-element.28), channel_id=1, source_target_pairs={{0,6},{2,4},{4,2},{6,0},{8,14},{10,12},{12,10},{14,8},{16,22},{18,... | collective-permute-start | bytes 1376264 | tf_op jit(solution)/shard_map/ppermute | solution.py:35
  26.8 2.3 %constant_dynamic-slice_fusion.1 = (bf16[256,1792]{1,0:T(8,128)(2,1)S(1)}, bf16[256,1792]{1,0:T(8,128)(2,1)S(1)}, bf16[256,1792]{1,0:T(8,128)(2,1)S(1)}, bf16[256,1792]{1,0:T(8,128)(2,1)S(1)}) fusion(bf16[256,7168]{1,0:T(8,128)(2,1)} %param.7, s32[]{:T(128)S(6)} %select_n.135, s32[]{:T(128)S(6)} %select_n.134, s32[]{:T(128)S(6)} %select_n.133, s32[]{:T(128)S(6)} %select_n.132), kind=kLoop, calls=%fused_computation.59 | loop fusion | bytes 7340048 | tf_op jit(solution)/shard_map/dynamic_slice | solution.py:45
  31.7 4.4 %collective-permute-start.4 = (bf16[256,1792]{1,0:T(8,128)(2,1)S(1)}, bf16[256,1792]{1,0:T(8,128)(2,1)S(1)}, u32[]{:S(2)}, u32[]{:S(2)}) collective-permute-start(bf16[256,1792]{1,0:T(8,128)(2,1)S(1)} %pad_maximum_fusion.refs_1_), channel_id=1, source_target_pairs={{0,8},{2,10},{4,12},{6,14},{8,0},{10,2},{12,4},{14,6},{16,24},{18,... | collective-permute-start | bytes 2752520 | tf_op jit(solution)/shard_map/ppermute | solution.py:41
  38.7 4.5 %collective-permute-start.14 = (bf16[64,1792]{1,0:T(8,128)(2,1)S(1)}, bf16[64,1792]{1,0:T(8,128)(2,1)S(1)}, u32[]{:S(2)}, u32[]{:S(2)}) collective-permute-start(bf16[64,1792]{1,0:T(8,128)(2,1)S(1)} %get-tuple-element.93), channel_id=1, source_target_pairs={{0,8},{2,10},{4,12},{6,14},{8,0},{10,2},{12,4},{14,6},{16,24},{18,... | collective-permute-start | bytes 688136 | tf_op jit(solution)/shard_map/ppermute | solution.py:41
  45.9 14.4 %collective-permute-done.14 = bf16[64,1792]{1,0:T(8,128)(2,1)S(1)} collective-permute-done((bf16[64,1792]{1,0:T(8,128)(2,1)S(1)}, bf16[64,1792]{1,0:T(8,128)(2,1)S(1)}, u32[]{:S(2)}, u32[]{:S(2)}) %collective-permute-start.14) | collective-permute-done | bytes 229408 | tf_op jit(solution)/shard_map/ppermute | solution.py:41
  60.8 4.7 %collective-permute-start.7 = (bf16[128,1792]{1,0:T(8,128)(2,1)S(1)}, bf16[128,1792]{1,0:T(8,128)(2,1)S(1)}, u32[]{:S(2)}, u32[]{:S(2)}) collective-permute-start(bf16[128,1792]{1,0:T(8,128)(2,1)S(1)} %collective-permute-done.5.refs_2_), channel_id=1, source_target_pairs={{0,8},{2,10},{4,12},{6,14},{8,0},{10,2},{12,4},{14,6},{16,24},{18,... | collective-permute-start | bytes 1376264 | tf_op jit(solution)/shard_map/ppermute | solution.py:41
  65.6 8.7 %collective-permute-done.7.refs_5_ = bf16[128,1792]{1,0:T(8,128)(2,1)S(1)} collective-permute-done((bf16[128,1792]{1,0:T(8,128)(2,1)S(1)}, bf16[128,1792]{1,0:T(8,128)(2,1)S(1)}, u32[]{:S(2)}, u32[]{:S(2)}) %collective-permute-start.7) | collective-permute-done | bytes 458784 | tf_op jit(solution)/shard_map/ppermute | solution.py:41
  77.5 4.6 %collective-permute-start.15 = (bf16[512,896]{1,0:T(8,128)(2,1)S(1)}, bf16[512,896]{1,0:T(8,128)(2,1)S(1)}, u32[]{:S(2)}, u32[]{:S(2)}) collective-permute-start(bf16[512,896]{1,0:T(8,128)(2,1)S(1)} %maximum_select_fusion), channel_id=1, source_target_pairs={{0,8},{2,10},{4,12},{6,14},{8,0},{10,2},{12,4},{14,6},{16,24},{18,... | collective-permute-start | bytes 2752520 | tf_op jit(solution)/shard_map/ppermute | solution.py:41
  84.4 23.2 %collective-permute-done.19 = bf16[64,1792]{1,0:T(8,128)(2,1)S(1)} collective-permute-done((bf16[64,1792]{1,0:T(8,128)(2,1)S(1)}, bf16[64,1792]{1,0:T(8,128)(2,1)S(1)}, u32[]{:S(2)}, u32[]{:S(2)}) %collective-permute-start.19) | collective-permute-done | bytes 229408 | tf_op jit(solution)/shard_map/ppermute | solution.py:41
  121.4 10.0 %shard_map.68 = (bf16[4,64,3072]{2,1,0:T(8,128)(2,1)S(1)}, bf16[4,64,3072]{2,1,0:T(8,128)(2,1)S(1)}) custom-call(s32[2]{0:T(128)S(1)} %pad_add_fusion.scalar_ref, bf16[128,1792]{1,0:T(8,128)(2,1)S(1)} %get-tuple-element.32.refs_0_, bf16[256,1792]{1,0:T(8,128)(2,1)S(1)} %copy-done.8, bf16[128,1792]{1,0:T(8,128)(2,1)S(1)} %copy-done.23, ...), custom_call_target="tpu_custom_call" | custom-call | flops 1000000 | bytes 100000 | tf_op jit(solution)/shard_map/pallas_call | solution.py:179
  132.3 4.2 %collective-permute-start.27 = (bf16[256,896]{1,0:T(8,128)(2,1)S(1)}, bf16[256,896]{1,0:T(8,128)(2,1)S(1)}, u32[]{:S(2)}, u32[]{:S(2)}) collective-permute-start(bf16[256,896]{1,0:T(8,128)(2,1)S(1)} %copy-done.35), channel_id=1, source_target_pairs={{0,8},{2,10},{4,12},{6,14},{8,0},{10,2},{12,4},{14,6},{16,24},{18,... | collective-permute-start | bytes 1376264 | tf_op jit(solution)/shard_map/ppermute | solution.py:41
  140.8 6.6 %collective-permute-done.27.refs_12_ = bf16[256,896]{1,0:T(8,128)(2,1)S(1)} collective-permute-done((bf16[256,896]{1,0:T(8,128)(2,1)S(1)}, bf16[256,896]{1,0:T(8,128)(2,1)S(1)}, u32[]{:S(2)}, u32[]{:S(2)}) %collective-permute-start.27) | collective-permute-done | bytes 458784 | tf_op jit(solution)/shard_map/ppermute | solution.py:41
  148.7 7.8 %shard_map.69 = (bf16[4,64,3072]{2,1,0:T(8,128)(2,1)S(1)}, bf16[4,64,3072]{2,1,0:T(8,128)(2,1)S(1)}) custom-call(s32[2]{0:T(128)S(1)} %pad_add_fusion.scalar_ref, bf16[512,896]{1,0:T(8,128)(2,1)S(1)} %maximum_select_fusion.1.refs_0_, bf16[256,896]{1,0:T(8,128)(2,1)} %collective-permute-done.18.refs_1_, bf16[256,896]{1,0:T(8,128)(2,1)S(1)} %collective-permute-done.28.refs_2_, ...), custom_call_target="tpu_custom_call" | custom-call | flops 1000000 | bytes 100000 | tf_op jit(solution)/shard_map/pallas_call | solution.py:179
  158.5 3.4 %collective-permute-done.29 = bf16[4,64,3072]{2,1,0:T(8,128)(2,1)S(1)} collective-permute-done((bf16[4,64,3072]{2,1,0:T(8,128)(2,1)S(1)}, bf16[4,64,3072]{2,1,0:T(8,128)(2,1)S(1)}, u32[]{:S(2)}, u32[]{:S(2)}) %collective-permute-start.29) | collective-permute-done | bytes 1572896 | tf_op jit(solution)/shard_map/ppermute | solution.py:204
  167.7 4.9 %collective-permute-start.26 = (bf16[64,1024]{1,0:T(8,128)(2,1)S(1)}, bf16[64,1024]{1,0:T(8,128)(2,1)S(1)}, u32[]{:S(2)}, u32[]{:S(2)}) collective-permute-start(bf16[64,1024]{1,0:T(8,128)(2,1)S(1)} %get-tuple-element.88), channel_id=1, source_target_pairs={{0,16},{2,18},{4,20},{6,22},{24,8},{26,10},{28,12},{30,14},{1,17},... | collective-permute-start | bytes 393224 | tf_op jit(solution)/shard_map/ppermute | solution.py:41
  172.6 3.2 %collective-permute-done.30 = bf16[64,3072]{1,0:T(8,128)(2,1)} collective-permute-done((bf16[64,3072]{1,0:T(8,128)(2,1)}, bf16[64,3072]{1,0:T(8,128)(2,1)}, u32[]{:S(2)}, u32[]{:S(2)}) %collective-permute-start.30) | collective-permute-done | bytes 393248 | tf_op jit(solution)/shard_map/ppermute | solution.py:35
  176.1 8.2 %collective-permute-done.32 = bf16[64,3072]{1,0:T(8,128)(2,1)} collective-permute-done((bf16[64,3072]{1,0:T(8,128)(2,1)}, bf16[64,3072]{1,0:T(8,128)(2,1)}, u32[]{:S(2)}, u32[]{:S(2)}) %collective-permute-start.32) | collective-permute-done | bytes 393248 | tf_op jit(solution)/shard_map/ppermute | solution.py:35
  191.4 3.2 %collective-permute-start.36 = (bf16[64,1024]{1,0:T(8,128)(2,1)S(1)}, bf16[64,1024]{1,0:T(8,128)(2,1)S(1)}, u32[]{:S(2)}, u32[]{:S(2)}) collective-permute-start(bf16[64,1024]{1,0:T(8,128)(2,1)S(1)} %get-tuple-element.50), channel_id=1, source_target_pairs={{0,24},{2,26},{4,28},{6,30},{24,0},{26,2},{28,4},{30,6},{1,25},{3,... | collective-permute-start | bytes 393224 | tf_op jit(solution)/shard_map/ppermute | solution.py:41
  198.6 7.4 %fusion = f32[256,7168]{1,0:T(8,128)} fusion(f32[256,7168]{1,0:T(8,128)} %param.9, bf16[64,1792]{1,0:T(8,128)(2,1)S(1)} %get-tuple-element.72, bf16[64,1792]{1,0:T(8,128)(2,1)S(1)} %get-tuple-element.73, bf16[64,1792]{1,0:T(8,128)(2,1)S(1)} %get-tuple-element.74, bf16[64,1792]{1,0:T(8,128)(2,1)S(1)} %get-tuple-element.71, f32[4096,64]{0,1:T(8,128)S(1)} %copy-done, ...), kind=kOutput, calls=%fused_computation.1 | convolution fusion | flops 244056064 | bytes 15630340 | tf_op jit(solution)/shard_map/dot_general | solution.py:101
  (171 shorter events, 60.7 us)
Async XLA Ops:
  6.2 17.7 %collective-permute-start.2 = (bf16[128,1792]{1,0:T(8,128)(2,1)S(1)}, bf16[128,1792]{1,0:T(8,128)(2,1)S(1)}, u32[]{:S(2)}, u32[]{:S(2)}) collective-permute-start(bf16[128,1792]{1,0:T(8,128)(2,1)S(1)} %get-tuple-element.61), channel_id=1, source_target_pairs={{0,4},{2,6},{4,0},{6,2},{8,12},{10,14},{12,8},{14,10},{16,20},{18,... | collective-permute-start | bytes 1376264 | tf_op jit(solution)/shard_map/ppermute | solution.py:35
  7.7 16.4 %collective-permute-start.3 = (bf16[128,1792]{1,0:T(8,128)(2,1)S(1)}, bf16[128,1792]{1,0:T(8,128)(2,1)S(1)}, u32[]{:S(2)}, u32[]{:S(2)}) collective-permute-start(bf16[128,1792]{1,0:T(8,128)(2,1)S(1)} %get-tuple-element.32.refs_0_), channel_id=1, source_target_pairs={{8,16},{10,18},{12,20},{14,22},{16,8},{18,10},{20,12},{22,14},{9,1... | collective-permute-start | bytes 1376264 | tf_op jit(solution)/shard_map/ppermute | solution.py:41
  8.4 18.5 %collective-permute-start = (bf16[128,1792]{1,0:T(8,128)(2,1)S(1)}, bf16[128,1792]{1,0:T(8,128)(2,1)}, u32[]{:S(2)}, u32[]{:S(2)}) collective-permute-start(bf16[128,1792]{1,0:T(8,128)(2,1)S(1)} %get-tuple-element.32.refs_0_), channel_id=1, source_target_pairs={{0,8},{2,10},{4,12},{6,14},{8,0},{10,2},{12,4},{14,6},{16,24},{18,... | collective-permute-start | bytes 1376264 | tf_op jit(solution)/shard_map/ppermute | solution.py:41
  20.6 17.6 %collective-permute-start.10 = (bf16[128,64]{1,0:T(8,128)(2,1)S(1)}, bf16[128,64]{1,0:T(8,128)(2,1)S(1)}, u32[]{:S(2)}, u32[]{:S(2)}) collective-permute-start(bf16[128,64]{1,0:T(8,128)(2,1)S(1)} %all_gather.3), channel_id=1, source_target_pairs={{0,6},{2,4},{4,2},{6,0},{8,14},{10,12},{12,10},{14,8},{16,22},{18,... | collective-permute-start | bytes 49160 | tf_op jit(solution)/shard_map/ppermute | solution.py:35
  30.8 45.3 %collective-permute-start.12 = (bf16[256,1792]{1,0:T(8,128)(2,1)S(1)}, bf16[256,1792]{1,0:T(8,128)(2,1)S(1)}, u32[]{:S(2)}, u32[]{:S(2)}) collective-permute-start(bf16[256,1792]{1,0:T(8,128)(2,1)S(1)} %pad_maximum_fusion.refs_1_), channel_id=1, source_target_pairs={{8,16},{10,18},{12,20},{14,22},{16,8},{18,10},{20,12},{22,14},{9,1... | collective-permute-start | bytes 2752520 | tf_op jit(solution)/shard_map/ppermute | solution.py:41
  31.7 33.9 %collective-permute-start.4 = (bf16[256,1792]{1,0:T(8,128)(2,1)S(1)}, bf16[256,1792]{1,0:T(8,128)(2,1)S(1)}, u32[]{:S(2)}, u32[]{:S(2)}) collective-permute-start(bf16[256,1792]{1,0:T(8,128)(2,1)S(1)} %pad_maximum_fusion.refs_1_), channel_id=1, source_target_pairs={{0,8},{2,10},{4,12},{6,14},{8,0},{10,2},{12,4},{14,6},{16,24},{18,... | collective-permute-start | bytes 2752520 | tf_op jit(solution)/shard_map/ppermute | solution.py:41
  37.5 23.3 %collective-permute-start.6 = (bf16[128,1792]{1,0:T(8,128)(2,1)S(1)}, bf16[128,1792]{1,0:T(8,128)(2,1)S(1)}, u32[]{:S(2)}, u32[]{:S(2)}) collective-permute-start(bf16[128,1792]{1,0:T(8,128)(2,1)S(1)} %collective-permute-done.5.refs_2_), channel_id=1, source_target_pairs={{8,16},{10,18},{12,20},{14,22},{16,8},{18,10},{20,12},{22,14},{9,1... | collective-permute-start | bytes 1376264 | tf_op jit(solution)/shard_map/ppermute | solution.py:41
  38.7 21.5 %collective-permute-start.14 = (bf16[64,1792]{1,0:T(8,128)(2,1)S(1)}, bf16[64,1792]{1,0:T(8,128)(2,1)S(1)}, u32[]{:S(2)}, u32[]{:S(2)}) collective-permute-start(bf16[64,1792]{1,0:T(8,128)(2,1)S(1)} %get-tuple-element.93), channel_id=1, source_target_pairs={{0,8},{2,10},{4,12},{6,14},{8,0},{10,2},{12,4},{14,6},{16,24},{18,... | collective-permute-start | bytes 688136 | tf_op jit(solution)/shard_map/ppermute | solution.py:41
  44.3 31.8 %collective-permute-start.13 = (bf16[256,1792]{1,0:T(8,128)(2,1)S(1)}, bf16[256,1792]{1,0:T(8,128)(2,1)S(1)}, u32[]{:S(2)}, u32[]{:S(2)}) collective-permute-start(bf16[256,1792]{1,0:T(8,128)(2,1)S(1)} %get-tuple-element.34), channel_id=1, source_target_pairs={{0,2},{2,0},{4,6},{6,4},{8,10},{10,8},{12,14},{14,12},{16,18},{18,... | collective-permute-start | bytes 2752520 | tf_op jit(solution)/shard_map/ppermute | solution.py:35
  60.3 21.8 %collective-permute-start.16 = (bf16[256,1792]{1,0:T(8,128)(2,1)S(1)}, bf16[256,1792]{1,0:T(8,128)(2,1)S(1)}, u32[]{:S(2)}, u32[]{:S(2)}) collective-permute-start(bf16[256,1792]{1,0:T(8,128)(2,1)S(1)} %get-tuple-element.36), channel_id=1, source_target_pairs={{0,4},{2,6},{4,0},{6,2},{8,12},{10,14},{12,8},{14,10},{16,20},{18,... | collective-permute-start | bytes 2752520 | tf_op jit(solution)/shard_map/ppermute | solution.py:35
  75.3 33.1 %collective-permute-start.11 = (bf16[512,896]{1,0:T(8,128)(2,1)S(1)}, bf16[512,896]{1,0:T(8,128)(2,1)S(1)}, u32[]{:S(2)}, u32[]{:S(2)}) collective-permute-start(bf16[512,896]{1,0:T(8,128)(2,1)S(1)} %pad_maximum_fusion.1), channel_id=1, source_target_pairs={{8,16},{10,18},{12,20},{14,22},{16,8},{18,10},{20,12},{22,14},{9,1... | collective-permute-start | bytes 2752520 | tf_op jit(solution)/shard_map/ppermute | solution.py:41
  77.5 30.9 %collective-permute-start.15 = (bf16[512,896]{1,0:T(8,128)(2,1)S(1)}, bf16[512,896]{1,0:T(8,128)(2,1)S(1)}, u32[]{:S(2)}, u32[]{:S(2)}) collective-permute-start(bf16[512,896]{1,0:T(8,128)(2,1)S(1)} %maximum_select_fusion), channel_id=1, source_target_pairs={{0,8},{2,10},{4,12},{6,14},{8,0},{10,2},{12,4},{14,6},{16,24},{18,... | collective-permute-start | bytes 2752520 | tf_op jit(solution)/shard_map/ppermute | solution.py:41
  82.1 28.7 %collective-permute-start.17 = (bf16[256,1792]{1,0:T(8,128)(2,1)S(1)}, bf16[256,1792]{1,0:T(8,128)(2,1)S(1)}, u32[]{:S(2)}, u32[]{:S(2)}) collective-permute-start(bf16[256,1792]{1,0:T(8,128)(2,1)S(1)} %get-tuple-element.37), channel_id=1, source_target_pairs={{0,6},{2,4},{4,2},{6,0},{8,14},{10,12},{12,10},{14,8},{16,22},{18,... | collective-permute-start | bytes 2752520 | tf_op jit(solution)/shard_map/ppermute | solution.py:35
  83.4 24.2 %collective-permute-start.19 = (bf16[64,1792]{1,0:T(8,128)(2,1)S(1)}, bf16[64,1792]{1,0:T(8,128)(2,1)S(1)}, u32[]{:S(2)}, u32[]{:S(2)}) collective-permute-start(bf16[64,1792]{1,0:T(8,128)(2,1)S(1)} %get-tuple-element.55), channel_id=1, source_target_pairs={{0,16},{2,18},{4,20},{6,22},{8,24},{10,26},{12,28},{14,30},{16,0},... | collective-permute-start | bytes 688136 | tf_op jit(solution)/shard_map/ppermute | solution.py:41
  109.3 22.0 %collective-permute-start.18 = (bf16[256,896]{1,0:T(8,128)(2,1)}, bf16[256,896]{1,0:T(8,128)(2,1)}, u32[]{:S(2)}, u32[]{:S(2)}) collective-permute-start(bf16[256,896]{1,0:T(8,128)(2,1)} %get-tuple-element.40), channel_id=1, source_target_pairs={{8,16},{10,18},{12,20},{14,22},{16,8},{18,10},{20,12},{22,14},{9,1... | collective-permute-start | bytes 1376264 | tf_op jit(solution)/shard_map/ppermute | solution.py:41
  112.1 19.3 %collective-permute-start.20 = (bf16[256,896]{1,0:T(8,128)(2,1)}, bf16[256,896]{1,0:T(8,128)(2,1)}, u32[]{:S(2)}, u32[]{:S(2)}) collective-permute-start(bf16[256,896]{1,0:T(8,128)(2,1)} %get-tuple-element.41), channel_id=1, source_target_pairs={{0,8},{2,10},{4,12},{6,14},{8,0},{10,2},{12,4},{14,6},{16,24},{18,... | collective-permute-start | bytes 1376264 | tf_op jit(solution)/shard_map/ppermute | solution.py:41
  131.4 17.2 %collective-permute-start.28 = (bf16[256,896]{1,0:T(8,128)(2,1)S(1)}, bf16[256,896]{1,0:T(8,128)(2,1)S(1)}, u32[]{:S(2)}, u32[]{:S(2)}) collective-permute-start(bf16[256,896]{1,0:T(8,128)(2,1)S(1)} %copy-done.34), channel_id=1, source_target_pairs={{8,16},{10,18},{12,20},{14,22},{16,8},{18,10},{20,12},{22,14},{9,1... | collective-permute-start | bytes 1376264 | tf_op jit(solution)/shard_map/ppermute | solution.py:41
  137.2 19.3 %collective-permute-start.22 = (bf16[64,3072]{1,0:T(8,128)(2,1)S(1)}, bf16[64,3072]{1,0:T(8,128)(2,1)S(1)}, u32[]{:S(2)}, u32[]{:S(2)}) collective-permute-start(bf16[64,3072]{1,0:T(8,128)(2,1)S(1)} %get-tuple-element.68), channel_id=1, source_target_pairs={{0,2},{2,0},{4,6},{6,4},{8,10},{10,8},{12,14},{14,12},{16,18},{18,... | collective-permute-start | bytes 1179656 | tf_op jit(solution)/shard_map/ppermute | solution.py:35
  137.9 18.9 %collective-permute-start.24 = (bf16[64,3072]{1,0:T(8,128)(2,1)S(1)}, bf16[64,3072]{1,0:T(8,128)(2,1)S(1)}, u32[]{:S(2)}, u32[]{:S(2)}) collective-permute-start(bf16[64,3072]{1,0:T(8,128)(2,1)S(1)} %get-tuple-element.69), channel_id=1, source_target_pairs={{0,6},{2,4},{4,2},{6,0},{8,14},{10,12},{12,10},{14,8},{16,22},{18,... | collective-permute-start | bytes 1179656 | tf_op jit(solution)/shard_map/ppermute | solution.py:35
  139.3 19.0 %collective-permute-start.23 = (bf16[64,3072]{1,0:T(8,128)(2,1)S(1)}, bf16[64,3072]{1,0:T(8,128)(2,1)S(1)}, u32[]{:S(2)}, u32[]{:S(2)}) collective-permute-start(bf16[64,3072]{1,0:T(8,128)(2,1)S(1)} %get-tuple-element.70), channel_id=1, source_target_pairs={{0,4},{2,6},{4,0},{6,2},{8,12},{10,14},{12,8},{14,10},{16,20},{18,... | collective-permute-start | bytes 1179656 | tf_op jit(solution)/shard_map/ppermute | solution.py:35
  165.2 19.1 %collective-permute-start.32 = (bf16[64,3072]{1,0:T(8,128)(2,1)}, bf16[64,3072]{1,0:T(8,128)(2,1)}, u32[]{:S(2)}, u32[]{:S(2)}) collective-permute-start(bf16[64,3072]{1,0:T(8,128)(2,1)} %get-tuple-element.66), channel_id=1, source_target_pairs={{0,6},{2,4},{4,2},{6,0},{8,14},{10,12},{12,10},{14,8},{16,22},{18,... | collective-permute-start | bytes 1179656 | tf_op jit(solution)/shard_map/ppermute | solution.py:35
  166.3 19.3 %collective-permute-start.31 = (bf16[64,3072]{1,0:T(8,128)(2,1)}, bf16[64,3072]{1,0:T(8,128)(2,1)}, u32[]{:S(2)}, u32[]{:S(2)}) collective-permute-start(bf16[64,3072]{1,0:T(8,128)(2,1)} %get-tuple-element.67), channel_id=1, source_target_pairs={{0,4},{2,6},{4,0},{6,2},{8,12},{10,14},{12,8},{14,10},{16,20},{18,... | collective-permute-start | bytes 1179656 | tf_op jit(solution)/shard_map/ppermute | solution.py:35
  167.0 23.7 %collective-permute-start.33 = (bf16[64,1024]{1,0:T(8,128)(2,1)S(1)}, bf16[64,1024]{1,0:T(8,128)(2,1)S(1)}, u32[]{:S(2)}, u32[]{:S(2)}) collective-permute-start(bf16[64,1024]{1,0:T(8,128)(2,1)S(1)} %get-tuple-element.88), channel_id=1, source_target_pairs={{8,16},{10,18},{12,20},{14,22},{16,8},{18,10},{20,12},{22,14},{9,1... | collective-permute-start | bytes 393224 | tf_op jit(solution)/shard_map/ppermute | solution.py:41
  167.7 23.1 %collective-permute-start.26 = (bf16[64,1024]{1,0:T(8,128)(2,1)S(1)}, bf16[64,1024]{1,0:T(8,128)(2,1)S(1)}, u32[]{:S(2)}, u32[]{:S(2)}) collective-permute-start(bf16[64,1024]{1,0:T(8,128)(2,1)S(1)} %get-tuple-element.88), channel_id=1, source_target_pairs={{0,16},{2,18},{4,20},{6,22},{24,8},{26,10},{28,12},{30,14},{1,17},... | collective-permute-start | bytes 393224 | tf_op jit(solution)/shard_map/ppermute | solution.py:41
  (52 other events, 476.4 us)

commit v10 on v8

--- a/solution.py
+++ b/solution.py
@@ -250,7 +250,6 @@
     first_x, first_y = across(first[1], 1), across(first[2], 2)
 
     panel = sum(tn(q, a) for q, a in zip(proj, [after(cuts[0], give), *plane]))
-    panel = panel + end_swap(after(panel.astype(bf16), first)).astype(f32)
 
     late0 = send(far0, jnp.concatenate(got, 0))
     sources = [after(late0, first), *far1, *near_m, *parts, got_a, *got]
@@ -272,14 +271,20 @@
     first = plane_sum(first[0], first_x, first_y, across(first[3], 3))
     give = after(give, first)
     second = (keep.astype(f32) + swap(give).astype(f32)).astype(bf16)
-    second = plane_sum(second[0], *[across(second[r], r) for r in range(1, PLANE)])
-    panel = (panel + lay.levels(after(panel.astype(bf16), second), 2).astype(f32)).astype(bf16)
+    arrived = [across(second[r], r) for r in range(1, PLANE)]
+    totals = plane_sum(second[0], *arrived)
+    part = panel.astype(bf16)
+    panel = panel + sum(lay.levels(part, s).astype(f32) for s in range(1, lay.line))
+    panel = panel.astype(bf16)
+    y1 = after(first[:, width:2 * width], panel)
+    panel = after(panel, totals)
     panel = jnp.stack([panel] + [across(panel, r) for r in range(1, PLANE)])
     panel = jnp.concatenate(
         [lax.dynamic_index_in_dim(panel, lay.place ^ p, 0, False) for p in range(PLANE)], 1
     )
     new_momentum = updated(lay, proj_basis, panel, momentum, tokens * lay.replicas)
-    y0, y1, early = [first[:, i * width:(i + 1) * width] for i in range(3)]
+    y0, early = first[:, :width], first[:, 2 * width:]
+    second = totals
     late, early_other, late_other = [second[:, i * width:(i + 1) * width] for i in range(3)]
 
     z1 = end_swap(y1)

time: 191 us -> 184 us (0.963)
  starting transfers between devices: 69.8 us -> 54.3 us
  waiting for transfers between devices: 66.1 us -> 73.4 us
    ppermute x20 -> x21, waiting for transfers between devices: 35.3 us -> 46.8 us  [levels(): return lax.ppermute(x, 'dp', pairs)]
    ppermute x20 -> x21, starting transfers between devices: 45.7 us -> 35.8 us  [levels(): return lax.ppermute(x, 'dp', pairs)]
    ppermute x18, starting transfers between devices: 24 us -> 18.4 us  [across(): return lax.ppermute(x, 'dp', [(d, d ^ r) for d in range(self.replicas)])]
    ppermute x18, waiting for transfers between devices: 29 us -> 24.2 us  [across(): return lax.ppermute(x, 'dp', [(d, d ^ r) for d in range(self.replicas)])]
    unnamed x68 -> x74, local copies, waits for them, and re-layouts: 6.63 us -> 8.43 us
  transfers between devices with their start and end apart: 40 -> 41, of which waited for: 21 -> 17; matrix products, arithmetic and copies ran while one was open for 10% -> 12% of each run, Pallas kernels for 10% -> 10%
where the time goes in v10:
time: 184 us; the launch traced here: 183 us
  waiting for transfers between devices  73.4 us (40%)
  starting transfers between devices  54.3 us (30%)
  Pallas kernels  18.5 us (10%)
  local copies, waits for them, and re-layouts  15.3 us (8%)
  other arithmetic  11.1 us (6%)
  matrix products  7.03 us (4%)
    ppermute x21, waiting for transfers between devices, levels(): return lax.ppermute(x, 'dp', pairs)  46.8 us
    ppermute x21, starting transfers between devices, levels(): return lax.ppermute(x, 'dp', pairs)  35.8 us
    ppermute x18, waiting for transfers between devices, across(): return lax.ppermute(x, 'dp', [(d, d ^ r) for d in range(self.replicas)])  24.2 us
    pallas_call x2, Pallas kernels, products(): pl.pallas_call(kernel, out_shape=(out, out), in_specs=[pl.BlockSpec(memor...  18.5 us
    ppermute x18, starting transfers between devices, across(): return lax.ppermute(x, 'dp', [(d, d ^ r) for d in range(self.replicas)])  18.4 us
    unnamed x74, local copies, waits for them, and re-layouts  8.43 us
    select_n x4, other arithmetic, line_of_four(): send = lambda a, w: jnp.where(inner, a, w)  4.45 us
    dot_general x1, matrix products, updated(): update = jnp.dot(basis_rows.astype(bf16), panel, preferred_element_type=f32)  4.36 us
  transfers between devices with their start and end apart: 41, of which 17 were waited for; matrix products, arithmetic and copies ran while one was open for 12% of the time, Pallas kernels for 10%

profile of v10, /device:TPU:0, one launch (start us, length us, event | category | flops | bytes accessed | tf_op | source)
XLA Modules:
  0.0 182.8 jit_solution(16470391049847863990)
XLA Ops:
  2.3 3.0 %collective-permute-start.1 = (bf16[128,1792]{1,0:T(8,128)(2,1)S(1)}, bf16[128,1792]{1,0:T(8,128)(2,1)S(1)}, u32[]{:S(2)}, u32[]{:S(2)}) collective-permute-start(bf16[128,1792]{1,0:T(8,128)(2,1)S(1)} %get-tuple-element.60), channel_id=1, source_target_pairs={{0,2},{2,0},{4,6},{6,4},{8,10},{10,8},{12,14},{14,12},{16,18},{18,... | collective-permute-start | bytes 1376264 | tf_op jit(solution)/shard_map/ppermute | solution.py:35
  9.1 6.7 %collective-permute-done.1 = bf16[128,1792]{1,0:T(8,128)(2,1)S(1)} collective-permute-done((bf16[128,1792]{1,0:T(8,128)(2,1)S(1)}, bf16[128,1792]{1,0:T(8,128)(2,1)S(1)}, u32[]{:S(2)}, u32[]{:S(2)}) %collective-permute-start.1) | collective-permute-done | bytes 458784 | tf_op jit(solution)/shard_map/ppermute | solution.py:35
  19.4 4.6 %collective-permute-start.4 = (bf16[256,1792]{1,0:T(8,128)(2,1)}, bf16[256,1792]{1,0:T(8,128)(2,1)}, u32[]{:S(2)}, u32[]{:S(2)}) collective-permute-start(bf16[256,1792]{1,0:T(8,128)(2,1)} %pad_maximum_fusion.refs_1_), channel_id=1, source_target_pairs={{0,8},{2,10},{4,12},{6,14},{8,0},{10,2},{12,4},{14,6},{16,24},{18,... | collective-permute-start | bytes 2752520 | tf_op jit(solution)/shard_map/ppermute | solution.py:41
  25.4 10.2 %collective-permute-done.5.refs_2_ = bf16[128,1792]{1,0:T(8,128)(2,1)} collective-permute-done((bf16[128,1792]{1,0:T(8,128)(2,1)S(1)}, bf16[128,1792]{1,0:T(8,128)(2,1)}, u32[]{:S(2)}, u32[]{:S(2)}) %collective-permute-start.5) | collective-permute-done | bytes 458784 | tf_op jit(solution)/shard_map/ppermute | solution.py:35
  36.5 2.3 %constant_dynamic-slice_fusion.1 = (bf16[256,1792]{1,0:T(8,128)(2,1)S(1)}, bf16[256,1792]{1,0:T(8,128)(2,1)S(1)}, bf16[256,1792]{1,0:T(8,128)(2,1)S(1)}, bf16[256,1792]{1,0:T(8,128)(2,1)S(1)}) fusion(bf16[256,7168]{1,0:T(8,128)(2,1)} %param.7, s32[]{:T(128)S(6)} %select_n.135, s32[]{:T(128)S(6)} %select_n.134, s32[]{:T(128)S(6)} %select_n.133, s32[]{:T(128)S(6)} %select_n.132), kind=kLoop, calls=%fused_computation.58 | loop fusion | bytes 7340048 | tf_op jit(solution)/shard_map/dynamic_slice | solution.py:45
  39.4 6.2 %collective-permute-done.4.refs_4_ = bf16[256,1792]{1,0:T(8,128)(2,1)} collective-permute-done((bf16[256,1792]{1,0:T(8,128)(2,1)}, bf16[256,1792]{1,0:T(8,128)(2,1)}, u32[]{:S(2)}, u32[]{:S(2)}) %collective-permute-start.4) | collective-permute-done | bytes 917536 | tf_op jit(solution)/shard_map/ppermute | solution.py:41
  47.3 5.6 %collective-permute-done.7.refs_5_ = bf16[128,1792]{1,0:T(8,128)(2,1)S(1)} collective-permute-done((bf16[128,1792]{1,0:T(8,128)(2,1)}, bf16[128,1792]{1,0:T(8,128)(2,1)S(1)}, u32[]{:S(2)}, u32[]{:S(2)}) %collective-permute-start.7) | collective-permute-done | bytes 458784 | tf_op jit(solution)/shard_map/ppermute | solution.py:41
  55.2 3.0 %collective-permute-done.10.refs_11_.refs_7_ = bf16[256,1792]{1,0:T(8,128)(2,1)S(1)} collective-permute-done((bf16[256,1792]{1,0:T(8,128)(2,1)S(1)}, bf16[256,1792]{1,0:T(8,128)(2,1)S(1)}, u32[]{:S(2)}, u32[]{:S(2)}) %collective-permute-start.10) | collective-permute-done | bytes 917536 | tf_op jit(solution)/shard_map/ppermute | solution.py:35
  59.5 3.9 %collective-permute-start.11 = (bf16[512,896]{1,0:T(8,128)(2,1)S(1)}, bf16[512,896]{1,0:T(8,128)(2,1)S(1)}, u32[]{:S(2)}, u32[]{:S(2)}) collective-permute-start(bf16[512,896]{1,0:T(8,128)(2,1)S(1)} %maximum_select_fusion), channel_id=1, source_target_pairs={{0,8},{2,10},{4,12},{6,14},{8,0},{10,2},{12,4},{14,6},{16,24},{18,... | collective-permute-start | bytes 2752520 | tf_op jit(solution)/shard_map/ppermute | solution.py:41
  63.4 2.4 %collective-permute-start.13 = (bf16[256,1792]{1,0:T(8,128)(2,1)S(1)}, bf16[256,1792]{1,0:T(8,128)(2,1)S(1)}, u32[]{:S(2)}, u32[]{:S(2)}) collective-permute-start(bf16[256,1792]{1,0:T(8,128)(2,1)S(1)} %get-tuple-element.34), channel_id=1, source_target_pairs={{0,6},{2,4},{4,2},{6,0},{8,14},{10,12},{12,10},{14,8},{16,22},{18,... | collective-permute-start | bytes 2752520 | tf_op jit(solution)/shard_map/ppermute | solution.py:35
  70.4 2.4 %collective-permute-start.17 = (bf16[128,64]{1,0:T(8,128)(2,1)S(1)}, bf16[128,64]{1,0:T(8,128)(2,1)S(1)}, u32[]{:S(2)}, u32[]{:S(2)}) collective-permute-start(bf16[128,64]{1,0:T(8,128)(2,1)S(1)} %all_gather.3), channel_id=1, source_target_pairs={{0,6},{2,4},{4,2},{6,0},{8,14},{10,12},{12,10},{14,8},{16,22},{18,... | collective-permute-start | bytes 49160 | tf_op jit(solution)/shard_map/ppermute | solution.py:35
  72.9 7.6 %collective-permute-done.11.refs_10_ = bf16[512,896]{1,0:T(8,128)(2,1)S(1)} collective-permute-done((bf16[512,896]{1,0:T(8,128)(2,1)S(1)}, bf16[512,896]{1,0:T(8,128)(2,1)S(1)}, u32[]{:S(2)}, u32[]{:S(2)}) %collective-permute-start.11) | collective-permute-done | bytes 917536 | tf_op jit(solution)/shard_map/ppermute | solution.py:41
  84.9 5.9 %collective-permute-start.18 = (bf16[256,896]{1,0:T(8,128)(2,1)}, bf16[256,896]{1,0:T(8,128)(2,1)}, u32[]{:S(2)}, u32[]{:S(2)}) collective-permute-start(bf16[256,896]{1,0:T(8,128)(2,1)} %get-tuple-element.39), channel_id=1, source_target_pairs={{0,8},{2,10},{4,12},{6,14},{8,0},{10,2},{12,4},{14,6},{16,24},{18,... | collective-permute-start | bytes 1376264 | tf_op jit(solution)/shard_map/ppermute | solution.py:41
  97.2 9.6 %shard_map.68 = (bf16[4,64,3072]{2,1,0:T(8,128)(2,1)S(1)}, bf16[4,64,3072]{2,1,0:T(8,128)(2,1)S(1)}) custom-call(s32[2]{0:T(128)S(1)} %pad_add_fusion.scalar_ref, bf16[128,1792]{1,0:T(8,128)(2,1)S(1)} %get-tuple-element.41.refs_0_, bf16[256,1792]{1,0:T(8,128)(2,1)} %pad_maximum_fusion.refs_1_, bf16[128,1792]{1,0:T(8,128)(2,1)} %collective-permute-done.5.refs_2_, ...), custom_call_target="tpu_custom_call" | custom-call | flops 1000000 | bytes 100000 | tf_op jit(solution)/shard_map/pallas_call | solution.py:179
  107.9 2.4 %collective-permute-done.19 = bf16[4,64,3072]{2,1,0:T(8,128)(2,1)S(1)} collective-permute-done((bf16[4,64,3072]{2,1,0:T(8,128)(2,1)S(1)}, bf16[4,64,3072]{2,1,0:T(8,128)(2,1)S(1)}, u32[]{:S(2)}, u32[]{:S(2)}) %collective-permute-start.19) | collective-permute-done | bytes 1572896 | tf_op jit(solution)/shard_map/ppermute | solution.py:204
  111.2 3.4 %collective-permute-start.20 = (bf16[64,3072]{1,0:T(8,128)(2,1)S(1)}, bf16[64,3072]{1,0:T(8,128)(2,1)S(1)}, u32[]{:S(2)}, u32[]{:S(2)}) collective-permute-start(bf16[64,3072]{1,0:T(8,128)(2,1)S(1)} %get-tuple-element.66), channel_id=1, source_target_pairs={{0,2},{2,0},{4,6},{6,4},{8,10},{10,8},{12,14},{14,12},{16,18},{18,... | collective-permute-start | bytes 1179656 | tf_op jit(solution)/shard_map/ppermute | solution.py:35
  114.6 5.3 %collective-permute-done.28.refs_12_ = bf16[256,896]{1,0:T(8,128)(2,1)S(1)} collective-permute-done((bf16[256,896]{1,0:T(8,128)(2,1)S(1)}, bf16[256,896]{1,0:T(8,128)(2,1)S(1)}, u32[]{:S(2)}, u32[]{:S(2)}) %collective-permute-start.28) | collective-permute-done | bytes 458784 | tf_op jit(solution)/shard_map/ppermute | solution.py:41
  121.2 8.9 %shard_map.69 = (bf16[4,64,3072]{2,1,0:T(8,128)(2,1)S(1)}, bf16[4,64,3072]{2,1,0:T(8,128)(2,1)}) custom-call(s32[2]{0:T(128)S(1)} %pad_add_fusion.scalar_ref, bf16[512,896]{1,0:T(8,128)(2,1)S(1)} %maximum_select_fusion.1.refs_0_, bf16[256,896]{1,0:T(8,128)(2,1)} %collective-permute-done.14.refs_1_, bf16[256,896]{1,0:T(8,128)(2,1)S(1)} %collective-permute-done.29.refs_2_, ...), custom_call_target="tpu_custom_call" | custom-call | flops 1000000 | bytes 100000 | tf_op jit(solution)/shard_map/pallas_call | solution.py:179
  141.7 2.4 %collective-permute-done.25 = bf16[64,1792]{1,0:T(8,128)(2,1)S(1)} collective-permute-done((bf16[64,1792]{1,0:T(8,128)(2,1)S(1)}, bf16[64,1792]{1,0:T(8,128)(2,1)S(1)}, u32[]{:S(2)}, u32[]{:S(2)}) %collective-permute-start.25) | collective-permute-done | bytes 229408 | tf_op jit(solution)/shard_map/ppermute | solution.py:41
  144.0 14.1 %collective-permute-done.24 = bf16[64,1792]{1,0:T(8,128)(2,1)S(1)} collective-permute-done((bf16[64,1792]{1,0:T(8,128)(2,1)S(1)}, bf16[64,1792]{1,0:T(8,128)(2,1)S(1)}, u32[]{:S(2)}, u32[]{:S(2)}) %collective-permute-start.24) | collective-permute-done | bytes 229408 | tf_op jit(solution)/shard_map/ppermute | solution.py:41
  163.6 2.5 %collective-permute-done.26 = bf16[64,1024]{1,0:T(8,128)(2,1)S(1)} collective-permute-done((bf16[64,1024]{1,0:T(8,128)(2,1)S(1)}, bf16[64,1024]{1,0:T(8,128)(2,1)S(1)}, u32[]{:S(2)}, u32[]{:S(2)}) %collective-permute-start.26) | collective-permute-done | bytes 131104 | tf_op jit(solution)/shard_map/ppermute | solution.py:41
  166.1 4.2 %collective-permute-start.37 = (bf16[64,1024]{1,0:T(8,128)(2,1)S(1)}, bf16[64,1024]{1,0:T(8,128)(2,1)S(1)}, u32[]{:S(2)}, u32[]{:S(2)}) collective-permute-start(bf16[64,1024]{1,0:T(8,128)(2,1)S(1)} %get-tuple-element.50), channel_id=1, source_target_pairs={{0,24},{2,26},{4,28},{6,30},{24,0},{26,2},{28,4},{30,6},{1,25},{3,... | collective-permute-start | bytes 393224 | tf_op jit(solution)/shard_map/ppermute | solution.py:41
  174.5 4.4 %fusion = f32[256,7168]{1,0:T(8,128)} fusion(f32[256,7168]{1,0:T(8,128)S(1)} %bitcast.47, bf16[64,1792]{1,0:T(8,128)(2,1)S(1)} %get-tuple-element.70, bf16[64,1792]{1,0:T(8,128)(2,1)S(1)} %get-tuple-element.71, bf16[64,1792]{1,0:T(8,128)(2,1)S(1)} %get-tuple-element.72, bf16[64,1792]{1,0:T(8,128)(2,1)S(1)} %get-tuple-element.69, f32[4096,64]{0,1:T(8,128)S(1)} %copy-done, ...), kind=kOutput, calls=%fused_computation.1 | convolution fusion | flops 244056064 | bytes 15630340 | tf_op jit(solution)/shard_map/dot_general | solution.py:101
  178.8 2.9 %collective-permute-done.36 = bf16[64,2048]{1,0:T(8,128)(2,1)S(1)} collective-permute-done((bf16[64,2048]{1,0:T(8,128)(2,1)S(1)}, bf16[64,2048]{1,0:T(8,128)(2,1)S(1)}, u32[]{:S(2)}, u32[]{:S(2)}) %collective-permute-start.36) | collective-permute-done | bytes 262176 | tf_op jit(solution)/shard_map/ppermute | solution.py:41
  (175 shorter events, 57.5 us)
Async XLA Ops:
  2.3 13.5 %collective-permute-start.1 = (bf16[128,1792]{1,0:T(8,128)(2,1)S(1)}, bf16[128,1792]{1,0:T(8,128)(2,1)S(1)}, u32[]{:S(2)}, u32[]{:S(2)}) collective-permute-start(bf16[128,1792]{1,0:T(8,128)(2,1)S(1)} %get-tuple-element.60), channel_id=1, source_target_pairs={{0,2},{2,0},{4,6},{6,4},{8,10},{10,8},{12,14},{14,12},{16,18},{18,... | collective-permute-start | bytes 1376264 | tf_op jit(solution)/shard_map/ppermute | solution.py:35
  19.4 26.1 %collective-permute-start.4 = (bf16[256,1792]{1,0:T(8,128)(2,1)}, bf16[256,1792]{1,0:T(8,128)(2,1)}, u32[]{:S(2)}, u32[]{:S(2)}) collective-permute-start(bf16[256,1792]{1,0:T(8,128)(2,1)} %pad_maximum_fusion.refs_1_), channel_id=1, source_target_pairs={{0,8},{2,10},{4,12},{6,14},{8,0},{10,2},{12,4},{14,6},{16,24},{18,... | collective-permute-start | bytes 2752520 | tf_op jit(solution)/shard_map/ppermute | solution.py:41
  24.5 30.6 %collective-permute-start.9 = (bf16[256,1792]{1,0:T(8,128)(2,1)}, bf16[256,1792]{1,0:T(8,128)(2,1)S(1)}, u32[]{:S(2)}, u32[]{:S(2)}) collective-permute-start(bf16[256,1792]{1,0:T(8,128)(2,1)} %pad_maximum_fusion.refs_1_), channel_id=1, source_target_pairs={{8,16},{10,18},{12,20},{14,22},{16,8},{18,10},{20,12},{22,14},{9,1... | collective-permute-start | bytes 2752520 | tf_op jit(solution)/shard_map/ppermute | solution.py:41
  35.5 17.3 %collective-permute-start.7 = (bf16[128,1792]{1,0:T(8,128)(2,1)}, bf16[128,1792]{1,0:T(8,128)(2,1)S(1)}, u32[]{:S(2)}, u32[]{:S(2)}) collective-permute-start(bf16[128,1792]{1,0:T(8,128)(2,1)} %collective-permute-done.5.refs_2_), channel_id=1, source_target_pairs={{0,8},{2,10},{4,12},{6,14},{8,0},{10,2},{12,4},{14,6},{16,24},{18,... | collective-permute-start | bytes 1376264 | tf_op jit(solution)/shard_map/ppermute | solution.py:41
  38.8 19.5 %collective-permute-start.10 = (bf16[256,1792]{1,0:T(8,128)(2,1)S(1)}, bf16[256,1792]{1,0:T(8,128)(2,1)S(1)}, u32[]{:S(2)}, u32[]{:S(2)}) collective-permute-start(bf16[256,1792]{1,0:T(8,128)(2,1)S(1)} %get-tuple-element.32), channel_id=1, source_target_pairs={{0,2},{2,0},{4,6},{6,4},{8,10},{10,8},{12,14},{14,12},{16,18},{18,... | collective-permute-start | bytes 2752520 | tf_op jit(solution)/shard_map/ppermute | solution.py:35
  45.6 17.8 %collective-permute-start.12 = (bf16[256,1792]{1,0:T(8,128)(2,1)S(1)}, bf16[256,1792]{1,0:T(8,128)(2,1)S(1)}, u32[]{:S(2)}, u32[]{:S(2)}) collective-permute-start(bf16[256,1792]{1,0:T(8,128)(2,1)S(1)} %get-tuple-element.33), channel_id=1, source_target_pairs={{0,4},{2,6},{4,0},{6,2},{8,12},{10,14},{12,8},{14,10},{16,20},{18,... | collective-permute-start | bytes 2752520 | tf_op jit(solution)/shard_map/ppermute | solution.py:35
  54.4 16.1 %collective-permute-start.8 = (bf16[512,896]{1,0:T(8,128)(2,1)S(1)}, bf16[512,896]{1,0:T(8,128)(2,1)S(1)}, u32[]{:S(2)}, u32[]{:S(2)}) collective-permute-start(bf16[512,896]{1,0:T(8,128)(2,1)S(1)} %pad_maximum_fusion.1), channel_id=1, source_target_pairs={{8,16},{10,18},{12,20},{14,22},{16,8},{18,10},{20,12},{22,14},{9,1... | collective-permute-start | bytes 2752520 | tf_op jit(solution)/shard_map/ppermute | solution.py:41
  59.5 21.0 %collective-permute-start.11 = (bf16[512,896]{1,0:T(8,128)(2,1)S(1)}, bf16[512,896]{1,0:T(8,128)(2,1)S(1)}, u32[]{:S(2)}, u32[]{:S(2)}) collective-permute-start(bf16[512,896]{1,0:T(8,128)(2,1)S(1)} %maximum_select_fusion), channel_id=1, source_target_pairs={{0,8},{2,10},{4,12},{6,14},{8,0},{10,2},{12,4},{14,6},{16,24},{18,... | collective-permute-start | bytes 2752520 | tf_op jit(solution)/shard_map/ppermute | solution.py:41
  63.4 20.3 %collective-permute-start.13 = (bf16[256,1792]{1,0:T(8,128)(2,1)S(1)}, bf16[256,1792]{1,0:T(8,128)(2,1)S(1)}, u32[]{:S(2)}, u32[]{:S(2)}) collective-permute-start(bf16[256,1792]{1,0:T(8,128)(2,1)S(1)} %get-tuple-element.34), channel_id=1, source_target_pairs={{0,6},{2,4},{4,2},{6,0},{8,14},{10,12},{12,10},{14,8},{16,22},{18,... | collective-permute-start | bytes 2752520 | tf_op jit(solution)/shard_map/ppermute | solution.py:35
  68.3 16.5 %collective-permute-start.15 = (bf16[128,64]{1,0:T(8,128)(2,1)S(1)}, bf16[128,64]{1,0:T(8,128)(2,1)S(1)}, u32[]{:S(2)}, u32[]{:S(2)}) collective-permute-start(bf16[128,64]{1,0:T(8,128)(2,1)S(1)} %all_gather.3), channel_id=1, source_target_pairs={{0,2},{2,0},{4,6},{6,4},{8,10},{10,8},{12,14},{14,12},{16,18},{18,... | collective-permute-start | bytes 49160 | tf_op jit(solution)/shard_map/ppermute | solution.py:35
  68.9 16.0 %collective-permute-start.16 = (bf16[128,64]{1,0:T(8,128)(2,1)S(1)}, bf16[128,64]{1,0:T(8,128)(2,1)S(1)}, u32[]{:S(2)}, u32[]{:S(2)}) collective-permute-start(bf16[128,64]{1,0:T(8,128)(2,1)S(1)} %all_gather.3), channel_id=1, source_target_pairs={{0,4},{2,6},{4,0},{6,2},{8,12},{10,14},{12,8},{14,10},{16,20},{18,... | collective-permute-start | bytes 49160 | tf_op jit(solution)/shard_map/ppermute | solution.py:35
  70.4 14.5 %collective-permute-start.17 = (bf16[128,64]{1,0:T(8,128)(2,1)S(1)}, bf16[128,64]{1,0:T(8,128)(2,1)S(1)}, u32[]{:S(2)}, u32[]{:S(2)}) collective-permute-start(bf16[128,64]{1,0:T(8,128)(2,1)S(1)} %all_gather.3), channel_id=1, source_target_pairs={{0,6},{2,4},{4,2},{6,0},{8,14},{10,12},{12,10},{14,8},{16,22},{18,... | collective-permute-start | bytes 49160 | tf_op jit(solution)/shard_map/ppermute | solution.py:35
  81.4 25.4 %collective-permute-start.14 = (bf16[256,896]{1,0:T(8,128)(2,1)}, bf16[256,896]{1,0:T(8,128)(2,1)}, u32[]{:S(2)}, u32[]{:S(2)}) collective-permute-start(bf16[256,896]{1,0:T(8,128)(2,1)} %get-tuple-element.37), channel_id=1, source_target_pairs={{8,16},{10,18},{12,20},{14,22},{16,8},{18,10},{20,12},{22,14},{9,1... | collective-permute-start | bytes 1376264 | tf_op jit(solution)/shard_map/ppermute | solution.py:41
  84.9 21.9 %collective-permute-start.18 = (bf16[256,896]{1,0:T(8,128)(2,1)}, bf16[256,896]{1,0:T(8,128)(2,1)}, u32[]{:S(2)}, u32[]{:S(2)}) collective-permute-start(bf16[256,896]{1,0:T(8,128)(2,1)} %get-tuple-element.39), channel_id=1, source_target_pairs={{0,8},{2,10},{4,12},{6,14},{8,0},{10,2},{12,4},{14,6},{16,24},{18,... | collective-permute-start | bytes 1376264 | tf_op jit(solution)/shard_map/ppermute | solution.py:41
  106.9 12.9 %collective-permute-start.28 = (bf16[256,896]{1,0:T(8,128)(2,1)S(1)}, bf16[256,896]{1,0:T(8,128)(2,1)S(1)}, u32[]{:S(2)}, u32[]{:S(2)}) collective-permute-start(bf16[256,896]{1,0:T(8,128)(2,1)S(1)} %copy-done.34), channel_id=1, source_target_pairs={{0,8},{2,10},{4,12},{6,14},{8,0},{10,2},{12,4},{14,6},{16,24},{18,... | collective-permute-start | bytes 1376264 | tf_op jit(solution)/shard_map/ppermute | solution.py:41
  107.0 14.1 %collective-permute-start.29 = (bf16[256,896]{1,0:T(8,128)(2,1)S(1)}, bf16[256,896]{1,0:T(8,128)(2,1)S(1)}, u32[]{:S(2)}, u32[]{:S(2)}) collective-permute-start(bf16[256,896]{1,0:T(8,128)(2,1)S(1)} %copy-done.33), channel_id=1, source_target_pairs={{8,16},{10,18},{12,20},{14,22},{16,8},{18,10},{20,12},{22,14},{9,1... | collective-permute-start | bytes 1376264 | tf_op jit(solution)/shard_map/ppermute | solution.py:41
  111.1 20.2 %collective-permute-start.22 = (bf16[64,3072]{1,0:T(8,128)(2,1)S(1)}, bf16[64,3072]{1,0:T(8,128)(2,1)S(1)}, u32[]{:S(2)}, u32[]{:S(2)}) collective-permute-start(bf16[64,3072]{1,0:T(8,128)(2,1)S(1)} %get-tuple-element.67), channel_id=1, source_target_pairs={{0,6},{2,4},{4,2},{6,0},{8,14},{10,12},{12,10},{14,8},{16,22},{18,... | collective-permute-start | bytes 1179656 | tf_op jit(solution)/shard_map/ppermute | solution.py:35
  111.1 20.1 %collective-permute-start.21 = (bf16[64,3072]{1,0:T(8,128)(2,1)S(1)}, bf16[64,3072]{1,0:T(8,128)(2,1)S(1)}, u32[]{:S(2)}, u32[]{:S(2)}) collective-permute-start(bf16[64,3072]{1,0:T(8,128)(2,1)S(1)} %get-tuple-element.68), channel_id=1, source_target_pairs={{0,4},{2,6},{4,0},{6,2},{8,12},{10,14},{12,8},{14,10},{16,20},{18,... | collective-permute-start | bytes 1179656 | tf_op jit(solution)/shard_map/ppermute | solution.py:35
  111.2 20.0 %collective-permute-start.20 = (bf16[64,3072]{1,0:T(8,128)(2,1)S(1)}, bf16[64,3072]{1,0:T(8,128)(2,1)S(1)}, u32[]{:S(2)}, u32[]{:S(2)}) collective-permute-start(bf16[64,3072]{1,0:T(8,128)(2,1)S(1)} %get-tuple-element.66), channel_id=1, source_target_pairs={{0,2},{2,0},{4,6},{6,4},{8,10},{10,8},{12,14},{14,12},{16,18},{18,... | collective-permute-start | bytes 1179656 | tf_op jit(solution)/shard_map/ppermute | solution.py:35
  135.8 22.4 %collective-permute-start.24 = (bf16[64,1792]{1,0:T(8,128)(2,1)S(1)}, bf16[64,1792]{1,0:T(8,128)(2,1)S(1)}, u32[]{:S(2)}, u32[]{:S(2)}) collective-permute-start(bf16[64,1792]{1,0:T(8,128)(2,1)S(1)} %get-tuple-element.91), channel_id=1, source_target_pairs={{0,16},{2,18},{4,20},{6,22},{8,24},{10,26},{12,28},{14,30},{16,0},... | collective-permute-start | bytes 688136 | tf_op jit(solution)/shard_map/ppermute | solution.py:41
  137.5 20.7 %collective-permute-start.23 = (bf16[64,1792]{1,0:T(8,128)(2,1)S(1)}, bf16[64,1792]{1,0:T(8,128)(2,1)S(1)}, u32[]{:S(2)}, u32[]{:S(2)}) collective-permute-start(bf16[64,1792]{1,0:T(8,128)(2,1)S(1)} %get-tuple-element.91), channel_id=1, source_target_pairs={{0,8},{2,10},{4,12},{6,14},{8,0},{10,2},{12,4},{14,6},{16,24},{18,... | collective-permute-start | bytes 688136 | tf_op jit(solution)/shard_map/ppermute | solution.py:41
  140.3 20.4 %collective-permute-start.33 = (bf16[64,3072]{1,0:T(8,128)(2,1)S(1)}, bf16[64,3072]{1,0:T(8,128)(2,1)S(1)}, u32[]{:S(2)}, u32[]{:S(2)}) collective-permute-start(bf16[64,3072]{1,0:T(8,128)(2,1)S(1)} %get-tuple-element.64), channel_id=1, source_target_pairs={{0,6},{2,4},{4,2},{6,0},{8,14},{10,12},{12,10},{14,8},{16,22},{18,... | collective-permute-start | bytes 1179656 | tf_op jit(solution)/shard_map/ppermute | solution.py:35
  141.1 20.9 %collective-permute-start.32 = (bf16[64,3072]{1,0:T(8,128)(2,1)S(1)}, bf16[64,3072]{1,0:T(8,128)(2,1)S(1)}, u32[]{:S(2)}, u32[]{:S(2)}) collective-permute-start(bf16[64,3072]{1,0:T(8,128)(2,1)S(1)} %get-tuple-element.65), channel_id=1, source_target_pairs={{0,4},{2,6},{4,0},{6,2},{8,12},{10,14},{12,8},{14,10},{16,20},{18,... | collective-permute-start | bytes 1179656 | tf_op jit(solution)/shard_map/ppermute | solution.py:35
  144.0 17.9 %collective-permute-start.31 = (bf16[64,3072]{1,0:T(8,128)(2,1)S(1)}, bf16[64,3072]{1,0:T(8,128)(2,1)S(1)}, u32[]{:S(2)}, u32[]{:S(2)}) collective-permute-start(bf16[64,3072]{1,0:T(8,128)(2,1)S(1)} %get-tuple-element.63), channel_id=1, source_target_pairs={{0,2},{2,0},{4,6},{6,4},{8,10},{10,8},{12,14},{14,12},{16,18},{18,... | collective-permute-start | bytes 1179656 | tf_op jit(solution)/shard_map/ppermute | solution.py:35
  (54 other events, 497.9 us)

commit v11 on v10

--- a/solution.py
+++ b/solution.py
@@ -290,7 +290,7 @@
     z1 = end_swap(y1)
     z3 = mid_swap(early)
     z2 = lay.levels(early, 2, (0, 3))
-    late, early_other = after((late, early_other), z1, z2, z3)
+    late, early_other = after((late, early_other), z2, z3)
     z2b = mid_swap(early_other)
     z_late = lay.levels(jnp.concatenate([late, late_other], 1), 2, (1, 2))
     z3b = lay.levels(late, 3, (0, 3))

time: 184 us -> 184 us (level)
    ppermute x21, waiting for transfers between devices: 46.8 us -> 44.1 us  [levels(): return lax.ppermute(x, 'dp', pairs)]
    ppermute x18, starting transfers between devices: 18.4 us -> 20.3 us  [across(): return lax.ppermute(x, 'dp', [(d, d ^ r) for d in range(self.replicas)])]
where the time goes in v11:
time: 184 us; the launch traced here: 183 us
  waiting for transfers between devices  71.8 us (39%)
  starting transfers between devices  56 us (30%)
  Pallas kernels  18.5 us (10%)
  local copies, waits for them, and re-layouts  15.3 us (8%)
  other arithmetic  11.1 us (6%)
  matrix products  7.02 us (4%)
    ppermute x21, waiting for transfers between devices, levels(): return lax.ppermute(x, 'dp', pairs)  44.1 us
    ppermute x21, starting transfers between devices, levels(): return lax.ppermute(x, 'dp', pairs)  35.5 us
    ppermute x18, waiting for transfers between devices, across(): return lax.ppermute(x, 'dp', [(d, d ^ r) for d in range(self.replicas)])  25.3 us
    ppermute x18, starting transfers between devices, across(): return lax.ppermute(x, 'dp', [(d, d ^ r) for d in range(self.replicas)])  20.3 us
    pallas_call x2, Pallas kernels, products(): pl.pallas_call(kernel, out_shape=(out, out), in_specs=[pl.BlockSpec(memor...  18.5 us
    unnamed x74, local copies, waits for them, and re-layouts  8.43 us
    select_n x4, other arithmetic, line_of_four(): send = lambda a, w: jnp.where(inner, a, w)  4.45 us
    dot_general x1, matrix products, updated(): update = jnp.dot(basis_rows.astype(bf16), panel, preferred_element_type=f32)  4.35 us
  transfers between devices with their start and end apart: 41, of which 17 were waited for; matrix products, arithmetic and copies ran while one was open for 12% of the time, Pallas kernels for 10%

profile of v11, /device:TPU:0, one launch (start us, length us, event | category | flops | bytes accessed | tf_op | source)
XLA Modules:
  0.0 183.0 jit_solution(7036345814609473869)
XLA Ops:
  2.3 3.0 %collective-permute-start.1 = (bf16[128,1792]{1,0:T(8,128)(2,1)S(1)}, bf16[128,1792]{1,0:T(8,128)(2,1)S(1)}, u32[]{:S(2)}, u32[]{:S(2)}) collective-permute-start(bf16[128,1792]{1,0:T(8,128)(2,1)S(1)} %get-tuple-element.60), channel_id=1, source_target_pairs={{0,2},{2,0},{4,6},{6,4},{8,10},{10,8},{12,14},{14,12},{16,18},{18,... | collective-permute-start | bytes 1376264 | tf_op jit(solution)/shard_map/ppermute | solution.py:35
  9.1 6.7 %collective-permute-done.1 = bf16[128,1792]{1,0:T(8,128)(2,1)S(1)} collective-permute-done((bf16[128,1792]{1,0:T(8,128)(2,1)S(1)}, bf16[128,1792]{1,0:T(8,128)(2,1)S(1)}, u32[]{:S(2)}, u32[]{:S(2)}) %collective-permute-start.1) | collective-permute-done | bytes 458784 | tf_op jit(solution)/shard_map/ppermute | solution.py:35
  19.4 4.6 %collective-permute-start.4 = (bf16[256,1792]{1,0:T(8,128)(2,1)}, bf16[256,1792]{1,0:T(8,128)(2,1)}, u32[]{:S(2)}, u32[]{:S(2)}) collective-permute-start(bf16[256,1792]{1,0:T(8,128)(2,1)} %pad_maximum_fusion.refs_1_), channel_id=1, source_target_pairs={{0,8},{2,10},{4,12},{6,14},{8,0},{10,2},{12,4},{14,6},{16,24},{18,... | collective-permute-start | bytes 2752520 | tf_op jit(solution)/shard_map/ppermute | solution.py:41
  25.4 10.2 %collective-permute-done.5.refs_2_ = bf16[128,1792]{1,0:T(8,128)(2,1)} collective-permute-done((bf16[128,1792]{1,0:T(8,128)(2,1)S(1)}, bf16[128,1792]{1,0:T(8,128)(2,1)}, u32[]{:S(2)}, u32[]{:S(2)}) %collective-permute-start.5) | collective-permute-done | bytes 458784 | tf_op jit(solution)/shard_map/ppermute | solution.py:35
  36.5 2.3 %constant_dynamic-slice_fusion.1 = (bf16[256,1792]{1,0:T(8,128)(2,1)S(1)}, bf16[256,1792]{1,0:T(8,128)(2,1)S(1)}, bf16[256,1792]{1,0:T(8,128)(2,1)S(1)}, bf16[256,1792]{1,0:T(8,128)(2,1)S(1)}) fusion(bf16[256,7168]{1,0:T(8,128)(2,1)} %param.7, s32[]{:T(128)S(6)} %select_n.135, s32[]{:T(128)S(6)} %select_n.134, s32[]{:T(128)S(6)} %select_n.133, s32[]{:T(128)S(6)} %select_n.132), kind=kLoop, calls=%fused_computation.58 | loop fusion | bytes 7340048 | tf_op jit(solution)/shard_map/dynamic_slice | solution.py:45
  39.4 6.2 %collective-permute-done.4.refs_4_ = bf16[256,1792]{1,0:T(8,128)(2,1)} collective-permute-done((bf16[256,1792]{1,0:T(8,128)(2,1)}, bf16[256,1792]{1,0:T(8,128)(2,1)}, u32[]{:S(2)}, u32[]{:S(2)}) %collective-permute-start.4) | collective-permute-done | bytes 917536 | tf_op jit(solution)/shard_map/ppermute | solution.py:41
  47.3 5.6 %collective-permute-done.7.refs_5_ = bf16[128,1792]{1,0:T(8,128)(2,1)S(1)} collective-permute-done((bf16[128,1792]{1,0:T(8,128)(2,1)}, bf16[128,1792]{1,0:T(8,128)(2,1)S(1)}, u32[]{:S(2)}, u32[]{:S(2)}) %collective-permute-start.7) | collective-permute-done | bytes 458784 | tf_op jit(solution)/shard_map/ppermute | solution.py:41
  55.2 3.0 %collective-permute-done.10.refs_11_.refs_7_ = bf16[256,1792]{1,0:T(8,128)(2,1)S(1)} collective-permute-done((bf16[256,1792]{1,0:T(8,128)(2,1)S(1)}, bf16[256,1792]{1,0:T(8,128)(2,1)S(1)}, u32[]{:S(2)}, u32[]{:S(2)}) %collective-permute-start.10) | collective-permute-done | bytes 917536 | tf_op jit(solution)/shard_map/ppermute | solution.py:35
  59.5 3.9 %collective-permute-start.11 = (bf16[512,896]{1,0:T(8,128)(2,1)S(1)}, bf16[512,896]{1,0:T(8,128)(2,1)S(1)}, u32[]{:S(2)}, u32[]{:S(2)}) collective-permute-start(bf16[512,896]{1,0:T(8,128)(2,1)S(1)} %maximum_select_fusion), channel_id=1, source_target_pairs={{0,8},{2,10},{4,12},{6,14},{8,0},{10,2},{12,4},{14,6},{16,24},{18,... | collective-permute-start | bytes 2752520 | tf_op jit(solution)/shard_map/ppermute | solution.py:41
  63.4 2.4 %collective-permute-start.13 = (bf16[256,1792]{1,0:T(8,128)(2,1)S(1)}, bf16[256,1792]{1,0:T(8,128)(2,1)S(1)}, u32[]{:S(2)}, u32[]{:S(2)}) collective-permute-start(bf16[256,1792]{1,0:T(8,128)(2,1)S(1)} %get-tuple-element.34), channel_id=1, source_target_pairs={{0,6},{2,4},{4,2},{6,0},{8,14},{10,12},{12,10},{14,8},{16,22},{18,... | collective-permute-start | bytes 2752520 | tf_op jit(solution)/shard_map/ppermute | solution.py:35
  70.4 2.4 %collective-permute-start.17 = (bf16[128,64]{1,0:T(8,128)(2,1)S(1)}, bf16[128,64]{1,0:T(8,128)(2,1)S(1)}, u32[]{:S(2)}, u32[]{:S(2)}) collective-permute-start(bf16[128,64]{1,0:T(8,128)(2,1)S(1)} %all_gather.3), channel_id=1, source_target_pairs={{0,6},{2,4},{4,2},{6,0},{8,14},{10,12},{12,10},{14,8},{16,22},{18,... | collective-permute-start | bytes 49160 | tf_op jit(solution)/shard_map/ppermute | solution.py:35
  72.9 7.6 %collective-permute-done.11.refs_10_ = bf16[512,896]{1,0:T(8,128)(2,1)S(1)} collective-permute-done((bf16[512,896]{1,0:T(8,128)(2,1)S(1)}, bf16[512,896]{1,0:T(8,128)(2,1)S(1)}, u32[]{:S(2)}, u32[]{:S(2)}) %collective-permute-start.11) | collective-permute-done | bytes 917536 | tf_op jit(solution)/shard_map/ppermute | solution.py:41
  84.9 5.9 %collective-permute-start.18 = (bf16[256,896]{1,0:T(8,128)(2,1)}, bf16[256,896]{1,0:T(8,128)(2,1)}, u32[]{:S(2)}, u32[]{:S(2)}) collective-permute-start(bf16[256,896]{1,0:T(8,128)(2,1)} %get-tuple-element.39), channel_id=1, source_target_pairs={{0,8},{2,10},{4,12},{6,14},{8,0},{10,2},{12,4},{14,6},{16,24},{18,... | collective-permute-start | bytes 1376264 | tf_op jit(solution)/shard_map/ppermute | solution.py:41
  97.2 9.6 %shard_map.68 = (bf16[4,64,3072]{2,1,0:T(8,128)(2,1)S(1)}, bf16[4,64,3072]{2,1,0:T(8,128)(2,1)S(1)}) custom-call(s32[2]{0:T(128)S(1)} %pad_add_fusion.scalar_ref, bf16[128,1792]{1,0:T(8,128)(2,1)S(1)} %get-tuple-element.41.refs_0_, bf16[256,1792]{1,0:T(8,128)(2,1)} %pad_maximum_fusion.refs_1_, bf16[128,1792]{1,0:T(8,128)(2,1)} %collective-permute-done.5.refs_2_, ...), custom_call_target="tpu_custom_call" | custom-call | flops 1000000 | bytes 100000 | tf_op jit(solution)/shard_map/pallas_call | solution.py:179
  107.9 2.4 %collective-permute-done.19 = bf16[4,64,3072]{2,1,0:T(8,128)(2,1)S(1)} collective-permute-done((bf16[4,64,3072]{2,1,0:T(8,128)(2,1)S(1)}, bf16[4,64,3072]{2,1,0:T(8,128)(2,1)S(1)}, u32[]{:S(2)}, u32[]{:S(2)}) %collective-permute-start.19) | collective-permute-done | bytes 1572896 | tf_op jit(solution)/shard_map/ppermute | solution.py:204
  111.2 3.4 %collective-permute-start.20 = (bf16[64,3072]{1,0:T(8,128)(2,1)S(1)}, bf16[64,3072]{1,0:T(8,128)(2,1)S(1)}, u32[]{:S(2)}, u32[]{:S(2)}) collective-permute-start(bf16[64,3072]{1,0:T(8,128)(2,1)S(1)} %get-tuple-element.66), channel_id=1, source_target_pairs={{0,2},{2,0},{4,6},{6,4},{8,10},{10,8},{12,14},{14,12},{16,18},{18,... | collective-permute-start | bytes 1179656 | tf_op jit(solution)/shard_map/ppermute | solution.py:35
  114.6 5.3 %collective-permute-done.28.refs_12_ = bf16[256,896]{1,0:T(8,128)(2,1)S(1)} collective-permute-done((bf16[256,896]{1,0:T(8,128)(2,1)S(1)}, bf16[256,896]{1,0:T(8,128)(2,1)S(1)}, u32[]{:S(2)}, u32[]{:S(2)}) %collective-permute-start.28) | collective-permute-done | bytes 458784 | tf_op jit(solution)/shard_map/ppermute | solution.py:41
  121.2 8.9 %shard_map.69 = (bf16[4,64,3072]{2,1,0:T(8,128)(2,1)S(1)}, bf16[4,64,3072]{2,1,0:T(8,128)(2,1)}) custom-call(s32[2]{0:T(128)S(1)} %pad_add_fusion.scalar_ref, bf16[512,896]{1,0:T(8,128)(2,1)S(1)} %maximum_select_fusion.1.refs_0_, bf16[256,896]{1,0:T(8,128)(2,1)} %collective-permute-done.14.refs_1_, bf16[256,896]{1,0:T(8,128)(2,1)S(1)} %collective-permute-done.29.refs_2_, ...), custom_call_target="tpu_custom_call" | custom-call | flops 1000000 | bytes 100000 | tf_op jit(solution)/shard_map/pallas_call | solution.py:179
  138.1 2.1 %add_convert_fusion = bf16[4,64,3072]{2,1,0:T(8,128)(2,1)S(1)} fusion(bf16[4,64,3072]{2,1,0:T(8,128)(2,1)} %collective-permute-done.30, bf16[4,64,3072]{2,1,0:T(8,128)(2,1)S(1)} %copy-done.22), kind=kLoop, calls=%fused_computation.2 | loop fusion | flops 3145728 | bytes 4718592 | tf_op jit(solution)/shard_map/convert_element_type | solution.py:273
  141.7 2.4 %collective-permute-done.25 = bf16[64,1792]{1,0:T(8,128)(2,1)S(1)} collective-permute-done((bf16[64,1792]{1,0:T(8,128)(2,1)S(1)}, bf16[64,1792]{1,0:T(8,128)(2,1)S(1)}, u32[]{:S(2)}, u32[]{:S(2)}) %collective-permute-start.25) | collective-permute-done | bytes 229408 | tf_op jit(solution)/shard_map/ppermute | solution.py:41
  144.0 14.1 %collective-permute-done.24 = bf16[64,1792]{1,0:T(8,128)(2,1)S(1)} collective-permute-done((bf16[64,1792]{1,0:T(8,128)(2,1)S(1)}, bf16[64,1792]{1,0:T(8,128)(2,1)S(1)}, u32[]{:S(2)}, u32[]{:S(2)}) %collective-permute-start.24) | collective-permute-done | bytes 229408 | tf_op jit(solution)/shard_map/ppermute | solution.py:41
  165.9 4.0 %collective-permute-start.37 = (bf16[64,1024]{1,0:T(8,128)(2,1)S(1)}, bf16[64,1024]{1,0:T(8,128)(2,1)S(1)}, u32[]{:S(2)}, u32[]{:S(2)}) collective-permute-start(bf16[64,1024]{1,0:T(8,128)(2,1)S(1)} %get-tuple-element.50), channel_id=1, source_target_pairs={{0,24},{2,26},{4,28},{6,30},{24,0},{26,2},{28,4},{30,6},{1,25},{3,... | collective-permute-start | bytes 393224 | tf_op jit(solution)/shard_map/ppermute | solution.py:41
  175.1 4.3 %fusion = f32[256,7168]{1,0:T(8,128)} fusion(f32[256,7168]{1,0:T(8,128)S(1)} %bitcast.47, bf16[64,1792]{1,0:T(8,128)(2,1)S(1)} %get-tuple-element.70, bf16[64,1792]{1,0:T(8,128)(2,1)S(1)} %get-tuple-element.71, bf16[64,1792]{1,0:T(8,128)(2,1)S(1)} %get-tuple-element.72, bf16[64,1792]{1,0:T(8,128)(2,1)S(1)} %get-tuple-element.69, f32[4096,64]{0,1:T(8,128)S(1)} %copy-done, ...), kind=kOutput, calls=%fused_computation.1 | convolution fusion | flops 244056064 | bytes 15630340 | tf_op jit(solution)/shard_map/dot_general | solution.py:101
  179.5 2.5 %collective-permute-done.36 = bf16[64,2048]{1,0:T(8,128)(2,1)S(1)} collective-permute-done((bf16[64,2048]{1,0:T(8,128)(2,1)S(1)}, bf16[64,2048]{1,0:T(8,128)(2,1)S(1)}, u32[]{:S(2)}, u32[]{:S(2)}) %collective-permute-start.36) | collective-permute-done | bytes 262176 | tf_op jit(solution)/shard_map/ppermute | solution.py:41
  (175 shorter events, 58.8 us)
Async XLA Ops:
  19.4 26.1 %collective-permute-start.4 = (bf16[256,1792]{1,0:T(8,128)(2,1)}, bf16[256,1792]{1,0:T(8,128)(2,1)}, u32[]{:S(2)}, u32[]{:S(2)}) collective-permute-start(bf16[256,1792]{1,0:T(8,128)(2,1)} %pad_maximum_fusion.refs_1_), channel_id=1, source_target_pairs={{0,8},{2,10},{4,12},{6,14},{8,0},{10,2},{12,4},{14,6},{16,24},{18,... | collective-permute-start | bytes 2752520 | tf_op jit(solution)/shard_map/ppermute | solution.py:41
  24.5 30.6 %collective-permute-start.9 = (bf16[256,1792]{1,0:T(8,128)(2,1)}, bf16[256,1792]{1,0:T(8,128)(2,1)S(1)}, u32[]{:S(2)}, u32[]{:S(2)}) collective-permute-start(bf16[256,1792]{1,0:T(8,128)(2,1)} %pad_maximum_fusion.refs_1_), channel_id=1, source_target_pairs={{8,16},{10,18},{12,20},{14,22},{16,8},{18,10},{20,12},{22,14},{9,1... | collective-permute-start | bytes 2752520 | tf_op jit(solution)/shard_map/ppermute | solution.py:41
  35.5 17.3 %collective-permute-start.7 = (bf16[128,1792]{1,0:T(8,128)(2,1)}, bf16[128,1792]{1,0:T(8,128)(2,1)S(1)}, u32[]{:S(2)}, u32[]{:S(2)}) collective-permute-start(bf16[128,1792]{1,0:T(8,128)(2,1)} %collective-permute-done.5.refs_2_), channel_id=1, source_target_pairs={{0,8},{2,10},{4,12},{6,14},{8,0},{10,2},{12,4},{14,6},{16,24},{18,... | collective-permute-start | bytes 1376264 | tf_op jit(solution)/shard_map/ppermute | solution.py:41
  38.8 19.5 %collective-permute-start.10 = (bf16[256,1792]{1,0:T(8,128)(2,1)S(1)}, bf16[256,1792]{1,0:T(8,128)(2,1)S(1)}, u32[]{:S(2)}, u32[]{:S(2)}) collective-permute-start(bf16[256,1792]{1,0:T(8,128)(2,1)S(1)} %get-tuple-element.32), channel_id=1, source_target_pairs={{0,2},{2,0},{4,6},{6,4},{8,10},{10,8},{12,14},{14,12},{16,18},{18,... | collective-permute-start | bytes 2752520 | tf_op jit(solution)/shard_map/ppermute | solution.py:35
  45.6 17.8 %collective-permute-start.12 = (bf16[256,1792]{1,0:T(8,128)(2,1)S(1)}, bf16[256,1792]{1,0:T(8,128)(2,1)S(1)}, u32[]{:S(2)}, u32[]{:S(2)}) collective-permute-start(bf16[256,1792]{1,0:T(8,128)(2,1)S(1)} %get-tuple-element.33), channel_id=1, source_target_pairs={{0,4},{2,6},{4,0},{6,2},{8,12},{10,14},{12,8},{14,10},{16,20},{18,... | collective-permute-start | bytes 2752520 | tf_op jit(solution)/shard_map/ppermute | solution.py:35
  54.4 16.1 %collective-permute-start.8 = (bf16[512,896]{1,0:T(8,128)(2,1)S(1)}, bf16[512,896]{1,0:T(8,128)(2,1)S(1)}, u32[]{:S(2)}, u32[]{:S(2)}) collective-permute-start(bf16[512,896]{1,0:T(8,128)(2,1)S(1)} %pad_maximum_fusion.1), channel_id=1, source_target_pairs={{8,16},{10,18},{12,20},{14,22},{16,8},{18,10},{20,12},{22,14},{9,1... | collective-permute-start | bytes 2752520 | tf_op jit(solution)/shard_map/ppermute | solution.py:41
  59.5 21.0 %collective-permute-start.11 = (bf16[512,896]{1,0:T(8,128)(2,1)S(1)}, bf16[512,896]{1,0:T(8,128)(2,1)S(1)}, u32[]{:S(2)}, u32[]{:S(2)}) collective-permute-start(bf16[512,896]{1,0:T(8,128)(2,1)S(1)} %maximum_select_fusion), channel_id=1, source_target_pairs={{0,8},{2,10},{4,12},{6,14},{8,0},{10,2},{12,4},{14,6},{16,24},{18,... | collective-permute-start | bytes 2752520 | tf_op jit(solution)/shard_map/ppermute | solution.py:41
  63.4 20.3 %collective-permute-start.13 = (bf16[256,1792]{1,0:T(8,128)(2,1)S(1)}, bf16[256,1792]{1,0:T(8,128)(2,1)S(1)}, u32[]{:S(2)}, u32[]{:S(2)}) collective-permute-start(bf16[256,1792]{1,0:T(8,128)(2,1)S(1)} %get-tuple-element.34), channel_id=1, source_target_pairs={{0,6},{2,4},{4,2},{6,0},{8,14},{10,12},{12,10},{14,8},{16,22},{18,... | collective-permute-start | bytes 2752520 | tf_op jit(solution)/shard_map/ppermute | solution.py:35
  68.3 16.5 %collective-permute-start.15 = (bf16[128,64]{1,0:T(8,128)(2,1)S(1)}, bf16[128,64]{1,0:T(8,128)(2,1)S(1)}, u32[]{:S(2)}, u32[]{:S(2)}) collective-permute-start(bf16[128,64]{1,0:T(8,128)(2,1)S(1)} %all_gather.3), channel_id=1, source_target_pairs={{0,2},{2,0},{4,6},{6,4},{8,10},{10,8},{12,14},{14,12},{16,18},{18,... | collective-permute-start | bytes 49160 | tf_op jit(solution)/shard_map/ppermute | solution.py:35
  68.9 16.0 %collective-permute-start.16 = (bf16[128,64]{1,0:T(8,128)(2,1)S(1)}, bf16[128,64]{1,0:T(8,128)(2,1)S(1)}, u32[]{:S(2)}, u32[]{:S(2)}) collective-permute-start(bf16[128,64]{1,0:T(8,128)(2,1)S(1)} %all_gather.3), channel_id=1, source_target_pairs={{0,4},{2,6},{4,0},{6,2},{8,12},{10,14},{12,8},{14,10},{16,20},{18,... | collective-permute-start | bytes 49160 | tf_op jit(solution)/shard_map/ppermute | solution.py:35
  70.4 14.5 %collective-permute-start.17 = (bf16[128,64]{1,0:T(8,128)(2,1)S(1)}, bf16[128,64]{1,0:T(8,128)(2,1)S(1)}, u32[]{:S(2)}, u32[]{:S(2)}) collective-permute-start(bf16[128,64]{1,0:T(8,128)(2,1)S(1)} %all_gather.3), channel_id=1, source_target_pairs={{0,6},{2,4},{4,2},{6,0},{8,14},{10,12},{12,10},{14,8},{16,22},{18,... | collective-permute-start | bytes 49160 | tf_op jit(solution)/shard_map/ppermute | solution.py:35
  81.4 25.4 %collective-permute-start.14 = (bf16[256,896]{1,0:T(8,128)(2,1)}, bf16[256,896]{1,0:T(8,128)(2,1)}, u32[]{:S(2)}, u32[]{:S(2)}) collective-permute-start(bf16[256,896]{1,0:T(8,128)(2,1)} %get-tuple-element.37), channel_id=1, source_target_pairs={{8,16},{10,18},{12,20},{14,22},{16,8},{18,10},{20,12},{22,14},{9,1... | collective-permute-start | bytes 1376264 | tf_op jit(solution)/shard_map/ppermute | solution.py:41
  84.9 21.9 %collective-permute-start.18 = (bf16[256,896]{1,0:T(8,128)(2,1)}, bf16[256,896]{1,0:T(8,128)(2,1)}, u32[]{:S(2)}, u32[]{:S(2)}) collective-permute-start(bf16[256,896]{1,0:T(8,128)(2,1)} %get-tuple-element.39), channel_id=1, source_target_pairs={{0,8},{2,10},{4,12},{6,14},{8,0},{10,2},{12,4},{14,6},{16,24},{18,... | collective-permute-start | bytes 1376264 | tf_op jit(solution)/shard_map/ppermute | solution.py:41
  107.0 14.1 %collective-permute-start.29 = (bf16[256,896]{1,0:T(8,128)(2,1)S(1)}, bf16[256,896]{1,0:T(8,128)(2,1)S(1)}, u32[]{:S(2)}, u32[]{:S(2)}) collective-permute-start(bf16[256,896]{1,0:T(8,128)(2,1)S(1)} %copy-done.33), channel_id=1, source_target_pairs={{8,16},{10,18},{12,20},{14,22},{16,8},{18,10},{20,12},{22,14},{9,1... | collective-permute-start | bytes 1376264 | tf_op jit(solution)/shard_map/ppermute | solution.py:41
  111.1 20.2 %collective-permute-start.22 = (bf16[64,3072]{1,0:T(8,128)(2,1)S(1)}, bf16[64,3072]{1,0:T(8,128)(2,1)S(1)}, u32[]{:S(2)}, u32[]{:S(2)}) collective-permute-start(bf16[64,3072]{1,0:T(8,128)(2,1)S(1)} %get-tuple-element.67), channel_id=1, source_target_pairs={{0,6},{2,4},{4,2},{6,0},{8,14},{10,12},{12,10},{14,8},{16,22},{18,... | collective-permute-start | bytes 1179656 | tf_op jit(solution)/shard_map/ppermute | solution.py:35
  111.1 20.1 %collective-permute-start.21 = (bf16[64,3072]{1,0:T(8,128)(2,1)S(1)}, bf16[64,3072]{1,0:T(8,128)(2,1)S(1)}, u32[]{:S(2)}, u32[]{:S(2)}) collective-permute-start(bf16[64,3072]{1,0:T(8,128)(2,1)S(1)} %get-tuple-element.68), channel_id=1, source_target_pairs={{0,4},{2,6},{4,0},{6,2},{8,12},{10,14},{12,8},{14,10},{16,20},{18,... | collective-permute-start | bytes 1179656 | tf_op jit(solution)/shard_map/ppermute | solution.py:35
  111.2 20.0 %collective-permute-start.20 = (bf16[64,3072]{1,0:T(8,128)(2,1)S(1)}, bf16[64,3072]{1,0:T(8,128)(2,1)S(1)}, u32[]{:S(2)}, u32[]{:S(2)}) collective-permute-start(bf16[64,3072]{1,0:T(8,128)(2,1)S(1)} %get-tuple-element.66), channel_id=1, source_target_pairs={{0,2},{2,0},{4,6},{6,4},{8,10},{10,8},{12,14},{14,12},{16,18},{18,... | collective-permute-start | bytes 1179656 | tf_op jit(solution)/shard_map/ppermute | solution.py:35
  135.8 22.4 %collective-permute-start.24 = (bf16[64,1792]{1,0:T(8,128)(2,1)S(1)}, bf16[64,1792]{1,0:T(8,128)(2,1)S(1)}, u32[]{:S(2)}, u32[]{:S(2)}) collective-permute-start(bf16[64,1792]{1,0:T(8,128)(2,1)S(1)} %get-tuple-element.91), channel_id=1, source_target_pairs={{0,16},{2,18},{4,20},{6,22},{8,24},{10,26},{12,28},{14,30},{16,0},... | collective-permute-start | bytes 688136 | tf_op jit(solution)/shard_map/ppermute | solution.py:41
  137.5 20.7 %collective-permute-start.23 = (bf16[64,1792]{1,0:T(8,128)(2,1)S(1)}, bf16[64,1792]{1,0:T(8,128)(2,1)S(1)}, u32[]{:S(2)}, u32[]{:S(2)}) collective-permute-start(bf16[64,1792]{1,0:T(8,128)(2,1)S(1)} %get-tuple-element.91), channel_id=1, source_target_pairs={{0,8},{2,10},{4,12},{6,14},{8,0},{10,2},{12,4},{14,6},{16,24},{18,... | collective-permute-start | bytes 688136 | tf_op jit(solution)/shard_map/ppermute | solution.py:41
  140.3 20.4 %collective-permute-start.33 = (bf16[64,3072]{1,0:T(8,128)(2,1)S(1)}, bf16[64,3072]{1,0:T(8,128)(2,1)S(1)}, u32[]{:S(2)}, u32[]{:S(2)}) collective-permute-start(bf16[64,3072]{1,0:T(8,128)(2,1)S(1)} %get-tuple-element.64), channel_id=1, source_target_pairs={{0,6},{2,4},{4,2},{6,0},{8,14},{10,12},{12,10},{14,8},{16,22},{18,... | collective-permute-start | bytes 1179656 | tf_op jit(solution)/shard_map/ppermute | solution.py:35
  141.1 20.9 %collective-permute-start.32 = (bf16[64,3072]{1,0:T(8,128)(2,1)S(1)}, bf16[64,3072]{1,0:T(8,128)(2,1)S(1)}, u32[]{:S(2)}, u32[]{:S(2)}) collective-permute-start(bf16[64,3072]{1,0:T(8,128)(2,1)S(1)} %get-tuple-element.65), channel_id=1, source_target_pairs={{0,4},{2,6},{4,0},{6,2},{8,12},{10,14},{12,8},{14,10},{16,20},{18,... | collective-permute-start | bytes 1179656 | tf_op jit(solution)/shard_map/ppermute | solution.py:35
  144.0 17.9 %collective-permute-start.31 = (bf16[64,3072]{1,0:T(8,128)(2,1)S(1)}, bf16[64,3072]{1,0:T(8,128)(2,1)S(1)}, u32[]{:S(2)}, u32[]{:S(2)}) collective-permute-start(bf16[64,3072]{1,0:T(8,128)(2,1)S(1)} %get-tuple-element.63), channel_id=1, source_target_pairs={{0,2},{2,0},{4,6},{6,4},{8,10},{10,8},{12,14},{14,12},{16,18},{18,... | collective-permute-start | bytes 1179656 | tf_op jit(solution)/shard_map/ppermute | solution.py:35
  160.7 18.7 %collective-permute-start.26 = (bf16[64,1024]{1,0:T(8,128)(2,1)S(1)}, bf16[64,1024]{1,0:T(8,128)(2,1)S(1)}, u32[]{:S(2)}, u32[]{:S(2)}) collective-permute-start(bf16[64,1024]{1,0:T(8,128)(2,1)S(1)} %get-tuple-element.42), channel_id=1, source_target_pairs={{0,8},{2,10},{4,12},{6,14},{8,0},{10,2},{12,4},{14,6},{16,24},{18,... | collective-permute-start | bytes 393224 | tf_op jit(solution)/shard_map/ppermute | solution.py:41
  165.9 13.6 %collective-permute-start.37 = (bf16[64,1024]{1,0:T(8,128)(2,1)S(1)}, bf16[64,1024]{1,0:T(8,128)(2,1)S(1)}, u32[]{:S(2)}, u32[]{:S(2)}) collective-permute-start(bf16[64,1024]{1,0:T(8,128)(2,1)S(1)} %get-tuple-element.50), channel_id=1, source_target_pairs={{0,24},{2,26},{4,28},{6,30},{24,0},{26,2},{28,4},{30,6},{1,25},{3,... | collective-permute-start | bytes 393224 | tf_op jit(solution)/shard_map/ppermute | solution.py:41
  (54 other events, 505.0 us)

commit v12 on v11

--- a/solution.py
+++ b/solution.py
@@ -216,7 +216,7 @@
     parts[1:3] = [across(after(parts[r], *plane), r) for r in (1, 2)]
     parts[3] = across(after(parts[3], *parts[1:3]), 3)
     joined = lambda x, c: jnp.concatenate([y[:, c] for y in x], 0)
-    near_e, near_m = [e0, after(e1, m2), e2], [m0, m1, m2]
+    near_e, near_m = [e0, after(e1, m1, m2), e2], [m0, m1, m2]
     e_high = joined(near_e, high)
     m_low = joined(near_m, low)
     far0 = mid_swap(joined(near_e, low))

time: 184 us -> 183 us (level)
  no operation moved by 1% of the time
where the time goes in v12:
time: 183 us; the launch traced here: 182 us
  waiting for transfers between devices  72.6 us (40%)
  starting transfers between devices  55.3 us (30%)
  Pallas kernels  18.4 us (10%)
  local copies, waits for them, and re-layouts  14.5 us (8%)
  other arithmetic  11.1 us (6%)
  matrix products  7.02 us (4%)
  blocking collectives  1.83 us (1%)
    ppermute x21, waiting for transfers between devices, levels(): return lax.ppermute(x, 'dp', pairs)  44 us
    ppermute x21, starting transfers between devices, levels(): return lax.ppermute(x, 'dp', pairs)  35.5 us
    ppermute x18, waiting for transfers between devices, across(): return lax.ppermute(x, 'dp', [(d, d ^ r) for d in range(self.replicas)])  26.1 us
    ppermute x18, starting transfers between devices, across(): return lax.ppermute(x, 'dp', [(d, d ^ r) for d in range(self.replicas)])  19.6 us
    pallas_call x2, Pallas kernels, products(): pl.pallas_call(kernel, out_shape=(out, out), in_specs=[pl.BlockSpec(memor...  18.4 us
    unnamed x74, local copies, waits for them, and re-layouts  7.6 us
    select_n x4, other arithmetic, line_of_four(): send = lambda a, w: jnp.where(inner, a, w)  4.45 us
    dot_general x1, matrix products, updated(): update = jnp.dot(basis_rows.astype(bf16), panel, preferred_element_type=f32)  4.35 us
  transfers between devices with their start and end apart: 41, of which 17 were waited for; matrix products, arithmetic and copies ran while one was open for 12% of the time, Pallas kernels for 10%

profile of v12, /device:TPU:0, one launch (start us, length us, event | category | flops | bytes accessed | tf_op | source)
XLA Modules:
  0.0 182.1 jit_solution(7408495175336507496)
XLA Ops:
  2.3 3.0 %collective-permute-start.1 = (bf16[128,1792]{1,0:T(8,128)(2,1)S(1)}, bf16[128,1792]{1,0:T(8,128)(2,1)S(1)}, u32[]{:S(2)}, u32[]{:S(2)}) collective-permute-start(bf16[128,1792]{1,0:T(8,128)(2,1)S(1)} %get-tuple-element.60), channel_id=1, source_target_pairs={{0,2},{2,0},{4,6},{6,4},{8,10},{10,8},{12,14},{14,12},{16,18},{18,... | collective-permute-start | bytes 1376264 | tf_op jit(solution)/shard_map/ppermute | solution.py:35
  9.1 6.7 %collective-permute-done.1 = bf16[128,1792]{1,0:T(8,128)(2,1)S(1)} collective-permute-done((bf16[128,1792]{1,0:T(8,128)(2,1)S(1)}, bf16[128,1792]{1,0:T(8,128)(2,1)S(1)}, u32[]{:S(2)}, u32[]{:S(2)}) %collective-permute-start.1) | collective-permute-done | bytes 458784 | tf_op jit(solution)/shard_map/ppermute | solution.py:35
  18.6 4.6 %collective-permute-start.4 = (bf16[256,1792]{1,0:T(8,128)(2,1)}, bf16[256,1792]{1,0:T(8,128)(2,1)}, u32[]{:S(2)}, u32[]{:S(2)}) collective-permute-start(bf16[256,1792]{1,0:T(8,128)(2,1)} %pad_maximum_fusion.refs_1_), channel_id=1, source_target_pairs={{0,8},{2,10},{4,12},{6,14},{8,0},{10,2},{12,4},{14,6},{16,24},{18,... | collective-permute-start | bytes 2752520 | tf_op jit(solution)/shard_map/ppermute | solution.py:41
  24.4 10.2 %collective-permute-done.6.refs_2_ = bf16[128,1792]{1,0:T(8,128)(2,1)} collective-permute-done((bf16[128,1792]{1,0:T(8,128)(2,1)S(1)}, bf16[128,1792]{1,0:T(8,128)(2,1)}, u32[]{:S(2)}, u32[]{:S(2)}) %collective-permute-start.6) | collective-permute-done | bytes 458784 | tf_op jit(solution)/shard_map/ppermute | solution.py:35
  36.4 2.3 %constant_dynamic-slice_fusion.1 = (bf16[256,1792]{1,0:T(8,128)(2,1)S(1)}, bf16[256,1792]{1,0:T(8,128)(2,1)S(1)}, bf16[256,1792]{1,0:T(8,128)(2,1)S(1)}, bf16[256,1792]{1,0:T(8,128)(2,1)S(1)}) fusion(bf16[256,7168]{1,0:T(8,128)(2,1)} %param.7, s32[]{:T(128)S(6)} %select_n.135, s32[]{:T(128)S(6)} %select_n.134, s32[]{:T(128)S(6)} %select_n.133, s32[]{:T(128)S(6)} %select_n.132), kind=kLoop, calls=%fused_computation.58 | loop fusion | bytes 7340048 | tf_op jit(solution)/shard_map/dynamic_slice | solution.py:45
  39.3 5.4 %collective-permute-done.4.refs_4_ = bf16[256,1792]{1,0:T(8,128)(2,1)} collective-permute-done((bf16[256,1792]{1,0:T(8,128)(2,1)}, bf16[256,1792]{1,0:T(8,128)(2,1)}, u32[]{:S(2)}, u32[]{:S(2)}) %collective-permute-start.4) | collective-permute-done | bytes 917536 | tf_op jit(solution)/shard_map/ppermute | solution.py:41
  46.5 5.5 %collective-permute-done.8.refs_5_ = bf16[128,1792]{1,0:T(8,128)(2,1)S(1)} collective-permute-done((bf16[128,1792]{1,0:T(8,128)(2,1)}, bf16[128,1792]{1,0:T(8,128)(2,1)S(1)}, u32[]{:S(2)}, u32[]{:S(2)}) %collective-permute-start.8) | collective-permute-done | bytes 458784 | tf_op jit(solution)/shard_map/ppermute | solution.py:41
  54.4 3.8 %collective-permute-done.10.refs_11_.refs_7_ = bf16[256,1792]{1,0:T(8,128)(2,1)S(1)} collective-permute-done((bf16[256,1792]{1,0:T(8,128)(2,1)S(1)}, bf16[256,1792]{1,0:T(8,128)(2,1)S(1)}, u32[]{:S(2)}, u32[]{:S(2)}) %collective-permute-start.10) | collective-permute-done | bytes 917536 | tf_op jit(solution)/shard_map/ppermute | solution.py:35
  59.4 3.8 %collective-permute-start.11 = (bf16[512,896]{1,0:T(8,128)(2,1)S(1)}, bf16[512,896]{1,0:T(8,128)(2,1)S(1)}, u32[]{:S(2)}, u32[]{:S(2)}) collective-permute-start(bf16[512,896]{1,0:T(8,128)(2,1)S(1)} %maximum_select_fusion), channel_id=1, source_target_pairs={{0,8},{2,10},{4,12},{6,14},{8,0},{10,2},{12,4},{14,6},{16,24},{18,... | collective-permute-start | bytes 2752520 | tf_op jit(solution)/shard_map/ppermute | solution.py:41
  63.2 2.4 %collective-permute-start.13 = (bf16[256,1792]{1,0:T(8,128)(2,1)S(1)}, bf16[256,1792]{1,0:T(8,128)(2,1)S(1)}, u32[]{:S(2)}, u32[]{:S(2)}) collective-permute-start(bf16[256,1792]{1,0:T(8,128)(2,1)S(1)} %get-tuple-element.34), channel_id=1, source_target_pairs={{0,6},{2,4},{4,2},{6,0},{8,14},{10,12},{12,10},{14,8},{16,22},{18,... | collective-permute-start | bytes 2752520 | tf_op jit(solution)/shard_map/ppermute | solution.py:35
  70.2 2.4 %collective-permute-start.17 = (bf16[128,64]{1,0:T(8,128)(2,1)S(1)}, bf16[128,64]{1,0:T(8,128)(2,1)S(1)}, u32[]{:S(2)}, u32[]{:S(2)}) collective-permute-start(bf16[128,64]{1,0:T(8,128)(2,1)S(1)} %all_gather.3), channel_id=1, source_target_pairs={{0,6},{2,4},{4,2},{6,0},{8,14},{10,12},{12,10},{14,8},{16,22},{18,... | collective-permute-start | bytes 49160 | tf_op jit(solution)/shard_map/ppermute | solution.py:35
  72.7 7.6 %collective-permute-done.11.refs_10_ = bf16[512,896]{1,0:T(8,128)(2,1)S(1)} collective-permute-done((bf16[512,896]{1,0:T(8,128)(2,1)S(1)}, bf16[512,896]{1,0:T(8,128)(2,1)S(1)}, u32[]{:S(2)}, u32[]{:S(2)}) %collective-permute-start.11) | collective-permute-done | bytes 917536 | tf_op jit(solution)/shard_map/ppermute | solution.py:41
  84.7 5.3 %collective-permute-start.18 = (bf16[256,896]{1,0:T(8,128)(2,1)}, bf16[256,896]{1,0:T(8,128)(2,1)}, u32[]{:S(2)}, u32[]{:S(2)}) collective-permute-start(bf16[256,896]{1,0:T(8,128)(2,1)} %get-tuple-element.39), channel_id=1, source_target_pairs={{0,8},{2,10},{4,12},{6,14},{8,0},{10,2},{12,4},{14,6},{16,24},{18,... | collective-permute-start | bytes 1376264 | tf_op jit(solution)/shard_map/ppermute | solution.py:41
  96.4 9.5 %shard_map.68 = (bf16[4,64,3072]{2,1,0:T(8,128)(2,1)S(1)}, bf16[4,64,3072]{2,1,0:T(8,128)(2,1)S(1)}) custom-call(s32[2]{0:T(128)S(1)} %pad_add_fusion.scalar_ref, bf16[128,1792]{1,0:T(8,128)(2,1)S(1)} %get-tuple-element.41.refs_0_, bf16[256,1792]{1,0:T(8,128)(2,1)} %pad_maximum_fusion.refs_1_, bf16[128,1792]{1,0:T(8,128)(2,1)} %collective-permute-done.6.refs_2_, ...), custom_call_target="tpu_custom_call" | custom-call | flops 1000000 | bytes 100000 | tf_op jit(solution)/shard_map/pallas_call | solution.py:179
  107.0 2.4 %collective-permute-done.19 = bf16[4,64,3072]{2,1,0:T(8,128)(2,1)S(1)} collective-permute-done((bf16[4,64,3072]{2,1,0:T(8,128)(2,1)S(1)}, bf16[4,64,3072]{2,1,0:T(8,128)(2,1)S(1)}, u32[]{:S(2)}, u32[]{:S(2)}) %collective-permute-start.19) | collective-permute-done | bytes 1572896 | tf_op jit(solution)/shard_map/ppermute | solution.py:204
  110.4 3.2 %collective-permute-start.20 = (bf16[64,3072]{1,0:T(8,128)(2,1)S(1)}, bf16[64,3072]{1,0:T(8,128)(2,1)S(1)}, u32[]{:S(2)}, u32[]{:S(2)}) collective-permute-start(bf16[64,3072]{1,0:T(8,128)(2,1)S(1)} %get-tuple-element.66), channel_id=1, source_target_pairs={{0,2},{2,0},{4,6},{6,4},{8,10},{10,8},{12,14},{14,12},{16,18},{18,... | collective-permute-start | bytes 1179656 | tf_op jit(solution)/shard_map/ppermute | solution.py:35
  113.7 5.3 %collective-permute-done.28.refs_12_ = bf16[256,896]{1,0:T(8,128)(2,1)S(1)} collective-permute-done((bf16[256,896]{1,0:T(8,128)(2,1)S(1)}, bf16[256,896]{1,0:T(8,128)(2,1)S(1)}, u32[]{:S(2)}, u32[]{:S(2)}) %collective-permute-start.28) | collective-permute-done | bytes 458784 | tf_op jit(solution)/shard_map/ppermute | solution.py:41
  120.2 8.9 %shard_map.69 = (bf16[4,64,3072]{2,1,0:T(8,128)(2,1)S(1)}, bf16[4,64,3072]{2,1,0:T(8,128)(2,1)}) custom-call(s32[2]{0:T(128)S(1)} %pad_add_fusion.scalar_ref, bf16[512,896]{1,0:T(8,128)(2,1)S(1)} %maximum_select_fusion.1.refs_0_, bf16[256,896]{1,0:T(8,128)(2,1)} %collective-permute-done.14.refs_1_, bf16[256,896]{1,0:T(8,128)(2,1)S(1)} %collective-permute-done.29.refs_2_, ...), custom_call_target="tpu_custom_call" | custom-call | flops 1000000 | bytes 100000 | tf_op jit(solution)/shard_map/pallas_call | solution.py:179
  137.2 2.1 %add_convert_fusion = bf16[4,64,3072]{2,1,0:T(8,128)(2,1)S(1)} fusion(bf16[4,64,3072]{2,1,0:T(8,128)(2,1)} %collective-permute-done.30, bf16[4,64,3072]{2,1,0:T(8,128)(2,1)S(1)} %copy-done.22), kind=kLoop, calls=%fused_computation.2 | loop fusion | flops 3145728 | bytes 4718592 | tf_op jit(solution)/shard_map/convert_element_type | solution.py:273
  140.7 2.4 %collective-permute-done.25 = bf16[64,1792]{1,0:T(8,128)(2,1)S(1)} collective-permute-done((bf16[64,1792]{1,0:T(8,128)(2,1)S(1)}, bf16[64,1792]{1,0:T(8,128)(2,1)S(1)}, u32[]{:S(2)}, u32[]{:S(2)}) %collective-permute-start.25) | collective-permute-done | bytes 229408 | tf_op jit(solution)/shard_map/ppermute | solution.py:41
  143.1 14.1 %collective-permute-done.24 = bf16[64,1792]{1,0:T(8,128)(2,1)S(1)} collective-permute-done((bf16[64,1792]{1,0:T(8,128)(2,1)S(1)}, bf16[64,1792]{1,0:T(8,128)(2,1)S(1)}, u32[]{:S(2)}, u32[]{:S(2)}) %collective-permute-start.24) | collective-permute-done | bytes 229408 | tf_op jit(solution)/shard_map/ppermute | solution.py:41
  164.9 4.0 %collective-permute-start.37 = (bf16[64,1024]{1,0:T(8,128)(2,1)S(1)}, bf16[64,1024]{1,0:T(8,128)(2,1)S(1)}, u32[]{:S(2)}, u32[]{:S(2)}) collective-permute-start(bf16[64,1024]{1,0:T(8,128)(2,1)S(1)} %get-tuple-element.50), channel_id=1, source_target_pairs={{0,24},{2,26},{4,28},{6,30},{24,0},{26,2},{28,4},{30,6},{1,25},{3,... | collective-permute-start | bytes 393224 | tf_op jit(solution)/shard_map/ppermute | solution.py:41
  174.2 4.3 %fusion = f32[256,7168]{1,0:T(8,128)} fusion(f32[256,7168]{1,0:T(8,128)S(1)} %bitcast.47, bf16[64,1792]{1,0:T(8,128)(2,1)S(1)} %get-tuple-element.70, bf16[64,1792]{1,0:T(8,128)(2,1)S(1)} %get-tuple-element.71, bf16[64,1792]{1,0:T(8,128)(2,1)S(1)} %get-tuple-element.72, bf16[64,1792]{1,0:T(8,128)(2,1)S(1)} %get-tuple-element.69, f32[4096,64]{0,1:T(8,128)S(1)} %copy-done, ...), kind=kOutput, calls=%fused_computation.1 | convolution fusion | flops 244056064 | bytes 15630340 | tf_op jit(solution)/shard_map/dot_general | solution.py:101
  178.6 2.5 %collective-permute-done.36 = bf16[64,2048]{1,0:T(8,128)(2,1)S(1)} collective-permute-done((bf16[64,2048]{1,0:T(8,128)(2,1)S(1)}, bf16[64,2048]{1,0:T(8,128)(2,1)S(1)}, u32[]{:S(2)}, u32[]{:S(2)}) %collective-permute-start.36) | collective-permute-done | bytes 262176 | tf_op jit(solution)/shard_map/ppermute | solution.py:41
  (175 shorter events, 58.7 us)
Async XLA Ops:
  18.6 26.2 %collective-permute-start.4 = (bf16[256,1792]{1,0:T(8,128)(2,1)}, bf16[256,1792]{1,0:T(8,128)(2,1)}, u32[]{:S(2)}, u32[]{:S(2)}) collective-permute-start(bf16[256,1792]{1,0:T(8,128)(2,1)} %pad_maximum_fusion.refs_1_), channel_id=1, source_target_pairs={{0,8},{2,10},{4,12},{6,14},{8,0},{10,2},{12,4},{14,6},{16,24},{18,... | collective-permute-start | bytes 2752520 | tf_op jit(solution)/shard_map/ppermute | solution.py:41
  23.7 22.8 %collective-permute-start.5 = (bf16[256,1792]{1,0:T(8,128)(2,1)}, bf16[256,1792]{1,0:T(8,128)(2,1)S(1)}, u32[]{:S(2)}, u32[]{:S(2)}) collective-permute-start(bf16[256,1792]{1,0:T(8,128)(2,1)} %pad_maximum_fusion.refs_1_), channel_id=1, source_target_pairs={{8,16},{10,18},{12,20},{14,22},{16,8},{18,10},{20,12},{22,14},{9,1... | collective-permute-start | bytes 2752520 | tf_op jit(solution)/shard_map/ppermute | solution.py:41
  34.7 17.4 %collective-permute-start.8 = (bf16[128,1792]{1,0:T(8,128)(2,1)}, bf16[128,1792]{1,0:T(8,128)(2,1)S(1)}, u32[]{:S(2)}, u32[]{:S(2)}) collective-permute-start(bf16[128,1792]{1,0:T(8,128)(2,1)} %collective-permute-done.6.refs_2_), channel_id=1, source_target_pairs={{0,8},{2,10},{4,12},{6,14},{8,0},{10,2},{12,4},{14,6},{16,24},{18,... | collective-permute-start | bytes 1376264 | tf_op jit(solution)/shard_map/ppermute | solution.py:41
  38.7 19.5 %collective-permute-start.10 = (bf16[256,1792]{1,0:T(8,128)(2,1)S(1)}, bf16[256,1792]{1,0:T(8,128)(2,1)S(1)}, u32[]{:S(2)}, u32[]{:S(2)}) collective-permute-start(bf16[256,1792]{1,0:T(8,128)(2,1)S(1)} %get-tuple-element.32), channel_id=1, source_target_pairs={{0,2},{2,0},{4,6},{6,4},{8,10},{10,8},{12,14},{14,12},{16,18},{18,... | collective-permute-start | bytes 2752520 | tf_op jit(solution)/shard_map/ppermute | solution.py:35
  44.7 18.4 %collective-permute-start.12 = (bf16[256,1792]{1,0:T(8,128)(2,1)S(1)}, bf16[256,1792]{1,0:T(8,128)(2,1)S(1)}, u32[]{:S(2)}, u32[]{:S(2)}) collective-permute-start(bf16[256,1792]{1,0:T(8,128)(2,1)S(1)} %get-tuple-element.33), channel_id=1, source_target_pairs={{0,4},{2,6},{4,0},{6,2},{8,12},{10,14},{12,8},{14,10},{16,20},{18,... | collective-permute-start | bytes 2752520 | tf_op jit(solution)/shard_map/ppermute | solution.py:35
  53.6 16.6 %collective-permute-start.9 = (bf16[512,896]{1,0:T(8,128)(2,1)S(1)}, bf16[512,896]{1,0:T(8,128)(2,1)S(1)}, u32[]{:S(2)}, u32[]{:S(2)}) collective-permute-start(bf16[512,896]{1,0:T(8,128)(2,1)S(1)} %pad_maximum_fusion.1), channel_id=1, source_target_pairs={{8,16},{10,18},{12,20},{14,22},{16,8},{18,10},{20,12},{22,14},{9,1... | collective-permute-start | bytes 2752520 | tf_op jit(solution)/shard_map/ppermute | solution.py:41
  59.4 20.9 %collective-permute-start.11 = (bf16[512,896]{1,0:T(8,128)(2,1)S(1)}, bf16[512,896]{1,0:T(8,128)(2,1)S(1)}, u32[]{:S(2)}, u32[]{:S(2)}) collective-permute-start(bf16[512,896]{1,0:T(8,128)(2,1)S(1)} %maximum_select_fusion), channel_id=1, source_target_pairs={{0,8},{2,10},{4,12},{6,14},{8,0},{10,2},{12,4},{14,6},{16,24},{18,... | collective-permute-start | bytes 2752520 | tf_op jit(solution)/shard_map/ppermute | solution.py:41
  63.2 20.3 %collective-permute-start.13 = (bf16[256,1792]{1,0:T(8,128)(2,1)S(1)}, bf16[256,1792]{1,0:T(8,128)(2,1)S(1)}, u32[]{:S(2)}, u32[]{:S(2)}) collective-permute-start(bf16[256,1792]{1,0:T(8,128)(2,1)S(1)} %get-tuple-element.34), channel_id=1, source_target_pairs={{0,6},{2,4},{4,2},{6,0},{8,14},{10,12},{12,10},{14,8},{16,22},{18,... | collective-permute-start | bytes 2752520 | tf_op jit(solution)/shard_map/ppermute | solution.py:35
  68.1 16.5 %collective-permute-start.15 = (bf16[128,64]{1,0:T(8,128)(2,1)S(1)}, bf16[128,64]{1,0:T(8,128)(2,1)S(1)}, u32[]{:S(2)}, u32[]{:S(2)}) collective-permute-start(bf16[128,64]{1,0:T(8,128)(2,1)S(1)} %all_gather.3), channel_id=1, source_target_pairs={{0,2},{2,0},{4,6},{6,4},{8,10},{10,8},{12,14},{14,12},{16,18},{18,... | collective-permute-start | bytes 49160 | tf_op jit(solution)/shard_map/ppermute | solution.py:35
  68.7 16.0 %collective-permute-start.16 = (bf16[128,64]{1,0:T(8,128)(2,1)S(1)}, bf16[128,64]{1,0:T(8,128)(2,1)S(1)}, u32[]{:S(2)}, u32[]{:S(2)}) collective-permute-start(bf16[128,64]{1,0:T(8,128)(2,1)S(1)} %all_gather.3), channel_id=1, source_target_pairs={{0,4},{2,6},{4,0},{6,2},{8,12},{10,14},{12,8},{14,10},{16,20},{18,... | collective-permute-start | bytes 49160 | tf_op jit(solution)/shard_map/ppermute | solution.py:35
  70.2 14.5 %collective-permute-start.17 = (bf16[128,64]{1,0:T(8,128)(2,1)S(1)}, bf16[128,64]{1,0:T(8,128)(2,1)S(1)}, u32[]{:S(2)}, u32[]{:S(2)}) collective-permute-start(bf16[128,64]{1,0:T(8,128)(2,1)S(1)} %all_gather.3), channel_id=1, source_target_pairs={{0,6},{2,4},{4,2},{6,0},{8,14},{10,12},{12,10},{14,8},{16,22},{18,... | collective-permute-start | bytes 49160 | tf_op jit(solution)/shard_map/ppermute | solution.py:35
  81.2 24.7 %collective-permute-start.14 = (bf16[256,896]{1,0:T(8,128)(2,1)}, bf16[256,896]{1,0:T(8,128)(2,1)}, u32[]{:S(2)}, u32[]{:S(2)}) collective-permute-start(bf16[256,896]{1,0:T(8,128)(2,1)} %get-tuple-element.37), channel_id=1, source_target_pairs={{8,16},{10,18},{12,20},{14,22},{16,8},{18,10},{20,12},{22,14},{9,1... | collective-permute-start | bytes 1376264 | tf_op jit(solution)/shard_map/ppermute | solution.py:41
  84.7 21.2 %collective-permute-start.18 = (bf16[256,896]{1,0:T(8,128)(2,1)}, bf16[256,896]{1,0:T(8,128)(2,1)}, u32[]{:S(2)}, u32[]{:S(2)}) collective-permute-start(bf16[256,896]{1,0:T(8,128)(2,1)} %get-tuple-element.39), channel_id=1, source_target_pairs={{0,8},{2,10},{4,12},{6,14},{8,0},{10,2},{12,4},{14,6},{16,24},{18,... | collective-permute-start | bytes 1376264 | tf_op jit(solution)/shard_map/ppermute | solution.py:41
  106.1 14.1 %collective-permute-start.29 = (bf16[256,896]{1,0:T(8,128)(2,1)S(1)}, bf16[256,896]{1,0:T(8,128)(2,1)S(1)}, u32[]{:S(2)}, u32[]{:S(2)}) collective-permute-start(bf16[256,896]{1,0:T(8,128)(2,1)S(1)} %copy-done.33), channel_id=1, source_target_pairs={{8,16},{10,18},{12,20},{14,22},{16,8},{18,10},{20,12},{22,14},{9,1... | collective-permute-start | bytes 1376264 | tf_op jit(solution)/shard_map/ppermute | solution.py:41
  110.1 20.2 %collective-permute-start.22 = (bf16[64,3072]{1,0:T(8,128)(2,1)S(1)}, bf16[64,3072]{1,0:T(8,128)(2,1)S(1)}, u32[]{:S(2)}, u32[]{:S(2)}) collective-permute-start(bf16[64,3072]{1,0:T(8,128)(2,1)S(1)} %get-tuple-element.67), channel_id=1, source_target_pairs={{0,6},{2,4},{4,2},{6,0},{8,14},{10,12},{12,10},{14,8},{16,22},{18,... | collective-permute-start | bytes 1179656 | tf_op jit(solution)/shard_map/ppermute | solution.py:35
  110.4 19.9 %collective-permute-start.21 = (bf16[64,3072]{1,0:T(8,128)(2,1)S(1)}, bf16[64,3072]{1,0:T(8,128)(2,1)S(1)}, u32[]{:S(2)}, u32[]{:S(2)}) collective-permute-start(bf16[64,3072]{1,0:T(8,128)(2,1)S(1)} %get-tuple-element.68), channel_id=1, source_target_pairs={{0,4},{2,6},{4,0},{6,2},{8,12},{10,14},{12,8},{14,10},{16,20},{18,... | collective-permute-start | bytes 1179656 | tf_op jit(solution)/shard_map/ppermute | solution.py:35
  110.4 19.9 %collective-permute-start.20 = (bf16[64,3072]{1,0:T(8,128)(2,1)S(1)}, bf16[64,3072]{1,0:T(8,128)(2,1)S(1)}, u32[]{:S(2)}, u32[]{:S(2)}) collective-permute-start(bf16[64,3072]{1,0:T(8,128)(2,1)S(1)} %get-tuple-element.66), channel_id=1, source_target_pairs={{0,2},{2,0},{4,6},{6,4},{8,10},{10,8},{12,14},{14,12},{16,18},{18,... | collective-permute-start | bytes 1179656 | tf_op jit(solution)/shard_map/ppermute | solution.py:35
  134.8 22.4 %collective-permute-start.24 = (bf16[64,1792]{1,0:T(8,128)(2,1)S(1)}, bf16[64,1792]{1,0:T(8,128)(2,1)S(1)}, u32[]{:S(2)}, u32[]{:S(2)}) collective-permute-start(bf16[64,1792]{1,0:T(8,128)(2,1)S(1)} %get-tuple-element.91), channel_id=1, source_target_pairs={{0,16},{2,18},{4,20},{6,22},{8,24},{10,26},{12,28},{14,30},{16,0},... | collective-permute-start | bytes 688136 | tf_op jit(solution)/shard_map/ppermute | solution.py:41
  136.6 20.7 %collective-permute-start.23 = (bf16[64,1792]{1,0:T(8,128)(2,1)S(1)}, bf16[64,1792]{1,0:T(8,128)(2,1)S(1)}, u32[]{:S(2)}, u32[]{:S(2)}) collective-permute-start(bf16[64,1792]{1,0:T(8,128)(2,1)S(1)} %get-tuple-element.91), channel_id=1, source_target_pairs={{0,8},{2,10},{4,12},{6,14},{8,0},{10,2},{12,4},{14,6},{16,24},{18,... | collective-permute-start | bytes 688136 | tf_op jit(solution)/shard_map/ppermute | solution.py:41
  139.4 20.4 %collective-permute-start.33 = (bf16[64,3072]{1,0:T(8,128)(2,1)S(1)}, bf16[64,3072]{1,0:T(8,128)(2,1)S(1)}, u32[]{:S(2)}, u32[]{:S(2)}) collective-permute-start(bf16[64,3072]{1,0:T(8,128)(2,1)S(1)} %get-tuple-element.64), channel_id=1, source_target_pairs={{0,6},{2,4},{4,2},{6,0},{8,14},{10,12},{12,10},{14,8},{16,22},{18,... | collective-permute-start | bytes 1179656 | tf_op jit(solution)/shard_map/ppermute | solution.py:35
  140.1 20.9 %collective-permute-start.32 = (bf16[64,3072]{1,0:T(8,128)(2,1)S(1)}, bf16[64,3072]{1,0:T(8,128)(2,1)S(1)}, u32[]{:S(2)}, u32[]{:S(2)}) collective-permute-start(bf16[64,3072]{1,0:T(8,128)(2,1)S(1)} %get-tuple-element.65), channel_id=1, source_target_pairs={{0,4},{2,6},{4,0},{6,2},{8,12},{10,14},{12,8},{14,10},{16,20},{18,... | collective-permute-start | bytes 1179656 | tf_op jit(solution)/shard_map/ppermute | solution.py:35
  143.1 17.9 %collective-permute-start.31 = (bf16[64,3072]{1,0:T(8,128)(2,1)S(1)}, bf16[64,3072]{1,0:T(8,128)(2,1)S(1)}, u32[]{:S(2)}, u32[]{:S(2)}) collective-permute-start(bf16[64,3072]{1,0:T(8,128)(2,1)S(1)} %get-tuple-element.63), channel_id=1, source_target_pairs={{0,2},{2,0},{4,6},{6,4},{8,10},{10,8},{12,14},{14,12},{16,18},{18,... | collective-permute-start | bytes 1179656 | tf_op jit(solution)/shard_map/ppermute | solution.py:35
  159.8 18.7 %collective-permute-start.26 = (bf16[64,1024]{1,0:T(8,128)(2,1)S(1)}, bf16[64,1024]{1,0:T(8,128)(2,1)S(1)}, u32[]{:S(2)}, u32[]{:S(2)}) collective-permute-start(bf16[64,1024]{1,0:T(8,128)(2,1)S(1)} %get-tuple-element.42), channel_id=1, source_target_pairs={{0,8},{2,10},{4,12},{6,14},{8,0},{10,2},{12,4},{14,6},{16,24},{18,... | collective-permute-start | bytes 393224 | tf_op jit(solution)/shard_map/ppermute | solution.py:41
  164.9 13.6 %collective-permute-start.37 = (bf16[64,1024]{1,0:T(8,128)(2,1)S(1)}, bf16[64,1024]{1,0:T(8,128)(2,1)S(1)}, u32[]{:S(2)}, u32[]{:S(2)}) collective-permute-start(bf16[64,1024]{1,0:T(8,128)(2,1)S(1)} %get-tuple-element.50), channel_id=1, source_target_pairs={{0,24},{2,26},{4,28},{6,30},{24,0},{26,2},{28,4},{30,6},{1,25},{3,... | collective-permute-start | bytes 393224 | tf_op jit(solution)/shard_map/ppermute | solution.py:41
  (54 other events, 507.9 us)
